TPU v7x, 256 devices: a whole 4x4x8 slice. The times are simulated.
256 devices in a mesh: dp: 2 (over x_hi), lat: 8 (over y, core), lon: 16 (over z, x_lo).
Axes of the slice: x: 4 (x_hi: 2, x_lo: 2; x = x_hi * 2 + x_lo), y: 4, z: 8, core: 2. Of those that a mesh axis runs over, the one named last changes fastest.
Arguments:
- state: float32 [2, 256, 512, 384], P('dp', 'lat', 'lon'), may hold values from -6 to 6
- cotangent: float32 [2, 256, 512, 384], P('dp', 'lat', 'lon'), may hold values from -6 to 6
- counts: int32 [32, 64], P('lat', 'lon'), may hold values from 0 to 64, as said below
- dw_kernel: float32 [1, 49, 384], replicated, may hold values from -0.875 to 0.875
- dw_bias: float32 [1, 384], replicated, may hold values from -3 to 3
- norm_gain: float32 [1, 384], replicated, may hold values from 0.1 to 1.9
- norm_bias: float32 [1, 384], replicated, may hold values from -3 to 3
- w_expand: bfloat16 [1, 1536, 384], replicated, may hold values from -0.3125 to 0.3125
- b_expand: float32 [1, 1536], replicated, may hold values from -3 to 3
- w_reduce: bfloat16 [1, 1536, 384], replicated, may hold values from -0.15625 to 0.15625
Outputs:
- grad_state: float32 [2, 256, 512, 384], P('dp', 'lat', 'lon')
- grad_expand: float32 [1, 1536, 384], P(None, ('dp', 'lat', 'lon'))
- grad_reduce: float32 [1, 1536, 384], P(None, ('dp', 'lat', 'lon'))
Inputs may be any that keep to these rules, and one draw needn't show every extreme that they name: `counts`: A tile with count 0 is land. In the tiles of the devices of one lat index (4 x 64 tiles) at most 192 have a positive count, and some such band reaches that number.
All inputs are finite; a program needn't handle non-finite values.
Results may differ from a plain program's by a relative error of at most 0.0056.
Values may be sent and summed in bfloat16 or wider, within the bound.
No kernel may reach another device: no remote copies, remote signals or barrier semaphores. Data moves between devices by JAX's collectives and lax.ppermute only.
A program may use at most 128 MiB of HBM per device.

v0:
```python
import math

import jax
import jax.numpy as jnp
from jax import lax
from jax.sharding import PartitionSpec as P

norm_eps = 1e-06
root_half = 0.7071067811865476
inv_root_two_pi = 0.3989422804014327


def with_halo(cells, sides, width, closed):
    for axis, dim in sides:
        count = lax.axis_size(axis)
        ends = count if closed else count - 1
        head = lax.slice_in_dim(cells, 0, width, axis=dim)
        tail = lax.slice_in_dim(cells, cells.shape[dim] - width, cells.shape[dim], axis=dim)
        cells = jnp.concatenate(
            [
                lax.ppermute(tail, axis, [(i, (i + 1) % count) for i in range(ends)]),
                cells,
                lax.ppermute(head, axis, [((i + 1) % count, i) for i in range(ends)]),
            ],
            axis=dim,
        )
    return cells


def cell_mask(counts, tile_side):
    per_cell = jnp.repeat(jnp.repeat(counts, tile_side, axis=0), tile_side, axis=1)
    row_place = lax.broadcasted_iota(jnp.int32, per_cell.shape, 0) % tile_side
    col_place = lax.broadcasted_iota(jnp.int32, per_cell.shape, 1) % tile_side
    return (row_place * tile_side + col_place < per_cell).astype(jnp.float32)


def pad_rims(grid):
    beside_all = with_halo(grid, (("lon", 1),), 3, True)
    return with_halo(beside_all, (("lat", 0),), 3, False)


def conv_apply(padded, kernel, flipped):
    row_count = padded.shape[-3] - 6
    col_count = padded.shape[-2] - 6
    summed = jnp.zeros(padded.shape[:-3] + (row_count, col_count, padded.shape[-1]), jnp.float32)
    for row_off in range(7):
        for col_off in range(7):
            row_start = 6 - row_off if flipped else row_off
            col_start = 6 - col_off if flipped else col_off
            window = padded[
                ..., row_start : row_start + row_count, col_start : col_start + col_count, :
            ]
            summed = summed + kernel[7 * row_off + col_off] * window
    return summed


def layer_stats(mixed_conv):
    mean_value = jnp.mean(mixed_conv, axis=-1, keepdims=True)
    centred = mixed_conv - mean_value
    inv_spread = lax.rsqrt(jnp.mean(centred * centred, axis=-1, keepdims=True) + norm_eps)
    return (centred * inv_spread, inv_spread)


def norm_backward(grad_normed, unit_conv, inv_spread, gain):
    grad_unit = grad_normed.astype(jnp.float32) * gain
    mean_grad = jnp.mean(grad_unit, axis=-1, keepdims=True)
    mean_cross = jnp.mean(grad_unit * unit_conv, axis=-1, keepdims=True)
    return (grad_unit - mean_grad - unit_conv * mean_cross) * inv_spread


def gelu_value(preact):
    return 0.5 * preact * (1.0 + lax.erf(preact * root_half))


def gelu_slope(preact):
    return 0.5 * (1.0 + lax.erf(preact * root_half)) + preact * inv_root_two_pi * jnp.exp(
        -0.5 * preact * preact
    )


def mlp_forward(normed_rows, expand_weight, expand_bias, reduce_weight):
    preact = jnp.dot(normed_rows, expand_weight.T, preferred_element_type=jnp.float32) + expand_bias
    hidden = gelu_value(preact).astype(jnp.bfloat16)
    branch = jnp.dot(hidden, reduce_weight, preferred_element_type=jnp.float32).astype(jnp.bfloat16)
    return (preact, hidden, branch)


def mlp_backward(normed_rows, preact, hidden, grad_branch, expand_weight, reduce_weight):
    grad_hidden = jnp.dot(grad_branch, reduce_weight.T, preferred_element_type=jnp.float32)
    grad_pre = (grad_hidden * gelu_slope(preact)).astype(jnp.bfloat16)
    grad_normed = jnp.dot(grad_pre, expand_weight, preferred_element_type=jnp.float32).astype(
        jnp.bfloat16
    )
    grad_e = jnp.dot(grad_pre.T, normed_rows, preferred_element_type=jnp.float32)
    grad_r = jnp.dot(hidden.T, grad_branch, preferred_element_type=jnp.float32)
    return (grad_normed, grad_e, grad_r)


def local(
    state, cotangent, counts, dw_kernel, dw_bias, norm_gain, norm_bias, w_expand, b_expand, w_reduce
):
    current = state[0]
    row_count, col_count, channels = current.shape
    tile_side = row_count // counts.shape[0]
    wet_cells = cell_mask(counts, tile_side)[:, :, None]
    layer_total = dw_kernel.shape[0]
    layer_index = 0
    mixed_conv = conv_apply(pad_rims(current), dw_kernel[layer_index], False) + dw_bias[layer_index]
    unit_conv, inv_spread = layer_stats(mixed_conv)
    normed = (unit_conv * norm_gain[layer_index] + norm_bias[layer_index]).astype(jnp.bfloat16)
    work_rows = normed.reshape(-1, channels)
    preact, hidden, branch = mlp_forward(
        work_rows, w_expand[layer_index], b_expand[layer_index], w_reduce[layer_index]
    )
    stored = [(unit_conv, inv_spread, work_rows, preact, hidden)]
    gradient = cotangent[0]
    grads_e = [None] * layer_total
    grads_r = [None] * layer_total
    for layer_index in reversed(range(layer_total)):
        unit_conv, inv_spread, work_rows, preact, hidden = stored[layer_index]
        masked = gradient * wet_cells
        grad_branch = masked.astype(jnp.bfloat16)
        grad_rows = grad_branch.reshape(-1, channels)
        grad_normed, grad_e, grad_r = mlp_backward(
            work_rows, preact, hidden, grad_rows, w_expand[layer_index], w_reduce[layer_index]
        )
        normed_grid = grad_normed.reshape(row_count, col_count, channels)
        grad_conv = norm_backward(normed_grid, unit_conv, inv_spread, norm_gain[layer_index])
        gradient = masked + conv_apply(pad_rims(grad_conv), dw_kernel[layer_index], True)
        grads_e[layer_index] = grad_e
        grads_r[layer_index] = grad_r
    stacked_e = jnp.stack(grads_e)
    stacked_r = jnp.stack(grads_r)
    shares = (
        lax.psum_scatter(stacked_e, ("dp", "lat", "lon"), scatter_dimension=1, tiled=True),
        lax.psum_scatter(stacked_r, ("dp", "lat", "lon"), scatter_dimension=1, tiled=True),
    )
    cell_total = (
        lax.axis_size("dp") * lax.axis_size("lat") * lax.axis_size("lon") * row_count * col_count
    )
    grad_scale = 1.0 / math.sqrt(cell_total)
    return (gradient[None], shares[0] * grad_scale, shares[1] * grad_scale)


def solution(mesh):
    in_specs = (
        P("dp", "lat", "lon", None),
        P("dp", "lat", "lon", None),
        P("lat", "lon"),
        P(),
        P(),
        P(),
        P(),
        P(),
        P(),
        P(),
    )
    out_specs = (
        P("dp", "lat", "lon", None),
        P(None, ("dp", "lat", "lon"), None),
        P(None, ("dp", "lat", "lon"), None),
    )
    return jax.shard_map(local, mesh=mesh, in_specs=in_specs, out_specs=out_specs, check_vma=False)
```

profile of v0, /device:TPU:32, one launch (start us, length us, event | category | flops | bytes accessed | tf_op | source)
XLA Modules:
  0.0 383.6 jit_solution(17208669039424007620)
XLA Ops:
  7.2 1.3 fusion.141
  8.5 1.6 collective-permute-start
  10.1 1.4 collective-permute-start.1
  11.5 0.8 copy.30
  13.3 2.5 multiply_convert_fusion.4
  15.9 2.6 fusion.128
  19.7 1.3 reduce.52
  21.6 1.6 slice_reduce_fusion.48
  23.3 1.3 collective-permute-start.2
  24.6 1.5 collective-permute-start.3
  26.7 3.0 collective-permute-done.3
  30.6 16.7 %fusion.138 = (f32[32,32]{1,0:T(8,128)S(1)}, f32[32,32,384]{2,1,0:T(8,128)S(1)}) fusion(f32[384]{0:T(512)S(1)} %copy-done.102, f32[35,38,384]{2,1,0:T(8,128)S(1)} %get-tuple-element.70, f32[384]{0:T(512)S(1)} %get-tuple-element.59, f32[384]{0:T(512)S(1)} %get-tuple-element.60, f32[384]{0:T(512)S(1)} %get-tuple-element.13, f32[384]{0:T(512)S(1)} %get-tuple-element.14, ...), kind=kLoop, calls=%fused_computation.328 | loop fusion | flops 41286656 | bytes 69581824 | tf_op jit(solution)/shard_map/reduce_sum | solution.py:58
  48.6 1.8 fusion.131
  50.4 3.4 fusion.4
  53.9 2.9 multiply_reduce_fusion.1
  57.4 1.4 div.17
  58.8 2.1 multiply_reduce_fusion
  60.9 2.2 subtract_multiply_fusion
  63.2 0.7 collective-permute-start.4
  63.8 2.3 collective-permute-start.5
  66.2 3.1 fusion.8
  69.9 5.1 %collective-permute-done.5 = f32[32,3,384]{2,1,0:T(4,128)S(1)} collective-permute-done((f32[32,3,384]{2,1,0:T(4,128)S(1)}, f32[32,3,384]{2,1,0:T(4,128)S(1)}, u32[]{:S(2)}, u32[]{:S(2)}) %collective-permute-start.5) | collective-permute-done | bytes 147488 | tf_op jit(solution)/shard_map/ppermute | solution.py:23
  75.0 1.3 collective-permute-start.6
  76.3 4.2 %collective-permute-start.7 = (f32[3,38,384]{2,1,0:T(8,128)S(1)}, f32[3,38,384]{2,1,0:T(8,128)}, u32[]{:S(2)}, u32[]{:S(2)}) collective-permute-start(f32[3,38,384]{2,1,0:T(8,128)S(1)} %get-tuple-element.68), channel_id=1, source_target_pairs={{0,16},{16,32},{32,48},{48,64},{64,80},{80,96},{96,112},{1,17},{17... | collective-permute-start | bytes 525320 | tf_op jit(solution)/shard_map/ppermute | solution.py:21
  80.5 1.9 convolution_bitcast_fusion
  82.4 8.3 %copy.36 = f32[1,1536,384]{2,0,1:T(1,128)} copy(f32[1,1536,384]{2,1,0:T(8,128)S(1)} %fusion.8) | data formatting | bytes 4718592 | tf_op jit(solution)/shard_map/stack | solution.py:133
  90.6 8.1 %copy.33 = f32[1,1536,384]{2,0,1:T(1,128)} copy(f32[1,1536,384]{2,1,0:T(8,128)S(1)} %convolution_bitcast_fusion) | data formatting | bytes 4718592 | tf_op jit(solution)/shard_map/stack | solution.py:132
  99.9 2.4 pad_maximum_fusion.1
  102.7 15.2 %fusion.81 = f32[1,32,32,384]{3,2,1,0:T(8,128)} fusion(f32[35,38,384]{2,1,0:T(8,128)S(1)} %get-tuple-element.66, f32[1,32,32,384]{3,2,1,0:T(8,128)} %param.11, f32[32,32,384]{2,1,0:T(8,128)} %copy-done.1, f32[32,3,384]{2,1,0:T(4,128)S(1)} %collective-permute-done.4, f32[32,3,384]{2,1,0:T(4,128)S(1)} %collective-permute-done.5, ...), kind=kLoop, calls=%fused_computation.106 | loop fusion | flops 41287680 | bytes 71153152 | tf_op jit(solution)/shard_map/broadcast_in_dim | solution.py:142
  117.9 256.2 %all-reduce.5.cloned.1.call-done = (f32[1,1536,384]{2,0,1:T(1,128)}, f32[1,1536,384]{2,0,1:T(1,128)}) async-done(((f32[1,1536,384]{2,0,1:T(1,128)}, f32[1,1536,384]{2,0,1:T(1,128)}), (f32[1,1536,384]{2,0,1:T(1,128)}, f32[1,1536,384]{2,0,1:T(1,128)})) %all-reduce.5.cloned.1.call-update) | async-done | bytes 4718608
  374.1 1.3 dynamic-slice_multiply_fusion.1
  375.4 1.3 dynamic-slice_multiply_fusion
  (260 shorter events, 7.1 us)
Async XLA Ops:
  7.2 41.4 %copy-start = (bf16[1,1536,384]{2,1,0:T(8,128)(2,1)S(1)}, bf16[1,1536,384]{2,1,0:T(8,128)(2,1)}, u32[]{:S(2)}) copy-start(bf16[1,1536,384]{2,1,0:T(8,128)(2,1)} %param.17) | copy-start | bytes 3538948
  7.2 366.9 %all-reduce.5.cloned.1.call-start = ((), (), s32[]{:S(2)}) async-start(), calls=%async_computation | async-start | bytes 9437184
  8.5 14.7 %collective-permute-start = (f32[32,3,384]{2,1,0:T(4,128)S(1)}, f32[32,3,384]{2,1,0:T(4,128)S(1)}, u32[]{:S(2)}, u32[]{:S(2)}) collective-permute-start(f32[32,3,384]{2,1,0:T(4,128)S(1)} %get-tuple-element.75), channel_id=1, source_target_pairs={{0,1},{1,2},{2,3},{3,4},{4,5},{5,6},{6,7},{7,8},{8,9},{9,10},{10,1... | collective-permute-start | bytes 442376 | tf_op jit(solution)/shard_map/ppermute | solution.py:21
  10.1 13.2 %collective-permute-start.1 = (f32[32,3,384]{2,1,0:T(4,128)S(1)}, f32[32,3,384]{2,1,0:T(4,128)S(1)}, u32[]{:S(2)}, u32[]{:S(2)}) collective-permute-start(f32[32,3,384]{2,1,0:T(4,128)S(1)} %get-tuple-element.76), channel_id=1, source_target_pairs={{1,0},{2,1},{3,2},{4,3},{5,4},{6,5},{7,6},{8,7},{9,8},{10,9},{11,1... | collective-permute-start | bytes 442376 | tf_op jit(solution)/shard_map/ppermute | solution.py:23
  15.8 7.4 %copy-start.2 = (f32[1,32,32,384]{3,2,1,0:T(8,128)S(1)}, f32[1,32,32,384]{3,2,1,0:T(8,128)}, u32[]{:S(2)}) copy-start(f32[1,32,32,384]{3,2,1,0:T(8,128)} %param.10) | copy-start | bytes 4718596
  15.9 5.1 %copy-start.105 = (f32[1,1536]{1,0:T(1,128)S(1)}, f32[1,1536]{1,0:T(1,128)}, u32[]{:S(2)}) copy-start(f32[1,1536]{1,0:T(1,128)} %param.18) | copy-start | bytes 18436
  21.6 4.5 %copy-start.11 = (f32[1,49,384]{2,0,1:T(1,128)S(1)}, f32[1,49,384]{2,0,1:T(1,128)}, u32[]{:S(2)}) copy-start(f32[1,49,384]{2,0,1:T(1,128)} %param.13) | copy-start | bytes 225796
  23.2 6.9 %copy-start.13 = (f32[384]{0:T(512)}, f32[384]{0:T(512)S(1)}, u32[]{:S(2)}) copy-start(f32[384]{0:T(512)S(1)} %get-tuple-element.12) | copy-start | bytes 4612
  23.2 6.9 %copy-start.15 = (f32[384]{0:T(512)}, f32[384]{0:T(512)S(1)}, u32[]{:S(2)}) copy-start(f32[384]{0:T(512)S(1)} %get-tuple-element.13) | copy-start | bytes 4612
  23.2 6.9 %copy-start.17 = (f32[384]{0:T(512)}, f32[384]{0:T(512)S(1)}, u32[]{:S(2)}) copy-start(f32[384]{0:T(512)S(1)} %get-tuple-element.14) | copy-start | bytes 4612
  23.2 6.9 %copy-start.19 = (f32[384]{0:T(512)}, f32[384]{0:T(512)S(1)}, u32[]{:S(2)}) copy-start(f32[384]{0:T(512)S(1)} %get-tuple-element.15) | copy-start | bytes 4612
  23.2 6.9 %copy-start.21 = (f32[384]{0:T(512)}, f32[384]{0:T(512)S(1)}, u32[]{:S(2)}) copy-start(f32[384]{0:T(512)S(1)} %get-tuple-element.16) | copy-start | bytes 4612
  23.2 6.9 %copy-start.23 = (f32[384]{0:T(512)}, f32[384]{0:T(512)S(1)}, u32[]{:S(2)}) copy-start(f32[384]{0:T(512)S(1)} %get-tuple-element.17) | copy-start | bytes 4612
  23.2 6.9 %copy-start.25 = (f32[384]{0:T(512)}, f32[384]{0:T(512)S(1)}, u32[]{:S(2)}) copy-start(f32[384]{0:T(512)S(1)} %get-tuple-element.18) | copy-start | bytes 4612
  23.3 3.4 collective-permute-start.2
  24.6 5.1 %collective-permute-start.3 = (f32[3,38,384]{2,1,0:T(8,128)S(1)}, f32[3,38,384]{2,1,0:T(8,128)S(1)}, u32[]{:S(2)}, u32[]{:S(2)}) collective-permute-start(f32[3,38,384]{2,1,0:T(8,128)S(1)} %get-tuple-element.72), channel_id=1, source_target_pairs={{16,0},{32,16},{48,32},{64,48},{80,64},{96,80},{112,96},{17,1},{33... | collective-permute-start | bytes 525320 | tf_op jit(solution)/shard_map/ppermute | solution.py:23
  26.2 4.0 %copy-start.53 = (f32[384]{0:T(512)}, f32[384]{0:T(512)S(1)}, u32[]{:S(2)}) copy-start(f32[384]{0:T(512)S(1)} %get-tuple-element.51) | copy-start | bytes 4612
  26.2 4.0 %copy-start.55 = (f32[384]{0:T(512)}, f32[384]{0:T(512)S(1)}, u32[]{:S(2)}) copy-start(f32[384]{0:T(512)S(1)} %get-tuple-element.52) | copy-start | bytes 4612
  26.2 4.0 %copy-start.57 = (f32[384]{0:T(512)}, f32[384]{0:T(512)S(1)}, u32[]{:S(2)}) copy-start(f32[384]{0:T(512)S(1)} %get-tuple-element.53) | copy-start | bytes 4612
  26.2 4.0 %copy-start.59 = (f32[384]{0:T(512)}, f32[384]{0:T(512)S(1)}, u32[]{:S(2)}) copy-start(f32[384]{0:T(512)S(1)} %get-tuple-element.54) | copy-start | bytes 4612
  26.2 4.0 %copy-start.61 = (f32[384]{0:T(512)}, f32[384]{0:T(512)S(1)}, u32[]{:S(2)}) copy-start(f32[384]{0:T(512)S(1)} %get-tuple-element.55) | copy-start | bytes 4612
  26.2 4.0 %copy-start.63 = (f32[384]{0:T(512)}, f32[384]{0:T(512)S(1)}, u32[]{:S(2)}) copy-start(f32[384]{0:T(512)S(1)} %get-tuple-element.56) | copy-start | bytes 4612
  26.2 4.0 %copy-start.65 = (f32[384]{0:T(512)}, f32[384]{0:T(512)S(1)}, u32[]{:S(2)}) copy-start(f32[384]{0:T(512)S(1)} %get-tuple-element.57) | copy-start | bytes 4612
  58.8 7.4 %copy-start.4 = (f32[1024,1536]{1,0:T(8,128)S(1)}, f32[1024,1536]{1,0:T(8,128)}, u32[]{:S(2)}) copy-start(f32[1024,1536]{1,0:T(8,128)} %copy-done.3) | copy-start | bytes 18874372
  60.9 5.3 %copy-start.5 = (bf16[1024,384]{1,0:T(8,128)(2,1)S(1)}, bf16[1024,384]{1,0:T(8,128)(2,1)}, u32[]{:S(2)}) copy-start(bf16[1024,384]{1,0:T(8,128)(2,1)} %fusion.128) | copy-start | bytes 2359300
  60.9 5.3 %copy-start.104 = (f32[1536]{0:T(1024)S(1)}, f32[1536]{0:T(1024)}, u32[]{:S(2)}) copy-start(f32[1536]{0:T(1024)} %reduce.53) | copy-start | bytes 18436
  63.1 11.9 %copy-start.1 = (f32[32,32,384]{2,1,0:T(8,128)}, f32[32,32,384]{2,1,0:T(8,128)S(1)}, u32[]{:S(2)}) copy-start(f32[32,32,384]{2,1,0:T(8,128)S(1)} %subtract_multiply_fusion) | copy-start | bytes 4718596
  63.2 6.8 %collective-permute-start.4 = (f32[32,3,384]{2,1,0:T(4,128)S(1)}, f32[32,3,384]{2,1,0:T(4,128)S(1)}, u32[]{:S(2)}, u32[]{:S(2)}) collective-permute-start(f32[32,3,384]{2,1,0:T(4,128)S(1)} %get-tuple-element.73), channel_id=1, source_target_pairs={{0,1},{1,2},{2,3},{3,4},{4,5},{5,6},{6,7},{7,8},{8,9},{9,10},{10,1... | collective-permute-start | bytes 442376 | tf_op jit(solution)/shard_map/ppermute | solution.py:21
  63.8 11.2 %collective-permute-start.5 = (f32[32,3,384]{2,1,0:T(4,128)S(1)}, f32[32,3,384]{2,1,0:T(4,128)S(1)}, u32[]{:S(2)}, u32[]{:S(2)}) collective-permute-start(f32[32,3,384]{2,1,0:T(4,128)S(1)} %get-tuple-element.74), channel_id=1, source_target_pairs={{1,0},{2,1},{3,2},{4,3},{5,4},{6,5},{7,6},{8,7},{9,8},{10,9},{11,1... | collective-permute-start | bytes 442376 | tf_op jit(solution)/shard_map/ppermute | solution.py:23
  66.2 14.4 %copy-start.110 = (bf16[1024,1536]{1,0:T(8,128)(2,1)S(1)}, bf16[1024,1536]{1,0:T(8,128)(2,1)}, u32[]{:S(2)}) copy-start(bf16[1024,1536]{1,0:T(8,128)(2,1)} %copy-done.109) | copy-start | bytes 9437188
  75.0 24.1 %collective-permute-start.6 = (f32[3,38,384]{2,1,0:T(8,128)S(1)}, f32[3,38,384]{2,1,0:T(8,128)S(1)}, u32[]{:S(2)}, u32[]{:S(2)}) collective-permute-start(f32[3,38,384]{2,1,0:T(8,128)S(1)} %get-tuple-element.67), channel_id=1, source_target_pairs={{16,0},{32,16},{48,32},{64,48},{80,64},{96,80},{112,96},{17,1},{33... | collective-permute-start | bytes 525320 | tf_op jit(solution)/shard_map/ppermute | solution.py:23
  76.3 23.5 %collective-permute-start.7 = (f32[3,38,384]{2,1,0:T(8,128)S(1)}, f32[3,38,384]{2,1,0:T(8,128)}, u32[]{:S(2)}, u32[]{:S(2)}) collective-permute-start(f32[3,38,384]{2,1,0:T(8,128)S(1)} %get-tuple-element.68), channel_id=1, source_target_pairs={{0,16},{16,32},{32,48},{48,64},{64,80},{80,96},{96,112},{1,17},{17... | collective-permute-start | bytes 525320 | tf_op jit(solution)/shard_map/ppermute | solution.py:21
  (88 other events, 300.5 us)
Sparse Core Ops, SparseCore 0:
  98.9 275.1 all-reduce.4
where the time goes:
time: 387 us; the launch traced here: 384 us
  waiting for transfers between devices  265 us (68%)
  other arithmetic  51.3 us (13%)
  local copies, waits for them, and re-layouts  24.1 us (6%)
  between operations  15.8 us (4%)
  starting transfers between devices  14.3 us (4%)
  matrix products  13.2 us (3%)
    unnamed x2, waiting for transfers between devices  256 us
    reduce_sum x1, other arithmetic, layer_stats(): mean_value = jnp.mean(mixed_conv, axis=-1, keepdims=True)  16.7 us
    broadcast_in_dim x1, other arithmetic, local(): return (gradient[None], shares[0] * grad_scale, shares[1] * grad_scale)  15.2 us
    another operation x1, local copies, waits for them, and re-layouts, local(): stacked_r = jnp.stack(grads_r)  8.25 us
    another operation x1, local copies, waits for them, and re-layouts, local(): stacked_e = jnp.stack(grads_e)  8.13 us
    ppermute x4, waiting for transfers between devices, with_halo(): lax.ppermute(head, axis, [((i + 1) % count, i) for i in range(ends)])  8.12 us
  transfers between devices with their start and end apart: 9, of which 4 were waited for; matrix products, arithmetic and copies ran while one was open for 13% of the time, Pallas kernels for 0%

commit v1 on v0

--- a/solution.py
+++ b/solution.py
@@ -1,3 +1,4 @@
+import itertools
 import math
 
 import jax
@@ -28,10 +29,12 @@
 
 
 def cell_mask(counts, tile_side):
-    per_cell = jnp.repeat(jnp.repeat(counts, tile_side, axis=0), tile_side, axis=1)
-    row_place = lax.broadcasted_iota(jnp.int32, per_cell.shape, 0) % tile_side
-    col_place = lax.broadcasted_iota(jnp.int32, per_cell.shape, 1) % tile_side
-    return (row_place * tile_side + col_place < per_cell).astype(jnp.float32)
+    tile_rows, tile_cols = counts.shape
+    shape = (tile_rows, tile_side, tile_cols, tile_side)
+    row_place = lax.broadcasted_iota(jnp.int32, shape, 1)
+    col_place = lax.broadcasted_iota(jnp.int32, shape, 3)
+    wet = (row_place * tile_side + col_place < counts[:, None, :, None]).astype(jnp.float32)
+    return wet.reshape(tile_rows * tile_side, tile_cols * tile_side)
 
 
 def pad_rims(grid):
@@ -96,6 +99,77 @@
     return (grad_normed, grad_e, grad_r)
 
 
+every_axis = ("dp", "lat", "lon")
+
+
+def device_pairs(move):
+    def flat(hi, y, core, z, lo):
+        return (hi * 8 + y * 2 + core) * 16 + z * 2 + lo
+
+    found = []
+    for hi, y, core, z, lo in itertools.product(range(2), range(4), range(2), range(8), range(2)):
+        found.append((flat(hi, y, core, z, lo), flat(*move(hi, y, core, z, lo))))
+    return found
+
+
+def plane_pairs(step, first):
+    def move(hi, y, core, z, lo):
+        if (core == 0) == first:
+            return (hi, (y + step) % 4, core, z, lo)
+        x = (2 * hi + lo + step) % 4
+        return (x // 2, y, core, z, x % 2)
+
+    return device_pairs(move)
+
+
+def scatter_direct(rows, place, pairs_of):
+    size = rows.shape[0] // 4
+    narrow = rows.astype(jnp.bfloat16)
+    total = lax.dynamic_slice_in_dim(rows, place * size, size, 0)
+    arrived = [
+        lax.ppermute(
+            lax.dynamic_slice_in_dim(narrow, ((place + step) % 4) * size, size, 0),
+            every_axis,
+            pairs_of(step),
+        )
+        for step in range(1, 4)
+    ]
+    for part in arrived:
+        total = total + part.astype(jnp.float32)
+    return total
+
+
+def scatter_halving(rows, z):
+    for bit in (4, 2, 1):
+        size = rows.shape[0] // 2
+        upper = (z // bit) % 2
+        arrived = lax.ppermute(
+            lax.dynamic_slice_in_dim(rows, (1 - upper) * size, size, 0),
+            every_axis,
+            device_pairs(lambda hi, y, core, z, lo, bit=bit: (hi, y, core, z ^ bit, lo)),
+        )
+        rows = lax.dynamic_slice_in_dim(rows, upper * size, size, 0) + arrived
+    return rows
+
+
+def scatter_rows(mine, arrived):
+    lat, lon = lax.axis_index("lat"), lax.axis_index("lon")
+    y, core, z, lo = lat // 2, lat % 2, lon // 2, lon % 2
+    x = 2 * lax.axis_index("dp") + lo
+    rows = mine + arrived.astype(jnp.float32)
+    rows = scatter_direct(rows, jnp.where(core == 0, y, x), lambda step: plane_pairs(step, True))
+    rows = scatter_direct(rows, jnp.where(core == 0, x, y), lambda step: plane_pairs(step, False))
+    return scatter_halving(rows, z)
+
+
+def arrange_rows(rows):
+    width = rows.shape[1]
+    parts = rows.reshape(2, 4, 2, 8, 2, -1, width)
+    first = parts[:, :, 0].transpose(1, 0, 3, 2, 4, 5)
+    second = parts[:, :, 1].transpose(0, 3, 1, 2, 4, 5)
+    return jnp.concatenate([first.reshape(-1, width), second.reshape(-1, width)])
+
+
 def local(
     state, cotangent, counts, dw_kernel, dw_bias, norm_gain, norm_bias, w_expand, b_expand, w_reduce
 ):
@@ -103,43 +177,39 @@
     row_count, col_count, channels = current.shape
     tile_side = row_count // counts.shape[0]
     wet_cells = cell_mask(counts, tile_side)[:, :, None]
-    layer_total = dw_kernel.shape[0]
-    layer_index = 0
-    mixed_conv = conv_apply(pad_rims(current), dw_kernel[layer_index], False) + dw_bias[layer_index]
+    expand_weight = arrange_rows(w_expand[0])
+    reduce_weight = arrange_rows(w_reduce[0])
+    expand_bias = arrange_rows(b_expand[0][:, None])[:, 0]
+    masked = cotangent[0] * wet_cells
+    grad_rows = masked.astype(jnp.bfloat16).reshape(-1, channels)
+    mixed_conv = conv_apply(pad_rims(current), dw_kernel[0], False) + dw_bias[0]
     unit_conv, inv_spread = layer_stats(mixed_conv)
-    normed = (unit_conv * norm_gain[layer_index] + norm_bias[layer_index]).astype(jnp.bfloat16)
+    normed = (unit_conv * norm_gain[0] + norm_bias[0]).astype(jnp.bfloat16)
     work_rows = normed.reshape(-1, channels)
-    preact, hidden, branch = mlp_forward(
-        work_rows, w_expand[layer_index], b_expand[layer_index], w_reduce[layer_index]
-    )
-    stored = [(unit_conv, inv_spread, work_rows, preact, hidden)]
-    gradient = cotangent[0]
-    grads_e = [None] * layer_total
-    grads_r = [None] * layer_total
-    for layer_index in reversed(range(layer_total)):
-        unit_conv, inv_spread, work_rows, preact, hidden = stored[layer_index]
-        masked = gradient * wet_cells
-        grad_branch = masked.astype(jnp.bfloat16)
-        grad_rows = grad_branch.reshape(-1, channels)
-        grad_normed, grad_e, grad_r = mlp_backward(
-            work_rows, preact, hidden, grad_rows, w_expand[layer_index], w_reduce[layer_index]
-        )
-        normed_grid = grad_normed.reshape(row_count, col_count, channels)
-        grad_conv = norm_backward(normed_grid, unit_conv, inv_spread, norm_gain[layer_index])
-        gradient = masked + conv_apply(pad_rims(grad_conv), dw_kernel[layer_index], True)
-        grads_e[layer_index] = grad_e
-        grads_r[layer_index] = grad_r
-    stacked_e = jnp.stack(grads_e)
-    stacked_r = jnp.stack(grads_r)
-    shares = (
-        lax.psum_scatter(stacked_e, ("dp", "lat", "lon"), scatter_dimension=1, tiled=True),
-        lax.psum_scatter(stacked_r, ("dp", "lat", "lon"), scatter_dimension=1, tiled=True),
-    )
+    preact = jnp.dot(work_rows, expand_weight.T, preferred_element_type=jnp.float32) + expand_bias
+    hidden = gelu_value(preact).astype(jnp.bfloat16)
+    grad_hidden = jnp.dot(grad_rows, reduce_weight.T, preferred_element_type=jnp.float32)
+    grad_pre = (grad_hidden * gelu_slope(preact)).astype(jnp.bfloat16)
+    grad_e = jnp.dot(grad_pre.T, work_rows, preferred_element_type=jnp.float32)
+    grad_r = jnp.dot(hidden.T, grad_rows, preferred_element_type=jnp.float32)
+    grads = jnp.concatenate([grad_e, grad_r], axis=1)
+    core = lax.axis_index("lat") % 2
+    half = grads.shape[0] // 2
+    send = lax.dynamic_slice_in_dim(grads, (1 - core) * half, half, 0).astype(jnp.bfloat16)
+    arrived = lax.ppermute(send, "lat", [(i, i ^ 1) for i in range(8)])
+    mine = lax.dynamic_slice_in_dim(grads, core * half, half, 0)
+    grad_normed = jnp.dot(grad_pre, expand_weight, preferred_element_type=jnp.float32).astype(
+        jnp.bfloat16
+    )
+    normed_grid = grad_normed.reshape(row_count, col_count, channels)
+    grad_conv = norm_backward(normed_grid, unit_conv, inv_spread, norm_gain[0])
+    gradient = masked + conv_apply(pad_rims(grad_conv), dw_kernel[0], True)
+    kept = scatter_rows(mine, arrived)
     cell_total = (
         lax.axis_size("dp") * lax.axis_size("lat") * lax.axis_size("lon") * row_count * col_count
     )
-    grad_scale = 1.0 / math.sqrt(cell_total)
-    return (gradient[None], shares[0] * grad_scale, shares[1] * grad_scale)
+    kept = kept * (1.0 / math.sqrt(cell_total))
+    return (gradient[None], kept[None, :, :channels], kept[None, :, channels:])
 
 
 def solution(mesh):

time: 387 us -> 171 us (0.44)
  the two profiles are of different devices: /device:TPU:32 before, /device:TPU:38 now
where the time goes in v1:
time: 171 us
  starting transfers between devices  43.7 us (26%)
  other arithmetic  38.6 us (23%)
  local copies, waits for them, and re-layouts  37.2 us (22%)
  waiting for transfers between devices  32.8 us (19%)
  matrix products  16 us (9%)
  between operations  2.19 us (1%)
    ppermute x3, starting transfers between devices, scatter_halving(): lax.ppermute(lax.dynamic_slice_in_dim(rows, (1 - upper) * size, size, 0),...  19.3 us
    ppermute x6, waiting for transfers between devices, scatter_direct(): lax.ppermute(lax.dynamic_slice_in_dim(narrow, (place + step) % 4 * size,...  17.1 us
    ppermute x3, waiting for transfers between devices, scatter_halving(): lax.ppermute(lax.dynamic_slice_in_dim(rows, (1 - upper) * size, size, 0),...  15.7 us
    broadcast_in_dim x1, other arithmetic, local(): return (gradient[None], kept[None, :, :channels], kept[None, :, channels:])  12.6 us
    reduce_sum x1, other arithmetic, layer_stats(): mean_value = jnp.mean(mixed_conv, axis=-1, keepdims=True)  12.5 us
    ppermute x4, starting transfers between devices, with_halo(): lax.ppermute(tail, axis, [(i, (i + 1) % count) for i in range(ends)])  10.5 us
    ppermute x6, starting transfers between devices, scatter_direct(): lax.ppermute(lax.dynamic_slice_in_dim(narrow, (place + step) % 4 * size,...  9.06 us
    unnamed x173, local copies, waits for them, and re-layouts  7.14 us
  transfers between devices with their start and end apart: 18, of which 7 were waited for; matrix products, arithmetic and copies ran while one was open for 29% of the time, Pallas kernels for 0%

profile of v1, /device:TPU:38, one launch (start us, length us, event | category | flops | bytes accessed | tf_op | source)
XLA Modules:
  0.0 170.6 jit_solution(15670413148972138861)
XLA Ops:
  0.6 2.0 %fusion.146 = (f32[32,3,384]{2,1,0:T(4,128)}, f32[32,3,384]{2,1,0:T(4,128)}) fusion(f32[32,32,384]{2,1,0:T(8,128)} %bitcast.58), kind=kLoop, calls=%fused_computation.356 | loop fusion | bytes 589824 | tf_op jit(solution)/shard_map/slice | solution.py:19
  2.7 2.2 %collective-permute-start = (f32[32,3,384]{2,1,0:T(4,128)}, f32[32,3,384]{2,1,0:T(4,128)S(1)}, u32[]{:S(2)}, u32[]{:S(2)}) collective-permute-start(f32[32,3,384]{2,1,0:T(4,128)} %get-tuple-element.78), channel_id=1, source_target_pairs={{0,1},{1,2},{2,3},{3,4},{4,5},{5,6},{6,7},{7,8},{8,9},{9,10},{10,1... | collective-permute-start | bytes 442376 | tf_op jit(solution)/shard_map/ppermute | solution.py:22
  5.6 1.6 slice_reduce_fusion.48
  11.2 2.2 %reshape_squeeze.6 = bf16[2,4,2,8,2,6,384]{6,5,4,3,2,1,0:T(8,128)(2,1)S(1)} reshape(bf16[1,1536,384]{2,1,0:T(8,128)(2,1)} %param.19) | data formatting | bytes 2359296 | tf_op jit(solution)/shard_map/reshape;squeeze | solution.py:167
  16.5 1.6 slice_reduce_fusion.47
  20.6 2.1 %collective-permute-start.2 = (f32[3,38,384]{2,1,0:T(8,128)}, f32[3,38,384]{2,1,0:T(8,128)}, u32[]{:S(2)}, u32[]{:S(2)}) collective-permute-start(f32[3,38,384]{2,1,0:T(8,128)} %get-tuple-element.70), channel_id=1, source_target_pairs={{0,16},{16,32},{32,48},{48,64},{64,80},{80,96},{96,112},{1,17},{17... | collective-permute-start | bytes 525320 | tf_op jit(solution)/shard_map/ppermute | solution.py:22
  32.5 2.0 %reshape.201 = bf16[768,384]{1,0:T(8,128)(2,1)} reshape(bf16[2,2,4,8,6,384]{5,4,3,2,1,0:T(8,128)(2,1)} %copy.18) | data formatting | bytes 1179648 | tf_op jit(solution)/shard_map/reshape | solution.py:170
  35.6 2.1 %reshape.197 = bf16[768,384]{1,0:T(8,128)(2,1)} reshape(bf16[4,2,2,8,6,384]{5,4,3,2,1,0:T(8,128)(2,1)} %copy.15) | data formatting | bytes 1179648 | tf_op jit(solution)/shard_map/reshape | solution.py:170
  39.5 1.9 %constant_dynamic-update-slice_fusion = bf16[1536,384]{1,0:T(8,128)(2,1)} fusion(bf16[1536,384]{1,0:T(8,128)(2,1)} %constant_dynamic-update-slice_fusion.1, bf16[768,384]{1,0:T(8,128)(2,1)} %reshape.201), kind=kLoop, calls=%fused_computation.285 | loop fusion | bytes 1179648 | tf_op jit(solution)/shard_map/concatenate | solution.py:170
  43.6 12.5 %fusion.143 = (f32[32,32]{1,0:T(8,128)S(1)}, f32[32,32,384]{2,1,0:T(8,128)S(1)}) fusion(f32[384]{0:T(512)} %reduce.51, f32[35,38,384]{2,1,0:T(8,128)S(1)} %get-tuple-element.69, f32[384]{0:T(512)} %get-tuple-element.56, f32[384]{0:T(512)} %get-tuple-element.57, f32[384]{0:T(512)S(1)} %get-tuple-element.10, f32[384]{0:T(512)S(1)} %get-tuple-element.11, ...), kind=kLoop, calls=%fused_computation.354 | loop fusion | flops 41286656 | bytes 69581824 | tf_op jit(solution)/shard_map/reduce_sum | solution.py:61
  57.7 1.8 %fusion.147 = f32[1024,1536]{1,0:T(8,128)S(1)} fusion(bf16[1024,384]{1,0:T(8,128)(2,1)S(1)} %bitcast.63, bf16[1536,384]{1,0:T(8,128)(2,1)S(1)} %copy-done.10), kind=kOutput, calls=%fused_computation.357 | convolution fusion | flops 1207959552 | bytes 8257536 | tf_op jit(solution)/shard_map/dot_general | solution.py:189
  59.6 3.4 %fusion.5 = f32[1536,384]{0,1:T(8,128)S(1)} fusion(bf16[1024,384]{1,0:T(8,128)(2,1)S(1)} %copy-done.12, f32[1024,1536]{1,0:T(8,128)S(1)} %fusion.147, f32[1536]{0:T(1024)S(1)} %maximum_reduce_fusion), kind=kOutput, calls=%fused_computation.12 | convolution fusion | flops 1217396736 | bytes 9443328 | tf_op jit(solution)/shard_map/dot_general | solution.py:194
  63.0 5.3 %fusion.4 = bf16[1024,1536]{1,0:T(8,128)(2,1)S(1)} fusion(f32[1024,1536]{1,0:T(8,128)S(1)} %fusion.147, bf16[1024,384]{1,0:T(8,128)(2,1)S(1)} %copy-done.12, f32[1536]{0:T(1024)S(1)} %maximum_reduce_fusion, bf16[768,384]{1,0:T(8,128)(2,1)S(1)} %copy-done.16, bf16[768,384]{1,0:T(8,128)(2,1)S(1)} %copy-done.15), kind=kOutput, calls=%fused_computation.5 | convolution fusion | flops 1227620352 | bytes 11409408 | tf_op jit(solution)/shard_map/dot_general | solution.py:191
  71.8 2.1 %collective-permute-start.8 = (bf16[768,768]{0,1:T(8,128)(2,1)}, bf16[768,768]{0,1:T(8,128)(2,1)}, u32[]{:S(2)}, u32[]{:S(2)}) collective-permute-start(bf16[768,768]{0,1:T(8,128)(2,1)} %fusion.9), channel_id=1, source_target_pairs={{0,16},{16,0},{32,48},{48,32},{64,80},{80,64},{96,112},{112,96},{1... | collective-permute-start | bytes 3538952 | tf_op jit(solution)/shard_map/ppermute | solution.py:199
  74.2 4.1 %multiply_reduce_fusion.1 = (f32[1024]{0:T(1024)S(1)}, f32[1024,384]{1,0:T(8,128)S(1)}) fusion(f32[384]{0:T(512)S(1)} %copy-done.20, bf16[1024,1536]{1,0:T(8,128)(2,1)} %copy-done.84, bf16[1536,384]{1,0:T(8,128)(2,1)} %constant_dynamic-update-slice_fusion), kind=kOutput, calls=%fused_computation.251 | convolution fusion | flops 1209531392 | bytes 5903872 | tf_op jit(solution)/shard_map/dot_general | solution.py:201
  80.6 1.9 %fusion.141 = (bf16[768,768]{0,1:T(8,128)(2,1)S(1)}, f32[768,768]{0,1:T(8,128)S(1)}) fusion(bf16[768,768]{0,1:T(8,128)(2,1)} %collective-permute-done.8, s32[]{:T(128)S(6)} %select_n.118, f32[1536,384]{0,1:T(8,128)S(1)} %copy-done.2, f32[1536,384]{0,1:T(8,128)} %copy-done.3), kind=kLoop, calls=%fused_computation.353 | loop fusion | flops 2359296 | bytes 9437188 | tf_op jit(solution)/shard_map/convert_element_type | solution.py:127
  83.0 1.7 %collective-permute-start.9 = (bf16[192,768]{0,1:T(8,128)(2,1)S(1)}, bf16[192,768]{0,1:T(8,128)(2,1)S(1)}, u32[]{:S(2)}, u32[]{:S(2)}) collective-permute-start(bf16[192,768]{0,1:T(8,128)(2,1)S(1)} %get-tuple-element.80), channel_id=1, source_target_pairs={{0,32},{1,33},{2,34},{3,35},{4,36},{5,37},{6,38},{7,39},{8,40},{9,... | collective-permute-start | bytes 884744 | tf_op jit(solution)/shard_map/ppermute | solution.py:130
  84.7 1.6 collective-permute-start.11
  86.3 2.0 %collective-permute-start.10 = (bf16[192,768]{0,1:T(8,128)(2,1)S(1)}, bf16[192,768]{0,1:T(8,128)(2,1)S(1)}, u32[]{:S(2)}, u32[]{:S(2)}) collective-permute-start(bf16[192,768]{0,1:T(8,128)(2,1)S(1)} %get-tuple-element.82), channel_id=1, source_target_pairs={{0,64},{1,65},{2,66},{3,67},{4,68},{5,69},{6,70},{7,71},{8,72},{9,... | collective-permute-start | bytes 884744 | tf_op jit(solution)/shard_map/ppermute | solution.py:130
  89.1 3.0 %collective-permute-done.9 = bf16[192,768]{0,1:T(8,128)(2,1)S(1)} collective-permute-done((bf16[192,768]{0,1:T(8,128)(2,1)S(1)}, bf16[192,768]{0,1:T(8,128)(2,1)S(1)}, u32[]{:S(2)}, u32[]{:S(2)}) %collective-permute-start.9) | collective-permute-done | bytes 294944 | tf_op jit(solution)/shard_map/ppermute | solution.py:130
  92.5 5.1 %collective-permute-done.10 = bf16[192,768]{0,1:T(8,128)(2,1)S(1)} collective-permute-done((bf16[192,768]{0,1:T(8,128)(2,1)S(1)}, bf16[192,768]{0,1:T(8,128)(2,1)S(1)}, u32[]{:S(2)}, u32[]{:S(2)}) %collective-permute-start.10) | collective-permute-done | bytes 294944 | tf_op jit(solution)/shard_map/ppermute | solution.py:130
  100.3 1.6 collective-permute-start.13
  102.0 3.1 %collective-permute-start.4 = (f32[32,3,384]{2,1,0:T(4,128)S(1)}, f32[32,3,384]{2,1,0:T(4,128)S(1)}, u32[]{:S(2)}, u32[]{:S(2)}) collective-permute-start(f32[32,3,384]{2,1,0:T(4,128)S(1)} %get-tuple-element.72), channel_id=1, source_target_pairs={{0,1},{1,2},{2,3},{3,4},{4,5},{5,6},{6,7},{7,8},{8,9},{9,10},{10,1... | collective-permute-start | bytes 442376 | tf_op jit(solution)/shard_map/ppermute | solution.py:22
  105.1 2.2 %collective-permute-done.14 = bf16[48,768]{0,1:T(8,128)(2,1)S(1)} collective-permute-done((bf16[48,768]{0,1:T(8,128)(2,1)S(1)}, bf16[48,768]{0,1:T(8,128)(2,1)S(1)}, u32[]{:S(2)}, u32[]{:S(2)}) %collective-permute-start.14) | collective-permute-done | bytes 73760 | tf_op jit(solution)/shard_map/ppermute | solution.py:130
  107.3 6.4 %collective-permute-done.13 = bf16[48,768]{0,1:T(8,128)(2,1)S(1)} collective-permute-done((bf16[48,768]{0,1:T(8,128)(2,1)S(1)}, bf16[48,768]{0,1:T(8,128)(2,1)S(1)}, u32[]{:S(2)}, u32[]{:S(2)}) %collective-permute-start.13) | collective-permute-done | bytes 73760 | tf_op jit(solution)/shard_map/ppermute | solution.py:130
  114.0 6.7 %collective-permute-start.15 = (f32[24,768]{0,1:T(8,128)S(1)}, f32[24,768]{0,1:T(8,128)S(1)}, u32[]{:S(2)}, u32[]{:S(2)}) collective-permute-start(f32[24,768]{0,1:T(8,128)S(1)} %constant_dynamic-slice_fusion.2), channel_id=1, source_target_pairs={{0,8},{1,9},{2,10},{3,11},{4,12},{5,13},{6,14},{7,15},{8,0},{9,1},... | collective-permute-start | bytes 221192 | tf_op jit(solution)/shard_map/ppermute | solution.py:146
  122.0 3.0 %collective-permute-start.7 = (f32[3,38,384]{2,1,0:T(8,128)S(1)}, f32[3,38,384]{2,1,0:T(8,128)S(1)}, u32[]{:S(2)}, u32[]{:S(2)}) collective-permute-start(f32[3,38,384]{2,1,0:T(8,128)S(1)} %get-tuple-element.67), channel_id=1, source_target_pairs={{0,16},{16,32},{32,48},{48,64},{64,80},{80,96},{96,112},{1,17},{17... | collective-permute-start | bytes 525320 | tf_op jit(solution)/shard_map/ppermute | solution.py:22
  125.1 5.1 %collective-permute-done.15 = f32[24,768]{0,1:T(8,128)S(1)} collective-permute-done((f32[24,768]{0,1:T(8,128)S(1)}, f32[24,768]{0,1:T(8,128)S(1)}, u32[]{:S(2)}, u32[]{:S(2)}) %collective-permute-start.15) | collective-permute-done | bytes 73760 | tf_op jit(solution)/shard_map/ppermute | solution.py:146
  130.5 8.7 %collective-permute-start.16 = (f32[12,768]{0,1:T(8,128)S(1)}, f32[12,768]{0,1:T(8,128)S(1)}, u32[]{:S(2)}, u32[]{:S(2)}) collective-permute-start(f32[12,768]{0,1:T(8,128)S(1)} %constant_dynamic-slice_fusion.1), channel_id=1, source_target_pairs={{0,4},{1,5},{2,6},{3,7},{4,0},{5,1},{6,2},{7,3},{8,12},{9,13},{10,... | collective-permute-start | bytes 110600 | tf_op jit(solution)/shard_map/ppermute | solution.py:146
  139.7 10.6 %collective-permute-done.16 = f32[12,768]{0,1:T(8,128)S(1)} collective-permute-done((f32[12,768]{0,1:T(8,128)S(1)}, f32[12,768]{0,1:T(8,128)S(1)}, u32[]{:S(2)}, u32[]{:S(2)}) %collective-permute-start.16) | collective-permute-done | bytes 36896 | tf_op jit(solution)/shard_map/ppermute | solution.py:146
  151.4 3.9 %collective-permute-start.17 = (f32[6,768]{0,1:T(8,128)}, f32[6,768]{0,1:T(8,128)}, u32[]{:S(2)}, u32[]{:S(2)}) collective-permute-start(f32[6,768]{0,1:T(8,128)} %constant_dynamic-slice_fusion), channel_id=1, source_target_pairs={{0,2},{1,3},{2,0},{3,1},{4,6},{5,7},{6,4},{7,5},{8,10},{9,11},{10,... | collective-permute-start | bytes 55304 | tf_op jit(solution)/shard_map/ppermute | solution.py:146
  155.4 12.6 %fusion.84 = f32[1,32,32,384]{3,2,1,0:T(8,128)} fusion(f32[35,38,384]{2,1,0:T(8,128)S(1)} %get-tuple-element.65, f32[1,32,32,384]{3,2,1,0:T(8,128)} %param.11, f32[32,32,384]{2,1,0:T(8,128)S(1)} %subtract_multiply_fusion, f32[32,3,384]{2,1,0:T(4,128)S(1)} %collective-permute-done.4, f32[32,3,384]{2,1,0:T(4,128)S(1)} %collective-permute-done.5, ...), kind=kLoop, calls=%fused_computation.112 | loop fusion | flops 41287680 | bytes 71153152 | tf_op jit(solution)/shard_map/broadcast_in_dim | solution.py:212
  (254 shorter events, 42.2 us)
Async XLA Ops:
  2.7 16.7 %collective-permute-start = (f32[32,3,384]{2,1,0:T(4,128)}, f32[32,3,384]{2,1,0:T(4,128)S(1)}, u32[]{:S(2)}, u32[]{:S(2)}) collective-permute-start(f32[32,3,384]{2,1,0:T(4,128)} %get-tuple-element.78), channel_id=1, source_target_pairs={{0,1},{1,2},{2,3},{3,4},{4,5},{5,6},{6,7},{7,8},{8,9},{9,10},{10,1... | collective-permute-start | bytes 442376 | tf_op jit(solution)/shard_map/ppermute | solution.py:22
  4.9 14.5 %collective-permute-start.1 = (f32[32,3,384]{2,1,0:T(4,128)}, f32[32,3,384]{2,1,0:T(4,128)S(1)}, u32[]{:S(2)}, u32[]{:S(2)}) collective-permute-start(f32[32,3,384]{2,1,0:T(4,128)} %get-tuple-element.79), channel_id=1, source_target_pairs={{1,0},{2,1},{3,2},{4,3},{5,4},{6,5},{7,6},{8,7},{9,8},{10,9},{11,1... | collective-permute-start | bytes 442376 | tf_op jit(solution)/shard_map/ppermute | solution.py:24
  7.2 35.9 %copy-start.21 = (f32[384]{0:T(512)}, f32[384]{0:T(512)S(1)}, u32[]{:S(2)}) copy-start(f32[384]{0:T(512)S(1)} %get-tuple-element.9) | copy-start | bytes 4612
  7.2 35.9 %copy-start.23 = (f32[384]{0:T(512)}, f32[384]{0:T(512)S(1)}, u32[]{:S(2)}) copy-start(f32[384]{0:T(512)S(1)} %get-tuple-element.10) | copy-start | bytes 4612
  7.2 35.9 %copy-start.25 = (f32[384]{0:T(512)}, f32[384]{0:T(512)S(1)}, u32[]{:S(2)}) copy-start(f32[384]{0:T(512)S(1)} %get-tuple-element.11) | copy-start | bytes 4612
  20.6 21.1 %collective-permute-start.2 = (f32[3,38,384]{2,1,0:T(8,128)}, f32[3,38,384]{2,1,0:T(8,128)}, u32[]{:S(2)}, u32[]{:S(2)}) collective-permute-start(f32[3,38,384]{2,1,0:T(8,128)} %get-tuple-element.70), channel_id=1, source_target_pairs={{0,16},{16,32},{32,48},{48,64},{64,80},{80,96},{96,112},{1,17},{17... | collective-permute-start | bytes 525320 | tf_op jit(solution)/shard_map/ppermute | solution.py:22
  22.8 19.0 %collective-permute-start.3 = (f32[3,38,384]{2,1,0:T(8,128)}, f32[3,38,384]{2,1,0:T(8,128)}, u32[]{:S(2)}, u32[]{:S(2)}) collective-permute-start(f32[3,38,384]{2,1,0:T(8,128)} %get-tuple-element.71), channel_id=1, source_target_pairs={{16,0},{32,16},{48,32},{64,48},{80,64},{96,80},{112,96},{17,1},{33... | collective-permute-start | bytes 525320 | tf_op jit(solution)/shard_map/ppermute | solution.py:24
  26.4 30.0 %copy-start.19 = (f32[384]{0:T(512)}, f32[384]{0:T(512)S(1)}, u32[]{:S(2)}) copy-start(f32[384]{0:T(512)S(1)} %reduce.52) | copy-start | bytes 4612
  71.8 7.7 %collective-permute-start.8 = (bf16[768,768]{0,1:T(8,128)(2,1)}, bf16[768,768]{0,1:T(8,128)(2,1)}, u32[]{:S(2)}, u32[]{:S(2)}) collective-permute-start(bf16[768,768]{0,1:T(8,128)(2,1)} %fusion.9), channel_id=1, source_target_pairs={{0,16},{16,0},{32,48},{48,32},{64,80},{80,64},{96,112},{112,96},{1... | collective-permute-start | bytes 3538952 | tf_op jit(solution)/shard_map/ppermute | solution.py:199
  83.0 9.1 %collective-permute-start.9 = (bf16[192,768]{0,1:T(8,128)(2,1)S(1)}, bf16[192,768]{0,1:T(8,128)(2,1)S(1)}, u32[]{:S(2)}, u32[]{:S(2)}) collective-permute-start(bf16[192,768]{0,1:T(8,128)(2,1)S(1)} %get-tuple-element.80), channel_id=1, source_target_pairs={{0,32},{1,33},{2,34},{3,35},{4,36},{5,37},{6,38},{7,39},{8,40},{9,... | collective-permute-start | bytes 884744 | tf_op jit(solution)/shard_map/ppermute | solution.py:130
  84.7 7.8 %collective-permute-start.11 = (bf16[192,768]{0,1:T(8,128)(2,1)S(1)}, bf16[192,768]{0,1:T(8,128)(2,1)S(1)}, u32[]{:S(2)}, u32[]{:S(2)}) collective-permute-start(bf16[192,768]{0,1:T(8,128)(2,1)S(1)} %get-tuple-element.81), channel_id=1, source_target_pairs={{0,96},{1,97},{2,98},{3,99},{4,100},{5,101},{6,102},{7,103},{8,104... | collective-permute-start | bytes 884744 | tf_op jit(solution)/shard_map/ppermute | solution.py:130
  86.3 11.3 %collective-permute-start.10 = (bf16[192,768]{0,1:T(8,128)(2,1)S(1)}, bf16[192,768]{0,1:T(8,128)(2,1)S(1)}, u32[]{:S(2)}, u32[]{:S(2)}) collective-permute-start(bf16[192,768]{0,1:T(8,128)(2,1)S(1)} %get-tuple-element.82), channel_id=1, source_target_pairs={{0,64},{1,65},{2,66},{3,67},{4,68},{5,69},{6,70},{7,71},{8,72},{9,... | collective-permute-start | bytes 884744 | tf_op jit(solution)/shard_map/ppermute | solution.py:130
  98.2 6.9 %collective-permute-start.12 = (bf16[48,768]{0,1:T(8,128)(2,1)S(1)}, bf16[48,768]{0,1:T(8,128)(2,1)S(1)}, u32[]{:S(2)}, u32[]{:S(2)}) collective-permute-start(bf16[48,768]{0,1:T(8,128)(2,1)S(1)} %get-tuple-element.85), channel_id=1, source_target_pairs={{0,1},{1,128},{2,3},{3,130},{4,5},{5,132},{6,7},{7,134},{8,9},{9,1... | collective-permute-start | bytes 221192 | tf_op jit(solution)/shard_map/ppermute | solution.py:130
  99.5 7.8 %collective-permute-start.14 = (bf16[48,768]{0,1:T(8,128)(2,1)S(1)}, bf16[48,768]{0,1:T(8,128)(2,1)S(1)}, u32[]{:S(2)}, u32[]{:S(2)}) collective-permute-start(bf16[48,768]{0,1:T(8,128)(2,1)S(1)} %get-tuple-element.86), channel_id=1, source_target_pairs={{0,129},{1,0},{2,131},{3,2},{4,133},{5,4},{6,135},{7,6},{8,137},{9... | collective-permute-start | bytes 221192 | tf_op jit(solution)/shard_map/ppermute | solution.py:130
  100.3 13.4 %collective-permute-start.13 = (bf16[48,768]{0,1:T(8,128)(2,1)S(1)}, bf16[48,768]{0,1:T(8,128)(2,1)S(1)}, u32[]{:S(2)}, u32[]{:S(2)}) collective-permute-start(bf16[48,768]{0,1:T(8,128)(2,1)S(1)} %get-tuple-element.87), channel_id=1, source_target_pairs={{0,128},{1,129},{2,130},{3,131},{4,132},{5,133},{6,134},{7,135},{8... | collective-permute-start | bytes 221192 | tf_op jit(solution)/shard_map/ppermute | solution.py:130
  102.0 18.7 %collective-permute-start.4 = (f32[32,3,384]{2,1,0:T(4,128)S(1)}, f32[32,3,384]{2,1,0:T(4,128)S(1)}, u32[]{:S(2)}, u32[]{:S(2)}) collective-permute-start(f32[32,3,384]{2,1,0:T(4,128)S(1)} %get-tuple-element.72), channel_id=1, source_target_pairs={{0,1},{1,2},{2,3},{3,4},{4,5},{5,6},{6,7},{7,8},{8,9},{9,10},{10,1... | collective-permute-start | bytes 442376 | tf_op jit(solution)/shard_map/ppermute | solution.py:22
  105.1 15.6 %collective-permute-start.5 = (f32[32,3,384]{2,1,0:T(4,128)S(1)}, f32[32,3,384]{2,1,0:T(4,128)S(1)}, u32[]{:S(2)}, u32[]{:S(2)}) collective-permute-start(f32[32,3,384]{2,1,0:T(4,128)S(1)} %get-tuple-element.73), channel_id=1, source_target_pairs={{1,0},{2,1},{3,2},{4,3},{5,4},{6,5},{7,6},{8,7},{9,8},{10,9},{11,1... | collective-permute-start | bytes 442376 | tf_op jit(solution)/shard_map/ppermute | solution.py:24
  114.0 16.2 %collective-permute-start.15 = (f32[24,768]{0,1:T(8,128)S(1)}, f32[24,768]{0,1:T(8,128)S(1)}, u32[]{:S(2)}, u32[]{:S(2)}) collective-permute-start(f32[24,768]{0,1:T(8,128)S(1)} %constant_dynamic-slice_fusion.2), channel_id=1, source_target_pairs={{0,8},{1,9},{2,10},{3,11},{4,12},{5,13},{6,14},{7,15},{8,0},{9,1},... | collective-permute-start | bytes 221192 | tf_op jit(solution)/shard_map/ppermute | solution.py:146
  120.7 18.5 %collective-permute-start.6 = (f32[3,38,384]{2,1,0:T(8,128)S(1)}, f32[3,38,384]{2,1,0:T(8,128)S(1)}, u32[]{:S(2)}, u32[]{:S(2)}) collective-permute-start(f32[3,38,384]{2,1,0:T(8,128)S(1)} %get-tuple-element.66), channel_id=1, source_target_pairs={{16,0},{32,16},{48,32},{64,48},{80,64},{96,80},{112,96},{17,1},{33... | collective-permute-start | bytes 525320 | tf_op jit(solution)/shard_map/ppermute | solution.py:24
  122.0 17.2 %collective-permute-start.7 = (f32[3,38,384]{2,1,0:T(8,128)S(1)}, f32[3,38,384]{2,1,0:T(8,128)S(1)}, u32[]{:S(2)}, u32[]{:S(2)}) collective-permute-start(f32[3,38,384]{2,1,0:T(8,128)S(1)} %get-tuple-element.67), channel_id=1, source_target_pairs={{0,16},{16,32},{32,48},{48,64},{64,80},{80,96},{96,112},{1,17},{17... | collective-permute-start | bytes 525320 | tf_op jit(solution)/shard_map/ppermute | solution.py:22
  130.5 19.7 %collective-permute-start.16 = (f32[12,768]{0,1:T(8,128)S(1)}, f32[12,768]{0,1:T(8,128)S(1)}, u32[]{:S(2)}, u32[]{:S(2)}) collective-permute-start(f32[12,768]{0,1:T(8,128)S(1)} %constant_dynamic-slice_fusion.1), channel_id=1, source_target_pairs={{0,4},{1,5},{2,6},{3,7},{4,0},{5,1},{6,2},{7,3},{8,12},{9,13},{10,... | collective-permute-start | bytes 110600 | tf_op jit(solution)/shard_map/ppermute | solution.py:146
  139.5 15.7 %copy-start.22 = (f32[384]{0:T(512)S(1)}, f32[384]{0:T(512)}, u32[]{:S(2)}) copy-start(f32[384]{0:T(512)} %copy-done.21) | copy-start | bytes 4612
  139.6 15.7 %copy-start.24 = (f32[384]{0:T(512)S(1)}, f32[384]{0:T(512)}, u32[]{:S(2)}) copy-start(f32[384]{0:T(512)} %copy-done.23) | copy-start | bytes 4612
  139.6 15.7 %copy-start.26 = (f32[384]{0:T(512)S(1)}, f32[384]{0:T(512)}, u32[]{:S(2)}) copy-start(f32[384]{0:T(512)} %copy-done.25) | copy-start | bytes 4612
  139.6 15.7 %copy-start.28 = (f32[384]{0:T(512)S(1)}, f32[384]{0:T(512)}, u32[]{:S(2)}) copy-start(f32[384]{0:T(512)} %get-tuple-element.12) | copy-start | bytes 4612
  139.6 15.7 %copy-start.30 = (f32[384]{0:T(512)S(1)}, f32[384]{0:T(512)}, u32[]{:S(2)}) copy-start(f32[384]{0:T(512)} %get-tuple-element.13) | copy-start | bytes 4612
  139.6 15.7 %copy-start.32 = (f32[384]{0:T(512)S(1)}, f32[384]{0:T(512)}, u32[]{:S(2)}) copy-start(f32[384]{0:T(512)} %get-tuple-element.14) | copy-start | bytes 4612
  139.6 15.7 %copy-start.34 = (f32[384]{0:T(512)S(1)}, f32[384]{0:T(512)}, u32[]{:S(2)}) copy-start(f32[384]{0:T(512)} %get-tuple-element.15) | copy-start | bytes 4612
  139.6 15.7 %copy-start.36 = (f32[384]{0:T(512)S(1)}, f32[384]{0:T(512)}, u32[]{:S(2)}) copy-start(f32[384]{0:T(512)} %get-tuple-element.16) | copy-start | bytes 4612
  139.6 15.7 %copy-start.38 = (f32[384]{0:T(512)S(1)}, f32[384]{0:T(512)}, u32[]{:S(2)}) copy-start(f32[384]{0:T(512)} %get-tuple-element.17) | copy-start | bytes 4612
  139.6 15.7 %copy-start.40 = (f32[384]{0:T(512)S(1)}, f32[384]{0:T(512)}, u32[]{:S(2)}) copy-start(f32[384]{0:T(512)} %get-tuple-element.18) | copy-start | bytes 4612
  151.4 16.6 %collective-permute-start.17 = (f32[6,768]{0,1:T(8,128)}, f32[6,768]{0,1:T(8,128)}, u32[]{:S(2)}, u32[]{:S(2)}) collective-permute-start(f32[6,768]{0,1:T(8,128)} %constant_dynamic-slice_fusion), channel_id=1, source_target_pairs={{0,2},{1,3},{2,0},{3,1},{4,6},{5,7},{6,4},{7,5},{8,10},{9,11},{10,... | collective-permute-start | bytes 55304 | tf_op jit(solution)/shard_map/ppermute | solution.py:146
  (71 other events, 228.1 us)

commit v2 on v1

v2 whole, which is shorter than its diff:
```python
import functools
import itertools
import math

import jax
import jax.numpy as jnp
from jax import lax
from jax.experimental import pallas as pl
from jax.experimental.pallas import tpu as pltpu
from jax.sharding import PartitionSpec as P

norm_eps = 1e-06
inv_root_two_pi = 0.3989422804014327
side = 32
reach = 3
lanes = 128
f32 = jnp.float32
bf16 = jnp.bfloat16
whole = pl.BlockSpec(memory_space=pltpu.VMEM)


def params(mib):
    return pltpu.CompilerParams(vmem_limit_bytes=mib * 1024 * 1024)


def cost(microseconds):
    return pl.CostEstimate(
        flops=int(microseconds * 1.15e9), bytes_accessed=2**20, transcendentals=0
    )


def tap_row(kernel_ref, flipped, p, q, cols):
    index = 7 * p + q
    if flipped:
        index = 48 - index
    return kernel_ref[index : index + 1, cols]


def shift_cols(rows, offset):
    if offset == 0:
        return rows
    count = rows.shape[0]
    turned = pltpu.roll(rows, (-offset) % count, 0)
    place = lax.broadcasted_iota(jnp.int32, (8, rows.shape[1]), 0)
    if offset > 0:
        last = jnp.where(place < 8 - offset, turned[count - 8 :], 0.0)
        return jnp.concatenate([turned[: count - 8], last], axis=0)
    first = jnp.where(place >= -offset, turned[:8], 0.0)
    return jnp.concatenate([first, turned[8:]], axis=0)


def inner_conv_body(flipped, cells_ref, kernel_ref, out_ref, padded):
    edge = reach * side
    total = side * side
    padded[0:edge] = jnp.zeros((edge, lanes), f32)
    padded[edge + total : 2 * edge + total] = jnp.zeros((edge, lanes), f32)
    padded[edge : edge + total] = cells_ref[...]

    def one_row(i, carry):
        base = pl.multiple_of(i * side, side)
        rows = [padded[pl.ds(base + p * side, side), :] for p in range(7)]
        result = None
        for q in range(7):
            summed = None
            for p in range(7):
                term = tap_row(kernel_ref, flipped, p, q, slice(None)) * rows[p]
                summed = term if summed is None else summed + term
            summed = shift_cols(summed, q - reach)
            result = summed if result is None else result + summed
        out_ref[pl.ds(base, side), :] = result
        return carry

    lax.fori_loop(0, side, one_row, 0)


def inner_conv(cells, kernel, flipped):
    total, channels = cells.shape
    block = pl.BlockSpec((total, lanes), lambda c: (0, c))
    return pl.pallas_call(
        functools.partial(inner_conv_body, flipped),
        out_shape=jax.ShapeDtypeStruct((total, channels), f32),
        grid=(channels // lanes,),
        in_specs=[block, pl.BlockSpec((49, lanes), lambda c: (0, c))],
        out_specs=block,
        scratch_shapes=[pltpu.VMEM((total + 2 * reach * side, lanes), f32)],
        compiler_params=params(16),
        cost_estimate=cost(7.8),
        name="inner_conv",
    )(cells, kernel)


def side_cols_body(low_ref, high_ref, first_ref, last_ref):
    for j in range(reach):
        first_ref[j] = low_ref[:, j, :].astype(bf16)
        last_ref[j] = high_ref[:, 8 - reach + j, :].astype(bf16)


def side_cols(cells):
    channels = cells.shape[1]
    grid3 = cells.reshape(side, side, channels)
    shape = jax.ShapeDtypeStruct((reach, side, channels), bf16)
    return pl.pallas_call(
        side_cols_body,
        out_shape=(shape, shape),
        grid=(1,),
        in_specs=[
            pl.BlockSpec((side, 8, channels), lambda g: (0, 0, 0)),
            pl.BlockSpec((side, 8, channels), lambda g: (0, side // 8 - 1, 0)),
        ],
        out_specs=[pl.BlockSpec((reach, side, channels), lambda g: (0, 0, 0))] * 2,
        compiler_params=params(16),
        cost_estimate=cost(1.0),
        name="side_cols",
    )(grid3, grid3)


def side_rows_body(top_ref, bottom_ref, left_ref, right_ref, up_ref, down_ref):
    channels = top_ref.shape[1]
    place = lax.broadcasted_iota(jnp.int32, (8, channels), 0)
    blank = jnp.zeros((8, channels), f32)
    left = [left_ref[h].astype(f32) for h in range(reach)]
    right = [right_ref[h].astype(f32) for h in range(reach)]
    for r in range(reach):
        for source, row, ref in ((top_ref, r, up_ref), (bottom_ref, side - reach + r, down_ref)):
            corner = blank
            for h in range(reach):
                corner = jnp.where(place == h, right[h][row : row + 1], corner)
                corner = jnp.where(place == 8 - reach + h, left[h][row : row + 1], corner)
            body = source[r * side : (r + 1) * side]
            ref[r] = jnp.concatenate([body, corner, blank], axis=0).astype(bf16)


def side_rows(cells, left, right):
    channels = cells.shape[1]
    shape = jax.ShapeDtypeStruct((reach, side + 16, channels), bf16)
    edge = reach * side
    return pl.pallas_call(
        side_rows_body,
        out_shape=(shape, shape),
        in_specs=[whole] * 4,
        out_specs=[whole] * 2,
        compiler_params=params(16),
        cost_estimate=cost(0.8),
        name="side_rows",
    )(cells[:edge], cells[-edge:], left, right)


def add_edges(flipped, kernel_ref, left_ref, right_ref, top_ref, bottom_ref, rows_sum, cols_sum):
    channels = kernel_ref.shape[1]
    for c in range(channels // lanes):
        cols = slice(c * lanes, (c + 1) * lanes)
        for low, ref in ((True, top_ref), (False, bottom_ref)):
            beyond = [ref[h, :, cols].astype(f32)[: side + 8] for h in range(reach)]
            for r in range(reach):
                result = None
                steps = [(h, h - r) for h in range(r, reach)] if low else [
                    (h, 6 + h - r) for h in range(0, r + 1)
                ]
                for q in range(7):
                    summed = None
                    for h, p in steps:
                        term = tap_row(kernel_ref, flipped, p, q, cols) * beyond[h]
                        summed = term if summed is None else summed + term
                    summed = pltpu.roll(summed, (reach - q) % (side + 8), 0) if q != reach else summed
                    result = summed if result is None else result + summed
                rows_sum[r if low else reach + r, :, cols] = result[:side]
        for low, ref in ((True, left_ref), (False, right_ref)):
            beyond = [ref[h, :, cols].astype(f32) for h in range(reach)]
            for r in range(reach):
                steps = [(h, h - r) for h in range(r, reach)] if low else [
                    (h, 6 + h - r) for h in range(0, r + 1)
                ]
                result = None
                for p in range(7):
                    summed = None
                    for h, q in steps:
                        term = tap_row(kernel_ref, flipped, p, q, cols) * beyond[h]
                        summed = term if summed is None else summed + term
                    summed = shift_cols(summed, p - reach)
                    result = summed if result is None else result + summed
                cols_sum[r if low else reach + r, :, cols] = result


def edged_row(i, conv_row, cols_sum):
    channels = conv_row.shape[1]
    place = lax.broadcasted_iota(jnp.int32, (8, channels), 0)
    first, last = conv_row[:8], conv_row[side - 8 :]
    for r in range(reach):
        first = first + jnp.where(place == r, cols_sum[r, pl.ds(i, 1), :], 0.0)
        last = last + jnp.where(place == 8 - reach + r, cols_sum[reach + r, pl.ds(i, 1), :], 0.0)
    return jnp.concatenate([first, conv_row[8 : side - 8], last], axis=0)


def each_row(step):
    def low(i, carry):
        step(i, i)
        return carry

    def middle(i, carry):
        step(i, None)
        return carry

    def high(i, carry):
        step(i, i - (side - 2 * reach))
        return carry

    lax.fori_loop(0, reach, low, 0)
    lax.fori_loop(reach, side - reach, middle, 0, unroll=2)
    lax.fori_loop(side - reach, side, high, 0)


def normalise_body(
    conv_ref, kernel_ref, left_ref, right_ref, top_ref, bottom_ref, bias_ref, gain_ref, shift_ref,
    unit_ref, spread_ref, normed_ref, flipped_ref, rows_sum, cols_sum,
):
    channels = conv_ref.shape[1]
    add_edges(False, kernel_ref, left_ref, right_ref, top_ref, bottom_ref, rows_sum, cols_sum)
    share = 1.0 / channels

    def step(i, outer):
        at = pl.ds(pl.multiple_of(i * side, side), side)
        value = edged_row(i, conv_ref[at, :], cols_sum)
        if outer is not None:
            value = value + rows_sum[outer]
        value = value + bias_ref[...]
        mean = jnp.sum(value, axis=1, keepdims=True) * share
        centred = value - mean
        spread = lax.rsqrt(jnp.sum(centred * centred, axis=1, keepdims=True) * share + norm_eps)
        unit = centred * spread
        unit_ref[at, :] = unit
        spread_ref[at, :] = jnp.broadcast_to(spread, (side, lanes))
        normed_ref[at, :] = (unit * gain_ref[...] + shift_ref[...]).astype(bf16)

    each_row(step)
    turn(normed_ref, flipped_ref)


def turn(source_ref, target_ref):
    for b in range(source_ref.shape[0] // 256):
        at = slice(b * 256, (b + 1) * 256)
        target_ref[:, at] = source_ref[at, :].T


def normalise(conv, kernel, left, right, top, bottom, bias, gain, shift):
    total, channels = conv.shape
    return pl.pallas_call(
        normalise_body,
        out_shape=(
            jax.ShapeDtypeStruct((total, channels), f32),
            jax.ShapeDtypeStruct((total, lanes), f32),
            jax.ShapeDtypeStruct((total, channels), bf16),
            jax.ShapeDtypeStruct((channels, total), bf16),
        ),
        in_specs=[whole] * 9,
        out_specs=[whole] * 4,
        scratch_shapes=[pltpu.VMEM((2 * reach, side, channels), f32)] * 2,
        compiler_params=params(32),
        cost_estimate=cost(6.2),
        name="normalise",
    )(conv, kernel, left, right, top, bottom, bias, gain, shift)


def wet_row(i, counts_ref):
    place = lax.broadcasted_iota(jnp.int32, (8, lanes), 0) + (i % 8) * 8
    pieces = []
    for t in range(side // 8):
        pieces.append(place < counts_ref[i // 8, t])
    return pieces


def masked_row(i, grad_row, counts_ref):
    channels = grad_row.shape[1]
    parts = []
    for t, wet in enumerate(wet_row(i, counts_ref)):
        piece = grad_row[t * 8 : (t + 1) * 8]
        parts.append(
            jnp.concatenate(
                [
                    jnp.where(wet, piece[:, c * lanes : (c + 1) * lanes], 0.0)
                    for c in range(channels // lanes)
                ],
                axis=1,
            )
        )
    return jnp.concatenate(parts, axis=0)


def mask_rows_body(counts_ref, grad_ref, rows_ref, flipped_ref):
    def step(i, carry):
        at = pl.ds(pl.multiple_of(i * side, side), side)
        rows_ref[at, :] = masked_row(i, grad_ref[at, :], counts_ref).astype(bf16)
        return carry

    lax.fori_loop(0, side, step, 0)
    turn(rows_ref, flipped_ref)


def mask_rows(counts, grad):
    total, channels = grad.shape
    return pl.pallas_call(
        mask_rows_body,
        out_shape=(
            jax.ShapeDtypeStruct((total, channels), bf16),
            jax.ShapeDtypeStruct((channels, total), bf16),
        ),
        in_specs=[pl.BlockSpec(memory_space=pltpu.SMEM), whole],
        out_specs=[whole] * 2,
        compiler_params=params(16),
        cost_estimate=cost(2.2),
        name="mask_rows",
    )(counts, grad)


def arrange_body(expand_ref, reduce_ref, bias_ref, expand_out, reduce_out, turned_out, bias_out):
    unit_row = lax.broadcasted_iota(jnp.int32, (48, 96), 0)
    unit_col = lax.broadcasted_iota(jnp.int32, (48, 96), 1)
    picks = [unit_col == (unit_row // 6) * 12 + lo * 6 + unit_row % 6 for lo in range(2)]
    chosen = [pick.astype(f32).astype(bf16) for pick in picks]
    for hi, y, core in itertools.product(range(2), range(4), range(2)):
        unit = (hi * 4 + y) * 2 + core
        at = slice(unit * 96, (unit + 1) * 96)
        expand, reduce = expand_ref[at, :], reduce_ref[at, :]
        bias = bias_ref[unit : unit + 1, :]
        for lo in range(2):
            x = 2 * hi + lo
            place = core * 16 + (y * 4 + x if core == 0 else x * 4 + y)
            to = slice(place * 48, (place + 1) * 48)
            expand_out[to, :] = jnp.dot(chosen[lo], expand, preferred_element_type=f32).astype(bf16)
            reduce_out[to, :] = jnp.dot(chosen[lo], reduce, preferred_element_type=f32).astype(bf16)
            column = jnp.sum(jnp.where(picks[lo], bias, 0.0), axis=1, keepdims=True)
            bias_out[to, :] = jnp.broadcast_to(column, (48, lanes))
    turn(expand_out, turned_out)


def arrange(expand, reduce, bias):
    units, channels = expand.shape
    shape = jax.ShapeDtypeStruct((units, channels), bf16)
    return pl.pallas_call(
        arrange_body,
        out_shape=(
            shape,
            shape,
            jax.ShapeDtypeStruct((channels, units), bf16),
            jax.ShapeDtypeStruct((units, lanes), f32),
        ),
        in_specs=[whole] * 3,
        out_specs=[whole] * 4,
        compiler_params=params(32),
        cost_estimate=cost(3.0),
        name="arrange",
    )(expand, reduce, bias.reshape(16, 96))


tail_slope = 0.3275911 * 0.7071067811865476
tail_terms = [
    0.5 * a for a in (0.254829592, -0.284496736, 1.421413741, -1.453152027, 1.061405429)
]
exp_scale = -0.5 * 1.4426950408889634


def gelu_pair(v):
    d = 1.0 + tail_slope * jnp.abs(v)
    t = pl.reciprocal(d, approx=True)
    t = t * (2.0 - d * t)
    poly = tail_terms[4]
    for a in reversed(tail_terms[:4]):
        poly = poly * t + a
    bell = jnp.exp2(v * v * exp_scale)
    tail = poly * t * bell
    below = jnp.where(v >= 0.0, 1.0 - tail, tail)
    return v * below, below + v * bell * inv_root_two_pi


def hidden_body(
    core_ref, normed_ref, normed_t_ref, grad_ref, grad_t_ref, expand_ref, reduce_ref, bias_ref,
    sums_ref, grad_pre_ref,
):
    channels = normed_ref.shape[1]
    total = normed_ref.shape[0]
    preact = jnp.dot(expand_ref[...], normed_t_ref[...], preferred_element_type=f32)
    grad_hidden = jnp.dot(reduce_ref[...], grad_t_ref[...], preferred_element_type=f32)
    bias = jnp.concatenate([bias_ref[...]] * (total // lanes), axis=1)
    value, slope = gelu_pair(preact + bias)
    hidden = value.astype(bf16)
    grad_pre = (grad_hidden * slope).astype(bf16)
    grad_pre_ref[...] = grad_pre
    sums_ref[:, :channels] = jnp.dot(grad_pre, normed_ref[...], preferred_element_type=f32).astype(
        sums_ref.dtype
    )
    sums_ref[:, channels:] = jnp.dot(hidden, grad_ref[...], preferred_element_type=f32).astype(
        sums_ref.dtype
    )


hidden_block = 256


def hidden_half(core, normed, normed_t, grad, grad_t, expand, reduce, bias, kind):
    total, channels = normed.shape
    half = expand.shape[0] // 2
    steps = half // hidden_block
    keep = lambda i, core: (0, 0)
    pick = lambda i, core: (core[0] * steps + i, 0)
    return pl.pallas_call(
        hidden_body,
        out_shape=(
            jax.ShapeDtypeStruct((half, 2 * channels), kind),
            jax.ShapeDtypeStruct((half, total), bf16),
        ),
        grid_spec=pltpu.PrefetchScalarGridSpec(
            num_scalar_prefetch=1,
            grid=(steps,),
            in_specs=[
                pl.BlockSpec((total, channels), keep),
                pl.BlockSpec((channels, total), keep),
                pl.BlockSpec((total, channels), keep),
                pl.BlockSpec((channels, total), keep),
                pl.BlockSpec((hidden_block, channels), pick),
                pl.BlockSpec((hidden_block, channels), pick),
                pl.BlockSpec((hidden_block, lanes), pick),
            ],
            out_specs=[
                pl.BlockSpec((hidden_block, 2 * channels), lambda i, core: (i, 0)),
                pl.BlockSpec((hidden_block, total), lambda i, core: (i, 0)),
            ],
        ),
        compiler_params=params(40),
        cost_estimate=cost(6.9),
        name="hidden_half",
    )(core, normed, normed_t, grad, grad_t, expand, reduce, bias)


def norm_back_body(
    core_ref, turned_ref, other_ref, mine_ref, unit_ref, spread_ref, gain_ref,
    conv_grad_ref, first_ref, last_ref,
):
    total, channels = unit_ref.shape
    half = turned_ref.shape[1] // 2
    core = core_ref[0]
    block = 256
    share = 1.0 / channels
    mine_weight = turned_ref[:, pl.ds(pl.multiple_of(core * half, half), half)]
    other_weight = turned_ref[:, pl.ds(pl.multiple_of((1 - core) * half, half), half)]
    for b in range(total // block):
        at = slice(b * block, (b + 1) * block)
        summed = jnp.dot(mine_weight, mine_ref[:, at], preferred_element_type=f32)
        summed = summed + jnp.dot(other_weight, other_ref[:, at], preferred_element_type=f32)
        grad_normed = summed.astype(bf16).T.astype(f32)
        unit = unit_ref[at, :]
        grad_unit = grad_normed * gain_ref[...]
        mean_grad = jnp.sum(grad_unit, axis=1, keepdims=True) * share
        mean_cross = jnp.sum(grad_unit * unit, axis=1, keepdims=True) * share
        spread = jnp.concatenate([spread_ref[at, :]] * (channels // lanes), axis=1)
        value = (grad_unit - mean_grad - unit * mean_cross) * spread
        conv_grad_ref[b * 8 : (b + 1) * 8] = value.reshape(block // side, side, channels)
    for j in range(reach):
        first_ref[j] = conv_grad_ref[:, j, :].astype(bf16)
        last_ref[j] = conv_grad_ref[:, side - reach + j, :].astype(bf16)


def norm_back(core, turned, other, mine, unit, spread, gain):
    total, channels = unit.shape
    shape = jax.ShapeDtypeStruct((reach, side, channels), bf16)
    found, first, last = pl.pallas_call(
        norm_back_body,
        out_shape=(jax.ShapeDtypeStruct((side, side, channels), f32), shape, shape),
        in_specs=[pl.BlockSpec(memory_space=pltpu.SMEM)] + [whole] * 6,
        out_specs=[whole] * 3,
        compiler_params=params(40),
        cost_estimate=cost(3.3),
        name="norm_back",
    )(core, turned, other, mine, unit, spread, gain)
    return found.reshape(total, channels), first, last


def finish_body(
    counts_ref, conv_ref, kernel_ref, left_ref, right_ref, top_ref, bottom_ref, grad_ref,
    out_ref, rows_sum, cols_sum,
):
    add_edges(True, kernel_ref, left_ref, right_ref, top_ref, bottom_ref, rows_sum, cols_sum)

    def step(i, outer):
        at = pl.ds(pl.multiple_of(i * side, side), side)
        value = edged_row(i, conv_ref[at, :], cols_sum)
        if outer is not None:
            value = value + rows_sum[outer]
        out_ref[at, :] = value + masked_row(i, grad_ref[at, :], counts_ref)

    each_row(step)


def finish(counts, conv, kernel, left, right, top, bottom, grad):
    total, channels = conv.shape
    return pl.pallas_call(
        finish_body,
        out_shape=jax.ShapeDtypeStruct((total, channels), f32),
        in_specs=[pl.BlockSpec(memory_space=pltpu.SMEM)] + [whole] * 7,
        out_specs=whole,
        scratch_shapes=[pltpu.VMEM((2 * reach, side, channels), f32)] * 2,
        compiler_params=params(32),
        cost_estimate=cost(3.1),
        name="finish",
    )(counts, conv, kernel, left, right, top, bottom, grad)


every_axis = ("dp", "lat", "lon")


def device_pairs(move):
    def flat(hi, y, core, z, lo):
        return (hi * 8 + y * 2 + core) * 16 + z * 2 + lo

    found = []
    for hi, y, core, z, lo in itertools.product(range(2), range(4), range(2), range(8), range(2)):
        found.append((flat(hi, y, core, z, lo), flat(*move(hi, y, core, z, lo))))
    return found


def plane_pairs(step, first):
    def move(hi, y, core, z, lo):
        if (core == 0) == first:
            return (hi, (y + step) % 4, core, z, lo)
        x = (2 * hi + lo + step) % 4
        return (x // 2, y, core, z, x % 2)

    return device_pairs(move)


def scatter_direct(rows, place, pairs_of):
    size = rows.shape[0] // 4
    narrow = rows.astype(jnp.bfloat16)
    total = lax.dynamic_slice_in_dim(rows, place * size, size, 0)
    arrived = [
        lax.ppermute(
            lax.dynamic_slice_in_dim(narrow, ((place + step) % 4) * size, size, 0),
            every_axis,
            pairs_of(step),
        )
        for step in range(1, 4)
    ]
    for part in arrived:
        total = total + part.astype(jnp.float32)
    return total


def scatter_halving(rows, z):
    for bit in (4, 2, 1):
        size = rows.shape[0] // 2
        upper = (z // bit) % 2
        arrived = lax.ppermute(
            lax.dynamic_slice_in_dim(rows, (1 - upper) * size, size, 0),
            every_axis,
            device_pairs(lambda hi, y, core, z, lo, bit=bit: (hi, y, core, z ^ bit, lo)),
        )
        rows = lax.dynamic_slice_in_dim(rows, upper * size, size, 0) + arrived
    return rows


def scatter_rows(mine, arrived):
    lat, lon = lax.axis_index("lat"), lax.axis_index("lon")
    y, core, z, lo = lat // 2, lat % 2, lon // 2, lon % 2
    x = 2 * lax.axis_index("dp") + lo
    rows = mine + arrived.astype(jnp.float32)
    rows = scatter_direct(rows, jnp.where(core == 0, y, x), lambda step: plane_pairs(step, True))
    rows = scatter_direct(rows, jnp.where(core == 0, x, y), lambda step: plane_pairs(step, False))
    return scatter_halving(rows, z)


def shifted(axis, step, closed):
    count = lax.axis_size(axis)
    found = []
    for i in range(count):
        j = i + step
        if closed or 0 <= j < count:
            found.append((i, j % count))
    return found


def lon_halo(first, last):
    left = lax.ppermute(last, "lon", shifted("lon", 1, True))
    right = lax.ppermute(first, "lon", shifted("lon", -1, True))
    return left, right


def lat_halo(up, down):
    top = lax.ppermute(down, "lat", shifted("lat", 1, False))
    bottom = lax.ppermute(up, "lat", shifted("lat", -1, False))
    return top, bottom


def local(
    state, cotangent, counts, dw_kernel, dw_bias, norm_gain, norm_bias, w_expand, b_expand, w_reduce
):
    channels = state.shape[-1]
    cells = state.reshape(-1, channels)
    grad = cotangent.reshape(-1, channels)
    total = cells.shape[0]
    kernel = dw_kernel[0]
    core = lax.axis_index("lat") % 2
    near = core.astype(jnp.int32).reshape(1)
    far = 1 - near

    left, right = lon_halo(*side_cols(cells))
    rows, rows_t = mask_rows(counts, grad)
    expand, reduce, expand_t, bias = arrange(w_expand[0], w_reduce[0], b_expand[0])
    top, bottom = lat_halo(*side_rows(cells, left, right))
    conv = inner_conv(cells, kernel, False)
    unit, spread, normed, normed_t = normalise(
        conv, kernel, left, right, top, bottom, dw_bias, norm_gain, norm_bias
    )

    sent, far_pre = hidden_half(
        far, normed, normed_t, rows, rows_t, expand, reduce, bias, jnp.bfloat16
    )
    arrived = lax.ppermute(sent, "lat", [(i, i ^ 1) for i in range(8)])
    mine, near_pre = hidden_half(
        near, normed, normed_t, rows, rows_t, expand, reduce, bias, jnp.float32
    )
    conv_grad, first, last = norm_back(near, expand_t, far_pre, near_pre, unit, spread, norm_gain)
    kept = scatter_rows(mine, arrived)
    left, right = lon_halo(first, last)
    top, bottom = lat_halo(*side_rows(conv_grad, left, right))
    back = inner_conv(conv_grad, kernel, True)
    gradient = finish(counts, back, kernel, left, right, top, bottom, grad)

    cells_all = lax.axis_size("dp") * lax.axis_size("lat") * lax.axis_size("lon") * total
    kept = kept * (1.0 / math.sqrt(cells_all))
    return (gradient.reshape(state.shape), kept[None, :, :channels], kept[None, :, channels:])


def solution(mesh):
    in_specs = (
        P("dp", "lat", "lon", None),
        P("dp", "lat", "lon", None),
        P("lat", "lon"),
        P(),
        P(),
        P(),
        P(),
        P(),
        P(),
        P(),
    )
    out_specs = (
        P("dp", "lat", "lon", None),
        P(None, ("dp", "lat", "lon"), None),
        P(None, ("dp", "lat", "lon"), None),
    )
    return jax.shard_map(local, mesh=mesh, in_specs=in_specs, out_specs=out_specs, check_vma=False)
```

time: 171 us -> 113 us (0.66)
  the two profiles are of different devices: /device:TPU:38 before, /device:TPU:1 now
where the time goes in v2:
time: 113 us
  Pallas kernels  39.4 us (35%)
  starting transfers between devices  37.2 us (33%)
  local copies, waits for them, and re-layouts  20.8 us (18%)
  waiting for transfers between devices  12.3 us (11%)
  other arithmetic  2.02 us (2%)
  between operations  1.18 us (1%)
    unnamed x79, local copies, waits for them, and re-layouts  20.5 us
    pallas_call x2, Pallas kernels, inner_conv(): pl.pallas_call(functools.partial(inner_conv_body, flipped), out_shape=jax...  14.2 us
    pallas_call x2, Pallas kernels, hidden_half(): pl.pallas_call(hidden_body, out_shape=(jax.ShapeDtypeStruct((half, 2 * ch...  12.3 us
    ppermute x2, starting transfers between devices, lat_halo(): top = lax.ppermute(down, 'lat', shifted('lat', 1, False))  10.9 us
    ppermute x2, starting transfers between devices, lon_halo(): right = lax.ppermute(first, 'lon', shifted('lon', -1, True))  7.94 us
    ppermute x6, starting transfers between devices, scatter_direct(): lax.ppermute(lax.dynamic_slice_in_dim(narrow, (place + step) % 4 * size,...  6.63 us
    ppermute x6, waiting for transfers between devices, scatter_direct(): lax.ppermute(lax.dynamic_slice_in_dim(narrow, (place + step) % 4 * size,...  5.17 us
    ppermute x2, waiting for transfers between devices, lat_halo(): bottom = lax.ppermute(up, 'lat', shifted('lat', -1, False))  4.95 us
  transfers between devices with their start and end apart: 18, of which 6 were waited for; matrix products, arithmetic and copies ran while one was open for 0% of the time, Pallas kernels for 25%

profile of v2, /device:TPU:1, one launch (start us, length us, event | category | flops | bytes accessed | tf_op | source)
XLA Modules:
  0.0 112.8 jit_solution(6467037918719364897)
XLA Ops:
  0.6 1.4 %copy-done = f32[1,32,32,384]{3,2,1,0:T(8,128)S(1)} copy-done((f32[1,32,32,384]{3,2,1,0:T(8,128)S(1)}, f32[1,32,32,384]{3,2,1,0:T(8,128)}, u32[]{:S(2)}) %copy-start) | copy-done | bytes 1572888
  2.5 2.1 %collective-permute-start = (bf16[3,32,384]{2,1,0:T(8,128)(2,1)S(1)}, bf16[3,32,384]{2,1,0:T(8,128)(2,1)S(1)}, u32[]{:S(2)}, u32[]{:S(2)}) collective-permute-start(bf16[3,32,384]{2,1,0:T(8,128)(2,1)S(1)} %get-tuple-element.27), channel_id=1, source_target_pairs={{0,1},{1,2},{2,3},{3,4},{4,5},{5,6},{6,7},{7,8},{8,9},{9,10},{10,1... | collective-permute-start | bytes 221192 | tf_op jit(solution)/shard_map/ppermute | solution.py:580
  4.6 5.4 %collective-permute-start.1 = (bf16[3,32,384]{2,1,0:T(8,128)(2,1)S(1)}, bf16[3,32,384]{2,1,0:T(8,128)(2,1)S(1)}, u32[]{:S(2)}, u32[]{:S(2)}) collective-permute-start(bf16[3,32,384]{2,1,0:T(8,128)(2,1)S(1)} %get-tuple-element.28), channel_id=1, source_target_pairs={{0,15},{1,0},{2,1},{3,2},{4,3},{5,4},{6,5},{7,6},{8,7},{9,8},{10,9... | collective-permute-start | bytes 221192 | tf_op jit(solution)/shard_map/ppermute | solution.py:581
  10.1 7.1 %inner_conv.2.conv_ref = f32[1024,384]{1,0:T(8,128)S(1)} custom-call(f32[1024,384]{1,0:T(8,128)S(1)} %bitcast.29, f32[49,384]{1,0:T(8,128)S(1)} %bitcast.23), custom_call_target="tpu_custom_call" | custom-call | flops 8970000384 | bytes 1048576 | tf_op jit(solution)/shard_map/inner_conv/pallas_call | solution.py:79
  17.3 1.1 %copy-done.30 = f32[1024,384]{1,0:T(8,128)} copy-done((f32[1024,384]{1,0:T(8,128)}, f32[1024,384]{1,0:T(8,128)S(1)}, u32[]{:S(2)}) %copy-start.30) | copy-done | bytes 1572888
  22.2 4.0 %collective-permute-start.2 = (bf16[3,48,384]{2,1,0:T(8,128)(2,1)S(1)}, bf16[3,48,384]{2,1,0:T(8,128)(2,1)S(1)}, u32[]{:S(2)}, u32[]{:S(2)}) collective-permute-start(bf16[3,48,384]{2,1,0:T(8,128)(2,1)S(1)} %get-tuple-element.29), channel_id=1, source_target_pairs={{0,16},{16,32},{32,48},{48,64},{64,80},{80,96},{96,112},{1,17},{17... | collective-permute-start | bytes 331784 | tf_op jit(solution)/shard_map/ppermute | solution.py:586
  26.3 1.9 %collective-permute-start.3 = (bf16[3,48,384]{2,1,0:T(8,128)(2,1)S(1)}, bf16[3,48,384]{2,1,0:T(8,128)(2,1)S(1)}, u32[]{:S(2)}, u32[]{:S(2)}) collective-permute-start(bf16[3,48,384]{2,1,0:T(8,128)(2,1)S(1)} %get-tuple-element.30), channel_id=1, source_target_pairs={{16,0},{32,16},{48,32},{64,48},{80,64},{96,80},{112,96},{17,1},{33... | collective-permute-start | bytes 331784 | tf_op jit(solution)/shard_map/ppermute | solution.py:587
  28.2 1.3 %mask_rows.1 = (bf16[1024,384]{1,0:T(8,128)(2,1)S(1)}, bf16[384,1024]{1,0:T(8,128)(2,1)S(1)}) custom-call(s32[4,4]{1,0:T(4,128)S(1)} %copy-done.5, f32[1024,384]{1,0:T(8,128)S(1)} %bitcast.31), custom_call_target="tpu_custom_call" | custom-call | flops 2529999872 | bytes 1048576 | tf_op jit(solution)/shard_map/mask_rows/pallas_call | solution.py:300
  32.3 1.8 %copy-done.31 = f32[1024,384]{1,0:T(8,128)S(1)} copy-done((f32[1024,384]{1,0:T(8,128)S(1)}, f32[1024,384]{1,0:T(8,128)}, u32[]{:S(2)}) %copy-start.31) | copy-done | bytes 1572888
  34.1 4.7 %normalise.1 = (f32[1024,384]{1,0:T(8,128)S(1)}, f32[1024,128]{1,0:T(8,128)S(1)}, bf16[1024,384]{1,0:T(8,128)(2,1)S(1)}, bf16[384,1024]{1,0:T(8,128)(2,1)S(1)}) custom-call(f32[1024,384]{1,0:T(8,128)S(1)} %copy-done.31, f32[49,384]{1,0:T(8,128)S(1)} %bitcast.24, bf16[3,32,384]{2,1,0:T(8,128)(2,1)S(1)} %collective-permute-done.left_ref, ...), custom_call_target="tpu_custom_call" | custom-call | flops 7129999872 | bytes 1048576 | tf_op jit(solution)/shard_map/normalise/pallas_call | solution.py:246
  38.9 1.2 %copy-done.9 = f32[1024,384]{1,0:T(8,128)} copy-done((f32[1024,384]{1,0:T(8,128)}, f32[1024,384]{1,0:T(8,128)S(1)}, u32[]{:S(2)}) %copy-start.9) | copy-done | bytes 1572888
  40.1 6.2 %hidden_half.2 = (bf16[768,768]{1,0:T(8,128)(2,1)S(1)}, bf16[768,1024]{1,0:T(8,128)(2,1)S(1)}) custom-call(s32[1]{0:T(128)S(6)} %sub.26.core_ref, bf16[1024,384]{1,0:T(8,128)(2,1)S(1)} %get-tuple-element.31.normed_ref, bf16[384,1024]{1,0:T(8,128)(2,1)S(1)} %get-tuple-element.32.normed_t_ref, bf16[1024,384]{1,0:T(8,128)(2,1)S(1)} %copy-done.16, ...), custom_call_target="tpu_custom_call" | custom-call | flops 7935000064 | bytes 1048576 | tf_op jit(solution)/shard_map/hidden_half/pallas_call | solution.py:404
  46.3 1.1 %copy-done.11 = bf16[768,1024]{1,0:T(8,128)(2,1)} copy-done((bf16[768,1024]{1,0:T(8,128)(2,1)}, bf16[768,1024]{1,0:T(8,128)(2,1)S(1)}, u32[]{:S(2)}) %copy-start.11) | copy-done | bytes 1572888
  47.4 1.1 %copy-done.17 = bf16[1024,384]{1,0:T(8,128)(2,1)S(1)} copy-done((bf16[1024,384]{1,0:T(8,128)(2,1)S(1)}, bf16[1024,384]{1,0:T(8,128)(2,1)}, u32[]{:S(2)}) %copy-start.17) | copy-done | bytes 786456
  48.6 1.1 %copy-done.20 = bf16[384,1024]{1,0:T(8,128)(2,1)S(1)} copy-done((bf16[384,1024]{1,0:T(8,128)(2,1)S(1)}, bf16[384,1024]{1,0:T(8,128)(2,1)}, u32[]{:S(2)}) %copy-start.20) | copy-done | bytes 786456
  49.7 1.3 %copy-done.23 = bf16[1536,384]{1,0:T(8,128)(2,1)S(1)} copy-done((bf16[1536,384]{1,0:T(8,128)(2,1)S(1)}, bf16[1536,384]{1,0:T(8,128)(2,1)}, u32[]{:S(2)}) %copy-start.23) | copy-done | bytes 1179672
  51.0 1.3 %copy-done.26 = bf16[1536,384]{1,0:T(8,128)(2,1)S(1)} copy-done((bf16[1536,384]{1,0:T(8,128)(2,1)S(1)}, bf16[1536,384]{1,0:T(8,128)(2,1)}, u32[]{:S(2)}) %copy-start.26) | copy-done | bytes 1179672
  55.7 6.1 %hidden_half.3 = (f32[768,768]{1,0:T(8,128)S(1)}, bf16[768,1024]{1,0:T(8,128)(2,1)S(1)}) custom-call(s32[1]{0:T(128)} %bitcast.core_ref, bf16[1024,384]{1,0:T(8,128)(2,1)S(1)} %copy-done.33, bf16[384,1024]{1,0:T(8,128)(2,1)S(1)} %copy-done.35, bf16[1024,384]{1,0:T(8,128)(2,1)S(1)} %copy-done.17, bf16[384,1024]{1,0:T(8,128)(2,1)S(1)} %copy-done.20, ...), custom_call_target="tpu_custom_call" | custom-call | flops 7935000064 | bytes 1048576 | tf_op jit(solution)/shard_map/hidden_half/pallas_call | solution.py:404
  61.8 1.8 %fusion.1 = (bf16[768,768]{1,0:T(8,128)(2,1)S(1)}, f32[768,768]{1,0:T(8,128)S(1)}) fusion(f32[768,768]{1,0:T(8,128)S(1)} %get-tuple-element.47, bf16[768,768]{1,0:T(8,128)(2,1)} %collective-permute-done.8), kind=kLoop, calls=%fused_computation.19 | loop fusion | flops 1769472 | bytes 7077888 | tf_op jit(solution)/shard_map/convert_element_type | solution.py:531
  63.7 2.5 %collective-permute-start.10 = (bf16[192,768]{1,0:T(8,128)(2,1)S(1)}, bf16[192,768]{1,0:T(8,128)(2,1)S(1)}, u32[]{:S(2)}, u32[]{:S(2)}) collective-permute-start(bf16[192,768]{1,0:T(8,128)(2,1)S(1)} %get-tuple-element.62), channel_id=1, source_target_pairs={{0,64},{1,65},{2,66},{3,67},{4,68},{5,69},{6,70},{7,71},{8,72},{9,... | collective-permute-start | bytes 884744 | tf_op jit(solution)/shard_map/ppermute | solution.py:534
  67.0 2.2 %norm_back.1 = (f32[32,32,384]{2,1,0:T(8,128)S(1)}, bf16[3,32,384]{2,1,0:T(8,128)(2,1)S(1)}, bf16[3,32,384]{2,1,0:T(8,128)(2,1)S(1)}) custom-call(s32[1]{0:T(128)} %bitcast.core_ref, bf16[384,1536]{1,0:T(8,128)(2,1)S(1)} %copy-done.14, bf16[768,1024]{1,0:T(8,128)(2,1)S(1)} %copy-done.12, bf16[768,1024]{1,0:T(8,128)(2,1)S(1)} %get-tuple-element.39.mine_ref, ...), custom_call_target="tpu_custom_call" | custom-call | flops 3795000064 | bytes 1048576 | tf_op jit(solution)/shard_map/norm_back/pallas_call | solution.py:464
  69.6 1.6 %collective-permute-done.10 = bf16[192,768]{1,0:T(8,128)(2,1)S(1)} collective-permute-done((bf16[192,768]{1,0:T(8,128)(2,1)S(1)}, bf16[192,768]{1,0:T(8,128)(2,1)S(1)}, u32[]{:S(2)}, u32[]{:S(2)}) %collective-permute-start.10) | collective-permute-done | bytes 294944 | tf_op jit(solution)/shard_map/ppermute | solution.py:534
  71.2 3.2 %collective-permute-done.9 = bf16[192,768]{1,0:T(8,128)(2,1)S(1)} collective-permute-done((bf16[192,768]{1,0:T(8,128)(2,1)S(1)}, bf16[192,768]{1,0:T(8,128)(2,1)S(1)}, u32[]{:S(2)}, u32[]{:S(2)}) %collective-permute-start.9) | collective-permute-done | bytes 294944 | tf_op jit(solution)/shard_map/ppermute | solution.py:534
  74.5 2.2 %collective-permute-start.14 = (bf16[48,768]{1,0:T(8,128)(2,1)S(1)}, bf16[48,768]{1,0:T(8,128)(2,1)S(1)}, u32[]{:S(2)}, u32[]{:S(2)}) collective-permute-start(bf16[48,768]{1,0:T(8,128)(2,1)S(1)} %get-tuple-element.64), channel_id=1, source_target_pairs={{0,129},{1,0},{2,131},{3,2},{4,133},{5,4},{6,135},{7,6},{8,137},{9... | collective-permute-start | bytes 221192 | tf_op jit(solution)/shard_map/ppermute | solution.py:534
  77.8 7.1 %inner_conv.3.conv_ref = f32[1024,384]{1,0:T(8,128)S(1)} custom-call(f32[1024,384]{1,0:T(8,128)S(1)} %bitcast.30, f32[49,384]{1,0:T(8,128)S(1)} %bitcast.25), custom_call_target="tpu_custom_call" | custom-call | flops 8970000384 | bytes 1048576 | tf_op jit(solution)/shard_map/inner_conv/pallas_call | solution.py:79
  85.0 4.5 %collective-permute-start.15 = (f32[24,768]{1,0:T(8,128)S(1)}, f32[24,768]{1,0:T(8,128)S(1)}, u32[]{:S(2)}, u32[]{:S(2)}) collective-permute-start(f32[24,768]{1,0:T(8,128)S(1)} %constant_dynamic-slice_fusion.2), channel_id=1, source_target_pairs={{0,8},{1,9},{2,10},{3,11},{4,12},{5,13},{6,14},{7,15},{8,0},{9,1},... | collective-permute-start | bytes 221192 | tf_op jit(solution)/shard_map/ppermute | solution.py:550
  90.6 2.6 %collective-permute-start.5 = (bf16[3,32,384]{2,1,0:T(8,128)(2,1)S(1)}, bf16[3,32,384]{2,1,0:T(8,128)(2,1)S(1)}, u32[]{:S(2)}, u32[]{:S(2)}) collective-permute-start(bf16[3,32,384]{2,1,0:T(8,128)(2,1)S(1)} %get-tuple-element.44), channel_id=1, source_target_pairs={{0,15},{1,0},{2,1},{3,2},{4,3},{5,4},{6,5},{7,6},{8,7},{9,8},{10,9... | collective-permute-start | bytes 221192 | tf_op jit(solution)/shard_map/ppermute | solution.py:581
  93.3 2.1 %collective-permute-done.4.left_ref = bf16[3,32,384]{2,1,0:T(8,128)(2,1)S(1)} collective-permute-done((bf16[3,32,384]{2,1,0:T(8,128)(2,1)S(1)}, bf16[3,32,384]{2,1,0:T(8,128)(2,1)S(1)}, u32[]{:S(2)}, u32[]{:S(2)}) %collective-permute-start.4) | collective-permute-done | bytes 73760 | tf_op jit(solution)/shard_map/ppermute | solution.py:580
  95.5 6.8 %collective-permute-start.6 = (bf16[3,48,384]{2,1,0:T(8,128)(2,1)S(1)}, bf16[3,48,384]{2,1,0:T(8,128)(2,1)S(1)}, u32[]{:S(2)}, u32[]{:S(2)}) collective-permute-start(bf16[3,48,384]{2,1,0:T(8,128)(2,1)S(1)} %get-tuple-element.45), channel_id=1, source_target_pairs={{0,16},{16,32},{32,48},{48,64},{64,80},{80,96},{96,112},{1,17},{17... | collective-permute-start | bytes 331784 | tf_op jit(solution)/shard_map/ppermute | solution.py:586
  102.4 1.9 %collective-permute-start.7 = (bf16[3,48,384]{2,1,0:T(8,128)(2,1)S(1)}, bf16[3,48,384]{2,1,0:T(8,128)(2,1)S(1)}, u32[]{:S(2)}, u32[]{:S(2)}) collective-permute-start(bf16[3,48,384]{2,1,0:T(8,128)(2,1)S(1)} %get-tuple-element.46), channel_id=1, source_target_pairs={{16,0},{32,16},{48,32},{64,48},{80,64},{96,80},{112,96},{17,1},{33... | collective-permute-start | bytes 331784 | tf_op jit(solution)/shard_map/ppermute | solution.py:587
  104.5 4.0 %collective-permute-done.7.bottom_ref = bf16[3,48,384]{2,1,0:T(8,128)(2,1)S(1)} collective-permute-done((bf16[3,48,384]{2,1,0:T(8,128)(2,1)S(1)}, bf16[3,48,384]{2,1,0:T(8,128)(2,1)S(1)}, u32[]{:S(2)}, u32[]{:S(2)}) %collective-permute-start.7) | collective-permute-done | bytes 110624 | tf_op jit(solution)/shard_map/ppermute | solution.py:587
  108.5 3.1 %finish.1 = f32[1024,384]{1,0:T(8,128)} custom-call(s32[4,4]{1,0:T(4,128)S(1)} %copy-done.5, f32[1024,384]{1,0:T(8,128)S(1)} %inner_conv.3.conv_ref, f32[49,384]{1,0:T(8,128)S(1)} %bitcast.26, bf16[3,32,384]{2,1,0:T(8,128)(2,1)S(1)} %collective-permute-done.4.left_ref, bf16[3,32,384]{2,1,0:T(8,128)(2,1)S(1)} %collective-permute-done.5.right_ref, ...), custom_call_target="tpu_custom_call" | custom-call | flops 3564999936 | bytes 1048576 | tf_op jit(solution)/shard_map/finish/pallas_call | solution.py:494
  (111 shorter events, 15.8 us)
Async XLA Ops:
  2.0 8.0 %copy-start.37 = (f32[1,1536]{1,0:T(1,128)S(1)}, f32[1,1536]{1,0:T(1,128)}, u32[]{:S(2)}) copy-start(f32[1,1536]{1,0:T(1,128)} %param.18) | copy-start | bytes 18436
  2.0 8.0 %copy-start.36 = (f32[1,49,384]{2,0,1:T(1,128)S(1)}, f32[1,49,384]{2,0,1:T(1,128)}, u32[]{:S(2)}) copy-start(f32[1,49,384]{2,0,1:T(1,128)} %param.13) | copy-start | bytes 225796
  2.0 8.1 %copy-start.1 = (f32[1,32,32,384]{3,2,1,0:T(8,128)S(1)}, f32[1,32,32,384]{3,2,1,0:T(8,128)}, u32[]{:S(2)}) copy-start(f32[1,32,32,384]{3,2,1,0:T(8,128)} %param.10) | copy-start | bytes 4718596
  2.5 17.9 %collective-permute-start = (bf16[3,32,384]{2,1,0:T(8,128)(2,1)S(1)}, bf16[3,32,384]{2,1,0:T(8,128)(2,1)S(1)}, u32[]{:S(2)}, u32[]{:S(2)}) collective-permute-start(bf16[3,32,384]{2,1,0:T(8,128)(2,1)S(1)} %get-tuple-element.27), channel_id=1, source_target_pairs={{0,1},{1,2},{2,3},{3,4},{4,5},{5,6},{6,7},{7,8},{8,9},{9,10},{10,1... | collective-permute-start | bytes 221192 | tf_op jit(solution)/shard_map/ppermute | solution.py:580
  4.6 15.8 %collective-permute-start.1 = (bf16[3,32,384]{2,1,0:T(8,128)(2,1)S(1)}, bf16[3,32,384]{2,1,0:T(8,128)(2,1)S(1)}, u32[]{:S(2)}, u32[]{:S(2)}) collective-permute-start(bf16[3,32,384]{2,1,0:T(8,128)(2,1)S(1)} %get-tuple-element.28), channel_id=1, source_target_pairs={{0,15},{1,0},{2,1},{3,2},{4,3},{5,4},{6,5},{7,6},{8,7},{9,8},{10,9... | collective-permute-start | bytes 221192 | tf_op jit(solution)/shard_map/ppermute | solution.py:581
  10.1 8.3 %copy-start.3 = (bf16[1,1536,384]{2,1,0:T(8,128)(2,1)S(1)}, bf16[1,1536,384]{2,1,0:T(8,128)(2,1)}, u32[]{:S(2)}) copy-start(bf16[1,1536,384]{2,1,0:T(8,128)(2,1)} %param.17) | copy-start | bytes 3538948
  10.1 8.3 %copy-start.4 = (bf16[1,1536,384]{2,1,0:T(8,128)(2,1)S(1)}, bf16[1,1536,384]{2,1,0:T(8,128)(2,1)}, u32[]{:S(2)}) copy-start(bf16[1,1536,384]{2,1,0:T(8,128)(2,1)} %param.19) | copy-start | bytes 3538948
  20.4 7.8 %copy-start.2 = (f32[1,32,32,384]{3,2,1,0:T(8,128)S(1)}, f32[1,32,32,384]{3,2,1,0:T(8,128)}, u32[]{:S(2)}) copy-start(f32[1,32,32,384]{3,2,1,0:T(8,128)} %param.11) | copy-start | bytes 4718596
  20.4 7.8 %copy-start.5 = (s32[4,4]{1,0:T(4,128)S(1)}, s32[4,4]{1,0:T(4,128)}, u32[]{:S(2)}) copy-start(s32[4,4]{1,0:T(4,128)} %counts_ref.3) | copy-start | bytes 196
  22.2 9.1 %collective-permute-start.2 = (bf16[3,48,384]{2,1,0:T(8,128)(2,1)S(1)}, bf16[3,48,384]{2,1,0:T(8,128)(2,1)S(1)}, u32[]{:S(2)}, u32[]{:S(2)}) collective-permute-start(bf16[3,48,384]{2,1,0:T(8,128)(2,1)S(1)} %get-tuple-element.29), channel_id=1, source_target_pairs={{0,16},{16,32},{32,48},{48,64},{64,80},{80,96},{96,112},{1,17},{17... | collective-permute-start | bytes 331784 | tf_op jit(solution)/shard_map/ppermute | solution.py:586
  26.3 6.1 %collective-permute-start.3 = (bf16[3,48,384]{2,1,0:T(8,128)(2,1)S(1)}, bf16[3,48,384]{2,1,0:T(8,128)(2,1)S(1)}, u32[]{:S(2)}, u32[]{:S(2)}) collective-permute-start(bf16[3,48,384]{2,1,0:T(8,128)(2,1)S(1)} %get-tuple-element.30), channel_id=1, source_target_pairs={{16,0},{32,16},{48,32},{64,48},{80,64},{96,80},{112,96},{17,1},{33... | collective-permute-start | bytes 331784 | tf_op jit(solution)/shard_map/ppermute | solution.py:587
  31.3 8.7 %copy-start.16 = (bf16[1024,384]{1,0:T(8,128)(2,1)S(1)}, bf16[1024,384]{1,0:T(8,128)(2,1)}, u32[]{:S(2)}) copy-start(bf16[1024,384]{1,0:T(8,128)(2,1)} %copy-done.15) | copy-start | bytes 2359300
  31.3 8.7 %copy-start.19 = (bf16[384,1024]{1,0:T(8,128)(2,1)S(1)}, bf16[384,1024]{1,0:T(8,128)(2,1)}, u32[]{:S(2)}) copy-start(bf16[384,1024]{1,0:T(8,128)(2,1)} %copy-done.18) | copy-start | bytes 2359300
  31.3 8.8 %copy-start.22 = (bf16[1536,384]{1,0:T(8,128)(2,1)S(1)}, bf16[1536,384]{1,0:T(8,128)(2,1)}, u32[]{:S(2)}) copy-start(bf16[1536,384]{1,0:T(8,128)(2,1)} %copy-done.21) | copy-start | bytes 3538948
  31.3 8.8 %copy-start.25 = (bf16[1536,384]{1,0:T(8,128)(2,1)S(1)}, bf16[1536,384]{1,0:T(8,128)(2,1)}, u32[]{:S(2)}) copy-start(bf16[1536,384]{1,0:T(8,128)(2,1)} %copy-done.24) | copy-start | bytes 3538948
  31.3 8.8 %copy-start.28 = (f32[1536,128]{1,0:T(8,128)S(1)}, f32[1536,128]{1,0:T(8,128)}, u32[]{:S(2)}) copy-start(f32[1536,128]{1,0:T(8,128)} %copy-done.27) | copy-start | bytes 2359300
  40.1 6.2 %copy-start.32 = (bf16[1024,384]{1,0:T(8,128)(2,1)}, bf16[1024,384]{1,0:T(8,128)(2,1)S(1)}, u32[]{:S(2)}) copy-start(bf16[1024,384]{1,0:T(8,128)(2,1)S(1)} %get-tuple-element.31.normed_ref) | copy-start | bytes 2359300
  40.1 6.2 %copy-start.34 = (bf16[384,1024]{1,0:T(8,128)(2,1)}, bf16[384,1024]{1,0:T(8,128)(2,1)S(1)}, u32[]{:S(2)}) copy-start(bf16[384,1024]{1,0:T(8,128)(2,1)S(1)} %get-tuple-element.32.normed_t_ref) | copy-start | bytes 2359300
  47.4 14.3 %collective-permute-start.8 = (bf16[768,768]{1,0:T(8,128)(2,1)S(1)}, bf16[768,768]{1,0:T(8,128)(2,1)}, u32[]{:S(2)}, u32[]{:S(2)}) collective-permute-start(bf16[768,768]{1,0:T(8,128)(2,1)S(1)} %get-tuple-element.48), channel_id=1, source_target_pairs={{0,16},{16,0},{32,48},{48,32},{64,80},{80,64},{96,112},{112,96},{1... | collective-permute-start | bytes 3538952 | tf_op jit(solution)/shard_map/ppermute | solution.py:615
  63.6 5.9 %collective-permute-start.11 = (bf16[192,768]{1,0:T(8,128)(2,1)S(1)}, bf16[192,768]{1,0:T(8,128)(2,1)S(1)}, u32[]{:S(2)}, u32[]{:S(2)}) collective-permute-start(bf16[192,768]{1,0:T(8,128)(2,1)S(1)} %get-tuple-element.61), channel_id=1, source_target_pairs={{0,96},{1,97},{2,98},{3,99},{4,100},{5,101},{6,102},{7,103},{8,104... | collective-permute-start | bytes 884744 | tf_op jit(solution)/shard_map/ppermute | solution.py:534
  63.7 7.5 %collective-permute-start.10 = (bf16[192,768]{1,0:T(8,128)(2,1)S(1)}, bf16[192,768]{1,0:T(8,128)(2,1)S(1)}, u32[]{:S(2)}, u32[]{:S(2)}) collective-permute-start(bf16[192,768]{1,0:T(8,128)(2,1)S(1)} %get-tuple-element.62), channel_id=1, source_target_pairs={{0,64},{1,65},{2,66},{3,67},{4,68},{5,69},{6,70},{7,71},{8,72},{9,... | collective-permute-start | bytes 884744 | tf_op jit(solution)/shard_map/ppermute | solution.py:534
  66.3 8.1 %collective-permute-start.9 = (bf16[192,768]{1,0:T(8,128)(2,1)S(1)}, bf16[192,768]{1,0:T(8,128)(2,1)S(1)}, u32[]{:S(2)}, u32[]{:S(2)}) collective-permute-start(bf16[192,768]{1,0:T(8,128)(2,1)S(1)} %get-tuple-element.60), channel_id=1, source_target_pairs={{0,32},{1,33},{2,34},{3,35},{4,36},{5,37},{6,38},{7,39},{8,40},{9,... | collective-permute-start | bytes 884744 | tf_op jit(solution)/shard_map/ppermute | solution.py:534
  74.5 10.4 %collective-permute-start.14 = (bf16[48,768]{1,0:T(8,128)(2,1)S(1)}, bf16[48,768]{1,0:T(8,128)(2,1)S(1)}, u32[]{:S(2)}, u32[]{:S(2)}) collective-permute-start(bf16[48,768]{1,0:T(8,128)(2,1)S(1)} %get-tuple-element.64), channel_id=1, source_target_pairs={{0,129},{1,0},{2,131},{3,2},{4,133},{5,4},{6,135},{7,6},{8,137},{9... | collective-permute-start | bytes 221192 | tf_op jit(solution)/shard_map/ppermute | solution.py:534
  76.7 8.2 %collective-permute-start.13 = (bf16[48,768]{1,0:T(8,128)(2,1)S(1)}, bf16[48,768]{1,0:T(8,128)(2,1)S(1)}, u32[]{:S(2)}, u32[]{:S(2)}) collective-permute-start(bf16[48,768]{1,0:T(8,128)(2,1)S(1)} %get-tuple-element.65), channel_id=1, source_target_pairs={{0,128},{1,129},{2,130},{3,131},{4,132},{5,133},{6,134},{7,135},{8... | collective-permute-start | bytes 221192 | tf_op jit(solution)/shard_map/ppermute | solution.py:534
  77.5 7.4 %collective-permute-start.12 = (bf16[48,768]{1,0:T(8,128)(2,1)S(1)}, bf16[48,768]{1,0:T(8,128)(2,1)S(1)}, u32[]{:S(2)}, u32[]{:S(2)}) collective-permute-start(bf16[48,768]{1,0:T(8,128)(2,1)S(1)} %get-tuple-element.63), channel_id=1, source_target_pairs={{0,1},{1,128},{2,3},{3,130},{4,5},{5,132},{6,7},{7,134},{8,9},{9,1... | collective-permute-start | bytes 221192 | tf_op jit(solution)/shard_map/ppermute | solution.py:534
  85.0 8.2 %collective-permute-start.15 = (f32[24,768]{1,0:T(8,128)S(1)}, f32[24,768]{1,0:T(8,128)S(1)}, u32[]{:S(2)}, u32[]{:S(2)}) collective-permute-start(f32[24,768]{1,0:T(8,128)S(1)} %constant_dynamic-slice_fusion.2), channel_id=1, source_target_pairs={{0,8},{1,9},{2,10},{3,11},{4,12},{5,13},{6,14},{7,15},{8,0},{9,1},... | collective-permute-start | bytes 221192 | tf_op jit(solution)/shard_map/ppermute | solution.py:550
  89.6 5.9 %collective-permute-start.4 = (bf16[3,32,384]{2,1,0:T(8,128)(2,1)S(1)}, bf16[3,32,384]{2,1,0:T(8,128)(2,1)S(1)}, u32[]{:S(2)}, u32[]{:S(2)}) collective-permute-start(bf16[3,32,384]{2,1,0:T(8,128)(2,1)S(1)} %get-tuple-element.43), channel_id=1, source_target_pairs={{0,1},{1,2},{2,3},{3,4},{4,5},{5,6},{6,7},{7,8},{8,9},{9,10},{10,1... | collective-permute-start | bytes 221192 | tf_op jit(solution)/shard_map/ppermute | solution.py:580
  90.6 4.8 %collective-permute-start.5 = (bf16[3,32,384]{2,1,0:T(8,128)(2,1)S(1)}, bf16[3,32,384]{2,1,0:T(8,128)(2,1)S(1)}, u32[]{:S(2)}, u32[]{:S(2)}) collective-permute-start(bf16[3,32,384]{2,1,0:T(8,128)(2,1)S(1)} %get-tuple-element.44), channel_id=1, source_target_pairs={{0,15},{1,0},{2,1},{3,2},{4,3},{5,4},{6,5},{7,6},{8,7},{9,8},{10,9... | collective-permute-start | bytes 221192 | tf_op jit(solution)/shard_map/ppermute | solution.py:581
  93.2 11.1 %collective-permute-start.16 = (f32[12,768]{1,0:T(8,128)S(1)}, f32[12,768]{1,0:T(8,128)S(1)}, u32[]{:S(2)}, u32[]{:S(2)}) collective-permute-start(f32[12,768]{1,0:T(8,128)S(1)} %constant_dynamic-slice_fusion.1), channel_id=1, source_target_pairs={{0,4},{1,5},{2,6},{3,7},{4,0},{5,1},{6,2},{7,3},{8,12},{9,13},{10,... | collective-permute-start | bytes 110600 | tf_op jit(solution)/shard_map/ppermute | solution.py:550
  95.5 8.9 %collective-permute-start.6 = (bf16[3,48,384]{2,1,0:T(8,128)(2,1)S(1)}, bf16[3,48,384]{2,1,0:T(8,128)(2,1)S(1)}, u32[]{:S(2)}, u32[]{:S(2)}) collective-permute-start(bf16[3,48,384]{2,1,0:T(8,128)(2,1)S(1)} %get-tuple-element.45), channel_id=1, source_target_pairs={{0,16},{16,32},{32,48},{48,64},{64,80},{80,96},{96,112},{1,17},{17... | collective-permute-start | bytes 331784 | tf_op jit(solution)/shard_map/ppermute | solution.py:586
  102.4 6.1 %collective-permute-start.7 = (bf16[3,48,384]{2,1,0:T(8,128)(2,1)S(1)}, bf16[3,48,384]{2,1,0:T(8,128)(2,1)S(1)}, u32[]{:S(2)}, u32[]{:S(2)}) collective-permute-start(bf16[3,48,384]{2,1,0:T(8,128)(2,1)S(1)} %get-tuple-element.46), channel_id=1, source_target_pairs={{16,0},{32,16},{48,32},{64,48},{80,64},{96,80},{112,96},{17,1},{33... | collective-permute-start | bytes 331784 | tf_op jit(solution)/shard_map/ppermute | solution.py:587
  104.4 7.2 %collective-permute-start.17 = (f32[6,768]{1,0:T(8,128)S(1)}, f32[6,768]{1,0:T(8,128)S(1)}, u32[]{:S(2)}, u32[]{:S(2)}) collective-permute-start(f32[6,768]{1,0:T(8,128)S(1)} %constant_dynamic-slice_fusion), channel_id=1, source_target_pairs={{0,2},{1,3},{2,0},{3,1},{4,6},{5,7},{6,4},{7,5},{8,10},{9,11},{10,... | collective-permute-start | bytes 55304 | tf_op jit(solution)/shard_map/ppermute | solution.py:550
  (24 other events, 48.2 us)

commit v3 on v2

--- a/solution.py
+++ b/solution.py
@@ -83,8 +83,8 @@
         in_specs=[block, pl.BlockSpec((49, lanes), lambda c: (0, c))],
         out_specs=block,
         scratch_shapes=[pltpu.VMEM((total + 2 * reach * side, lanes), f32)],
-        compiler_params=params(16),
-        cost_estimate=cost(7.8),
+        compiler_params=params(6),
+        cost_estimate=cost(7.0),
         name="inner_conv",
     )(cells, kernel)
 
@@ -108,7 +108,7 @@
             pl.BlockSpec((side, 8, channels), lambda g: (0, side // 8 - 1, 0)),
         ],
         out_specs=[pl.BlockSpec((reach, side, channels), lambda g: (0, 0, 0))] * 2,
-        compiler_params=params(16),
+        compiler_params=params(4),
         cost_estimate=cost(1.0),
         name="side_cols",
     )(grid3, grid3)
@@ -139,7 +139,7 @@
         out_shape=(shape, shape),
         in_specs=[whole] * 4,
         out_specs=[whole] * 2,
-        compiler_params=params(16),
+        compiler_params=params(6),
         cost_estimate=cost(0.8),
         name="side_rows",
     )(cells[:edge], cells[-edge:], left, right)
@@ -254,8 +254,8 @@
         in_specs=[whole] * 9,
         out_specs=[whole] * 4,
         scratch_shapes=[pltpu.VMEM((2 * reach, side, channels), f32)] * 2,
-        compiler_params=params(32),
-        cost_estimate=cost(6.2),
+        compiler_params=params(12),
+        cost_estimate=cost(4.8),
         name="normalise",
     )(conv, kernel, left, right, top, bottom, bias, gain, shift)
 
@@ -305,8 +305,8 @@
         ),
         in_specs=[pl.BlockSpec(memory_space=pltpu.SMEM), whole],
         out_specs=[whole] * 2,
-        compiler_params=params(16),
-        cost_estimate=cost(2.2),
+        compiler_params=params(8),
+        cost_estimate=cost(1.3),
         name="mask_rows",
     )(counts, grad)
 
@@ -345,8 +345,8 @@
         ),
         in_specs=[whole] * 3,
         out_specs=[whole] * 4,
-        compiler_params=params(32),
-        cost_estimate=cost(3.0),
+        compiler_params=params(12),
+        cost_estimate=cost(1.1),
         name="arrange",
     )(expand, reduce, bias.reshape(16, 96))
 
@@ -424,8 +424,8 @@
                 pl.BlockSpec((hidden_block, total), lambda i, core: (i, 0)),
             ],
         ),
-        compiler_params=params(40),
-        cost_estimate=cost(6.9),
+        compiler_params=params(20),
+        cost_estimate=cost(6.1),
         name="hidden_half",
     )(core, normed, normed_t, grad, grad_t, expand, reduce, bias)
 
@@ -466,8 +466,8 @@
         out_shape=(jax.ShapeDtypeStruct((side, side, channels), f32), shape, shape),
         in_specs=[pl.BlockSpec(memory_space=pltpu.SMEM)] + [whole] * 6,
         out_specs=[whole] * 3,
-        compiler_params=params(40),
-        cost_estimate=cost(3.3),
+        compiler_params=params(14),
+        cost_estimate=cost(2.2),
         name="norm_back",
     )(core, turned, other, mine, unit, spread, gain)
     return found.reshape(total, channels), first, last
@@ -497,10 +497,61 @@
         in_specs=[pl.BlockSpec(memory_space=pltpu.SMEM)] + [whole] * 7,
         out_specs=whole,
         scratch_shapes=[pltpu.VMEM((2 * reach, side, channels), f32)] * 2,
-        compiler_params=params(32),
+        compiler_params=params(12),
         cost_estimate=cost(3.1),
         name="finish",
     )(counts, conv, kernel, left, right, top, bottom, grad)
+
+
+def combine_body(place_ref, mine_ref, arrived_ref, own_ref, *sent_refs):
+    size = own_ref.shape[0]
+    for step in range(4):
+        chunk = lax.rem(place_ref[0] + step, 4)
+        at = pl.ds(pl.multiple_of(chunk * size, size), size)
+        total = mine_ref[at, :] + arrived_ref[at, :].astype(f32)
+        if step == 0:
+            own_ref[...] = total
+        else:
+            sent_refs[step - 1][...] = total.astype(bf16)
+
+
+def combine(place, mine, arrived):
+    size, width = mine.shape[0] // 4, mine.shape[1]
+    sent = jax.ShapeDtypeStruct((size, width), bf16)
+    return pl.pallas_call(
+        combine_body,
+        out_shape=(jax.ShapeDtypeStruct((size, width), f32), sent, sent, sent),
+        in_specs=[pl.BlockSpec(memory_space=pltpu.SMEM), whole, whole],
+        out_specs=[whole] * 4,
+        compiler_params=params(10),
+        cost_estimate=cost(0.7),
+        name="combine",
+    )(place, mine, arrived)
+
+
+def last_sum_body(scale, place_ref, rows_ref, arrived_ref, expand_ref, reduce_ref):
+    size = arrived_ref.shape[0]
+    channels = expand_ref.shape[2]
+    low, high = rows_ref[:size], rows_ref[size:]
+    total = (jnp.where(place_ref[0] == 0, low, high) + arrived_ref[...]) * scale
+    for r in range(size):
+        expand_ref[r] = total[r : r + 1, :channels]
+        reduce_ref[r] = total[r : r + 1, channels:]
+
+
+def last_sum(place, rows, arrived, scale):
+    size, width = arrived.shape
+    shape = jax.ShapeDtypeStruct((size, 1, width // 2), f32)
+    expand, reduce = pl.pallas_call(
+        functools.partial(last_sum_body, scale),
+        out_shape=(shape, shape),
+        in_specs=[pl.BlockSpec(memory_space=pltpu.SMEM), whole, whole],
+        out_specs=[whole] * 2,
+        compiler_params=params(4),
+        cost_estimate=cost(0.5),
+        name="last_sum",
+    )(place, rows, arrived)
+    return expand.transpose(1, 0, 2), reduce.transpose(1, 0, 2)
 
 
 every_axis = ("dp", "lat", "lon")
@@ -526,10 +577,16 @@
     return device_pairs(move)
 
 
+def add_parts(own, parts):
+    for part in parts:
+        own = own + part.astype(jnp.float32)
+    return own
+
+
 def scatter_direct(rows, place, pairs_of):
     size = rows.shape[0] // 4
     narrow = rows.astype(jnp.bfloat16)
-    total = lax.dynamic_slice_in_dim(rows, place * size, size, 0)
+    own = lax.dynamic_slice_in_dim(rows, place * size, size, 0)
     arrived = [
         lax.ppermute(
             lax.dynamic_slice_in_dim(narrow, ((place + step) % 4) * size, size, 0),
@@ -538,9 +595,7 @@
         )
         for step in range(1, 4)
     ]
-    for part in arrived:
-        total = total + part.astype(jnp.float32)
-    return total
+    return add_parts(own, arrived)
 
 
 def scatter_halving(rows, z):
@@ -552,18 +607,9 @@
             every_axis,
             device_pairs(lambda hi, y, core, z, lo, bit=bit: (hi, y, core, z ^ bit, lo)),
         )
-        rows = lax.dynamic_slice_in_dim(rows, upper * size, size, 0) + arrived
-    return rows
-
-
-def scatter_rows(mine, arrived):
-    lat, lon = lax.axis_index("lat"), lax.axis_index("lon")
-    y, core, z, lo = lat // 2, lat % 2, lon // 2, lon % 2
-    x = 2 * lax.axis_index("dp") + lo
-    rows = mine + arrived.astype(jnp.float32)
-    rows = scatter_direct(rows, jnp.where(core == 0, y, x), lambda step: plane_pairs(step, True))
-    rows = scatter_direct(rows, jnp.where(core == 0, x, y), lambda step: plane_pairs(step, False))
-    return scatter_halving(rows, z)
+        if bit > 1:
+            rows = lax.dynamic_slice_in_dim(rows, upper * size, size, 0) + arrived
+    return rows, arrived, upper
 
 
 def shifted(axis, step, closed):
@@ -616,16 +662,28 @@
     mine, near_pre = hidden_half(
         near, normed, normed_t, rows, rows_t, expand, reduce, bias, jnp.float32
     )
+    lon = lax.axis_index("lon")
+    z, x = lon // 2, 2 * lax.axis_index("dp") + lon % 2
+    y = lax.axis_index("lat") // 2
+    first_place, second_place = jnp.where(core == 0, y, x), jnp.where(core == 0, x, y)
+    own, *sent = combine(first_place.astype(jnp.int32).reshape(1), mine, arrived)
+    sent, near_pre = lax.optimization_barrier((sent, near_pre))
+    parts = [lax.ppermute(s, every_axis, plane_pairs(i + 1, True)) for i, s in enumerate(sent)]
     conv_grad, first, last = norm_back(near, expand_t, far_pre, near_pre, unit, spread, norm_gain)
-    kept = scatter_rows(mine, arrived)
     left, right = lon_halo(first, last)
+    back = inner_conv(conv_grad, kernel, True)
+    own, parts, back, left, right = lax.optimization_barrier((own, parts, back, left, right))
+    summed = add_parts(own, parts)
     top, bottom = lat_halo(*side_rows(conv_grad, left, right))
-    back = inner_conv(conv_grad, kernel, True)
+    summed = scatter_direct(summed, second_place, lambda step: plane_pairs(step, False))
+    summed, arrived, upper = scatter_halving(summed, z)
     gradient = finish(counts, back, kernel, left, right, top, bottom, grad)
 
     cells_all = lax.axis_size("dp") * lax.axis_size("lat") * lax.axis_size("lon") * total
-    kept = kept * (1.0 / math.sqrt(cells_all))
-    return (gradient.reshape(state.shape), kept[None, :, :channels], kept[None, :, channels:])
+    kept = last_sum(
+        upper.astype(jnp.int32).reshape(1), summed, arrived, 1.0 / math.sqrt(cells_all)
+    )
+    return (gradient.reshape(state.shape), *kept)
 
 
 def solution(mesh):

time: 113 us -> 107 us (0.947)
  the two profiles are of different devices: /device:TPU:1 before, /device:TPU:33 now
where the time goes in v3:
time: 107 us
  Pallas kernels  40.3 us (38%)
  starting transfers between devices  39.5 us (37%)
  local copies, waits for them, and re-layouts  14.4 us (13%)
  waiting for transfers between devices  11.4 us (11%)
  between operations  1.13 us (1%)
    unnamed x69, local copies, waits for them, and re-layouts  14.2 us
    pallas_call x2, Pallas kernels, inner_conv(): pl.pallas_call(functools.partial(inner_conv_body, flipped), out_shape=jax...  14.2 us
    ppermute x2, starting transfers between devices, lat_halo(): top = lax.ppermute(down, 'lat', shifted('lat', 1, False))  13.4 us
    pallas_call x2, Pallas kernels, hidden_half(): pl.pallas_call(hidden_body, out_shape=(jax.ShapeDtypeStruct((half, 2 * ch...  12.3 us
    ppermute x3, starting transfers between devices, scatter_halving(): lax.ppermute(lax.dynamic_slice_in_dim(rows, (1 - upper) * size, size, 0),...  8.23 us
    ppermute x2, waiting for transfers between devices, lat_halo(): bottom = lax.ppermute(up, 'lat', shifted('lat', -1, False))  5.64 us
    ppermute x3, starting transfers between devices, local(): lax.ppermute(s, every_axis, plane_pairs(i + 1, True))  4.87 us
    pallas_call x1, Pallas kernels, normalise(): pl.pallas_call(normalise_body, out_shape=(jax.ShapeDtypeStruct((total, ch...  4.72 us
  transfers between devices with their start and end apart: 18, of which 5 were waited for; matrix products, arithmetic and copies ran while one was open for 0% of the time, Pallas kernels for 26%

profile of v3, /device:TPU:33, one launch (start us, length us, event | category | flops | bytes accessed | tf_op | source)
XLA Modules:
  0.0 106.9 jit_solution(11663135663578818400)
XLA Ops:
  0.6 1.4 %copy-done = f32[1,32,32,384]{3,2,1,0:T(8,128)S(1)} copy-done((f32[1,32,32,384]{3,2,1,0:T(8,128)S(1)}, f32[1,32,32,384]{3,2,1,0:T(8,128)}, u32[]{:S(2)}) %copy-start) | copy-done | bytes 1572888
  2.5 1.3 %collective-permute-start = (bf16[3,32,384]{2,1,0:T(8,128)(2,1)S(1)}, bf16[3,32,384]{2,1,0:T(8,128)(2,1)S(1)}, u32[]{:S(2)}, u32[]{:S(2)}) collective-permute-start(bf16[3,32,384]{2,1,0:T(8,128)(2,1)S(1)} %get-tuple-element.43), channel_id=1, source_target_pairs={{0,1},{1,2},{2,3},{3,4},{4,5},{5,6},{6,7},{7,8},{8,9},{9,10},{10,1... | collective-permute-start | bytes 221192 | tf_op jit(solution)/shard_map/ppermute | solution.py:626
  3.8 1.2 %collective-permute-start.1 = (bf16[3,32,384]{2,1,0:T(8,128)(2,1)S(1)}, bf16[3,32,384]{2,1,0:T(8,128)(2,1)S(1)}, u32[]{:S(2)}, u32[]{:S(2)}) collective-permute-start(bf16[3,32,384]{2,1,0:T(8,128)(2,1)S(1)} %get-tuple-element.44), channel_id=1, source_target_pairs={{0,15},{1,0},{2,1},{3,2},{4,3},{5,4},{6,5},{7,6},{8,7},{9,8},{10,9... | collective-permute-start | bytes 221192 | tf_op jit(solution)/shard_map/ppermute | solution.py:627
  5.1 7.1 %inner_conv.2.conv_ref = f32[1024,384]{1,0:T(8,128)S(1)} custom-call(f32[1024,384]{1,0:T(8,128)S(1)} %bitcast.29, f32[49,384]{1,0:T(8,128)S(1)} %bitcast.23), custom_call_target="tpu_custom_call" | custom-call | flops 8049999872 | bytes 1048576 | tf_op jit(solution)/shard_map/inner_conv/pallas_call | solution.py:79
  12.2 1.3 %mask_rows.1 = (bf16[1024,384]{1,0:T(8,128)(2,1)S(1)}, bf16[384,1024]{1,0:T(8,128)(2,1)S(1)}) custom-call(s32[4,4]{1,0:T(4,128)S(1)} %copy-done.6, f32[1024,384]{1,0:T(8,128)S(1)} %bitcast.31), custom_call_target="tpu_custom_call" | custom-call | flops 1495000064 | bytes 1048576 | tf_op jit(solution)/shard_map/mask_rows/pallas_call | solution.py:300
  13.7 4.6 %collective-permute-start.2 = (bf16[3,48,384]{2,1,0:T(8,128)(2,1)S(1)}, bf16[3,48,384]{2,1,0:T(8,128)(2,1)S(1)}, u32[]{:S(2)}, u32[]{:S(2)}) collective-permute-start(bf16[3,48,384]{2,1,0:T(8,128)(2,1)S(1)} %get-tuple-element.45), channel_id=1, source_target_pairs={{0,16},{16,32},{32,48},{48,64},{64,80},{80,96},{96,112},{1,17},{17... | collective-permute-start | bytes 331784 | tf_op jit(solution)/shard_map/ppermute | solution.py:632
  18.3 1.9 %collective-permute-start.3 = (bf16[3,48,384]{2,1,0:T(8,128)(2,1)S(1)}, bf16[3,48,384]{2,1,0:T(8,128)(2,1)S(1)}, u32[]{:S(2)}, u32[]{:S(2)}) collective-permute-start(bf16[3,48,384]{2,1,0:T(8,128)(2,1)S(1)} %get-tuple-element.46), channel_id=1, source_target_pairs={{16,0},{32,16},{48,32},{64,48},{80,64},{96,80},{112,96},{17,1},{33... | collective-permute-start | bytes 331784 | tf_op jit(solution)/shard_map/ppermute | solution.py:633
  22.4 1.9 %collective-permute-done.3.bottom_ref = bf16[3,48,384]{2,1,0:T(8,128)(2,1)S(1)} collective-permute-done((bf16[3,48,384]{2,1,0:T(8,128)(2,1)S(1)}, bf16[3,48,384]{2,1,0:T(8,128)(2,1)S(1)}, u32[]{:S(2)}, u32[]{:S(2)}) %collective-permute-start.3) | collective-permute-done | bytes 110624 | tf_op jit(solution)/shard_map/ppermute | solution.py:633
  24.3 4.7 %normalise.1 = (f32[1024,384]{1,0:T(8,128)S(1)}, f32[1024,128]{1,0:T(8,128)S(1)}, bf16[1024,384]{1,0:T(8,128)(2,1)S(1)}, bf16[384,1024]{1,0:T(8,128)(2,1)S(1)}) custom-call(f32[1024,384]{1,0:T(8,128)S(1)} %inner_conv.2.conv_ref, f32[49,384]{1,0:T(8,128)S(1)} %bitcast.24, bf16[3,32,384]{2,1,0:T(8,128)(2,1)S(1)} %collective-permute-done.left_ref, ...), custom_call_target="tpu_custom_call" | custom-call | flops 5520000000 | bytes 1048576 | tf_op jit(solution)/shard_map/normalise/pallas_call | solution.py:246
  29.1 1.2 %copy-done.16 = f32[1024,384]{1,0:T(8,128)} copy-done((f32[1024,384]{1,0:T(8,128)}, f32[1024,384]{1,0:T(8,128)S(1)}, u32[]{:S(2)}) %copy-start.16) | copy-done | bytes 1572888
  30.3 6.2 %hidden_half.3 = (bf16[768,768]{1,0:T(8,128)(2,1)S(1)}, bf16[768,1024]{1,0:T(8,128)(2,1)S(1)}) custom-call(s32[1]{0:T(128)S(6)} %sub.27.core_ref, bf16[1024,384]{1,0:T(8,128)(2,1)S(1)} %get-tuple-element.47.normed_ref, bf16[384,1024]{1,0:T(8,128)(2,1)S(1)} %get-tuple-element.48.normed_t_ref, bf16[1024,384]{1,0:T(8,128)(2,1)S(1)} %get-tuple-element.49.grad_ref, ...), custom_call_target="tpu_custom_call" | custom-call | flops 7015000064 | bytes 1048576 | tf_op jit(solution)/shard_map/hidden_half/pallas_call | solution.py:404
  36.5 1.1 %copy-done.18 = bf16[768,1024]{1,0:T(8,128)(2,1)} copy-done((bf16[768,1024]{1,0:T(8,128)(2,1)}, bf16[768,1024]{1,0:T(8,128)(2,1)S(1)}, u32[]{:S(2)}) %copy-start.18) | copy-done | bytes 1572888
  37.7 1.3 %copy-done.13 = bf16[1536,384]{1,0:T(8,128)(2,1)S(1)} copy-done((bf16[1536,384]{1,0:T(8,128)(2,1)S(1)}, bf16[1536,384]{1,0:T(8,128)(2,1)}, u32[]{:S(2)}) %copy-start.13) | copy-done | bytes 1179672
  38.9 1.3 %copy-done.15 = bf16[1536,384]{1,0:T(8,128)(2,1)S(1)} copy-done((bf16[1536,384]{1,0:T(8,128)(2,1)S(1)}, bf16[1536,384]{1,0:T(8,128)(2,1)}, u32[]{:S(2)}) %copy-start.15) | copy-done | bytes 1179672
  45.9 6.1 %hidden_half.2 = (f32[768,768]{1,0:T(8,128)S(1)}, bf16[768,1024]{1,0:T(8,128)(2,1)S(1)}) custom-call(s32[1]{0:T(128)} %bitcast.1.core_ref, bf16[1024,384]{1,0:T(8,128)(2,1)S(1)} %copy-done.29, bf16[384,1024]{1,0:T(8,128)(2,1)S(1)} %copy-done.31, bf16[1024,384]{1,0:T(8,128)(2,1)S(1)} %copy-done.23, bf16[384,1024]{1,0:T(8,128)(2,1)S(1)} %copy-done.25, ...), custom_call_target="tpu_custom_call" | custom-call | flops 7015000064 | bytes 1048576 | tf_op jit(solution)/shard_map/hidden_half/pallas_call | solution.py:404
  52.7 2.6 %collective-permute-start.6 = (bf16[192,768]{1,0:T(8,128)(2,1)S(1)}, bf16[192,768]{1,0:T(8,128)(2,1)S(1)}, u32[]{:S(2)}, u32[]{:S(2)}) collective-permute-start(bf16[192,768]{1,0:T(8,128)(2,1)S(1)} %get-tuple-element.62), channel_id=1, source_target_pairs={{0,64},{1,65},{2,66},{3,67},{4,68},{5,69},{6,70},{7,71},{8,72},{9,... | collective-permute-start | bytes 884744 | tf_op jit(solution)/shard_map/ppermute | solution.py:671
  55.3 1.9 %collective-permute-start.7 = (bf16[192,768]{1,0:T(8,128)(2,1)S(1)}, bf16[192,768]{1,0:T(8,128)(2,1)S(1)}, u32[]{:S(2)}, u32[]{:S(2)}) collective-permute-start(bf16[192,768]{1,0:T(8,128)(2,1)S(1)} %get-tuple-element.63), channel_id=1, source_target_pairs={{0,96},{1,97},{2,98},{3,99},{4,100},{5,101},{6,102},{7,103},{8,104... | collective-permute-start | bytes 884744 | tf_op jit(solution)/shard_map/ppermute | solution.py:671
  57.2 2.1 %norm_back.1 = (f32[32,32,384]{2,1,0:T(8,128)S(1)}, bf16[3,32,384]{2,1,0:T(8,128)(2,1)S(1)}, bf16[3,32,384]{2,1,0:T(8,128)(2,1)S(1)}) custom-call(s32[1]{0:T(128)} %bitcast.1.core_ref, bf16[384,1536]{1,0:T(8,128)(2,1)S(1)} %copy-done.11, bf16[768,1024]{1,0:T(8,128)(2,1)S(1)} %copy-done.19, bf16[768,1024]{1,0:T(8,128)(2,1)S(1)} %get-tuple-element.66.mine_ref, ...), custom_call_target="tpu_custom_call" | custom-call | flops 2529999872 | bytes 1048576 | tf_op jit(solution)/shard_map/norm_back/pallas_call | solution.py:464
  59.4 2.8 %collective-permute-start.9 = (bf16[3,32,384]{2,1,0:T(8,128)(2,1)S(1)}, bf16[3,32,384]{2,1,0:T(8,128)(2,1)S(1)}, u32[]{:S(2)}, u32[]{:S(2)}) collective-permute-start(bf16[3,32,384]{2,1,0:T(8,128)(2,1)S(1)} %get-tuple-element.71), channel_id=1, source_target_pairs={{0,15},{1,0},{2,1},{3,2},{4,3},{5,4},{6,5},{7,6},{8,7},{9,8},{10,9... | collective-permute-start | bytes 221192 | tf_op jit(solution)/shard_map/ppermute | solution.py:627
  62.2 7.1 %inner_conv.3.conv_ref = f32[1024,384]{1,0:T(8,128)S(1)} custom-call(f32[1024,384]{1,0:T(8,128)S(1)} %bitcast.30, f32[49,384]{1,0:T(8,128)S(1)} %bitcast.25), custom_call_target="tpu_custom_call" | custom-call | flops 8049999872 | bytes 1048576 | tf_op jit(solution)/shard_map/inner_conv/pallas_call | solution.py:79
  69.3 1.1 %copy-done.26 = f32[1024,384]{1,0:T(8,128)} copy-done((f32[1024,384]{1,0:T(8,128)}, f32[1024,384]{1,0:T(8,128)S(1)}, u32[]{:S(2)}) %copy-start.26) | copy-done | bytes 1572888
  70.7 1.5 %collective-permute-start.14 = (bf16[48,768]{1,0:T(8,128)(2,1)S(1)}, bf16[48,768]{1,0:T(8,128)(2,1)S(1)}, u32[]{:S(2)}, u32[]{:S(2)}) collective-permute-start(bf16[48,768]{1,0:T(8,128)(2,1)S(1)} %get-tuple-element.90), channel_id=1, source_target_pairs={{0,129},{1,0},{2,131},{3,2},{4,133},{5,4},{6,135},{7,6},{8,137},{9... | collective-permute-start | bytes 221192 | tf_op jit(solution)/shard_map/ppermute | solution.py:591
  72.2 1.6 %collective-permute-start.13 = (bf16[48,768]{1,0:T(8,128)(2,1)S(1)}, bf16[48,768]{1,0:T(8,128)(2,1)S(1)}, u32[]{:S(2)}, u32[]{:S(2)}) collective-permute-start(bf16[48,768]{1,0:T(8,128)(2,1)S(1)} %get-tuple-element.91), channel_id=1, source_target_pairs={{0,128},{1,129},{2,130},{3,131},{4,132},{5,133},{6,134},{7,135},{8... | collective-permute-start | bytes 221192 | tf_op jit(solution)/shard_map/ppermute | solution.py:591
  74.2 2.7 %collective-permute-done.13 = bf16[48,768]{1,0:T(8,128)(2,1)S(1)} collective-permute-done((bf16[48,768]{1,0:T(8,128)(2,1)S(1)}, bf16[48,768]{1,0:T(8,128)(2,1)S(1)}, u32[]{:S(2)}, u32[]{:S(2)}) %collective-permute-start.13) | collective-permute-done | bytes 73760 | tf_op jit(solution)/shard_map/ppermute | solution.py:591
  76.9 1.3 %collective-permute-done.12 = bf16[48,768]{1,0:T(8,128)(2,1)S(1)} collective-permute-done((bf16[48,768]{1,0:T(8,128)(2,1)S(1)}, bf16[48,768]{1,0:T(8,128)(2,1)S(1)}, u32[]{:S(2)}, u32[]{:S(2)}) %collective-permute-start.12) | collective-permute-done | bytes 73760 | tf_op jit(solution)/shard_map/ppermute | solution.py:591
  78.3 6.0 %collective-permute-start.15 = (f32[24,768]{1,0:T(8,128)S(1)}, f32[24,768]{1,0:T(8,128)S(1)}, u32[]{:S(2)}, u32[]{:S(2)}) collective-permute-start(f32[24,768]{1,0:T(8,128)S(1)} %constant_dynamic-slice_fusion.2), channel_id=1, source_target_pairs={{0,8},{1,9},{2,10},{3,11},{4,12},{5,13},{6,14},{7,15},{8,0},{9,1},... | collective-permute-start | bytes 221192 | tf_op jit(solution)/shard_map/ppermute | solution.py:605
  84.3 1.7 %collective-permute-done.15 = f32[24,768]{1,0:T(8,128)S(1)} collective-permute-done((f32[24,768]{1,0:T(8,128)S(1)}, f32[24,768]{1,0:T(8,128)S(1)}, u32[]{:S(2)}, u32[]{:S(2)}) %collective-permute-start.15) | collective-permute-done | bytes 73760 | tf_op jit(solution)/shard_map/ppermute | solution.py:605
  86.1 2.1 %collective-permute-start.16 = (f32[12,768]{1,0:T(8,128)S(1)}, f32[12,768]{1,0:T(8,128)S(1)}, u32[]{:S(2)}, u32[]{:S(2)}) collective-permute-start(f32[12,768]{1,0:T(8,128)S(1)} %constant_dynamic-slice_fusion.1), channel_id=1, source_target_pairs={{0,4},{1,5},{2,6},{3,7},{4,0},{5,1},{6,2},{7,3},{8,12},{9,13},{10,... | collective-permute-start | bytes 110600 | tf_op jit(solution)/shard_map/ppermute | solution.py:605
  88.3 8.8 %collective-permute-start.10 = (bf16[3,48,384]{2,1,0:T(8,128)(2,1)S(1)}, bf16[3,48,384]{2,1,0:T(8,128)(2,1)S(1)}, u32[]{:S(2)}, u32[]{:S(2)}) collective-permute-start(bf16[3,48,384]{2,1,0:T(8,128)(2,1)S(1)} %get-tuple-element.75), channel_id=1, source_target_pairs={{0,16},{16,32},{32,48},{48,64},{64,80},{80,96},{96,112},{1,17},{17... | collective-permute-start | bytes 331784 | tf_op jit(solution)/shard_map/ppermute | solution.py:632
  97.1 2.2 %collective-permute-start.11 = (bf16[3,48,384]{2,1,0:T(8,128)(2,1)S(1)}, bf16[3,48,384]{2,1,0:T(8,128)(2,1)S(1)}, u32[]{:S(2)}, u32[]{:S(2)}) collective-permute-start(bf16[3,48,384]{2,1,0:T(8,128)(2,1)S(1)} %get-tuple-element.76), channel_id=1, source_target_pairs={{16,0},{32,16},{48,32},{64,48},{80,64},{96,80},{112,96},{17,1},{33... | collective-permute-start | bytes 331784 | tf_op jit(solution)/shard_map/ppermute | solution.py:633
  99.5 3.7 %collective-permute-done.11.bottom_ref = bf16[3,48,384]{2,1,0:T(8,128)(2,1)S(1)} collective-permute-done((bf16[3,48,384]{2,1,0:T(8,128)(2,1)S(1)}, bf16[3,48,384]{2,1,0:T(8,128)(2,1)S(1)}, u32[]{:S(2)}, u32[]{:S(2)}) %collective-permute-start.11) | collective-permute-done | bytes 110624 | tf_op jit(solution)/shard_map/ppermute | solution.py:633
  103.2 3.1 %finish.1 = f32[1024,384]{1,0:T(8,128)} custom-call(s32[4,4]{1,0:T(4,128)S(1)} %copy-done.6, f32[1024,384]{1,0:T(8,128)S(1)} %copy-done.27, f32[49,384]{1,0:T(8,128)S(1)} %bitcast.26, bf16[3,32,384]{2,1,0:T(8,128)(2,1)S(1)} %collective-permute-done.8.left_ref, bf16[3,32,384]{2,1,0:T(8,128)(2,1)S(1)} %collective-permute-done.9.right_ref, ...), custom_call_target="tpu_custom_call" | custom-call | flops 3564999936 | bytes 1048576 | tf_op jit(solution)/shard_map/finish/pallas_call | solution.py:494
  (99 shorter events, 10.7 us)
Async XLA Ops:
  2.5 11.1 %collective-permute-start = (bf16[3,32,384]{2,1,0:T(8,128)(2,1)S(1)}, bf16[3,32,384]{2,1,0:T(8,128)(2,1)S(1)}, u32[]{:S(2)}, u32[]{:S(2)}) collective-permute-start(bf16[3,32,384]{2,1,0:T(8,128)(2,1)S(1)} %get-tuple-element.43), channel_id=1, source_target_pairs={{0,1},{1,2},{2,3},{3,4},{4,5},{5,6},{6,7},{7,8},{8,9},{9,10},{10,1... | collective-permute-start | bytes 221192 | tf_op jit(solution)/shard_map/ppermute | solution.py:626
  3.8 9.8 %collective-permute-start.1 = (bf16[3,32,384]{2,1,0:T(8,128)(2,1)S(1)}, bf16[3,32,384]{2,1,0:T(8,128)(2,1)S(1)}, u32[]{:S(2)}, u32[]{:S(2)}) collective-permute-start(bf16[3,32,384]{2,1,0:T(8,128)(2,1)S(1)} %get-tuple-element.44), channel_id=1, source_target_pairs={{0,15},{1,0},{2,1},{3,2},{4,3},{5,4},{6,5},{7,6},{8,7},{9,8},{10,9... | collective-permute-start | bytes 221192 | tf_op jit(solution)/shard_map/ppermute | solution.py:627
  5.1 7.1 %copy-start.2 = (f32[1,32,32,384]{3,2,1,0:T(8,128)S(1)}, f32[1,32,32,384]{3,2,1,0:T(8,128)}, u32[]{:S(2)}) copy-start(f32[1,32,32,384]{3,2,1,0:T(8,128)} %param.11) | copy-start | bytes 4718596
  5.1 7.1 %copy-start.6 = (s32[4,4]{1,0:T(4,128)S(1)}, s32[4,4]{1,0:T(4,128)}, u32[]{:S(2)}) copy-start(s32[4,4]{1,0:T(4,128)} %counts_ref.3) | copy-start | bytes 196
  13.5 16.7 %copy-start.22 = (bf16[1024,384]{1,0:T(8,128)(2,1)}, bf16[1024,384]{1,0:T(8,128)(2,1)S(1)}, u32[]{:S(2)}) copy-start(bf16[1024,384]{1,0:T(8,128)(2,1)S(1)} %get-tuple-element.49.grad_ref) | copy-start | bytes 2359300
  13.5 16.7 %copy-start.24 = (bf16[384,1024]{1,0:T(8,128)(2,1)}, bf16[384,1024]{1,0:T(8,128)(2,1)S(1)}, u32[]{:S(2)}) copy-start(bf16[384,1024]{1,0:T(8,128)(2,1)S(1)} %get-tuple-element.50.grad_t_ref) | copy-start | bytes 2359300
  13.6 6.6 %copy-start.4 = (bf16[1,1536,384]{2,1,0:T(8,128)(2,1)S(1)}, bf16[1,1536,384]{2,1,0:T(8,128)(2,1)}, u32[]{:S(2)}) copy-start(bf16[1,1536,384]{2,1,0:T(8,128)(2,1)} %param.17) | copy-start | bytes 3538948
  13.6 6.6 %copy-start.5 = (bf16[1,1536,384]{2,1,0:T(8,128)(2,1)S(1)}, bf16[1,1536,384]{2,1,0:T(8,128)(2,1)}, u32[]{:S(2)}) copy-start(bf16[1,1536,384]{2,1,0:T(8,128)(2,1)} %param.19) | copy-start | bytes 3538948
  13.7 8.7 %collective-permute-start.2 = (bf16[3,48,384]{2,1,0:T(8,128)(2,1)S(1)}, bf16[3,48,384]{2,1,0:T(8,128)(2,1)S(1)}, u32[]{:S(2)}, u32[]{:S(2)}) collective-permute-start(bf16[3,48,384]{2,1,0:T(8,128)(2,1)S(1)} %get-tuple-element.45), channel_id=1, source_target_pairs={{0,16},{16,32},{32,48},{48,64},{64,80},{80,96},{96,112},{1,17},{17... | collective-permute-start | bytes 331784 | tf_op jit(solution)/shard_map/ppermute | solution.py:632
  18.3 6.1 %collective-permute-start.3 = (bf16[3,48,384]{2,1,0:T(8,128)(2,1)S(1)}, bf16[3,48,384]{2,1,0:T(8,128)(2,1)S(1)}, u32[]{:S(2)}, u32[]{:S(2)}) collective-permute-start(bf16[3,48,384]{2,1,0:T(8,128)(2,1)S(1)} %get-tuple-element.46), channel_id=1, source_target_pairs={{16,0},{32,16},{48,32},{64,48},{80,64},{96,80},{112,96},{17,1},{33... | collective-permute-start | bytes 331784 | tf_op jit(solution)/shard_map/ppermute | solution.py:633
  22.4 7.9 %copy-start.12 = (bf16[1536,384]{1,0:T(8,128)(2,1)}, bf16[1536,384]{1,0:T(8,128)(2,1)S(1)}, u32[]{:S(2)}) copy-start(bf16[1536,384]{1,0:T(8,128)(2,1)S(1)} %get-tuple-element.51.expand_ref) | copy-start | bytes 3538948
  22.4 7.9 %copy-start.14 = (bf16[1536,384]{1,0:T(8,128)(2,1)}, bf16[1536,384]{1,0:T(8,128)(2,1)S(1)}, u32[]{:S(2)}) copy-start(bf16[1536,384]{1,0:T(8,128)(2,1)S(1)} %get-tuple-element.52.reduce_ref) | copy-start | bytes 3538948
  22.4 7.9 %copy-start.20 = (f32[1536,128]{1,0:T(8,128)}, f32[1536,128]{1,0:T(8,128)S(1)}, u32[]{:S(2)}) copy-start(f32[1536,128]{1,0:T(8,128)S(1)} %get-tuple-element.53.bias_ref) | copy-start | bytes 2359300
  30.3 6.2 %copy-start.28 = (bf16[1024,384]{1,0:T(8,128)(2,1)}, bf16[1024,384]{1,0:T(8,128)(2,1)S(1)}, u32[]{:S(2)}) copy-start(bf16[1024,384]{1,0:T(8,128)(2,1)S(1)} %get-tuple-element.47.normed_ref) | copy-start | bytes 2359300
  30.3 6.2 %copy-start.30 = (bf16[384,1024]{1,0:T(8,128)(2,1)}, bf16[384,1024]{1,0:T(8,128)(2,1)S(1)}, u32[]{:S(2)}) copy-start(bf16[384,1024]{1,0:T(8,128)(2,1)S(1)} %get-tuple-element.48.normed_t_ref) | copy-start | bytes 2359300
  37.7 14.3 %collective-permute-start.4 = (bf16[768,768]{1,0:T(8,128)(2,1)S(1)}, bf16[768,768]{1,0:T(8,128)(2,1)S(1)}, u32[]{:S(2)}, u32[]{:S(2)}) collective-permute-start(bf16[768,768]{1,0:T(8,128)(2,1)S(1)} %get-tuple-element.55), channel_id=1, source_target_pairs={{0,16},{16,0},{32,48},{48,32},{64,80},{80,64},{96,112},{112,96},{1... | collective-permute-start | bytes 3538952 | tf_op jit(solution)/shard_map/ppermute | solution.py:661
  45.9 11.3 %copy-start.19 = (bf16[768,1024]{1,0:T(8,128)(2,1)S(1)}, bf16[768,1024]{1,0:T(8,128)(2,1)}, u32[]{:S(2)}) copy-start(bf16[768,1024]{1,0:T(8,128)(2,1)} %copy-done.18) | copy-start | bytes 4718596
  52.3 18.2 %collective-permute-start.5 = (bf16[192,768]{1,0:T(8,128)(2,1)S(1)}, bf16[192,768]{1,0:T(8,128)(2,1)S(1)}, u32[]{:S(2)}, u32[]{:S(2)}) collective-permute-start(bf16[192,768]{1,0:T(8,128)(2,1)S(1)} %get-tuple-element.61), channel_id=1, source_target_pairs={{0,32},{1,33},{2,34},{3,35},{4,36},{5,37},{6,38},{7,39},{8,40},{9,... | collective-permute-start | bytes 884744 | tf_op jit(solution)/shard_map/ppermute | solution.py:671
  52.7 17.8 %collective-permute-start.6 = (bf16[192,768]{1,0:T(8,128)(2,1)S(1)}, bf16[192,768]{1,0:T(8,128)(2,1)S(1)}, u32[]{:S(2)}, u32[]{:S(2)}) collective-permute-start(bf16[192,768]{1,0:T(8,128)(2,1)S(1)} %get-tuple-element.62), channel_id=1, source_target_pairs={{0,64},{1,65},{2,66},{3,67},{4,68},{5,69},{6,70},{7,71},{8,72},{9,... | collective-permute-start | bytes 884744 | tf_op jit(solution)/shard_map/ppermute | solution.py:671
  55.3 15.2 %collective-permute-start.7 = (bf16[192,768]{1,0:T(8,128)(2,1)S(1)}, bf16[192,768]{1,0:T(8,128)(2,1)S(1)}, u32[]{:S(2)}, u32[]{:S(2)}) collective-permute-start(bf16[192,768]{1,0:T(8,128)(2,1)S(1)} %get-tuple-element.63), channel_id=1, source_target_pairs={{0,96},{1,97},{2,98},{3,99},{4,100},{5,101},{6,102},{7,103},{8,104... | collective-permute-start | bytes 884744 | tf_op jit(solution)/shard_map/ppermute | solution.py:671
  59.3 11.1 %collective-permute-start.8 = (bf16[3,32,384]{2,1,0:T(8,128)(2,1)S(1)}, bf16[3,32,384]{2,1,0:T(8,128)(2,1)S(1)}, u32[]{:S(2)}, u32[]{:S(2)}) collective-permute-start(bf16[3,32,384]{2,1,0:T(8,128)(2,1)S(1)} %get-tuple-element.70), channel_id=1, source_target_pairs={{0,1},{1,2},{2,3},{3,4},{4,5},{5,6},{6,7},{7,8},{8,9},{9,10},{10,1... | collective-permute-start | bytes 221192 | tf_op jit(solution)/shard_map/ppermute | solution.py:626
  59.4 11.0 %collective-permute-start.9 = (bf16[3,32,384]{2,1,0:T(8,128)(2,1)S(1)}, bf16[3,32,384]{2,1,0:T(8,128)(2,1)S(1)}, u32[]{:S(2)}, u32[]{:S(2)}) collective-permute-start(bf16[3,32,384]{2,1,0:T(8,128)(2,1)S(1)} %get-tuple-element.71), channel_id=1, source_target_pairs={{0,15},{1,0},{2,1},{3,2},{4,3},{5,4},{6,5},{7,6},{8,7},{9,8},{10,9... | collective-permute-start | bytes 221192 | tf_op jit(solution)/shard_map/ppermute | solution.py:627
  70.7 3.5 %collective-permute-start.14 = (bf16[48,768]{1,0:T(8,128)(2,1)S(1)}, bf16[48,768]{1,0:T(8,128)(2,1)S(1)}, u32[]{:S(2)}, u32[]{:S(2)}) collective-permute-start(bf16[48,768]{1,0:T(8,128)(2,1)S(1)} %get-tuple-element.90), channel_id=1, source_target_pairs={{0,129},{1,0},{2,131},{3,2},{4,133},{5,4},{6,135},{7,6},{8,137},{9... | collective-permute-start | bytes 221192 | tf_op jit(solution)/shard_map/ppermute | solution.py:591
  72.2 4.7 %collective-permute-start.13 = (bf16[48,768]{1,0:T(8,128)(2,1)S(1)}, bf16[48,768]{1,0:T(8,128)(2,1)S(1)}, u32[]{:S(2)}, u32[]{:S(2)}) collective-permute-start(bf16[48,768]{1,0:T(8,128)(2,1)S(1)} %get-tuple-element.91), channel_id=1, source_target_pairs={{0,128},{1,129},{2,130},{3,131},{4,132},{5,133},{6,134},{7,135},{8... | collective-permute-start | bytes 221192 | tf_op jit(solution)/shard_map/ppermute | solution.py:591
  73.8 4.4 %collective-permute-start.12 = (bf16[48,768]{1,0:T(8,128)(2,1)S(1)}, bf16[48,768]{1,0:T(8,128)(2,1)S(1)}, u32[]{:S(2)}, u32[]{:S(2)}) collective-permute-start(bf16[48,768]{1,0:T(8,128)(2,1)S(1)} %get-tuple-element.89), channel_id=1, source_target_pairs={{0,1},{1,128},{2,3},{3,130},{4,5},{5,132},{6,7},{7,134},{8,9},{9,1... | collective-permute-start | bytes 221192 | tf_op jit(solution)/shard_map/ppermute | solution.py:591
  78.3 7.7 %collective-permute-start.15 = (f32[24,768]{1,0:T(8,128)S(1)}, f32[24,768]{1,0:T(8,128)S(1)}, u32[]{:S(2)}, u32[]{:S(2)}) collective-permute-start(f32[24,768]{1,0:T(8,128)S(1)} %constant_dynamic-slice_fusion.2), channel_id=1, source_target_pairs={{0,8},{1,9},{2,10},{3,11},{4,12},{5,13},{6,14},{7,15},{8,0},{9,1},... | collective-permute-start | bytes 221192 | tf_op jit(solution)/shard_map/ppermute | solution.py:605
  86.1 13.3 %collective-permute-start.16 = (f32[12,768]{1,0:T(8,128)S(1)}, f32[12,768]{1,0:T(8,128)S(1)}, u32[]{:S(2)}, u32[]{:S(2)}) collective-permute-start(f32[12,768]{1,0:T(8,128)S(1)} %constant_dynamic-slice_fusion.1), channel_id=1, source_target_pairs={{0,4},{1,5},{2,6},{3,7},{4,0},{5,1},{6,2},{7,3},{8,12},{9,13},{10,... | collective-permute-start | bytes 110600 | tf_op jit(solution)/shard_map/ppermute | solution.py:605
  88.2 15.0 %copy-start.3 = (f32[1,32,32,384]{3,2,1,0:T(8,128)S(1)}, f32[1,32,32,384]{3,2,1,0:T(8,128)}, u32[]{:S(2)}) copy-start(f32[1,32,32,384]{3,2,1,0:T(8,128)} %param.11) | copy-start | bytes 4718596
  88.2 15.0 %copy-start.27 = (f32[1024,384]{1,0:T(8,128)S(1)}, f32[1024,384]{1,0:T(8,128)}, u32[]{:S(2)}) copy-start(f32[1024,384]{1,0:T(8,128)} %copy-done.26) | copy-start | bytes 4718596
  88.3 11.2 %collective-permute-start.10 = (bf16[3,48,384]{2,1,0:T(8,128)(2,1)S(1)}, bf16[3,48,384]{2,1,0:T(8,128)(2,1)S(1)}, u32[]{:S(2)}, u32[]{:S(2)}) collective-permute-start(bf16[3,48,384]{2,1,0:T(8,128)(2,1)S(1)} %get-tuple-element.75), channel_id=1, source_target_pairs={{0,16},{16,32},{32,48},{48,64},{64,80},{80,96},{96,112},{1,17},{17... | collective-permute-start | bytes 331784 | tf_op jit(solution)/shard_map/ppermute | solution.py:632
  97.1 6.1 %collective-permute-start.11 = (bf16[3,48,384]{2,1,0:T(8,128)(2,1)S(1)}, bf16[3,48,384]{2,1,0:T(8,128)(2,1)S(1)}, u32[]{:S(2)}, u32[]{:S(2)}) collective-permute-start(bf16[3,48,384]{2,1,0:T(8,128)(2,1)S(1)} %get-tuple-element.76), channel_id=1, source_target_pairs={{16,0},{32,16},{48,32},{64,48},{80,64},{96,80},{112,96},{17,1},{33... | collective-permute-start | bytes 331784 | tf_op jit(solution)/shard_map/ppermute | solution.py:633
  99.4 6.9 %collective-permute-start.17 = (f32[6,768]{1,0:T(8,128)S(1)}, f32[6,768]{1,0:T(8,128)S(1)}, u32[]{:S(2)}, u32[]{:S(2)}) collective-permute-start(f32[6,768]{1,0:T(8,128)S(1)} %constant_dynamic-slice_fusion), channel_id=1, source_target_pairs={{0,2},{1,3},{2,0},{3,1},{4,6},{5,7},{6,4},{7,5},{8,10},{9,11},{10,... | collective-permute-start | bytes 55304 | tf_op jit(solution)/shard_map/ppermute | solution.py:605
  (20 other events, 45.6 us)

commit v4 on v3

--- a/solution.py
+++ b/solution.py
@@ -33,7 +33,7 @@
     index = 7 * p + q
     if flipped:
         index = 48 - index
-    return kernel_ref[index : index + 1, cols]
+    return kernel_ref[index, :, cols]
 
 
 def shift_cols(rows, offset):
@@ -49,42 +49,48 @@
     return jnp.concatenate([first, turned[8:]], axis=0)
 
 
-def inner_conv_body(flipped, cells_ref, kernel_ref, out_ref, padded):
+def inner_conv_body(flipped, parts, cells_ref, kernel_ref, *refs):
+    outs, padded = refs[:-1], refs[-1]
     edge = reach * side
     total = side * side
     padded[0:edge] = jnp.zeros((edge, lanes), f32)
     padded[edge + total : 2 * edge + total] = jnp.zeros((edge, lanes), f32)
-    padded[edge : edge + total] = cells_ref[...]
-
-    def one_row(i, carry):
-        base = pl.multiple_of(i * side, side)
-        rows = [padded[pl.ds(base + p * side, side), :] for p in range(7)]
-        result = None
-        for q in range(7):
-            summed = None
-            for p in range(7):
-                term = tap_row(kernel_ref, flipped, p, q, slice(None)) * rows[p]
-                summed = term if summed is None else summed + term
-            summed = shift_cols(summed, q - reach)
-            result = summed if result is None else result + summed
-        out_ref[pl.ds(base, side), :] = result
-        return carry
-
-    lax.fori_loop(0, side, one_row, 0)
-
-
-def inner_conv(cells, kernel, flipped):
-    total, channels = cells.shape
-    block = pl.BlockSpec((total, lanes), lambda c: (0, c))
-    return pl.pallas_call(
-        functools.partial(inner_conv_body, flipped),
-        out_shape=jax.ShapeDtypeStruct((total, channels), f32),
-        grid=(channels // lanes,),
-        in_specs=[block, pl.BlockSpec((49, lanes), lambda c: (0, c))],
-        out_specs=block,
+    for part, out_ref in zip(parts, outs):
+        cols = slice(part * lanes, (part + 1) * lanes)
+        padded[edge : edge + total] = cells_ref[:, cols]
+
+        def two_rows(i, carry):
+            base = pl.multiple_of(i * (2 * side), 2 * side)
+            rows = [padded[pl.ds(base + p * side, side), :] for p in range(8)]
+            results = [None, None]
+            for q in range(7):
+                sums = [None, None]
+                for p in range(7):
+                    tap = tap_row(kernel_ref, flipped, p, q, cols)
+                    for g in range(2):
+                        term = tap * rows[p + g]
+                        sums[g] = term if sums[g] is None else sums[g] + term
+                for g in range(2):
+                    moved = shift_cols(sums[g], q - reach)
+                    results[g] = moved if results[g] is None else results[g] + moved
+            for g in range(2):
+                out_ref[pl.ds(base + g * side, side), :] = results[g]
+            return carry
+
+        lax.fori_loop(0, side // 2, two_rows, 0)
+
+
+def inner_conv(cells, kernel, flipped, parts):
+    total = cells.shape[0]
+    shape = jax.ShapeDtypeStruct((total, lanes), f32)
+    return pl.pallas_call(
+        functools.partial(inner_conv_body, flipped, parts),
+        out_shape=(shape,) * len(parts),
+        in_specs=[whole] * 2,
+        out_specs=[whole] * len(parts),
         scratch_shapes=[pltpu.VMEM((total + 2 * reach * side, lanes), f32)],
         compiler_params=params(6),
-        cost_estimate=cost(7.0),
+        cost_estimate=cost(2.3 * len(parts)),
         name="inner_conv",
     )(cells, kernel)
 
@@ -109,44 +115,43 @@
         ],
         out_specs=[pl.BlockSpec((reach, side, channels), lambda g: (0, 0, 0))] * 2,
         compiler_params=params(4),
-        cost_estimate=cost(1.0),
+        cost_estimate=cost(0.5),
         name="side_cols",
     )(grid3, grid3)
 
 
-def side_rows_body(top_ref, bottom_ref, left_ref, right_ref, up_ref, down_ref):
-    channels = top_ref.shape[1]
+def side_rows_body(cells_ref, left_ref, right_ref, up_ref, down_ref):
+    channels = cells_ref.shape[1]
     place = lax.broadcasted_iota(jnp.int32, (8, channels), 0)
     blank = jnp.zeros((8, channels), f32)
     left = [left_ref[h].astype(f32) for h in range(reach)]
     right = [right_ref[h].astype(f32) for h in range(reach)]
     for r in range(reach):
-        for source, row, ref in ((top_ref, r, up_ref), (bottom_ref, side - reach + r, down_ref)):
+        for row, ref in ((r, up_ref), (side - reach + r, down_ref)):
             corner = blank
             for h in range(reach):
                 corner = jnp.where(place == h, right[h][row : row + 1], corner)
                 corner = jnp.where(place == 8 - reach + h, left[h][row : row + 1], corner)
-            body = source[r * side : (r + 1) * side]
+            body = cells_ref[row * side : (row + 1) * side]
             ref[r] = jnp.concatenate([body, corner, blank], axis=0).astype(bf16)
 
 
 def side_rows(cells, left, right):
     channels = cells.shape[1]
     shape = jax.ShapeDtypeStruct((reach, side + 16, channels), bf16)
-    edge = reach * side
     return pl.pallas_call(
         side_rows_body,
         out_shape=(shape, shape),
-        in_specs=[whole] * 4,
+        in_specs=[whole] * 3,
         out_specs=[whole] * 2,
         compiler_params=params(6),
-        cost_estimate=cost(0.8),
+        cost_estimate=cost(0.5),
         name="side_rows",
-    )(cells[:edge], cells[-edge:], left, right)
+    )(cells, left, right)
 
 
 def add_edges(flipped, kernel_ref, left_ref, right_ref, top_ref, bottom_ref, rows_sum, cols_sum):
-    channels = kernel_ref.shape[1]
+    channels = kernel_ref.shape[2]
     for c in range(channels // lanes):
         cols = slice(c * lanes, (c + 1) * lanes)
         for low, ref in ((True, top_ref), (False, bottom_ref)):
@@ -209,17 +214,22 @@
     lax.fori_loop(side - reach, side, high, 0)
 
 
+def conv_rows(refs, at):
+    return jnp.concatenate([ref[at, :] for ref in refs], axis=1)
+
+
 def normalise_body(
-    conv_ref, kernel_ref, left_ref, right_ref, top_ref, bottom_ref, bias_ref, gain_ref, shift_ref,
+    conv0_ref, conv1_ref, conv2_ref, kernel_ref, left_ref, right_ref, top_ref, bottom_ref, bias_ref, gain_ref, shift_ref,
     unit_ref, spread_ref, normed_ref, flipped_ref, rows_sum, cols_sum,
 ):
-    channels = conv_ref.shape[1]
+    channels = kernel_ref.shape[2]
+    conv_refs = (conv0_ref, conv1_ref, conv2_ref)
     add_edges(False, kernel_ref, left_ref, right_ref, top_ref, bottom_ref, rows_sum, cols_sum)
     share = 1.0 / channels
 
     def step(i, outer):
         at = pl.ds(pl.multiple_of(i * side, side), side)
-        value = edged_row(i, conv_ref[at, :], cols_sum)
+        value = edged_row(i, conv_rows(conv_refs, at), cols_sum)
         if outer is not None:
             value = value + rows_sum[outer]
         value = value + bias_ref[...]
@@ -242,7 +252,7 @@
 
 
 def normalise(conv, kernel, left, right, top, bottom, bias, gain, shift):
-    total, channels = conv.shape
+    total, channels = conv[0].shape[0], kernel.shape[2]
     return pl.pallas_call(
         normalise_body,
         out_shape=(
@@ -251,13 +261,13 @@
             jax.ShapeDtypeStruct((total, channels), bf16),
             jax.ShapeDtypeStruct((channels, total), bf16),
         ),
-        in_specs=[whole] * 9,
+        in_specs=[whole] * 11,
         out_specs=[whole] * 4,
         scratch_shapes=[pltpu.VMEM((2 * reach, side, channels), f32)] * 2,
         compiler_params=params(12),
         cost_estimate=cost(4.8),
         name="normalise",
-    )(conv, kernel, left, right, top, bottom, bias, gain, shift)
+    )(*conv, kernel, left, right, top, bottom, bias, gain, shift)
 
 
 def wet_row(i, counts_ref):
@@ -320,7 +330,7 @@
         unit = (hi * 4 + y) * 2 + core
         at = slice(unit * 96, (unit + 1) * 96)
         expand, reduce = expand_ref[at, :], reduce_ref[at, :]
-        bias = bias_ref[unit : unit + 1, :]
+        bias = bias_ref[:, at]
         for lo in range(2):
             x = 2 * hi + lo
             place = core * 16 + (y * 4 + x if core == 0 else x * 4 + y)
@@ -348,7 +358,7 @@
         compiler_params=params(12),
         cost_estimate=cost(1.1),
         name="arrange",
-    )(expand, reduce, bias.reshape(16, 96))
+    )(expand, reduce, bias)
 
 
 tail_slope = 0.3275911 * 0.7071067811865476
@@ -360,8 +370,7 @@
 
 def gelu_pair(v):
     d = 1.0 + tail_slope * jnp.abs(v)
-    t = pl.reciprocal(d, approx=True)
-    t = t * (2.0 - d * t)
+    t = pltpu.reciprocal(d, approx=True)
     poly = tail_terms[4]
     for a in reversed(tail_terms[:4]):
         poly = poly * t + a
@@ -371,72 +380,163 @@
     return v * below, below + v * bell * inv_root_two_pi
 
 
-def hidden_body(
-    core_ref, normed_ref, normed_t_ref, grad_ref, grad_t_ref, expand_ref, reduce_ref, bias_ref,
-    sums_ref, grad_pre_ref,
-):
-    channels = normed_ref.shape[1]
+def own_place():
+    lat, lon = lax.axis_index("lat"), lax.axis_index("lon")
+    x = 2 * lax.axis_index("dp") + (lon & 1)
+    return lat & 1, x, lat >> 1, lon >> 1
+
+
+def phase_place(second):
+    core, x, y, _ = own_place()
+    along_y = core == (1 if second else 0)
+    return jnp.where(along_y, y, x)
+
+
+def hidden_rows(cells, source, rows, grad_pre_ref, to):
+    normed_ref, normed_t_ref, grad_ref, grad_t_ref, expand_ref, reduce_ref, bias_ref = cells
     total = normed_ref.shape[0]
-    preact = jnp.dot(expand_ref[...], normed_t_ref[...], preferred_element_type=f32)
-    grad_hidden = jnp.dot(reduce_ref[...], grad_t_ref[...], preferred_element_type=f32)
-    bias = jnp.concatenate([bias_ref[...]] * (total // lanes), axis=1)
+    at = pl.ds(source, rows)
+    preact = jnp.dot(expand_ref[at, :], normed_t_ref[...], preferred_element_type=f32)
+    grad_hidden = jnp.dot(reduce_ref[at, :], grad_t_ref[...], preferred_element_type=f32)
+    bias = jnp.concatenate([bias_ref[at, :]] * (total // lanes), axis=1)
     value, slope = gelu_pair(preact + bias)
     hidden = value.astype(bf16)
     grad_pre = (grad_hidden * slope).astype(bf16)
-    grad_pre_ref[...] = grad_pre
-    sums_ref[:, :channels] = jnp.dot(grad_pre, normed_ref[...], preferred_element_type=f32).astype(
-        sums_ref.dtype
+    grad_pre_ref[pl.ds(to, rows), :] = grad_pre
+    return (
+        jnp.dot(grad_pre, normed_ref[...], preferred_element_type=f32),
+        jnp.dot(hidden, grad_ref[...], preferred_element_type=f32),
     )
-    sums_ref[:, channels:] = jnp.dot(hidden, grad_ref[...], preferred_element_type=f32).astype(
-        sums_ref.dtype
-    )
-
-
-hidden_block = 256
-
-
-def hidden_half(core, normed, normed_t, grad, grad_t, expand, reduce, bias, kind):
-    total, channels = normed.shape
-    half = expand.shape[0] // 2
-    steps = half // hidden_block
-    keep = lambda i, core: (0, 0)
-    pick = lambda i, core: (core[0] * steps + i, 0)
-    return pl.pallas_call(
-        hidden_body,
+
+
+def far_body(*refs):
+    cells, (sent_ref, grad_pre_ref) = refs[:7], refs[7:]
+    half = grad_pre_ref.shape[0]
+    channels = refs[0].shape[1]
+    base = (1 - own_place()[0]) * half
+    rows = 256
+    for b in range(half // rows):
+        source = pl.multiple_of(base + b * rows, rows)
+        expand, reduce = hidden_rows(cells, source, rows, grad_pre_ref, b * rows)
+        at = slice(b * rows, (b + 1) * rows)
+        sent_ref[at, :channels] = expand.astype(bf16)
+        sent_ref[at, channels:] = reduce.astype(bf16)
+
+
+def hidden_far(*cells):
+    total, channels = cells[0].shape
+    half = cells[4].shape[0] // 2
+    return pl.pallas_call(
+        far_body,
         out_shape=(
-            jax.ShapeDtypeStruct((half, 2 * channels), kind),
+            jax.ShapeDtypeStruct((half, 2 * channels), bf16),
             jax.ShapeDtypeStruct((half, total), bf16),
         ),
-        grid_spec=pltpu.PrefetchScalarGridSpec(
-            num_scalar_prefetch=1,
-            grid=(steps,),
-            in_specs=[
-                pl.BlockSpec((total, channels), keep),
-                pl.BlockSpec((channels, total), keep),
-                pl.BlockSpec((total, channels), keep),
-                pl.BlockSpec((channels, total), keep),
-                pl.BlockSpec((hidden_block, channels), pick),
-                pl.BlockSpec((hidden_block, channels), pick),
-                pl.BlockSpec((hidden_block, lanes), pick),
-            ],
-            out_specs=[
-                pl.BlockSpec((hidden_block, 2 * channels), lambda i, core: (i, 0)),
-                pl.BlockSpec((hidden_block, total), lambda i, core: (i, 0)),
-            ],
+        in_specs=[whole] * 7,
+        out_specs=[whole] * 2,
+        compiler_params=params(16),
+        cost_estimate=cost(5.8),
+        name="hidden_far",
+    )(*cells)
+
+
+def near_first_body(*refs):
+    cells, (sums_ref, grad_pre_ref) = refs[:7], refs[7:]
+    half = grad_pre_ref.shape[0]
+    channels = refs[0].shape[1]
+    size = half // 4
+    core, place = own_place()[0], phase_place(False)
+    for step in (1, 2):
+        chunk = pl.multiple_of(lax.rem(place + step, 4) * size, size)
+        source = pl.multiple_of(core * half + chunk, size)
+        expand, reduce = hidden_rows(cells, source, size, grad_pre_ref, chunk)
+        at = slice((step - 1) * size, step * size)
+        sums_ref[at, :channels] = expand
+        sums_ref[at, channels:] = reduce
+
+
+def near_first(*cells):
+    total, channels = cells[0].shape
+    half = cells[4].shape[0] // 2
+    return pl.pallas_call(
+        near_first_body,
+        out_shape=(
+            jax.ShapeDtypeStruct((half // 2, 2 * channels), f32),
+            jax.ShapeDtypeStruct((half, total), bf16),
         ),
-        compiler_params=params(20),
-        cost_estimate=cost(6.1),
-        name="hidden_half",
-    )(core, normed, normed_t, grad, grad_t, expand, reduce, bias)
+        in_specs=[whole] * 7,
+        out_specs=[whole] * 2,
+        compiler_params=params(16),
+        cost_estimate=cost(3.0),
+        name="near_first",
+    )(*cells)
+
+
+def near_sends_body(sums_ref, arrived_ref, *sent_refs):
+    size = sent_refs[0].shape[0]
+    place = phase_place(False)
+    for step in (1, 2):
+        chunk = pl.multiple_of(lax.rem(place + step, 4) * size, size)
+        total = sums_ref[(step - 1) * size : step * size] + arrived_ref[pl.ds(chunk, size), :].astype(f32)
+        sent_refs[step - 1][...] = total.astype(bf16)
+
+
+def near_sends(sums, arrived):
+    size, width = sums.shape[0] // 2, sums.shape[1]
+    sent = jax.ShapeDtypeStruct((size, width), bf16)
+    return pl.pallas_call(
+        near_sends_body,
+        out_shape=(sent, sent),
+        in_specs=[whole] * 2,
+        out_specs=[whole] * 2,
+        compiler_params=params(6),
+        cost_estimate=cost(0.3),
+        name="near_sends",
+    )(sums, arrived)
+
+
+def near_last_body(*refs):
+    cells, (arrived_ref, _, own_ref, sent_ref, grad_pre_ref) = refs[:7], refs[7:]
+    half = grad_pre_ref.shape[0]
+    channels = refs[0].shape[1]
+    size = half // 4
+    core, place = own_place()[0], phase_place(False)
+    for step, ref in ((3, sent_ref), (0, own_ref)):
+        chunk = pl.multiple_of(lax.rem(place + step, 4) * size, size)
+        source = pl.multiple_of(core * half + chunk, size)
+        expand, reduce = hidden_rows(cells, source, size, grad_pre_ref, chunk)
+        other = arrived_ref[pl.ds(chunk, size), :].astype(f32)
+        ref[:, :channels] = (expand + other[:, :channels]).astype(ref.dtype)
+        ref[:, channels:] = (reduce + other[:, channels:]).astype(ref.dtype)
+
+
+def near_last(*inputs):
+    cells, grad_pre = inputs[:7], inputs[8]
+    channels = cells[0].shape[1]
+    size = cells[4].shape[0] // 8
+    return pl.pallas_call(
+        near_last_body,
+        out_shape=(
+            jax.ShapeDtypeStruct((size, 2 * channels), f32),
+            jax.ShapeDtypeStruct((size, 2 * channels), bf16),
+            jax.ShapeDtypeStruct(grad_pre.shape, bf16),
+        ),
+        in_specs=[whole] * 9,
+        out_specs=[whole] * 3,
+        input_output_aliases={8: 2},
+        compiler_params=params(16),
+        cost_estimate=cost(3.0),
+        name="near_last",
+    )(*inputs)
 
 
 def norm_back_body(
-    core_ref, turned_ref, other_ref, mine_ref, unit_ref, spread_ref, gain_ref,
+    turned_ref, other_ref, mine_ref, unit_ref, spread_ref, gain_ref,
     conv_grad_ref, first_ref, last_ref,
 ):
     total, channels = unit_ref.shape
     half = turned_ref.shape[1] // 2
-    core = core_ref[0]
+    core = own_place()[0]
     block = 256
     share = 1.0 / channels
     mine_weight = turned_ref[:, pl.ds(pl.multiple_of(core * half, half), half)]
@@ -458,30 +558,31 @@
         last_ref[j] = conv_grad_ref[:, side - reach + j, :].astype(bf16)
 
 
-def norm_back(core, turned, other, mine, unit, spread, gain):
+def norm_back(turned, other, mine, unit, spread, gain):
     total, channels = unit.shape
     shape = jax.ShapeDtypeStruct((reach, side, channels), bf16)
     found, first, last = pl.pallas_call(
         norm_back_body,
         out_shape=(jax.ShapeDtypeStruct((side, side, channels), f32), shape, shape),
-        in_specs=[pl.BlockSpec(memory_space=pltpu.SMEM)] + [whole] * 6,
+        in_specs=[whole] * 6,
         out_specs=[whole] * 3,
         compiler_params=params(14),
         cost_estimate=cost(2.2),
         name="norm_back",
-    )(core, turned, other, mine, unit, spread, gain)
+    )(turned, other, mine, unit, spread, gain)
     return found.reshape(total, channels), first, last
 
 
 def finish_body(
-    counts_ref, conv_ref, kernel_ref, left_ref, right_ref, top_ref, bottom_ref, grad_ref,
-    out_ref, rows_sum, cols_sum,
+    counts_ref, conv0_ref, conv1_ref, conv2_ref, kernel_ref, left_ref, right_ref, top_ref, bottom_ref,
+    grad_ref, out_ref, rows_sum, cols_sum,
 ):
+    conv_refs = (conv0_ref, conv1_ref, conv2_ref)
     add_edges(True, kernel_ref, left_ref, right_ref, top_ref, bottom_ref, rows_sum, cols_sum)
 
     def step(i, outer):
         at = pl.ds(pl.multiple_of(i * side, side), side)
-        value = edged_row(i, conv_ref[at, :], cols_sum)
+        value = edged_row(i, conv_rows(conv_refs, at), cols_sum)
         if outer is not None:
             value = value + rows_sum[outer]
         out_ref[at, :] = value + masked_row(i, grad_ref[at, :], counts_ref)
@@ -490,67 +591,92 @@
 
 
 def finish(counts, conv, kernel, left, right, top, bottom, grad):
-    total, channels = conv.shape
+    total, channels = grad.shape
     return pl.pallas_call(
         finish_body,
         out_shape=jax.ShapeDtypeStruct((total, channels), f32),
-        in_specs=[pl.BlockSpec(memory_space=pltpu.SMEM)] + [whole] * 7,
+        in_specs=[pl.BlockSpec(memory_space=pltpu.SMEM)] + [whole] * 9,
         out_specs=whole,
         scratch_shapes=[pltpu.VMEM((2 * reach, side, channels), f32)] * 2,
         compiler_params=params(12),
         cost_estimate=cost(3.1),
         name="finish",
-    )(counts, conv, kernel, left, right, top, bottom, grad)
-
-
-def combine_body(place_ref, mine_ref, arrived_ref, own_ref, *sent_refs):
-    size = own_ref.shape[0]
+    )(counts, *conv, kernel, left, right, top, bottom, grad)
+
+
+def split_four_body(own_ref, first_ref, second_ref, third_ref, kept_ref, *sent_refs):
+    size = kept_ref.shape[0]
+    place = phase_place(True)
     for step in range(4):
-        chunk = lax.rem(place_ref[0] + step, 4)
-        at = pl.ds(pl.multiple_of(chunk * size, size), size)
-        total = mine_ref[at, :] + arrived_ref[at, :].astype(f32)
+        at = pl.ds(pl.multiple_of(lax.rem(place + step, 4) * size, size), size)
+        total = own_ref[at, :]
+        for ref in (first_ref, second_ref, third_ref):
+            total = total + ref[at, :].astype(f32)
         if step == 0:
-            own_ref[...] = total
+            kept_ref[...] = total
         else:
             sent_refs[step - 1][...] = total.astype(bf16)
 
 
-def combine(place, mine, arrived):
-    size, width = mine.shape[0] // 4, mine.shape[1]
+def split_four(own, parts):
+    size, width = own.shape[0] // 4, own.shape[1]
     sent = jax.ShapeDtypeStruct((size, width), bf16)
     return pl.pallas_call(
-        combine_body,
+        split_four_body,
         out_shape=(jax.ShapeDtypeStruct((size, width), f32), sent, sent, sent),
-        in_specs=[pl.BlockSpec(memory_space=pltpu.SMEM), whole, whole],
+        in_specs=[whole] * 4,
         out_specs=[whole] * 4,
-        compiler_params=params(10),
-        cost_estimate=cost(0.7),
-        name="combine",
-    )(place, mine, arrived)
-
-
-def last_sum_body(scale, place_ref, rows_ref, arrived_ref, expand_ref, reduce_ref):
-    size = arrived_ref.shape[0]
+        compiler_params=params(4),
+        cost_estimate=cost(0.3),
+        name="split_four",
+    )(own, *parts)
+
+
+def split_two_body(bit, own_ref, *refs):
+    part_refs, (kept_ref, sent_ref) = refs[:-2], refs[-2:]
+    size = kept_ref.shape[0]
+    total = own_ref[...]
+    for ref in part_refs:
+        total = total + ref[...].astype(f32)
+    low, high = total[:size], total[size:]
+    upper = (own_place()[3] & bit) != 0
+    kept_ref[...] = jnp.where(upper, high, low)
+    sent_ref[...] = jnp.where(upper, low, high)
+
+
+def split_two(bit, own, parts):
+    shape = jax.ShapeDtypeStruct((own.shape[0] // 2, own.shape[1]), f32)
+    return pl.pallas_call(
+        functools.partial(split_two_body, bit),
+        out_shape=(shape, shape),
+        in_specs=[whole] * (1 + len(parts)),
+        out_specs=[whole] * 2,
+        compiler_params=params(4),
+        cost_estimate=cost(0.2),
+        name="split_two",
+    )(own, *parts)
+
+
+def last_sum_body(scale, own_ref, arrived_ref, expand_ref, reduce_ref):
     channels = expand_ref.shape[2]
-    low, high = rows_ref[:size], rows_ref[size:]
-    total = (jnp.where(place_ref[0] == 0, low, high) + arrived_ref[...]) * scale
-    for r in range(size):
+    total = (own_ref[...] + arrived_ref[...]) * scale
+    for r in range(total.shape[0]):
         expand_ref[r] = total[r : r + 1, :channels]
         reduce_ref[r] = total[r : r + 1, channels:]
 
 
-def last_sum(place, rows, arrived, scale):
-    size, width = arrived.shape
+def last_sum(own, arrived, scale):
+    size, width = own.shape
     shape = jax.ShapeDtypeStruct((size, 1, width // 2), f32)
     expand, reduce = pl.pallas_call(
         functools.partial(last_sum_body, scale),
         out_shape=(shape, shape),
-        in_specs=[pl.BlockSpec(memory_space=pltpu.SMEM), whole, whole],
+        in_specs=[whole] * 2,
         out_specs=[whole] * 2,
         compiler_params=params(4),
-        cost_estimate=cost(0.5),
+        cost_estimate=cost(0.4),
         name="last_sum",
-    )(place, rows, arrived)
+    )(own, arrived)
     return expand.transpose(1, 0, 2), reduce.transpose(1, 0, 2)
 
 
@@ -577,39 +703,8 @@
     return device_pairs(move)
 
 
-def add_parts(own, parts):
-    for part in parts:
-        own = own + part.astype(jnp.float32)
-    return own
-
-
-def scatter_direct(rows, place, pairs_of):
-    size = rows.shape[0] // 4
-    narrow = rows.astype(jnp.bfloat16)
-    own = lax.dynamic_slice_in_dim(rows, place * size, size, 0)
-    arrived = [
-        lax.ppermute(
-            lax.dynamic_slice_in_dim(narrow, ((place + step) % 4) * size, size, 0),
-            every_axis,
-            pairs_of(step),
-        )
-        for step in range(1, 4)
-    ]
-    return add_parts(own, arrived)
-
-
-def scatter_halving(rows, z):
-    for bit in (4, 2, 1):
-        size = rows.shape[0] // 2
-        upper = (z // bit) % 2
-        arrived = lax.ppermute(
-            lax.dynamic_slice_in_dim(rows, (1 - upper) * size, size, 0),
-            every_axis,
-            device_pairs(lambda hi, y, core, z, lo, bit=bit: (hi, y, core, z ^ bit, lo)),
-        )
-        if bit > 1:
-            rows = lax.dynamic_slice_in_dim(rows, upper * size, size, 0) + arrived
-    return rows, arrived, upper
+def halving_pairs(bit):
+    return device_pairs(lambda hi, y, core, z, lo: (hi, y, core, z ^ bit, lo))
 
 
 def shifted(axis, step, closed):
@@ -634,6 +729,10 @@
     return top, bottom
 
 
+def after(value, *others):
+    return lax.optimization_barrier((value, others))[0]
+
+
 def local(
     state, cotangent, counts, dw_kernel, dw_bias, norm_gain, norm_bias, w_expand, b_expand, w_reduce
 ):
@@ -641,48 +740,56 @@
     cells = state.reshape(-1, channels)
     grad = cotangent.reshape(-1, channels)
     total = cells.shape[0]
-    kernel = dw_kernel[0]
-    core = lax.axis_index("lat") % 2
-    near = core.astype(jnp.int32).reshape(1)
-    far = 1 - near
+    kernel = dw_kernel.transpose(1, 0, 2)
 
     left, right = lon_halo(*side_cols(cells))
+    conv = inner_conv(cells, kernel, False, (0, 1, 2))
     rows, rows_t = mask_rows(counts, grad)
-    expand, reduce, expand_t, bias = arrange(w_expand[0], w_reduce[0], b_expand[0])
     top, bottom = lat_halo(*side_rows(cells, left, right))
-    conv = inner_conv(cells, kernel, False)
+    expand, reduce, expand_t, bias = arrange(w_expand[0], w_reduce[0], b_expand)
     unit, spread, normed, normed_t = normalise(
         conv, kernel, left, right, top, bottom, dw_bias, norm_gain, norm_bias
     )
 
-    sent, far_pre = hidden_half(
-        far, normed, normed_t, rows, rows_t, expand, reduce, bias, jnp.bfloat16
-    )
+    inputs = (normed, normed_t, rows, rows_t, expand, reduce, bias)
+    sent, far_pre = hidden_far(*inputs)
     arrived = lax.ppermute(sent, "lat", [(i, i ^ 1) for i in range(8)])
-    mine, near_pre = hidden_half(
-        near, normed, normed_t, rows, rows_t, expand, reduce, bias, jnp.float32
-    )
-    lon = lax.axis_index("lon")
-    z, x = lon // 2, 2 * lax.axis_index("dp") + lon % 2
-    y = lax.axis_index("lat") // 2
-    first_place, second_place = jnp.where(core == 0, y, x), jnp.where(core == 0, x, y)
-    own, *sent = combine(first_place.astype(jnp.int32).reshape(1), mine, arrived)
-    sent, near_pre = lax.optimization_barrier((sent, near_pre))
-    parts = [lax.ppermute(s, every_axis, plane_pairs(i + 1, True)) for i, s in enumerate(sent)]
-    conv_grad, first, last = norm_back(near, expand_t, far_pre, near_pre, unit, spread, norm_gain)
+    sums, near_pre = near_first(*inputs)
+    one, two = near_sends(sums, arrived)
+    part_one = lax.ppermute(one, every_axis, plane_pairs(1, True))
+    part_two = lax.ppermute(two, every_axis, plane_pairs(2, True))
+    own, three, near_pre = near_last(*inputs, arrived, after(near_pre, one, two))
+    part_three = lax.ppermute(three, every_axis, plane_pairs(3, True))
+
+    far_pre = after(far_pre, three)
+    conv_grad, first, last = norm_back(expand_t, far_pre, near_pre, unit, spread, norm_gain)
     left, right = lon_halo(first, last)
-    back = inner_conv(conv_grad, kernel, True)
-    own, parts, back, left, right = lax.optimization_barrier((own, parts, back, left, right))
-    summed = add_parts(own, parts)
-    top, bottom = lat_halo(*side_rows(conv_grad, left, right))
-    summed = scatter_direct(summed, second_place, lambda step: plane_pairs(step, False))
-    summed, arrived, upper = scatter_halving(summed, z)
+
+    own, parts = after((own, (part_one, part_two, part_three)), left, right)
+    own, *sent = split_four(own, parts)
+    parts = [lax.ppermute(s, every_axis, plane_pairs(i + 1, False)) for i, s in enumerate(sent)]
+    conv_grad = after(conv_grad, sent)
+    up, down = side_rows(conv_grad, left, right)
+    back = inner_conv(conv_grad, kernel, True, (0,))
+
+    own, sent = split_two(4, *after((own, parts), up, down, back))
+    top, bottom = lat_halo(up, down)
+    arrived = lax.ppermute(sent, every_axis, halving_pairs(4))
+    conv_grad = after(conv_grad, sent)
+    back += inner_conv(conv_grad, kernel, True, (1,))
+
+    own, sent = split_two(2, *after((own, [arrived]), back))
+    arrived = lax.ppermute(sent, every_axis, halving_pairs(2))
+    conv_grad = after(conv_grad, sent)
+    back += inner_conv(conv_grad, kernel, True, (2,))
+
+    own, sent = split_two(1, *after((own, [arrived]), back, top, bottom))
+    arrived = lax.ppermute(sent, every_axis, halving_pairs(1))
+    grad = after(grad, sent)
     gradient = finish(counts, back, kernel, left, right, top, bottom, grad)
 
     cells_all = lax.axis_size("dp") * lax.axis_size("lat") * lax.axis_size("lon") * total
-    kept = last_sum(
-        upper.astype(jnp.int32).reshape(1), summed, arrived, 1.0 / math.sqrt(cells_all)
-    )
+    kept = last_sum(own, arrived, 1.0 / math.sqrt(cells_all))
     return (gradient.reshape(state.shape), *kept)
 
 

time: 107 us -> 90.5 us (0.85)
  the two profiles are of different devices: /device:TPU:33 before, /device:TPU:32 now
where the time goes in v4:
time: 90.5 us; the launch traced here: 89.7 us
  starting transfers between devices  43 us (48%)
  Pallas kernels  38.4 us (42%)
  waiting for transfers between devices  5.81 us (6%)
  local copies, waits for them, and re-layouts  1.45 us (2%)
  between operations  0.97 us (1%)
    pallas_call x4, Pallas kernels, inner_conv(): pl.pallas_call(functools.partial(inner_conv_body, flipped, parts), out_sh...  12.9 us
    ppermute x1, starting transfers between devices, local(): arrived = lax.ppermute(sent, every_axis, halving_pairs(2))  7.48 us
    ppermute x1, starting transfers between devices, local(): arrived = lax.ppermute(sent, every_axis, halving_pairs(4))  5.93 us
    ppermute x3, starting transfers between devices, local(): lax.ppermute(s, every_axis, plane_pairs(i + 1, False))  5.5 us
    pallas_call x1, Pallas kernels, hidden_far(): pl.pallas_call(far_body, out_shape=(jax.ShapeDtypeStruct((half, 2 * chann...  5.42 us
    pallas_call x1, Pallas kernels, normalise(): pl.pallas_call(normalise_body, out_shape=(jax.ShapeDtypeStruct((total, ch...  4.74 us
    ppermute x2, starting transfers between devices, lat_halo(): top = lax.ppermute(down, 'lat', shifted('lat', 1, False))  4.46 us
    ppermute x2, starting transfers between devices, lon_halo(): right = lax.ppermute(first, 'lon', shifted('lon', -1, True))  3.76 us
  transfers between devices with their start and end apart: 18, of which 4 were waited for; matrix products, arithmetic and copies ran while one was open for 0% of the time, Pallas kernels for 30%

profile of v4, /device:TPU:32, one launch (start us, length us, event | category | flops | bytes accessed | tf_op | source)
XLA Modules:
  0.0 89.7 jit_solution(2448679097920316048)
XLA Ops:
  0.6 1.4 %copy-done = f32[1,32,32,384]{3,2,1,0:T(8,128)S(1)} copy-done((f32[1,32,32,384]{3,2,1,0:T(8,128)S(1)}, f32[1,32,32,384]{3,2,1,0:T(8,128)}, u32[]{:S(2)}) %copy-start) | copy-done | bytes 1572888
  2.5 1.6 %collective-permute-start = (bf16[3,32,384]{2,1,0:T(8,128)(2,1)S(1)}, bf16[3,32,384]{2,1,0:T(8,128)(2,1)S(1)}, u32[]{:S(2)}, u32[]{:S(2)}) collective-permute-start(bf16[3,32,384]{2,1,0:T(8,128)(2,1)S(1)} %get-tuple-element.68), channel_id=1, source_target_pairs={{0,1},{1,2},{2,3},{3,4},{4,5},{5,6},{6,7},{7,8},{8,9},{9,10},{10,1... | collective-permute-start | bytes 221192 | tf_op jit(solution)/shard_map/ppermute | solution.py:721
  4.1 1.4 %collective-permute-start.1 = (bf16[3,32,384]{2,1,0:T(8,128)(2,1)S(1)}, bf16[3,32,384]{2,1,0:T(8,128)(2,1)S(1)}, u32[]{:S(2)}, u32[]{:S(2)}) collective-permute-start(bf16[3,32,384]{2,1,0:T(8,128)(2,1)S(1)} %get-tuple-element.69), channel_id=1, source_target_pairs={{0,15},{1,0},{2,1},{3,2},{4,3},{5,4},{6,5},{7,6},{8,7},{9,8},{10,9... | collective-permute-start | bytes 221192 | tf_op jit(solution)/shard_map/ppermute | solution.py:722
  5.5 6.4 %inner_conv.4 = (f32[1024,128]{1,0:T(8,128)S(1)}, f32[1024,128]{1,0:T(8,128)S(1)}, f32[1024,128]{1,0:T(8,128)S(1)}) custom-call(f32[1024,384]{1,0:T(8,128)S(1)} %bitcast.12, f32[49,1,384]{2,1,0:T(1,128)S(1)} %bitcast.18), custom_call_target="tpu_custom_call" | custom-call | flops 7935000064 | bytes 1048576 | tf_op jit(solution)/shard_map/inner_conv/pallas_call | solution.py:86
  12.0 1.3 %mask_rows.1 = (bf16[1024,384]{1,0:T(8,128)(2,1)S(1)}, bf16[384,1024]{1,0:T(8,128)(2,1)S(1)}) custom-call(s32[4,4]{1,0:T(4,128)S(1)} %copy-done.7, f32[1024,384]{1,0:T(8,128)S(1)} %bitcast.14), custom_call_target="tpu_custom_call" | custom-call | flops 1495000064 | bytes 1048576 | tf_op jit(solution)/shard_map/mask_rows/pallas_call | solution.py:310
  13.4 1.4 %collective-permute-start.2 = (bf16[3,48,384]{2,1,0:T(8,128)(2,1)S(1)}, bf16[3,48,384]{2,1,0:T(8,128)(2,1)S(1)}, u32[]{:S(2)}, u32[]{:S(2)}) collective-permute-start(bf16[3,48,384]{2,1,0:T(8,128)(2,1)S(1)} %get-tuple-element.70), channel_id=1, source_target_pairs={{0,16},{16,32},{32,48},{48,64},{64,80},{80,96},{96,112},{1,17},{17... | collective-permute-start | bytes 331784 | tf_op jit(solution)/shard_map/ppermute | solution.py:727
  14.8 1.3 %collective-permute-start.3 = (bf16[3,48,384]{2,1,0:T(8,128)(2,1)S(1)}, bf16[3,48,384]{2,1,0:T(8,128)(2,1)S(1)}, u32[]{:S(2)}, u32[]{:S(2)}) collective-permute-start(bf16[3,48,384]{2,1,0:T(8,128)(2,1)S(1)} %get-tuple-element.71), channel_id=1, source_target_pairs={{16,0},{32,16},{48,32},{64,48},{80,64},{96,80},{112,96},{17,1},{33... | collective-permute-start | bytes 331784 | tf_op jit(solution)/shard_map/ppermute | solution.py:728
  16.2 1.5 %arrange.1 = (bf16[1536,384]{1,0:T(8,128)(2,1)S(1)}, bf16[1536,384]{1,0:T(8,128)(2,1)S(1)}, bf16[384,1536]{1,0:T(8,128)(2,1)S(1)}, f32[1536,128]{1,0:T(8,128)S(1)}) custom-call(bf16[1536,384]{1,0:T(8,128)(2,1)S(1)} %bitcast.16, bf16[1536,384]{1,0:T(8,128)(2,1)S(1)} %bitcast.17, f32[1,1536]{1,0:T(1,128)S(1)} %copy-done.6), custom_call_target="tpu_custom_call" | custom-call | flops 1264999936 | bytes 1048576 | tf_op jit(solution)/shard_map/arrange/pallas_call | solution.py:348
  17.7 2.1 %collective-permute-done.3.bottom_ref = bf16[3,48,384]{2,1,0:T(8,128)(2,1)S(1)} collective-permute-done((bf16[3,48,384]{2,1,0:T(8,128)(2,1)S(1)}, bf16[3,48,384]{2,1,0:T(8,128)(2,1)S(1)}, u32[]{:S(2)}, u32[]{:S(2)}) %collective-permute-start.3) | collective-permute-done | bytes 110624 | tf_op jit(solution)/shard_map/ppermute | solution.py:728
  19.9 4.7 %normalise.1 = (f32[1024,384]{1,0:T(8,128)S(1)}, f32[1024,128]{1,0:T(8,128)S(1)}, bf16[1024,384]{1,0:T(8,128)(2,1)S(1)}, bf16[384,1024]{1,0:T(8,128)(2,1)S(1)}) custom-call(f32[1024,128]{1,0:T(8,128)S(1)} %get-tuple-element.65.conv0_ref, f32[1024,128]{1,0:T(8,128)S(1)} %get-tuple-element.66.conv1_ref, f32[1024,128]{1,0:T(8,128)S(1)} %get-tuple-element.67.conv2_ref, ...), custom_call_target="tpu_custom_call" | custom-call | flops 5520000000 | bytes 1048576 | tf_op jit(solution)/shard_map/normalise/pallas_call | solution.py:256
  24.6 5.4 %hidden_far.1 = (bf16[768,768]{1,0:T(8,128)(2,1)S(1)}, bf16[768,1024]{1,0:T(8,128)(2,1)S(1)}) custom-call(bf16[1024,384]{1,0:T(8,128)(2,1)S(1)} %get-tuple-element.72.refs_0_, bf16[384,1024]{1,0:T(8,128)(2,1)S(1)} %get-tuple-element.73.refs_1_, bf16[1024,384]{1,0:T(8,128)(2,1)S(1)} %get-tuple-element.74.refs_2_, ...), custom_call_target="tpu_custom_call" | custom-call | flops 6670000128 | bytes 1048576 | tf_op jit(solution)/shard_map/hidden_far/pallas_call | solution.py:429
  30.0 3.6 %collective-permute-start.4 = (bf16[768,768]{1,0:T(8,128)(2,1)S(1)}, bf16[768,768]{1,0:T(8,128)(2,1)S(1)}, u32[]{:S(2)}, u32[]{:S(2)}) collective-permute-start(bf16[768,768]{1,0:T(8,128)(2,1)S(1)} %get-tuple-element.80), channel_id=1, source_target_pairs={{0,16},{16,0},{32,48},{48,32},{64,80},{80,64},{96,112},{112,96},{1... | collective-permute-start | bytes 3538952 | tf_op jit(solution)/shard_map/ppermute | solution.py:756
  33.6 2.9 %near_first.1 = (f32[384,768]{1,0:T(8,128)S(1)}, bf16[768,1024]{1,0:T(8,128)(2,1)S(1)}) custom-call(bf16[1024,384]{1,0:T(8,128)(2,1)S(1)} %get-tuple-element.72.refs_0_, bf16[384,1024]{1,0:T(8,128)(2,1)S(1)} %get-tuple-element.73.refs_1_, bf16[1024,384]{1,0:T(8,128)(2,1)S(1)} %get-tuple-element.74.refs_2_, bf16[384,1024]{1,0:T(8,128)(2,1)S(1)} %get-tuple-element.75.refs_3_, ...), custom_call_target="tpu_custom_call" | custom-call | flops 3449999872 | bytes 1048576 | tf_op jit(solution)/shard_map/near_first/pallas_call | solution.py:461
  36.7 1.7 %collective-permute-start.5 = (bf16[192,768]{1,0:T(8,128)(2,1)S(1)}, bf16[192,768]{1,0:T(8,128)(2,1)S(1)}, u32[]{:S(2)}, u32[]{:S(2)}) collective-permute-start(bf16[192,768]{1,0:T(8,128)(2,1)S(1)} %get-tuple-element.83), channel_id=1, source_target_pairs={{0,32},{1,33},{2,34},{3,35},{4,36},{5,37},{6,38},{7,39},{8,40},{9,... | collective-permute-start | bytes 884744 | tf_op jit(solution)/shard_map/ppermute | solution.py:759
  38.3 1.4 %collective-permute-start.6 = (bf16[192,768]{1,0:T(8,128)(2,1)S(1)}, bf16[192,768]{1,0:T(8,128)(2,1)S(1)}, u32[]{:S(2)}, u32[]{:S(2)}) collective-permute-start(bf16[192,768]{1,0:T(8,128)(2,1)S(1)} %get-tuple-element.84), channel_id=1, source_target_pairs={{0,64},{1,65},{2,66},{3,67},{4,68},{5,69},{6,70},{7,71},{8,72},{9,... | collective-permute-start | bytes 884744 | tf_op jit(solution)/shard_map/ppermute | solution.py:760
  39.7 2.9 %near_last.1 = (f32[192,768]{1,0:T(8,128)S(1)}, bf16[192,768]{1,0:T(8,128)(2,1)S(1)}, bf16[768,1024]{1,0:T(8,128)(2,1)S(1)}) custom-call(bf16[1024,384]{1,0:T(8,128)(2,1)S(1)} %get-tuple-element.72.refs_0_, bf16[384,1024]{1,0:T(8,128)(2,1)S(1)} %get-tuple-element.73.refs_1_, ...), custom_call_target="tpu_custom_call", output_to_operand_aliasing={{2}: (8, {})} | custom-call | flops 3449999872 | bytes 1048576 | tf_op jit(solution)/shard_map/near_last/pallas_call | solution.py:517
  42.6 2.6 %collective-permute-start.7 = (bf16[192,768]{1,0:T(8,128)(2,1)S(1)}, bf16[192,768]{1,0:T(8,128)(2,1)S(1)}, u32[]{:S(2)}, u32[]{:S(2)}) collective-permute-start(bf16[192,768]{1,0:T(8,128)(2,1)S(1)} %get-tuple-element.86), channel_id=1, source_target_pairs={{0,96},{1,97},{2,98},{3,99},{4,100},{5,101},{6,102},{7,103},{8,104... | collective-permute-start | bytes 884744 | tf_op jit(solution)/shard_map/ppermute | solution.py:762
  45.2 2.2 %norm_back.1 = (f32[32,32,384]{2,1,0:T(8,128)S(1)}, bf16[3,32,384]{2,1,0:T(8,128)(2,1)S(1)}, bf16[3,32,384]{2,1,0:T(8,128)(2,1)S(1)}) custom-call(bf16[384,1536]{1,0:T(8,128)(2,1)S(1)} %get-tuple-element.64.turned_ref, bf16[768,1024]{1,0:T(8,128)(2,1)S(1)} %get-tuple-element.87.other_ref, bf16[768,1024]{1,0:T(8,128)(2,1)S(1)} %get-tuple-element.88.mine_ref, ...), custom_call_target="tpu_custom_call" | custom-call | flops 2529999872 | bytes 1048576 | tf_op jit(solution)/shard_map/norm_back/pallas_call | solution.py:564
  48.1 2.3 %collective-permute-start.9 = (bf16[3,32,384]{2,1,0:T(8,128)(2,1)S(1)}, bf16[3,32,384]{2,1,0:T(8,128)(2,1)S(1)}, u32[]{:S(2)}, u32[]{:S(2)}) collective-permute-start(bf16[3,32,384]{2,1,0:T(8,128)(2,1)S(1)} %get-tuple-element.94), channel_id=1, source_target_pairs={{0,15},{1,0},{2,1},{3,2},{4,3},{5,4},{6,5},{7,6},{8,7},{9,8},{10,9... | collective-permute-start | bytes 221192 | tf_op jit(solution)/shard_map/ppermute | solution.py:722
  50.4 2.4 %collective-permute-done.8.left_ref = bf16[3,32,384]{2,1,0:T(8,128)(2,1)S(1)} collective-permute-done((bf16[3,32,384]{2,1,0:T(8,128)(2,1)S(1)}, bf16[3,32,384]{2,1,0:T(8,128)(2,1)S(1)}, u32[]{:S(2)}, u32[]{:S(2)}) %collective-permute-start.8) | collective-permute-done | bytes 73760 | tf_op jit(solution)/shard_map/ppermute | solution.py:721
  52.9 0.9 %collective-permute-done.9.right_ref = bf16[3,32,384]{2,1,0:T(8,128)(2,1)S(1)} collective-permute-done((bf16[3,32,384]{2,1,0:T(8,128)(2,1)S(1)}, bf16[3,32,384]{2,1,0:T(8,128)(2,1)S(1)}, u32[]{:S(2)}, u32[]{:S(2)}) %collective-permute-start.9) | collective-permute-done | bytes 73760 | tf_op jit(solution)/shard_map/ppermute | solution.py:722
  54.0 2.4 %collective-permute-start.10 = (bf16[48,768]{1,0:T(8,128)(2,1)S(1)}, bf16[48,768]{1,0:T(8,128)(2,1)S(1)}, u32[]{:S(2)}, u32[]{:S(2)}) collective-permute-start(bf16[48,768]{1,0:T(8,128)(2,1)S(1)} %get-tuple-element.99), channel_id=1, source_target_pairs={{0,1},{1,128},{2,3},{3,130},{4,5},{5,132},{6,7},{7,134},{8,9},{9,1... | collective-permute-start | bytes 221192 | tf_op jit(solution)/shard_map/ppermute | solution.py:770
  56.4 3.0 %collective-permute-start.11 = (bf16[48,768]{1,0:T(8,128)(2,1)S(1)}, bf16[48,768]{1,0:T(8,128)(2,1)S(1)}, u32[]{:S(2)}, u32[]{:S(2)}) collective-permute-start(bf16[48,768]{1,0:T(8,128)(2,1)S(1)} %get-tuple-element.100), channel_id=1, source_target_pairs={{0,128},{1,129},{2,130},{3,131},{4,132},{5,133},{6,134},{7,135},{8... | collective-permute-start | bytes 221192 | tf_op jit(solution)/shard_map/ppermute | solution.py:770
  59.5 2.1 %inner_conv.5.conv0_ref = f32[1024,128]{1,0:T(8,128)S(1)} custom-call(f32[1024,384]{1,0:T(8,128)S(1)} %bitcast.24, f32[49,1,384]{2,1,0:T(1,128)S(1)} %bitcast.20), custom_call_target="tpu_custom_call" | custom-call | flops 2644999936 | bytes 1048576 | tf_op jit(solution)/shard_map/inner_conv/pallas_call | solution.py:86
  61.7 1.3 %collective-permute-start.15 = (bf16[3,48,384]{2,1,0:T(8,128)(2,1)S(1)}, bf16[3,48,384]{2,1,0:T(8,128)(2,1)S(1)}, u32[]{:S(2)}, u32[]{:S(2)}) collective-permute-start(bf16[3,48,384]{2,1,0:T(8,128)(2,1)S(1)} %get-tuple-element.104), channel_id=1, source_target_pairs={{16,0},{32,16},{48,32},{64,48},{80,64},{96,80},{112,96},{17,1},{33... | collective-permute-start | bytes 331784 | tf_op jit(solution)/shard_map/ppermute | solution.py:728
  63.0 3.0 %collective-permute-start.14 = (bf16[3,48,384]{2,1,0:T(8,128)(2,1)S(1)}, bf16[3,48,384]{2,1,0:T(8,128)(2,1)S(1)}, u32[]{:S(2)}, u32[]{:S(2)}) collective-permute-start(bf16[3,48,384]{2,1,0:T(8,128)(2,1)S(1)} %get-tuple-element.105), channel_id=1, source_target_pairs={{0,16},{16,32},{32,48},{48,64},{64,80},{80,96},{96,112},{1,17},{17... | collective-permute-start | bytes 331784 | tf_op jit(solution)/shard_map/ppermute | solution.py:727
  66.1 5.9 %collective-permute-start.13 = (f32[24,768]{1,0:T(8,128)S(1)}, f32[24,768]{1,0:T(8,128)S(1)}, u32[]{:S(2)}, u32[]{:S(2)}) collective-permute-start(f32[24,768]{1,0:T(8,128)S(1)} %get-tuple-element.110), channel_id=1, source_target_pairs={{0,8},{1,9},{2,10},{3,11},{4,12},{5,13},{6,14},{7,15},{8,0},{9,1},... | collective-permute-start | bytes 221192 | tf_op jit(solution)/shard_map/ppermute | solution.py:777
  72.0 2.1 %inner_conv.6.conv1_ref = f32[1024,128]{1,0:T(8,128)S(1)} custom-call(f32[1024,384]{1,0:T(8,128)S(1)} %bitcast.26, f32[49,1,384]{2,1,0:T(1,128)S(1)} %bitcast.21), custom_call_target="tpu_custom_call" | custom-call | flops 2644999936 | bytes 1048576 | tf_op jit(solution)/shard_map/inner_conv/pallas_call | solution.py:86
  74.5 7.5 %collective-permute-start.16 = (f32[12,768]{1,0:T(8,128)S(1)}, f32[12,768]{1,0:T(8,128)S(1)}, u32[]{:S(2)}, u32[]{:S(2)}) collective-permute-start(f32[12,768]{1,0:T(8,128)S(1)} %get-tuple-element.115), channel_id=1, source_target_pairs={{0,4},{1,5},{2,6},{3,7},{4,0},{5,1},{6,2},{7,3},{8,12},{9,13},{10,... | collective-permute-start | bytes 110600 | tf_op jit(solution)/shard_map/ppermute | solution.py:782
  82.0 2.1 %inner_conv.7.conv2_ref = f32[1024,128]{1,0:T(8,128)S(1)} custom-call(f32[1024,384]{1,0:T(8,128)S(1)} %bitcast.27, f32[49,1,384]{2,1,0:T(1,128)S(1)} %bitcast.22), custom_call_target="tpu_custom_call" | custom-call | flops 2644999936 | bytes 1048576 | tf_op jit(solution)/shard_map/inner_conv/pallas_call | solution.py:86
  84.2 1.8 %collective-permute-start.17 = (f32[6,768]{1,0:T(8,128)S(1)}, f32[6,768]{1,0:T(8,128)S(1)}, u32[]{:S(2)}, u32[]{:S(2)}) collective-permute-start(f32[6,768]{1,0:T(8,128)S(1)} %get-tuple-element.120), channel_id=1, source_target_pairs={{0,2},{1,3},{2,0},{3,1},{4,6},{5,7},{6,4},{7,5},{8,10},{9,11},{10,... | collective-permute-start | bytes 55304 | tf_op jit(solution)/shard_map/ppermute | solution.py:787
  86.0 3.1 %finish.1 = f32[1024,384]{1,0:T(8,128)} custom-call(s32[4,4]{1,0:T(4,128)S(1)} %copy-done.7, f32[1024,128]{1,0:T(8,128)S(1)} %inner_conv.5.conv0_ref, f32[1024,128]{1,0:T(8,128)S(1)} %inner_conv.6.conv1_ref, f32[1024,128]{1,0:T(8,128)S(1)} %inner_conv.7.conv2_ref, f32[49,1,384]{2,1,0:T(1,128)S(1)} %bitcast.23, ...), custom_call_target="tpu_custom_call" | custom-call | flops 3564999936 | bytes 1048576 | tf_op jit(solution)/shard_map/finish/pallas_call | solution.py:595
  (47 shorter events, 2.6 us)
Async XLA Ops:
  0.6 1.4 %copy-start = (f32[1,32,32,384]{3,2,1,0:T(8,128)S(1)}, f32[1,32,32,384]{3,2,1,0:T(8,128)}, u32[]{:S(2)}) copy-start(f32[1,32,32,384]{3,2,1,0:T(8,128)} %param.10) | copy-start | bytes 4718596
  2.0 3.5 %copy-start.1 = (f32[1,32,32,384]{3,2,1,0:T(8,128)S(1)}, f32[1,32,32,384]{3,2,1,0:T(8,128)}, u32[]{:S(2)}) copy-start(f32[1,32,32,384]{3,2,1,0:T(8,128)} %param.10) | copy-start | bytes 4718596
  2.0 3.5 %copy-start.5 = (f32[1,49,384]{2,0,1:T(1,128)S(1)}, f32[1,49,384]{2,0,1:T(1,128)}, u32[]{:S(2)}) copy-start(f32[1,49,384]{2,0,1:T(1,128)} %param.13) | copy-start | bytes 225796
  2.5 10.8 %collective-permute-start = (bf16[3,32,384]{2,1,0:T(8,128)(2,1)S(1)}, bf16[3,32,384]{2,1,0:T(8,128)(2,1)S(1)}, u32[]{:S(2)}, u32[]{:S(2)}) collective-permute-start(bf16[3,32,384]{2,1,0:T(8,128)(2,1)S(1)} %get-tuple-element.68), channel_id=1, source_target_pairs={{0,1},{1,2},{2,3},{3,4},{4,5},{5,6},{6,7},{7,8},{8,9},{9,10},{10,1... | collective-permute-start | bytes 221192 | tf_op jit(solution)/shard_map/ppermute | solution.py:721
  4.1 9.3 %collective-permute-start.1 = (bf16[3,32,384]{2,1,0:T(8,128)(2,1)S(1)}, bf16[3,32,384]{2,1,0:T(8,128)(2,1)S(1)}, u32[]{:S(2)}, u32[]{:S(2)}) collective-permute-start(bf16[3,32,384]{2,1,0:T(8,128)(2,1)S(1)} %get-tuple-element.69), channel_id=1, source_target_pairs={{0,15},{1,0},{2,1},{3,2},{4,3},{5,4},{6,5},{7,6},{8,7},{9,8},{10,9... | collective-permute-start | bytes 221192 | tf_op jit(solution)/shard_map/ppermute | solution.py:722
  5.5 6.4 %copy-start.2 = (f32[1,32,32,384]{3,2,1,0:T(8,128)S(1)}, f32[1,32,32,384]{3,2,1,0:T(8,128)}, u32[]{:S(2)}) copy-start(f32[1,32,32,384]{3,2,1,0:T(8,128)} %param.11) | copy-start | bytes 4718596
  5.5 6.4 %copy-start.7 = (s32[4,4]{1,0:T(4,128)S(1)}, s32[4,4]{1,0:T(4,128)}, u32[]{:S(2)}) copy-start(s32[4,4]{1,0:T(4,128)} %counts_ref.3) | copy-start | bytes 196
  12.0 4.2 %copy-start.4 = (bf16[1,1536,384]{2,1,0:T(8,128)(2,1)S(1)}, bf16[1,1536,384]{2,1,0:T(8,128)(2,1)}, u32[]{:S(2)}) copy-start(bf16[1,1536,384]{2,1,0:T(8,128)(2,1)} %param.19) | copy-start | bytes 3538948
  13.3 2.9 %copy-start.3 = (bf16[1,1536,384]{2,1,0:T(8,128)(2,1)S(1)}, bf16[1,1536,384]{2,1,0:T(8,128)(2,1)}, u32[]{:S(2)}) copy-start(bf16[1,1536,384]{2,1,0:T(8,128)(2,1)} %param.17) | copy-start | bytes 3538948
  13.3 2.9 %copy-start.6 = (f32[1,1536]{1,0:T(1,128)S(1)}, f32[1,1536]{1,0:T(1,128)}, u32[]{:S(2)}) copy-start(f32[1,1536]{1,0:T(1,128)} %bias_ref.2) | copy-start | bytes 18436
  13.4 4.3 %collective-permute-start.2 = (bf16[3,48,384]{2,1,0:T(8,128)(2,1)S(1)}, bf16[3,48,384]{2,1,0:T(8,128)(2,1)S(1)}, u32[]{:S(2)}, u32[]{:S(2)}) collective-permute-start(bf16[3,48,384]{2,1,0:T(8,128)(2,1)S(1)} %get-tuple-element.70), channel_id=1, source_target_pairs={{0,16},{16,32},{32,48},{48,64},{64,80},{80,96},{96,112},{1,17},{17... | collective-permute-start | bytes 331784 | tf_op jit(solution)/shard_map/ppermute | solution.py:727
  14.8 5.0 %collective-permute-start.3 = (bf16[3,48,384]{2,1,0:T(8,128)(2,1)S(1)}, bf16[3,48,384]{2,1,0:T(8,128)(2,1)S(1)}, u32[]{:S(2)}, u32[]{:S(2)}) collective-permute-start(bf16[3,48,384]{2,1,0:T(8,128)(2,1)S(1)} %get-tuple-element.71), channel_id=1, source_target_pairs={{16,0},{32,16},{48,32},{64,48},{80,64},{96,80},{112,96},{17,1},{33... | collective-permute-start | bytes 331784 | tf_op jit(solution)/shard_map/ppermute | solution.py:728
  16.2 3.7 %copy-start.8 = (f32[1,384]{1,0:T(1,128)S(1)}, f32[1,384]{1,0:T(1,128)}, u32[]{:S(2)}) copy-start(f32[1,384]{1,0:T(1,128)} %bias_ref.3) | copy-start | bytes 4612
  16.2 3.7 %copy-start.9 = (f32[1,384]{1,0:T(1,128)S(1)}, f32[1,384]{1,0:T(1,128)}, u32[]{:S(2)}) copy-start(f32[1,384]{1,0:T(1,128)} %shift_ref.1) | copy-start | bytes 4612
  16.2 3.7 %copy-start.10 = (f32[1,384]{1,0:T(1,128)S(1)}, f32[1,384]{1,0:T(1,128)}, u32[]{:S(2)}) copy-start(f32[1,384]{1,0:T(1,128)} %gain_ref.3) | copy-start | bytes 4612
  30.0 6.5 %collective-permute-start.4 = (bf16[768,768]{1,0:T(8,128)(2,1)S(1)}, bf16[768,768]{1,0:T(8,128)(2,1)S(1)}, u32[]{:S(2)}, u32[]{:S(2)}) collective-permute-start(bf16[768,768]{1,0:T(8,128)(2,1)S(1)} %get-tuple-element.80), channel_id=1, source_target_pairs={{0,16},{16,0},{32,48},{48,32},{64,80},{80,64},{96,112},{112,96},{1... | collective-permute-start | bytes 3538952 | tf_op jit(solution)/shard_map/ppermute | solution.py:756
  36.7 17.1 %collective-permute-start.5 = (bf16[192,768]{1,0:T(8,128)(2,1)S(1)}, bf16[192,768]{1,0:T(8,128)(2,1)S(1)}, u32[]{:S(2)}, u32[]{:S(2)}) collective-permute-start(bf16[192,768]{1,0:T(8,128)(2,1)S(1)} %get-tuple-element.83), channel_id=1, source_target_pairs={{0,32},{1,33},{2,34},{3,35},{4,36},{5,37},{6,38},{7,39},{8,40},{9,... | collective-permute-start | bytes 884744 | tf_op jit(solution)/shard_map/ppermute | solution.py:759
  38.3 15.5 %collective-permute-start.6 = (bf16[192,768]{1,0:T(8,128)(2,1)S(1)}, bf16[192,768]{1,0:T(8,128)(2,1)S(1)}, u32[]{:S(2)}, u32[]{:S(2)}) collective-permute-start(bf16[192,768]{1,0:T(8,128)(2,1)S(1)} %get-tuple-element.84), channel_id=1, source_target_pairs={{0,64},{1,65},{2,66},{3,67},{4,68},{5,69},{6,70},{7,71},{8,72},{9,... | collective-permute-start | bytes 884744 | tf_op jit(solution)/shard_map/ppermute | solution.py:760
  42.6 11.1 %collective-permute-start.7 = (bf16[192,768]{1,0:T(8,128)(2,1)S(1)}, bf16[192,768]{1,0:T(8,128)(2,1)S(1)}, u32[]{:S(2)}, u32[]{:S(2)}) collective-permute-start(bf16[192,768]{1,0:T(8,128)(2,1)S(1)} %get-tuple-element.86), channel_id=1, source_target_pairs={{0,96},{1,97},{2,98},{3,99},{4,100},{5,101},{6,102},{7,103},{8,104... | collective-permute-start | bytes 884744 | tf_op jit(solution)/shard_map/ppermute | solution.py:762
  47.4 5.4 %collective-permute-start.8 = (bf16[3,32,384]{2,1,0:T(8,128)(2,1)S(1)}, bf16[3,32,384]{2,1,0:T(8,128)(2,1)S(1)}, u32[]{:S(2)}, u32[]{:S(2)}) collective-permute-start(bf16[3,32,384]{2,1,0:T(8,128)(2,1)S(1)} %get-tuple-element.93), channel_id=1, source_target_pairs={{0,1},{1,2},{2,3},{3,4},{4,5},{5,6},{6,7},{7,8},{8,9},{9,10},{10,1... | collective-permute-start | bytes 221192 | tf_op jit(solution)/shard_map/ppermute | solution.py:721
  48.1 5.7 %collective-permute-start.9 = (bf16[3,32,384]{2,1,0:T(8,128)(2,1)S(1)}, bf16[3,32,384]{2,1,0:T(8,128)(2,1)S(1)}, u32[]{:S(2)}, u32[]{:S(2)}) collective-permute-start(bf16[3,32,384]{2,1,0:T(8,128)(2,1)S(1)} %get-tuple-element.94), channel_id=1, source_target_pairs={{0,15},{1,0},{2,1},{3,2},{4,3},{5,4},{6,5},{7,6},{8,7},{9,8},{10,9... | collective-permute-start | bytes 221192 | tf_op jit(solution)/shard_map/ppermute | solution.py:722
  54.0 12.1 %collective-permute-start.10 = (bf16[48,768]{1,0:T(8,128)(2,1)S(1)}, bf16[48,768]{1,0:T(8,128)(2,1)S(1)}, u32[]{:S(2)}, u32[]{:S(2)}) collective-permute-start(bf16[48,768]{1,0:T(8,128)(2,1)S(1)} %get-tuple-element.99), channel_id=1, source_target_pairs={{0,1},{1,128},{2,3},{3,130},{4,5},{5,132},{6,7},{7,134},{8,9},{9,1... | collective-permute-start | bytes 221192 | tf_op jit(solution)/shard_map/ppermute | solution.py:770
  56.4 9.6 %collective-permute-start.11 = (bf16[48,768]{1,0:T(8,128)(2,1)S(1)}, bf16[48,768]{1,0:T(8,128)(2,1)S(1)}, u32[]{:S(2)}, u32[]{:S(2)}) collective-permute-start(bf16[48,768]{1,0:T(8,128)(2,1)S(1)} %get-tuple-element.100), channel_id=1, source_target_pairs={{0,128},{1,129},{2,130},{3,131},{4,132},{5,133},{6,134},{7,135},{8... | collective-permute-start | bytes 221192 | tf_op jit(solution)/shard_map/ppermute | solution.py:770
  59.4 6.6 %collective-permute-start.12 = (bf16[48,768]{1,0:T(8,128)(2,1)S(1)}, bf16[48,768]{1,0:T(8,128)(2,1)S(1)}, u32[]{:S(2)}, u32[]{:S(2)}) collective-permute-start(bf16[48,768]{1,0:T(8,128)(2,1)S(1)} %get-tuple-element.101), channel_id=1, source_target_pairs={{0,129},{1,0},{2,131},{3,2},{4,133},{5,4},{6,135},{7,6},{8,137},{9... | collective-permute-start | bytes 221192 | tf_op jit(solution)/shard_map/ppermute | solution.py:770
  61.7 22.5 %collective-permute-start.15 = (bf16[3,48,384]{2,1,0:T(8,128)(2,1)S(1)}, bf16[3,48,384]{2,1,0:T(8,128)(2,1)S(1)}, u32[]{:S(2)}, u32[]{:S(2)}) collective-permute-start(bf16[3,48,384]{2,1,0:T(8,128)(2,1)S(1)} %get-tuple-element.104), channel_id=1, source_target_pairs={{16,0},{32,16},{48,32},{64,48},{80,64},{96,80},{112,96},{17,1},{33... | collective-permute-start | bytes 331784 | tf_op jit(solution)/shard_map/ppermute | solution.py:728
  63.0 21.2 %collective-permute-start.14 = (bf16[3,48,384]{2,1,0:T(8,128)(2,1)S(1)}, bf16[3,48,384]{2,1,0:T(8,128)(2,1)S(1)}, u32[]{:S(2)}, u32[]{:S(2)}) collective-permute-start(bf16[3,48,384]{2,1,0:T(8,128)(2,1)S(1)} %get-tuple-element.105), channel_id=1, source_target_pairs={{0,16},{16,32},{32,48},{48,64},{64,80},{80,96},{96,112},{1,17},{17... | collective-permute-start | bytes 331784 | tf_op jit(solution)/shard_map/ppermute | solution.py:727
  66.1 8.4 %collective-permute-start.13 = (f32[24,768]{1,0:T(8,128)S(1)}, f32[24,768]{1,0:T(8,128)S(1)}, u32[]{:S(2)}, u32[]{:S(2)}) collective-permute-start(f32[24,768]{1,0:T(8,128)S(1)} %get-tuple-element.110), channel_id=1, source_target_pairs={{0,8},{1,9},{2,10},{3,11},{4,12},{5,13},{6,14},{7,15},{8,0},{9,1},... | collective-permute-start | bytes 221192 | tf_op jit(solution)/shard_map/ppermute | solution.py:777
  74.5 9.7 %collective-permute-start.16 = (f32[12,768]{1,0:T(8,128)S(1)}, f32[12,768]{1,0:T(8,128)S(1)}, u32[]{:S(2)}, u32[]{:S(2)}) collective-permute-start(f32[12,768]{1,0:T(8,128)S(1)} %get-tuple-element.115), channel_id=1, source_target_pairs={{0,4},{1,5},{2,6},{3,7},{4,0},{5,1},{6,2},{7,3},{8,12},{9,13},{10,... | collective-permute-start | bytes 110600 | tf_op jit(solution)/shard_map/ppermute | solution.py:782
  84.2 4.9 %collective-permute-start.17 = (f32[6,768]{1,0:T(8,128)S(1)}, f32[6,768]{1,0:T(8,128)S(1)}, u32[]{:S(2)}, u32[]{:S(2)}) collective-permute-start(f32[6,768]{1,0:T(8,128)S(1)} %get-tuple-element.120), channel_id=1, source_target_pairs={{0,2},{1,3},{2,0},{3,1},{4,6},{5,7},{6,4},{7,5},{8,10},{9,11},{10,... | collective-permute-start | bytes 55304 | tf_op jit(solution)/shard_map/ppermute | solution.py:787

commit v5 on v4

--- a/solution.py
+++ b/solution.py
@@ -95,29 +95,34 @@
     )(cells, kernel)
 
 
-def side_cols_body(low_ref, high_ref, first_ref, last_ref):
+def side_cols_body(cells_ref, first_ref, last_ref, low, high, sems):
+    copies = [
+        pltpu.make_async_copy(cells_ref.at[:, pl.ds(0, 8), :], low, sems.at[0]),
+        pltpu.make_async_copy(cells_ref.at[:, pl.ds(side - 8, 8), :], high, sems.at[1]),
+    ]
+    for copy in copies:
+        copy.start()
+    copies[0].wait()
     for j in range(reach):
-        first_ref[j] = low_ref[:, j, :].astype(bf16)
-        last_ref[j] = high_ref[:, 8 - reach + j, :].astype(bf16)
+        first_ref[j] = low[:, j, :].astype(bf16)
+    copies[1].wait()
+    for j in range(reach):
+        last_ref[j] = high[:, 8 - reach + j, :].astype(bf16)
 
 
 def side_cols(cells):
     channels = cells.shape[1]
-    grid3 = cells.reshape(side, side, channels)
     shape = jax.ShapeDtypeStruct((reach, side, channels), bf16)
     return pl.pallas_call(
         side_cols_body,
         out_shape=(shape, shape),
-        grid=(1,),
-        in_specs=[
-            pl.BlockSpec((side, 8, channels), lambda g: (0, 0, 0)),
-            pl.BlockSpec((side, 8, channels), lambda g: (0, side // 8 - 1, 0)),
-        ],
-        out_specs=[pl.BlockSpec((reach, side, channels), lambda g: (0, 0, 0))] * 2,
-        compiler_params=params(4),
-        cost_estimate=cost(0.5),
+        in_specs=[pl.BlockSpec(memory_space=pltpu.HBM)],
+        out_specs=[whole] * 2,
+        scratch_shapes=[pltpu.VMEM((side, 8, channels), f32)] * 2 + [pltpu.SemaphoreType.DMA((2,))],
+        compiler_params=params(58),
+        cost_estimate=cost(1.0),
         name="side_cols",
-    )(grid3, grid3)
+    )(cells.reshape(side, side, channels))
 
 
 def side_rows_body(cells_ref, left_ref, right_ref, up_ref, down_ref):
@@ -209,9 +214,9 @@
         step(i, i - (side - 2 * reach))
         return carry
 
-    lax.fori_loop(0, reach, low, 0)
-    lax.fori_loop(reach, side - reach, middle, 0, unroll=2)
-    lax.fori_loop(side - reach, side, high, 0)
+    lax.fori_loop(0, reach, low, 0, unroll=reach)
+    lax.fori_loop(reach, side - reach, middle, 0, unroll=side // 2 - reach)
+    lax.fori_loop(side - reach, side, high, 0, unroll=reach)
 
 
 def conv_rows(refs, at):
@@ -220,7 +225,7 @@
 
 def normalise_body(
     conv0_ref, conv1_ref, conv2_ref, kernel_ref, left_ref, right_ref, top_ref, bottom_ref, bias_ref, gain_ref, shift_ref,
-    unit_ref, spread_ref, normed_ref, flipped_ref, rows_sum, cols_sum,
+    unit_ref, spread_ref, normed_ref, rows_sum, cols_sum,
 ):
     channels = kernel_ref.shape[2]
     conv_refs = (conv0_ref, conv1_ref, conv2_ref)
@@ -242,7 +247,6 @@
         normed_ref[at, :] = (unit * gain_ref[...] + shift_ref[...]).astype(bf16)
 
     each_row(step)
-    turn(normed_ref, flipped_ref)
 
 
 def turn(source_ref, target_ref):
@@ -259,13 +263,12 @@
             jax.ShapeDtypeStruct((total, channels), f32),
             jax.ShapeDtypeStruct((total, lanes), f32),
             jax.ShapeDtypeStruct((total, channels), bf16),
-            jax.ShapeDtypeStruct((channels, total), bf16),
         ),
         in_specs=[whole] * 11,
-        out_specs=[whole] * 4,
+        out_specs=[whole] * 3,
         scratch_shapes=[pltpu.VMEM((2 * reach, side, channels), f32)] * 2,
         compiler_params=params(12),
-        cost_estimate=cost(4.8),
+        cost_estimate=cost(2.8),
         name="normalise",
     )(*conv, kernel, left, right, top, bottom, bias, gain, shift)
 
@@ -295,28 +298,24 @@
     return jnp.concatenate(parts, axis=0)
 
 
-def mask_rows_body(counts_ref, grad_ref, rows_ref, flipped_ref):
+def mask_rows_body(counts_ref, grad_ref, rows_ref):
     def step(i, carry):
         at = pl.ds(pl.multiple_of(i * side, side), side)
         rows_ref[at, :] = masked_row(i, grad_ref[at, :], counts_ref).astype(bf16)
         return carry
 
-    lax.fori_loop(0, side, step, 0)
-    turn(rows_ref, flipped_ref)
+    lax.fori_loop(0, side, step, 0, unroll=2)
 
 
 def mask_rows(counts, grad):
     total, channels = grad.shape
     return pl.pallas_call(
         mask_rows_body,
-        out_shape=(
-            jax.ShapeDtypeStruct((total, channels), bf16),
-            jax.ShapeDtypeStruct((channels, total), bf16),
-        ),
+        out_shape=jax.ShapeDtypeStruct((total, channels), bf16),
         in_specs=[pl.BlockSpec(memory_space=pltpu.SMEM), whole],
-        out_specs=[whole] * 2,
+        out_specs=whole,
         compiler_params=params(8),
-        cost_estimate=cost(1.3),
+        cost_estimate=cost(0.9),
         name="mask_rows",
     )(counts, grad)
 
@@ -356,7 +355,7 @@
         in_specs=[whole] * 3,
         out_specs=[whole] * 4,
         compiler_params=params(12),
-        cost_estimate=cost(1.1),
+        cost_estimate=cost(1.5),
         name="arrange",
     )(expand, reduce, bias)
 
@@ -392,12 +391,16 @@
     return jnp.where(along_y, y, x)
 
 
+def dot_rows(left, right):
+    return lax.dot_general(left, right, (((1,), (1,)), ((), ())), preferred_element_type=f32)
+
+
 def hidden_rows(cells, source, rows, grad_pre_ref, to):
-    normed_ref, normed_t_ref, grad_ref, grad_t_ref, expand_ref, reduce_ref, bias_ref = cells
+    normed_ref, grad_ref, expand_ref, reduce_ref, bias_ref = cells
     total = normed_ref.shape[0]
     at = pl.ds(source, rows)
-    preact = jnp.dot(expand_ref[at, :], normed_t_ref[...], preferred_element_type=f32)
-    grad_hidden = jnp.dot(reduce_ref[at, :], grad_t_ref[...], preferred_element_type=f32)
+    preact = dot_rows(expand_ref[at, :], normed_ref[...])
+    grad_hidden = dot_rows(reduce_ref[at, :], grad_ref[...])
     bias = jnp.concatenate([bias_ref[at, :]] * (total // lanes), axis=1)
     value, slope = gelu_pair(preact + bias)
     hidden = value.astype(bf16)
@@ -410,7 +413,7 @@
 
 
 def far_body(*refs):
-    cells, (sent_ref, grad_pre_ref) = refs[:7], refs[7:]
+    cells, (sent_ref, grad_pre_ref) = refs[:5], refs[5:]
     half = grad_pre_ref.shape[0]
     channels = refs[0].shape[1]
     base = (1 - own_place()[0]) * half
@@ -425,14 +428,14 @@
 
 def hidden_far(*cells):
     total, channels = cells[0].shape
-    half = cells[4].shape[0] // 2
+    half = cells[2].shape[0] // 2
     return pl.pallas_call(
         far_body,
         out_shape=(
             jax.ShapeDtypeStruct((half, 2 * channels), bf16),
             jax.ShapeDtypeStruct((half, total), bf16),
         ),
-        in_specs=[whole] * 7,
+        in_specs=[whole] * 5,
         out_specs=[whole] * 2,
         compiler_params=params(16),
         cost_estimate=cost(5.8),
@@ -441,7 +444,7 @@
 
 
 def near_first_body(*refs):
-    cells, (sums_ref, grad_pre_ref) = refs[:7], refs[7:]
+    cells, (sums_ref, grad_pre_ref) = refs[:5], refs[5:]
     half = grad_pre_ref.shape[0]
     channels = refs[0].shape[1]
     size = half // 4
@@ -457,14 +460,14 @@
 
 def near_first(*cells):
     total, channels = cells[0].shape
-    half = cells[4].shape[0] // 2
+    half = cells[2].shape[0] // 2
     return pl.pallas_call(
         near_first_body,
         out_shape=(
             jax.ShapeDtypeStruct((half // 2, 2 * channels), f32),
             jax.ShapeDtypeStruct((half, total), bf16),
         ),
-        in_specs=[whole] * 7,
+        in_specs=[whole] * 5,
         out_specs=[whole] * 2,
         compiler_params=params(16),
         cost_estimate=cost(3.0),
@@ -496,7 +499,7 @@
 
 
 def near_last_body(*refs):
-    cells, (arrived_ref, _, own_ref, sent_ref, grad_pre_ref) = refs[:7], refs[7:]
+    cells, (arrived_ref, _, own_ref, sent_ref, grad_pre_ref) = refs[:5], refs[5:]
     half = grad_pre_ref.shape[0]
     channels = refs[0].shape[1]
     size = half // 4
@@ -511,9 +514,9 @@
 
 
 def near_last(*inputs):
-    cells, grad_pre = inputs[:7], inputs[8]
+    cells, grad_pre = inputs[:5], inputs[6]
     channels = cells[0].shape[1]
-    size = cells[4].shape[0] // 8
+    size = cells[2].shape[0] // 8
     return pl.pallas_call(
         near_last_body,
         out_shape=(
@@ -521,9 +524,9 @@
             jax.ShapeDtypeStruct((size, 2 * channels), bf16),
             jax.ShapeDtypeStruct(grad_pre.shape, bf16),
         ),
-        in_specs=[whole] * 9,
+        in_specs=[whole] * 7,
         out_specs=[whole] * 3,
-        input_output_aliases={8: 2},
+        input_output_aliases={6: 2},
         compiler_params=params(16),
         cost_estimate=cost(3.0),
         name="near_last",
@@ -578,28 +581,49 @@
     grad_ref, out_ref, rows_sum, cols_sum,
 ):
     conv_refs = (conv0_ref, conv1_ref, conv2_ref)
-    add_edges(True, kernel_ref, left_ref, right_ref, top_ref, bottom_ref, rows_sum, cols_sum)
-
-    def step(i, outer):
-        at = pl.ds(pl.multiple_of(i * side, side), side)
-        value = edged_row(i, conv_rows(conv_refs, at), cols_sum)
-        if outer is not None:
-            value = value + rows_sum[outer]
-        out_ref[at, :] = value + masked_row(i, grad_ref[at, :], counts_ref)
-
-    each_row(step)
+    rows = out_ref.shape[0] // side
+    steps = side // rows
+    block = pl.program_id(0)
+
+    @pl.when(block == 0)
+    def _():
+        add_edges(True, kernel_ref, left_ref, right_ref, top_ref, bottom_ref, rows_sum, cols_sum)
+
+    def write(outer_of):
+        for r in range(rows):
+            i = block * rows + r
+            at = pl.ds(pl.multiple_of(i * side, side), side)
+            value = edged_row(i, conv_rows(conv_refs, at), cols_sum)
+            outer = outer_of(r)
+            if outer is not None:
+                value = value + rows_sum[outer]
+            out_ref[r * side : (r + 1) * side, :] = value + masked_row(i, grad_ref[at, :], counts_ref)
+
+    @pl.when(block == 0)
+    def _():
+        write(lambda r: r if r < reach else None)
+
+    @pl.when(jnp.logical_and(block > 0, block < steps - 1))
+    def _():
+        write(lambda r: None)
+
+    @pl.when(block == steps - 1)
+    def _():
+        write(lambda r: r - (rows - 2 * reach) if r >= rows - reach else None)
 
 
 def finish(counts, conv, kernel, left, right, top, bottom, grad):
     total, channels = grad.shape
+    rows = 8
     return pl.pallas_call(
         finish_body,
         out_shape=jax.ShapeDtypeStruct((total, channels), f32),
+        grid=(side // rows,),
         in_specs=[pl.BlockSpec(memory_space=pltpu.SMEM)] + [whole] * 9,
-        out_specs=whole,
+        out_specs=pl.BlockSpec((rows * side, channels), lambda b: (b, 0)),
         scratch_shapes=[pltpu.VMEM((2 * reach, side, channels), f32)] * 2,
         compiler_params=params(12),
-        cost_estimate=cost(3.1),
+        cost_estimate=cost(2.2),
         name="finish",
     )(counts, *conv, kernel, left, right, top, bottom, grad)
 
@@ -743,15 +767,17 @@
     kernel = dw_kernel.transpose(1, 0, 2)
 
     left, right = lon_halo(*side_cols(cells))
-    conv = inner_conv(cells, kernel, False, (0, 1, 2))
-    rows, rows_t = mask_rows(counts, grad)
-    top, bottom = lat_halo(*side_rows(cells, left, right))
+    rows = mask_rows(counts, grad)
     expand, reduce, expand_t, bias = arrange(w_expand[0], w_reduce[0], b_expand)
-    unit, spread, normed, normed_t = normalise(
+    left, right = after((left, right), rows, bias)
+    up, down = side_rows(cells, left, right)
+    top, bottom = lat_halo(up, down)
+    conv = inner_conv(after(cells, up, down), kernel, False, (0, 1, 2))
+    unit, spread, normed = normalise(
         conv, kernel, left, right, top, bottom, dw_bias, norm_gain, norm_bias
     )
 
-    inputs = (normed, normed_t, rows, rows_t, expand, reduce, bias)
+    inputs = (normed, rows, expand, reduce, bias)
     sent, far_pre = hidden_far(*inputs)
     arrived = lax.ppermute(sent, "lat", [(i, i ^ 1) for i in range(8)])
     sums, near_pre = near_first(*inputs)
@@ -764,15 +790,15 @@
     far_pre = after(far_pre, three)
     conv_grad, first, last = norm_back(expand_t, far_pre, near_pre, unit, spread, norm_gain)
     left, right = lon_halo(first, last)
-
-    own, parts = after((own, (part_one, part_two, part_three)), left, right)
+    back = inner_conv(after(conv_grad, first, last), kernel, True, (0,))
+
+    own, parts = after((own, (part_one, part_two, part_three)), left, right, back)
     own, *sent = split_four(own, parts)
     parts = [lax.ppermute(s, every_axis, plane_pairs(i + 1, False)) for i, s in enumerate(sent)]
     conv_grad = after(conv_grad, sent)
     up, down = side_rows(conv_grad, left, right)
-    back = inner_conv(conv_grad, kernel, True, (0,))
-
-    own, sent = split_two(4, *after((own, parts), up, down, back))
+
+    own, sent = split_two(4, *after((own, parts), up, down))
     top, bottom = lat_halo(up, down)
     arrived = lax.ppermute(sent, every_axis, halving_pairs(4))
     conv_grad = after(conv_grad, sent)

time: 90.5 us -> 86 us (0.950)
  local copies, waits for them, and re-layouts: 1.45 us -> 0.05 us
  starting transfers between devices: 43 us -> 41.8 us
    ppermute x1, starting transfers between devices: 7.48 us -> 4.08 us  [local(): arrived = lax.ppermute(sent, every_axis, halving_pairs(2))]
    ppermute x1, starting transfers between devices: 1.76 us -> 4.62 us  [local(): arrived = lax.ppermute(sent, every_axis, halving_pairs(1))]
    pallas_call x1, Pallas kernels: 4.74 us -> 1.92 us  [normalise(): pl.pallas_call(normalise_body, out_shape=(jax.ShapeDtypeStruct((total, ch...]
    ppermute x1, starting transfers between devices: 3.61 us -> 1.46 us  [local(): arrived = lax.ppermute(sent, 'lat', [(i, i ^ 1) for i in range(8)])]
    ppermute x2, waiting for transfers between devices: 2.12 us -> 0.01 us  [lat_halo(): bottom = lax.ppermute(up, 'lat', shifted('lat', -1, False))]
    ppermute x2, starting transfers between devices: 4.46 us -> 6.07 us  [lat_halo(): top = lax.ppermute(down, 'lat', shifted('lat', 1, False))]
    unnamed x22 -> x20, local copies, waits for them, and re-layouts: 1.45 us -> 0.05 us
    pallas_call x2, Pallas kernels: 1.75 us -> 3.07 us  [the longest x1 2.09 us: side_cols(): pl.pallas_call(side_cols_body, out_shape=(shape, shape), in_specs=[pl.Blo...]
  transfers between devices with their start and end apart: 18 -> 18, of which waited for: 4 -> 4; matrix products, arithmetic and copies ran while one was open for 0% -> 0% of each run, Pallas kernels for 30% -> 32%
where the time goes in v5:
time: 86 us; the launch traced here: 85.8 us
  starting transfers between devices  41.8 us (49%)
  Pallas kernels  37.7 us (44%)
  waiting for transfers between devices  5.22 us (6%)
  between operations  0.97 us (1%)
    pallas_call x4, Pallas kernels, inner_conv(): pl.pallas_call(functools.partial(inner_conv_body, flipped, parts), out_sh...  12.9 us
    ppermute x1, starting transfers between devices, local(): arrived = lax.ppermute(sent, every_axis, halving_pairs(4))  6.39 us
    ppermute x2, starting transfers between devices, lat_halo(): top = lax.ppermute(down, 'lat', shifted('lat', 1, False))  6.07 us
    ppermute x3, starting transfers between devices, local(): lax.ppermute(s, every_axis, plane_pairs(i + 1, False))  5.63 us
    pallas_call x1, Pallas kernels, hidden_far(): pl.pallas_call(far_body, out_shape=(jax.ShapeDtypeStruct((half, 2 * chann...  5.47 us
    ppermute x1, starting transfers between devices, local(): arrived = lax.ppermute(sent, every_axis, halving_pairs(1))  4.62 us
    ppermute x1, starting transfers between devices, local(): arrived = lax.ppermute(sent, every_axis, halving_pairs(2))  4.08 us
    pallas_call x1, Pallas kernels, finish(): pl.pallas_call(finish_body, out_shape=jax.ShapeDtypeStruct((total, channe...  3.34 us
  transfers between devices with their start and end apart: 18, of which 4 were waited for; matrix products, arithmetic and copies ran while one was open for 0% of the time, Pallas kernels for 32%

profile of v5, /device:TPU:32, one launch (start us, length us, event | category | flops | bytes accessed | tf_op | source)
XLA Modules:
  0.0 85.8 jit_solution(16795209550290668851)
XLA Ops:
  0.7 2.1 %side_cols.1 = (bf16[3,32,384]{2,1,0:T(8,128)(2,1)}, bf16[3,32,384]{2,1,0:T(8,128)(2,1)}) custom-call(f32[32,32,384]{2,1,0:T(8,128)} %bitcast.10), custom_call_target="tpu_custom_call" | custom-call | flops 1150000000 | bytes 1048576 | tf_op jit(solution)/shard_map/side_cols/pallas_call | solution.py:116
  2.8 1.6 %collective-permute-start = (bf16[3,32,384]{2,1,0:T(8,128)(2,1)}, bf16[3,32,384]{2,1,0:T(8,128)(2,1)S(1)}, u32[]{:S(2)}, u32[]{:S(2)}) collective-permute-start(bf16[3,32,384]{2,1,0:T(8,128)(2,1)} %get-tuple-element.66), channel_id=1, source_target_pairs={{0,1},{1,2},{2,3},{3,4},{4,5},{5,6},{6,7},{7,8},{8,9},{9,10},{10,1... | collective-permute-start | bytes 221192 | tf_op jit(solution)/shard_map/ppermute | solution.py:745
  4.3 1.4 %collective-permute-start.1 = (bf16[3,32,384]{2,1,0:T(8,128)(2,1)}, bf16[3,32,384]{2,1,0:T(8,128)(2,1)S(1)}, u32[]{:S(2)}, u32[]{:S(2)}) collective-permute-start(bf16[3,32,384]{2,1,0:T(8,128)(2,1)} %get-tuple-element.67), channel_id=1, source_target_pairs={{0,15},{1,0},{2,1},{3,2},{4,3},{5,4},{6,5},{7,6},{8,7},{9,8},{10,9... | collective-permute-start | bytes 221192 | tf_op jit(solution)/shard_map/ppermute | solution.py:746
  5.8 1.5 %arrange.1 = (bf16[1536,384]{1,0:T(8,128)(2,1)S(1)}, bf16[1536,384]{1,0:T(8,128)(2,1)S(1)}, bf16[384,1536]{1,0:T(8,128)(2,1)S(1)}, f32[1536,128]{1,0:T(8,128)S(1)}) custom-call(bf16[1536,384]{1,0:T(8,128)(2,1)S(1)} %bitcast.15, bf16[1536,384]{1,0:T(8,128)(2,1)S(1)} %bitcast.16, f32[1,1536]{1,0:T(1,128)S(1)} %copy-done.5), custom_call_target="tpu_custom_call" | custom-call | flops 1724999936 | bytes 1048576 | tf_op jit(solution)/shard_map/arrange/pallas_call | solution.py:347
  7.3 1.0 %mask_rows.1.refs_1_ = bf16[1024,384]{1,0:T(8,128)(2,1)S(1)} custom-call(s32[4,4]{1,0:T(4,128)S(1)} %copy-done.6, f32[1024,384]{1,0:T(8,128)S(1)} %bitcast.13), custom_call_target="tpu_custom_call" | custom-call | flops 1035000000 | bytes 1048576 | tf_op jit(solution)/shard_map/mask_rows/pallas_call | solution.py:312
  8.4 1.2 %collective-permute-done.1.right_ref = bf16[3,32,384]{2,1,0:T(8,128)(2,1)S(1)} collective-permute-done((bf16[3,32,384]{2,1,0:T(8,128)(2,1)}, bf16[3,32,384]{2,1,0:T(8,128)(2,1)S(1)}, u32[]{:S(2)}, u32[]{:S(2)}) %collective-permute-start.1) | collective-permute-done | bytes 73760 | tf_op jit(solution)/shard_map/ppermute | solution.py:746
  9.6 1.3 %collective-permute-start.3 = (bf16[3,48,384]{2,1,0:T(8,128)(2,1)S(1)}, bf16[3,48,384]{2,1,0:T(8,128)(2,1)S(1)}, u32[]{:S(2)}, u32[]{:S(2)}) collective-permute-start(bf16[3,48,384]{2,1,0:T(8,128)(2,1)S(1)} %get-tuple-element.71), channel_id=1, source_target_pairs={{16,0},{32,16},{48,32},{64,48},{80,64},{96,80},{112,96},{17,1},{33... | collective-permute-start | bytes 331784 | tf_op jit(solution)/shard_map/ppermute | solution.py:752
  10.9 3.0 %collective-permute-start.2 = (bf16[3,48,384]{2,1,0:T(8,128)(2,1)S(1)}, bf16[3,48,384]{2,1,0:T(8,128)(2,1)S(1)}, u32[]{:S(2)}, u32[]{:S(2)}) collective-permute-start(bf16[3,48,384]{2,1,0:T(8,128)(2,1)S(1)} %get-tuple-element.72), channel_id=1, source_target_pairs={{0,16},{16,32},{32,48},{48,64},{64,80},{80,96},{96,112},{1,17},{17... | collective-permute-start | bytes 331784 | tf_op jit(solution)/shard_map/ppermute | solution.py:751
  14.0 6.4 %inner_conv.4 = (f32[1024,128]{1,0:T(8,128)S(1)}, f32[1024,128]{1,0:T(8,128)S(1)}, f32[1024,128]{1,0:T(8,128)S(1)}) custom-call(f32[1024,384]{1,0:T(8,128)S(1)} %bitcast.12, f32[49,1,384]{2,1,0:T(1,128)S(1)} %bitcast.17), custom_call_target="tpu_custom_call" | custom-call | flops 7935000064 | bytes 1048576 | tf_op jit(solution)/shard_map/inner_conv/pallas_call | solution.py:86
  20.5 1.9 %normalise.1 = (f32[1024,384]{1,0:T(8,128)S(1)}, f32[1024,128]{1,0:T(8,128)S(1)}, bf16[1024,384]{1,0:T(8,128)(2,1)S(1)}) custom-call(f32[1024,128]{1,0:T(8,128)S(1)} %get-tuple-element.74.conv0_ref, f32[1024,128]{1,0:T(8,128)S(1)} %get-tuple-element.75.conv1_ref, f32[1024,128]{1,0:T(8,128)S(1)} %get-tuple-element.76.conv2_ref, f32[49,1,384]{2,1,0:T(1,128)S(1)} %bitcast.18, ...), custom_call_target="tpu_custom_call" | custom-call | flops 3220000000 | bytes 1048576 | tf_op jit(solution)/shard_map/normalise/pallas_call | solution.py:260
  22.4 5.5 %hidden_far.1 = (bf16[768,768]{1,0:T(8,128)(2,1)S(1)}, bf16[768,1024]{1,0:T(8,128)(2,1)S(1)}) custom-call(bf16[1024,384]{1,0:T(8,128)(2,1)S(1)} %get-tuple-element.77.refs_0_, bf16[1024,384]{1,0:T(8,128)(2,1)S(1)} %mask_rows.1.refs_1_, bf16[1536,384]{1,0:T(8,128)(2,1)S(1)} %get-tuple-element.78.refs_2_, bf16[1536,384]{1,0:T(8,128)(2,1)S(1)} %get-tuple-element.79.refs_3_, ...), custom_call_target="tpu_custom_call" | custom-call | flops 6670000128 | bytes 1048576 | tf_op jit(solution)/shard_map/hidden_far/pallas_call | solution.py:432
  27.9 1.5 %collective-permute-start.4 = (bf16[768,768]{1,0:T(8,128)(2,1)S(1)}, bf16[768,768]{1,0:T(8,128)(2,1)S(1)}, u32[]{:S(2)}, u32[]{:S(2)}) collective-permute-start(bf16[768,768]{1,0:T(8,128)(2,1)S(1)} %get-tuple-element.81), channel_id=1, source_target_pairs={{0,16},{16,0},{32,48},{48,32},{64,80},{80,64},{96,112},{112,96},{1... | collective-permute-start | bytes 3538952 | tf_op jit(solution)/shard_map/ppermute | solution.py:782
  29.3 3.1 %near_first.1 = (f32[384,768]{1,0:T(8,128)S(1)}, bf16[768,1024]{1,0:T(8,128)(2,1)S(1)}) custom-call(bf16[1024,384]{1,0:T(8,128)(2,1)S(1)} %get-tuple-element.77.refs_0_, bf16[1024,384]{1,0:T(8,128)(2,1)S(1)} %mask_rows.1.refs_1_, bf16[1536,384]{1,0:T(8,128)(2,1)S(1)} %get-tuple-element.78.refs_2_, bf16[1536,384]{1,0:T(8,128)(2,1)S(1)} %get-tuple-element.79.refs_3_, ...), custom_call_target="tpu_custom_call" | custom-call | flops 3449999872 | bytes 1048576 | tf_op jit(solution)/shard_map/near_first/pallas_call | solution.py:464
  32.6 1.7 %collective-permute-start.5 = (bf16[192,768]{1,0:T(8,128)(2,1)S(1)}, bf16[192,768]{1,0:T(8,128)(2,1)S(1)}, u32[]{:S(2)}, u32[]{:S(2)}) collective-permute-start(bf16[192,768]{1,0:T(8,128)(2,1)S(1)} %get-tuple-element.84), channel_id=1, source_target_pairs={{0,32},{1,33},{2,34},{3,35},{4,36},{5,37},{6,38},{7,39},{8,40},{9,... | collective-permute-start | bytes 884744 | tf_op jit(solution)/shard_map/ppermute | solution.py:785
  34.3 1.7 %collective-permute-start.6 = (bf16[192,768]{1,0:T(8,128)(2,1)S(1)}, bf16[192,768]{1,0:T(8,128)(2,1)S(1)}, u32[]{:S(2)}, u32[]{:S(2)}) collective-permute-start(bf16[192,768]{1,0:T(8,128)(2,1)S(1)} %get-tuple-element.85), channel_id=1, source_target_pairs={{0,64},{1,65},{2,66},{3,67},{4,68},{5,69},{6,70},{7,71},{8,72},{9,... | collective-permute-start | bytes 884744 | tf_op jit(solution)/shard_map/ppermute | solution.py:786
  36.0 3.2 %near_last.1 = (f32[192,768]{1,0:T(8,128)S(1)}, bf16[192,768]{1,0:T(8,128)(2,1)S(1)}, bf16[768,1024]{1,0:T(8,128)(2,1)S(1)}) custom-call(bf16[1024,384]{1,0:T(8,128)(2,1)S(1)} %get-tuple-element.77.refs_0_, bf16[1024,384]{1,0:T(8,128)(2,1)S(1)} %mask_rows.1.refs_1_, ...), custom_call_target="tpu_custom_call", output_to_operand_aliasing={{2}: (6, {})} | custom-call | flops 3449999872 | bytes 1048576 | tf_op jit(solution)/shard_map/near_last/pallas_call | solution.py:520
  39.2 2.3 %collective-permute-start.7 = (bf16[192,768]{1,0:T(8,128)(2,1)S(1)}, bf16[192,768]{1,0:T(8,128)(2,1)S(1)}, u32[]{:S(2)}, u32[]{:S(2)}) collective-permute-start(bf16[192,768]{1,0:T(8,128)(2,1)S(1)} %get-tuple-element.87), channel_id=1, source_target_pairs={{0,96},{1,97},{2,98},{3,99},{4,100},{5,101},{6,102},{7,103},{8,104... | collective-permute-start | bytes 884744 | tf_op jit(solution)/shard_map/ppermute | solution.py:788
  41.5 2.2 %norm_back.1 = (f32[32,32,384]{2,1,0:T(8,128)S(1)}, bf16[3,32,384]{2,1,0:T(8,128)(2,1)S(1)}, bf16[3,32,384]{2,1,0:T(8,128)(2,1)S(1)}) custom-call(bf16[384,1536]{1,0:T(8,128)(2,1)S(1)} %get-tuple-element.65.turned_ref, bf16[768,1024]{1,0:T(8,128)(2,1)S(1)} %get-tuple-element.88.other_ref, bf16[768,1024]{1,0:T(8,128)(2,1)S(1)} %get-tuple-element.89.mine_ref, ...), custom_call_target="tpu_custom_call" | custom-call | flops 2529999872 | bytes 1048576 | tf_op jit(solution)/shard_map/norm_back/pallas_call | solution.py:567
  43.7 1.8 %collective-permute-start.9 = (bf16[3,32,384]{2,1,0:T(8,128)(2,1)S(1)}, bf16[3,32,384]{2,1,0:T(8,128)(2,1)S(1)}, u32[]{:S(2)}, u32[]{:S(2)}) collective-permute-start(bf16[3,32,384]{2,1,0:T(8,128)(2,1)S(1)} %get-tuple-element.93), channel_id=1, source_target_pairs={{0,15},{1,0},{2,1},{3,2},{4,3},{5,4},{6,5},{7,6},{8,7},{9,8},{10,9... | collective-permute-start | bytes 221192 | tf_op jit(solution)/shard_map/ppermute | solution.py:746
  46.0 2.1 %inner_conv.5.conv0_ref = f32[1024,128]{1,0:T(8,128)S(1)} custom-call(f32[1024,384]{1,0:T(8,128)S(1)} %bitcast.23, f32[49,1,384]{2,1,0:T(1,128)S(1)} %bitcast.19), custom_call_target="tpu_custom_call" | custom-call | flops 2644999936 | bytes 1048576 | tf_op jit(solution)/shard_map/inner_conv/pallas_call | solution.py:86
  48.2 2.6 %collective-permute-done.8.left_ref = bf16[3,32,384]{2,1,0:T(8,128)(2,1)S(1)} collective-permute-done((bf16[3,32,384]{2,1,0:T(8,128)(2,1)S(1)}, bf16[3,32,384]{2,1,0:T(8,128)(2,1)S(1)}, u32[]{:S(2)}, u32[]{:S(2)}) %collective-permute-start.8) | collective-permute-done | bytes 73760 | tf_op jit(solution)/shard_map/ppermute | solution.py:745
  51.4 3.0 %collective-permute-start.11 = (bf16[48,768]{1,0:T(8,128)(2,1)S(1)}, bf16[48,768]{1,0:T(8,128)(2,1)S(1)}, u32[]{:S(2)}, u32[]{:S(2)}) collective-permute-start(bf16[48,768]{1,0:T(8,128)(2,1)S(1)} %get-tuple-element.102), channel_id=1, source_target_pairs={{0,128},{1,129},{2,130},{3,131},{4,132},{5,133},{6,134},{7,135},{8... | collective-permute-start | bytes 221192 | tf_op jit(solution)/shard_map/ppermute | solution.py:797
  54.4 2.2 %collective-permute-start.12 = (bf16[48,768]{1,0:T(8,128)(2,1)S(1)}, bf16[48,768]{1,0:T(8,128)(2,1)S(1)}, u32[]{:S(2)}, u32[]{:S(2)}) collective-permute-start(bf16[48,768]{1,0:T(8,128)(2,1)S(1)} %get-tuple-element.103), channel_id=1, source_target_pairs={{0,129},{1,0},{2,131},{3,2},{4,133},{5,4},{6,135},{7,6},{8,137},{9... | collective-permute-start | bytes 221192 | tf_op jit(solution)/shard_map/ppermute | solution.py:797
  56.6 1.3 %collective-permute-start.15 = (bf16[3,48,384]{2,1,0:T(8,128)(2,1)S(1)}, bf16[3,48,384]{2,1,0:T(8,128)(2,1)S(1)}, u32[]{:S(2)}, u32[]{:S(2)}) collective-permute-start(bf16[3,48,384]{2,1,0:T(8,128)(2,1)S(1)} %get-tuple-element.106), channel_id=1, source_target_pairs={{16,0},{32,16},{48,32},{64,48},{80,64},{96,80},{112,96},{17,1},{33... | collective-permute-start | bytes 331784 | tf_op jit(solution)/shard_map/ppermute | solution.py:752
  57.9 3.0 %collective-permute-start.14 = (bf16[3,48,384]{2,1,0:T(8,128)(2,1)S(1)}, bf16[3,48,384]{2,1,0:T(8,128)(2,1)S(1)}, u32[]{:S(2)}, u32[]{:S(2)}) collective-permute-start(bf16[3,48,384]{2,1,0:T(8,128)(2,1)S(1)} %get-tuple-element.107), channel_id=1, source_target_pairs={{0,16},{16,32},{32,48},{48,64},{64,80},{80,96},{96,112},{1,17},{17... | collective-permute-start | bytes 331784 | tf_op jit(solution)/shard_map/ppermute | solution.py:751
  61.1 6.4 %collective-permute-start.13 = (f32[24,768]{1,0:T(8,128)S(1)}, f32[24,768]{1,0:T(8,128)S(1)}, u32[]{:S(2)}, u32[]{:S(2)}) collective-permute-start(f32[24,768]{1,0:T(8,128)S(1)} %get-tuple-element.112), channel_id=1, source_target_pairs={{0,8},{1,9},{2,10},{3,11},{4,12},{5,13},{6,14},{7,15},{8,0},{9,1},... | collective-permute-start | bytes 221192 | tf_op jit(solution)/shard_map/ppermute | solution.py:803
  67.4 2.1 %inner_conv.6.conv1_ref = f32[1024,128]{1,0:T(8,128)S(1)} custom-call(f32[1024,384]{1,0:T(8,128)S(1)} %bitcast.25, f32[49,1,384]{2,1,0:T(1,128)S(1)} %bitcast.20), custom_call_target="tpu_custom_call" | custom-call | flops 2644999936 | bytes 1048576 | tf_op jit(solution)/shard_map/inner_conv/pallas_call | solution.py:86
  69.6 1.3 %collective-permute-done.13.refs_0_ = f32[24,768]{1,0:T(8,128)S(1)} collective-permute-done((f32[24,768]{1,0:T(8,128)S(1)}, f32[24,768]{1,0:T(8,128)S(1)}, u32[]{:S(2)}, u32[]{:S(2)}) %collective-permute-start.13) | collective-permute-done | bytes 73760 | tf_op jit(solution)/shard_map/ppermute | solution.py:803
  70.9 4.1 %collective-permute-start.16 = (f32[12,768]{1,0:T(8,128)S(1)}, f32[12,768]{1,0:T(8,128)S(1)}, u32[]{:S(2)}, u32[]{:S(2)}) collective-permute-start(f32[12,768]{1,0:T(8,128)S(1)} %get-tuple-element.117), channel_id=1, source_target_pairs={{0,4},{1,5},{2,6},{3,7},{4,0},{5,1},{6,2},{7,3},{8,12},{9,13},{10,... | collective-permute-start | bytes 110600 | tf_op jit(solution)/shard_map/ppermute | solution.py:808
  75.0 2.1 %inner_conv.7.conv2_ref = f32[1024,128]{1,0:T(8,128)S(1)} custom-call(f32[1024,384]{1,0:T(8,128)S(1)} %bitcast.26, f32[49,1,384]{2,1,0:T(1,128)S(1)} %bitcast.21), custom_call_target="tpu_custom_call" | custom-call | flops 2644999936 | bytes 1048576 | tf_op jit(solution)/shard_map/inner_conv/pallas_call | solution.py:86
  77.2 4.6 %collective-permute-start.17 = (f32[6,768]{1,0:T(8,128)S(1)}, f32[6,768]{1,0:T(8,128)S(1)}, u32[]{:S(2)}, u32[]{:S(2)}) collective-permute-start(f32[6,768]{1,0:T(8,128)S(1)} %get-tuple-element.122), channel_id=1, source_target_pairs={{0,2},{1,3},{2,0},{3,1},{4,6},{5,7},{6,4},{7,5},{8,10},{9,11},{10,... | collective-permute-start | bytes 55304 | tf_op jit(solution)/shard_map/ppermute | solution.py:813
  81.9 3.3 %finish.1 = f32[1024,384]{1,0:T(8,128)} custom-call(s32[4,4]{1,0:T(4,128)S(1)} %copy-done.6, f32[1024,128]{1,0:T(8,128)S(1)} %inner_conv.5.conv0_ref, f32[1024,128]{1,0:T(8,128)S(1)} %inner_conv.6.conv1_ref, f32[1024,128]{1,0:T(8,128)S(1)} %inner_conv.7.conv2_ref, f32[49,1,384]{2,1,0:T(1,128)S(1)} %bitcast.22, ...), custom_call_target="tpu_custom_call" | custom-call | flops 2529999872 | bytes 1048576 | tf_op jit(solution)/shard_map/finish/pallas_call | solution.py:618
  (45 shorter events, 2.2 us)
Async XLA Ops:
  0.6 5.1 %copy-start.2 = (bf16[1,1536,384]{2,1,0:T(8,128)(2,1)S(1)}, bf16[1,1536,384]{2,1,0:T(8,128)(2,1)}, u32[]{:S(2)}) copy-start(bf16[1,1536,384]{2,1,0:T(8,128)(2,1)} %param.17) | copy-start | bytes 3538948
  0.6 5.1 %copy-start.3 = (bf16[1,1536,384]{2,1,0:T(8,128)(2,1)S(1)}, bf16[1,1536,384]{2,1,0:T(8,128)(2,1)}, u32[]{:S(2)}) copy-start(bf16[1,1536,384]{2,1,0:T(8,128)(2,1)} %param.19) | copy-start | bytes 3538948
  0.7 5.1 %copy-start.5 = (f32[1,1536]{1,0:T(1,128)S(1)}, f32[1,1536]{1,0:T(1,128)}, u32[]{:S(2)}) copy-start(f32[1,1536]{1,0:T(1,128)} %bias_ref.2) | copy-start | bytes 18436
  2.8 5.6 %collective-permute-start = (bf16[3,32,384]{2,1,0:T(8,128)(2,1)}, bf16[3,32,384]{2,1,0:T(8,128)(2,1)S(1)}, u32[]{:S(2)}, u32[]{:S(2)}) collective-permute-start(bf16[3,32,384]{2,1,0:T(8,128)(2,1)} %get-tuple-element.66), channel_id=1, source_target_pairs={{0,1},{1,2},{2,3},{3,4},{4,5},{5,6},{6,7},{7,8},{8,9},{9,10},{10,1... | collective-permute-start | bytes 221192 | tf_op jit(solution)/shard_map/ppermute | solution.py:745
  4.3 5.2 %collective-permute-start.1 = (bf16[3,32,384]{2,1,0:T(8,128)(2,1)}, bf16[3,32,384]{2,1,0:T(8,128)(2,1)S(1)}, u32[]{:S(2)}, u32[]{:S(2)}) collective-permute-start(bf16[3,32,384]{2,1,0:T(8,128)(2,1)} %get-tuple-element.67), channel_id=1, source_target_pairs={{0,15},{1,0},{2,1},{3,2},{4,3},{5,4},{6,5},{7,6},{8,7},{9,8},{10,9... | collective-permute-start | bytes 221192 | tf_op jit(solution)/shard_map/ppermute | solution.py:746
  5.8 1.5 %copy-start.1 = (f32[1,32,32,384]{3,2,1,0:T(8,128)S(1)}, f32[1,32,32,384]{3,2,1,0:T(8,128)}, u32[]{:S(2)}) copy-start(f32[1,32,32,384]{3,2,1,0:T(8,128)} %param.11) | copy-start | bytes 4718596
  5.8 1.5 %copy-start.6 = (s32[4,4]{1,0:T(4,128)S(1)}, s32[4,4]{1,0:T(4,128)}, u32[]{:S(2)}) copy-start(s32[4,4]{1,0:T(4,128)} %counts_ref.3) | copy-start | bytes 196
  7.3 2.2 %copy-start = (f32[1,32,32,384]{3,2,1,0:T(8,128)S(1)}, f32[1,32,32,384]{3,2,1,0:T(8,128)}, u32[]{:S(2)}) copy-start(f32[1,32,32,384]{3,2,1,0:T(8,128)} %param.10) | copy-start | bytes 4718596
  8.3 5.6 %copy-start.4 = (f32[1,49,384]{2,0,1:T(1,128)S(1)}, f32[1,49,384]{2,0,1:T(1,128)}, u32[]{:S(2)}) copy-start(f32[1,49,384]{2,0,1:T(1,128)} %param.13) | copy-start | bytes 225796
  9.6 10.8 %collective-permute-start.3 = (bf16[3,48,384]{2,1,0:T(8,128)(2,1)S(1)}, bf16[3,48,384]{2,1,0:T(8,128)(2,1)S(1)}, u32[]{:S(2)}, u32[]{:S(2)}) collective-permute-start(bf16[3,48,384]{2,1,0:T(8,128)(2,1)S(1)} %get-tuple-element.71), channel_id=1, source_target_pairs={{16,0},{32,16},{48,32},{64,48},{80,64},{96,80},{112,96},{17,1},{33... | collective-permute-start | bytes 331784 | tf_op jit(solution)/shard_map/ppermute | solution.py:752
  10.9 9.5 %collective-permute-start.2 = (bf16[3,48,384]{2,1,0:T(8,128)(2,1)S(1)}, bf16[3,48,384]{2,1,0:T(8,128)(2,1)S(1)}, u32[]{:S(2)}, u32[]{:S(2)}) collective-permute-start(bf16[3,48,384]{2,1,0:T(8,128)(2,1)S(1)} %get-tuple-element.72), channel_id=1, source_target_pairs={{0,16},{16,32},{32,48},{48,64},{64,80},{80,96},{96,112},{1,17},{17... | collective-permute-start | bytes 331784 | tf_op jit(solution)/shard_map/ppermute | solution.py:751
  14.0 6.5 %copy-start.7 = (f32[1,384]{1,0:T(1,128)S(1)}, f32[1,384]{1,0:T(1,128)}, u32[]{:S(2)}) copy-start(f32[1,384]{1,0:T(1,128)} %bias_ref.3) | copy-start | bytes 4612
  14.0 6.5 %copy-start.8 = (f32[1,384]{1,0:T(1,128)S(1)}, f32[1,384]{1,0:T(1,128)}, u32[]{:S(2)}) copy-start(f32[1,384]{1,0:T(1,128)} %shift_ref.1) | copy-start | bytes 4612
  14.0 6.5 %copy-start.9 = (f32[1,384]{1,0:T(1,128)S(1)}, f32[1,384]{1,0:T(1,128)}, u32[]{:S(2)}) copy-start(f32[1,384]{1,0:T(1,128)} %gain_ref.3) | copy-start | bytes 4612
  27.9 4.6 %collective-permute-start.4 = (bf16[768,768]{1,0:T(8,128)(2,1)S(1)}, bf16[768,768]{1,0:T(8,128)(2,1)S(1)}, u32[]{:S(2)}, u32[]{:S(2)}) collective-permute-start(bf16[768,768]{1,0:T(8,128)(2,1)S(1)} %get-tuple-element.81), channel_id=1, source_target_pairs={{0,16},{16,0},{32,48},{48,32},{64,80},{80,64},{96,112},{112,96},{1... | collective-permute-start | bytes 3538952 | tf_op jit(solution)/shard_map/ppermute | solution.py:782
  32.6 18.2 %collective-permute-start.5 = (bf16[192,768]{1,0:T(8,128)(2,1)S(1)}, bf16[192,768]{1,0:T(8,128)(2,1)S(1)}, u32[]{:S(2)}, u32[]{:S(2)}) collective-permute-start(bf16[192,768]{1,0:T(8,128)(2,1)S(1)} %get-tuple-element.84), channel_id=1, source_target_pairs={{0,32},{1,33},{2,34},{3,35},{4,36},{5,37},{6,38},{7,39},{8,40},{9,... | collective-permute-start | bytes 884744 | tf_op jit(solution)/shard_map/ppermute | solution.py:785
  34.3 16.5 %collective-permute-start.6 = (bf16[192,768]{1,0:T(8,128)(2,1)S(1)}, bf16[192,768]{1,0:T(8,128)(2,1)S(1)}, u32[]{:S(2)}, u32[]{:S(2)}) collective-permute-start(bf16[192,768]{1,0:T(8,128)(2,1)S(1)} %get-tuple-element.85), channel_id=1, source_target_pairs={{0,64},{1,65},{2,66},{3,67},{4,68},{5,69},{6,70},{7,71},{8,72},{9,... | collective-permute-start | bytes 884744 | tf_op jit(solution)/shard_map/ppermute | solution.py:786
  39.2 11.6 %collective-permute-start.7 = (bf16[192,768]{1,0:T(8,128)(2,1)S(1)}, bf16[192,768]{1,0:T(8,128)(2,1)S(1)}, u32[]{:S(2)}, u32[]{:S(2)}) collective-permute-start(bf16[192,768]{1,0:T(8,128)(2,1)S(1)} %get-tuple-element.87), channel_id=1, source_target_pairs={{0,96},{1,97},{2,98},{3,99},{4,100},{5,101},{6,102},{7,103},{8,104... | collective-permute-start | bytes 884744 | tf_op jit(solution)/shard_map/ppermute | solution.py:788
  43.7 4.5 %collective-permute-start.9 = (bf16[3,32,384]{2,1,0:T(8,128)(2,1)S(1)}, bf16[3,32,384]{2,1,0:T(8,128)(2,1)S(1)}, u32[]{:S(2)}, u32[]{:S(2)}) collective-permute-start(bf16[3,32,384]{2,1,0:T(8,128)(2,1)S(1)} %get-tuple-element.93), channel_id=1, source_target_pairs={{0,15},{1,0},{2,1},{3,2},{4,3},{5,4},{6,5},{7,6},{8,7},{9,8},{10,9... | collective-permute-start | bytes 221192 | tf_op jit(solution)/shard_map/ppermute | solution.py:746
  45.4 5.4 %collective-permute-start.8 = (bf16[3,32,384]{2,1,0:T(8,128)(2,1)S(1)}, bf16[3,32,384]{2,1,0:T(8,128)(2,1)S(1)}, u32[]{:S(2)}, u32[]{:S(2)}) collective-permute-start(bf16[3,32,384]{2,1,0:T(8,128)(2,1)S(1)} %get-tuple-element.94), channel_id=1, source_target_pairs={{0,1},{1,2},{2,3},{3,4},{4,5},{5,6},{6,7},{7,8},{8,9},{9,10},{10,1... | collective-permute-start | bytes 221192 | tf_op jit(solution)/shard_map/ppermute | solution.py:745
  50.9 10.0 %collective-permute-start.10 = (bf16[48,768]{1,0:T(8,128)(2,1)S(1)}, bf16[48,768]{1,0:T(8,128)(2,1)S(1)}, u32[]{:S(2)}, u32[]{:S(2)}) collective-permute-start(bf16[48,768]{1,0:T(8,128)(2,1)S(1)} %get-tuple-element.101), channel_id=1, source_target_pairs={{0,1},{1,128},{2,3},{3,130},{4,5},{5,132},{6,7},{7,134},{8,9},{9,1... | collective-permute-start | bytes 221192 | tf_op jit(solution)/shard_map/ppermute | solution.py:797
  51.4 9.6 %collective-permute-start.11 = (bf16[48,768]{1,0:T(8,128)(2,1)S(1)}, bf16[48,768]{1,0:T(8,128)(2,1)S(1)}, u32[]{:S(2)}, u32[]{:S(2)}) collective-permute-start(bf16[48,768]{1,0:T(8,128)(2,1)S(1)} %get-tuple-element.102), channel_id=1, source_target_pairs={{0,128},{1,129},{2,130},{3,131},{4,132},{5,133},{6,134},{7,135},{8... | collective-permute-start | bytes 221192 | tf_op jit(solution)/shard_map/ppermute | solution.py:797
  54.4 6.6 %collective-permute-start.12 = (bf16[48,768]{1,0:T(8,128)(2,1)S(1)}, bf16[48,768]{1,0:T(8,128)(2,1)S(1)}, u32[]{:S(2)}, u32[]{:S(2)}) collective-permute-start(bf16[48,768]{1,0:T(8,128)(2,1)S(1)} %get-tuple-element.103), channel_id=1, source_target_pairs={{0,129},{1,0},{2,131},{3,2},{4,133},{5,4},{6,135},{7,6},{8,137},{9... | collective-permute-start | bytes 221192 | tf_op jit(solution)/shard_map/ppermute | solution.py:797
  56.6 20.6 %collective-permute-start.15 = (bf16[3,48,384]{2,1,0:T(8,128)(2,1)S(1)}, bf16[3,48,384]{2,1,0:T(8,128)(2,1)S(1)}, u32[]{:S(2)}, u32[]{:S(2)}) collective-permute-start(bf16[3,48,384]{2,1,0:T(8,128)(2,1)S(1)} %get-tuple-element.106), channel_id=1, source_target_pairs={{16,0},{32,16},{48,32},{64,48},{80,64},{96,80},{112,96},{17,1},{33... | collective-permute-start | bytes 331784 | tf_op jit(solution)/shard_map/ppermute | solution.py:752
  57.9 19.3 %collective-permute-start.14 = (bf16[3,48,384]{2,1,0:T(8,128)(2,1)S(1)}, bf16[3,48,384]{2,1,0:T(8,128)(2,1)S(1)}, u32[]{:S(2)}, u32[]{:S(2)}) collective-permute-start(bf16[3,48,384]{2,1,0:T(8,128)(2,1)S(1)} %get-tuple-element.107), channel_id=1, source_target_pairs={{0,16},{16,32},{32,48},{48,64},{64,80},{80,96},{96,112},{1,17},{17... | collective-permute-start | bytes 331784 | tf_op jit(solution)/shard_map/ppermute | solution.py:751
  61.1 9.9 %collective-permute-start.13 = (f32[24,768]{1,0:T(8,128)S(1)}, f32[24,768]{1,0:T(8,128)S(1)}, u32[]{:S(2)}, u32[]{:S(2)}) collective-permute-start(f32[24,768]{1,0:T(8,128)S(1)} %get-tuple-element.112), channel_id=1, source_target_pairs={{0,8},{1,9},{2,10},{3,11},{4,12},{5,13},{6,14},{7,15},{8,0},{9,1},... | collective-permute-start | bytes 221192 | tf_op jit(solution)/shard_map/ppermute | solution.py:803
  70.9 6.3 %collective-permute-start.16 = (f32[12,768]{1,0:T(8,128)S(1)}, f32[12,768]{1,0:T(8,128)S(1)}, u32[]{:S(2)}, u32[]{:S(2)}) collective-permute-start(f32[12,768]{1,0:T(8,128)S(1)} %get-tuple-element.117), channel_id=1, source_target_pairs={{0,4},{1,5},{2,6},{3,7},{4,0},{5,1},{6,2},{7,3},{8,12},{9,13},{10,... | collective-permute-start | bytes 110600 | tf_op jit(solution)/shard_map/ppermute | solution.py:808
  77.2 8.0 %collective-permute-start.17 = (f32[6,768]{1,0:T(8,128)S(1)}, f32[6,768]{1,0:T(8,128)S(1)}, u32[]{:S(2)}, u32[]{:S(2)}) collective-permute-start(f32[6,768]{1,0:T(8,128)S(1)} %get-tuple-element.122), channel_id=1, source_target_pairs={{0,2},{1,3},{2,0},{3,1},{4,6},{5,7},{6,4},{7,5},{8,10},{9,11},{10,... | collective-permute-start | bytes 55304 | tf_op jit(solution)/shard_map/ppermute | solution.py:813

commit v6 on v5

--- a/solution.py
+++ b/solution.py
@@ -156,11 +156,15 @@
 
 
 def add_edges(flipped, kernel_ref, left_ref, right_ref, top_ref, bottom_ref, rows_sum, cols_sum):
+    lat = lax.axis_index("lat")
     channels = kernel_ref.shape[2]
     for c in range(channels // lanes):
         cols = slice(c * lanes, (c + 1) * lanes)
         for low, ref in ((True, top_ref), (False, bottom_ref)):
-            beyond = [ref[h, :, cols].astype(f32)[: side + 8] for h in range(reach)]
+            outside = lat == (0 if low else lax.axis_size("lat") - 1)
+            beyond = [
+                jnp.where(outside, 0.0, ref[h, :, cols].astype(f32)[: side + 8]) for h in range(reach)
+            ]
             for r in range(reach):
                 result = None
                 steps = [(h, h - r) for h in range(r, reach)] if low else [
@@ -395,17 +399,21 @@
     return lax.dot_general(left, right, (((1,), (1,)), ((), ())), preferred_element_type=f32)
 
 
-def hidden_rows(cells, source, rows, grad_pre_ref, to):
+def hidden_rows(cells, sources, rows, grad_pre_ref, places):
     normed_ref, grad_ref, expand_ref, reduce_ref, bias_ref = cells
     total = normed_ref.shape[0]
-    at = pl.ds(source, rows)
-    preact = dot_rows(expand_ref[at, :], normed_ref[...])
-    grad_hidden = dot_rows(reduce_ref[at, :], grad_ref[...])
-    bias = jnp.concatenate([bias_ref[at, :]] * (total // lanes), axis=1)
+
+    def gather(ref):
+        return jnp.concatenate([ref[pl.ds(source, rows), :] for source in sources], axis=0)
+
+    preact = dot_rows(gather(expand_ref), normed_ref[...])
+    grad_hidden = dot_rows(gather(reduce_ref), grad_ref[...])
+    bias = jnp.concatenate([gather(bias_ref)] * (total // lanes), axis=1)
     value, slope = gelu_pair(preact + bias)
     hidden = value.astype(bf16)
     grad_pre = (grad_hidden * slope).astype(bf16)
-    grad_pre_ref[pl.ds(to, rows), :] = grad_pre
+    for n, place in enumerate(places):
+        grad_pre_ref[pl.ds(place, rows), :] = grad_pre[n * rows : (n + 1) * rows]
     return (
         jnp.dot(grad_pre, normed_ref[...], preferred_element_type=f32),
         jnp.dot(hidden, grad_ref[...], preferred_element_type=f32),
@@ -417,10 +425,10 @@
     half = grad_pre_ref.shape[0]
     channels = refs[0].shape[1]
     base = (1 - own_place()[0]) * half
-    rows = 256
+    rows = half // 2
     for b in range(half // rows):
         source = pl.multiple_of(base + b * rows, rows)
-        expand, reduce = hidden_rows(cells, source, rows, grad_pre_ref, b * rows)
+        expand, reduce = hidden_rows(cells, [source], rows, grad_pre_ref, [b * rows])
         at = slice(b * rows, (b + 1) * rows)
         sent_ref[at, :channels] = expand.astype(bf16)
         sent_ref[at, channels:] = reduce.astype(bf16)
@@ -449,13 +457,11 @@
     channels = refs[0].shape[1]
     size = half // 4
     core, place = own_place()[0], phase_place(False)
-    for step in (1, 2):
-        chunk = pl.multiple_of(lax.rem(place + step, 4) * size, size)
-        source = pl.multiple_of(core * half + chunk, size)
-        expand, reduce = hidden_rows(cells, source, size, grad_pre_ref, chunk)
-        at = slice((step - 1) * size, step * size)
-        sums_ref[at, :channels] = expand
-        sums_ref[at, channels:] = reduce
+    chunks = [pl.multiple_of(lax.rem(place + step, 4) * size, size) for step in (1, 2)]
+    sources = [pl.multiple_of(core * half + chunk, size) for chunk in chunks]
+    expand, reduce = hidden_rows(cells, sources, size, grad_pre_ref, chunks)
+    sums_ref[:, :channels] = expand
+    sums_ref[:, channels:] = reduce
 
 
 def near_first(*cells):
@@ -504,13 +510,14 @@
     channels = refs[0].shape[1]
     size = half // 4
     core, place = own_place()[0], phase_place(False)
-    for step, ref in ((3, sent_ref), (0, own_ref)):
-        chunk = pl.multiple_of(lax.rem(place + step, 4) * size, size)
-        source = pl.multiple_of(core * half + chunk, size)
-        expand, reduce = hidden_rows(cells, source, size, grad_pre_ref, chunk)
+    chunks = [pl.multiple_of(lax.rem(place + step, 4) * size, size) for step in (3, 0)]
+    sources = [pl.multiple_of(core * half + chunk, size) for chunk in chunks]
+    expand, reduce = hidden_rows(cells, sources, size, grad_pre_ref, chunks)
+    for n, (chunk, ref) in enumerate(zip(chunks, (sent_ref, own_ref))):
+        at = slice(n * size, (n + 1) * size)
         other = arrived_ref[pl.ds(chunk, size), :].astype(f32)
-        ref[:, :channels] = (expand + other[:, :channels]).astype(ref.dtype)
-        ref[:, channels:] = (reduce + other[:, channels:]).astype(ref.dtype)
+        ref[:, :channels] = (expand[at] + other[:, :channels]).astype(ref.dtype)
+        ref[:, channels:] = (reduce[at] + other[:, channels:]).astype(ref.dtype)
 
 
 def near_last(*inputs):
@@ -570,7 +577,7 @@
         in_specs=[whole] * 6,
         out_specs=[whole] * 3,
         compiler_params=params(14),
-        cost_estimate=cost(2.2),
+        cost_estimate=cost(0.2),
         name="norm_back",
     )(turned, other, mine, unit, spread, gain)
     return found.reshape(total, channels), first, last
@@ -656,28 +663,56 @@
     )(own, *parts)
 
 
-def split_two_body(bit, own_ref, *refs):
+def split_two_body(own_ref, *refs):
     part_refs, (kept_ref, sent_ref) = refs[:-2], refs[-2:]
     size = kept_ref.shape[0]
     total = own_ref[...]
     for ref in part_refs:
         total = total + ref[...].astype(f32)
     low, high = total[:size], total[size:]
-    upper = (own_place()[3] & bit) != 0
+    upper = (own_place()[3] & 1) != 0
     kept_ref[...] = jnp.where(upper, high, low)
     sent_ref[...] = jnp.where(upper, low, high)
 
 
-def split_two(bit, own, parts):
+def split_two(own, parts):
     shape = jax.ShapeDtypeStruct((own.shape[0] // 2, own.shape[1]), f32)
     return pl.pallas_call(
-        functools.partial(split_two_body, bit),
+        split_two_body,
         out_shape=(shape, shape),
         in_specs=[whole] * (1 + len(parts)),
         out_specs=[whole] * 2,
         compiler_params=params(4),
         cost_estimate=cost(0.2),
         name="split_two",
+    )(own, *parts)
+
+
+def split_ring_body(own_ref, first_ref, second_ref, third_ref, kept_ref, *sent_refs):
+    size = kept_ref.shape[0]
+    total = own_ref[...]
+    for ref in (first_ref, second_ref, third_ref):
+        total = total + ref[...].astype(f32)
+    chunks = [total[c * size : (c + 1) * size] for c in range(4)]
+    place = own_place()[3] >> 1
+    for step, ref in enumerate((kept_ref, *sent_refs)):
+        wanted = (place + step) & 3
+        found = chunks[0]
+        for c in range(1, 4):
+            found = jnp.where(wanted == c, chunks[c], found)
+        ref[...] = found
+
+
+def split_ring(own, parts):
+    shape = jax.ShapeDtypeStruct((own.shape[0] // 4, own.shape[1]), f32)
+    return pl.pallas_call(
+        split_ring_body,
+        out_shape=(shape,) * 4,
+        in_specs=[whole] * 4,
+        out_specs=[whole] * 4,
+        compiler_params=params(4),
+        cost_estimate=cost(0.2),
+        name="split_ring",
     )(own, *parts)
 
 
@@ -727,29 +762,28 @@
     return device_pairs(move)
 
 
-def halving_pairs(bit):
-    return device_pairs(lambda hi, y, core, z, lo: (hi, y, core, z ^ bit, lo))
-
-
-def shifted(axis, step, closed):
+def ring_pairs(step):
+    return device_pairs(lambda hi, y, core, z, lo: (hi, y, core, (z + 2 * step) % 8, lo))
+
+
+def last_pairs():
+    return device_pairs(lambda hi, y, core, z, lo: (hi, y, core, z ^ 1, lo))
+
+
+def shifted(axis, step):
     count = lax.axis_size(axis)
-    found = []
-    for i in range(count):
-        j = i + step
-        if closed or 0 <= j < count:
-            found.append((i, j % count))
-    return found
+    return [(i, (i + step) % count) for i in range(count)]
 
 
 def lon_halo(first, last):
-    left = lax.ppermute(last, "lon", shifted("lon", 1, True))
-    right = lax.ppermute(first, "lon", shifted("lon", -1, True))
+    left = lax.ppermute(last, "lon", shifted("lon", 1))
+    right = lax.ppermute(first, "lon", shifted("lon", -1))
     return left, right
 
 
 def lat_halo(up, down):
-    top = lax.ppermute(down, "lat", shifted("lat", 1, False))
-    bottom = lax.ppermute(up, "lat", shifted("lat", -1, False))
+    top = lax.ppermute(down, "lat", shifted("lat", 1))
+    bottom = lax.ppermute(up, "lat", shifted("lat", -1))
     return top, bottom
 
 
@@ -769,10 +803,11 @@
     left, right = lon_halo(*side_cols(cells))
     rows = mask_rows(counts, grad)
     expand, reduce, expand_t, bias = arrange(w_expand[0], w_reduce[0], b_expand)
-    left, right = after((left, right), rows, bias)
+    conv = inner_conv(after(cells, rows), kernel, False, (0,))
+    left, right = after((left, right), rows, bias, conv)
     up, down = side_rows(cells, left, right)
     top, bottom = lat_halo(up, down)
-    conv = inner_conv(after(cells, up, down), kernel, False, (0, 1, 2))
+    conv += inner_conv(after(cells, up, down), kernel, False, (1, 2))
     unit, spread, normed = normalise(
         conv, kernel, left, right, top, bottom, dw_bias, norm_gain, norm_bias
     )
@@ -787,30 +822,22 @@
     own, three, near_pre = near_last(*inputs, arrived, after(near_pre, one, two))
     part_three = lax.ppermute(three, every_axis, plane_pairs(3, True))
 
-    far_pre = after(far_pre, three)
+    far_pre, part_one, part_two = after((far_pre, part_one, part_two), three)
     conv_grad, first, last = norm_back(expand_t, far_pre, near_pre, unit, spread, norm_gain)
     left, right = lon_halo(first, last)
-    back = inner_conv(after(conv_grad, first, last), kernel, True, (0,))
-
-    own, parts = after((own, (part_one, part_two, part_three)), left, right, back)
+    own, parts = after((own, (part_one, part_two, part_three)), first, last)
     own, *sent = split_four(own, parts)
     parts = [lax.ppermute(s, every_axis, plane_pairs(i + 1, False)) for i, s in enumerate(sent)]
-    conv_grad = after(conv_grad, sent)
-    up, down = side_rows(conv_grad, left, right)
-
-    own, sent = split_two(4, *after((own, parts), up, down))
+    back = inner_conv(after(conv_grad, sent), kernel, True, (0, 1))
+    up, down = side_rows(*after((conv_grad, left, right), back))
+
+    own, *sent = split_ring(*after((own, parts), up, down))
+    parts = [lax.ppermute(s, every_axis, ring_pairs(i + 1)) for i, s in enumerate(sent)]
     top, bottom = lat_halo(up, down)
-    arrived = lax.ppermute(sent, every_axis, halving_pairs(4))
-    conv_grad = after(conv_grad, sent)
-    back += inner_conv(conv_grad, kernel, True, (1,))
-
-    own, sent = split_two(2, *after((own, [arrived]), back))
-    arrived = lax.ppermute(sent, every_axis, halving_pairs(2))
-    conv_grad = after(conv_grad, sent)
-    back += inner_conv(conv_grad, kernel, True, (2,))
-
-    own, sent = split_two(1, *after((own, [arrived]), back, top, bottom))
-    arrived = lax.ppermute(sent, every_axis, halving_pairs(1))
+    back += inner_conv(after(conv_grad, sent), kernel, True, (2,))
+
+    own, sent = split_two(*after((own, parts), back, top, bottom))
+    arrived = lax.ppermute(sent, every_axis, last_pairs())
     grad = after(grad, sent)
     gradient = finish(counts, back, kernel, left, right, top, bottom, grad)
 

time: 86 us -> 77.3 us (0.90)
  starting transfers between devices: 41.8 us -> 30.8 us
  waiting for transfers between devices: 5.22 us -> 8.3 us
  Pallas kernels: 37.7 us -> 36.7 us
    ppermute x11 -> x12, starting transfers between devices: 29 us -> 20.3 us  [the longest x3 10.5 us: local(): lax.ppermute(s, every_axis, ring_pairs(i + 1))]
    ppermute x1, waiting for transfers between devices: 0.01 us -> 3.66 us  [local(): part_two = lax.ppermute(two, every_axis, plane_pairs(2, True))]
    ppermute x1, starting transfers between devices: 2.33 us -> 0.63 us  [local(): part_three = lax.ppermute(three, every_axis, plane_pairs(3, True))]
    ppermute x1, starting transfers between devices: 1.73 us -> 3.39 us  [local(): part_two = lax.ppermute(two, every_axis, plane_pairs(2, True))]
    ppermute x11 -> x12, waiting for transfers between devices: 5.21 us -> 3.63 us  [the longest x2 3.42 us: lat_halo(): top = lax.ppermute(down, 'lat', shifted('lat', 1))]
    ppermute x1, starting transfers between devices: 1.65 us -> 0.42 us  [local(): part_one = lax.ppermute(one, every_axis, plane_pairs(1, True))]
    ppermute x1, starting transfers between devices: 1.46 us -> 0.27 us  [local(): arrived = lax.ppermute(sent, 'lat', [(i, i ^ 1) for i in range(8)])]
  transfers between devices with their start and end apart: 18 -> 19, of which waited for: 4 -> 6; matrix products, arithmetic and copies ran while one was open for 0% -> 0% of each run, Pallas kernels for 32% -> 35%
where the time goes in v6:
time: 77.3 us; the launch traced here: 77.2 us
  Pallas kernels  36.7 us (47%)
  starting transfers between devices  30.8 us (40%)
  waiting for transfers between devices  8.3 us (11%)
  between operations  0.89 us (1%)
    pallas_call x4, Pallas kernels, inner_conv(): pl.pallas_call(functools.partial(inner_conv_body, flipped, parts), out_sh...  13.2 us
    ppermute x3, starting transfers between devices, local(): lax.ppermute(s, every_axis, ring_pairs(i + 1))  10.5 us
    ppermute x3, starting transfers between devices, local(): lax.ppermute(s, every_axis, plane_pairs(i + 1, False))  5.72 us
    pallas_call x1, Pallas kernels, hidden_far(): pl.pallas_call(far_body, out_shape=(jax.ShapeDtypeStruct((half, 2 * chann...  5.17 us
    ppermute x1, waiting for transfers between devices, local(): part_two = lax.ppermute(two, every_axis, plane_pairs(2, True))  3.66 us
    ppermute x2, waiting for transfers between devices, lat_halo(): top = lax.ppermute(down, 'lat', shifted('lat', 1))  3.42 us
    ppermute x1, starting transfers between devices, local(): part_two = lax.ppermute(two, every_axis, plane_pairs(2, True))  3.39 us
    pallas_call x1, Pallas kernels, finish(): pl.pallas_call(finish_body, out_shape=jax.ShapeDtypeStruct((total, channe...  3.36 us
  transfers between devices with their start and end apart: 19, of which 6 were waited for; matrix products, arithmetic and copies ran while one was open for 0% of the time, Pallas kernels for 35%

profile of v6, /device:TPU:32, one launch (start us, length us, event | category | flops | bytes accessed | tf_op | source)
XLA Modules:
  0.0 77.2 jit_solution(1039163385643457410)
XLA Ops:
  0.7 2.1 %side_cols.1 = (bf16[3,32,384]{2,1,0:T(8,128)(2,1)}, bf16[3,32,384]{2,1,0:T(8,128)(2,1)}) custom-call(f32[32,32,384]{2,1,0:T(8,128)} %bitcast.10), custom_call_target="tpu_custom_call" | custom-call | flops 1150000000 | bytes 1048576 | tf_op jit(solution)/shard_map/side_cols/pallas_call | solution.py:116
  2.7 1.6 %collective-permute-start = (bf16[3,32,384]{2,1,0:T(8,128)(2,1)}, bf16[3,32,384]{2,1,0:T(8,128)(2,1)S(1)}, u32[]{:S(2)}, u32[]{:S(2)}) collective-permute-start(bf16[3,32,384]{2,1,0:T(8,128)(2,1)} %get-tuple-element.72), channel_id=1, source_target_pairs={{0,1},{1,2},{2,3},{3,4},{4,5},{5,6},{6,7},{7,8},{8,9},{9,10},{10,1... | collective-permute-start | bytes 221192 | tf_op jit(solution)/shard_map/ppermute | solution.py:779
  4.3 1.4 %collective-permute-start.1 = (bf16[3,32,384]{2,1,0:T(8,128)(2,1)}, bf16[3,32,384]{2,1,0:T(8,128)(2,1)S(1)}, u32[]{:S(2)}, u32[]{:S(2)}) collective-permute-start(bf16[3,32,384]{2,1,0:T(8,128)(2,1)} %get-tuple-element.73), channel_id=1, source_target_pairs={{0,15},{1,0},{2,1},{3,2},{4,3},{5,4},{6,5},{7,6},{8,7},{9,8},{10,9... | collective-permute-start | bytes 221192 | tf_op jit(solution)/shard_map/ppermute | solution.py:780
  5.7 1.0 %mask_rows.1.refs_1_ = bf16[1024,384]{1,0:T(8,128)(2,1)S(1)} custom-call(s32[4,4]{1,0:T(4,128)S(1)} %copy-done.7, f32[1024,384]{1,0:T(8,128)S(1)} %bitcast.14), custom_call_target="tpu_custom_call" | custom-call | flops 1035000000 | bytes 1048576 | tf_op jit(solution)/shard_map/mask_rows/pallas_call | solution.py:316
  7.1 2.2 %inner_conv.4.conv0_ref = f32[1024,128]{1,0:T(8,128)S(1)} custom-call(f32[1024,384]{1,0:T(8,128)S(1)} %bitcast.11, f32[49,1,384]{2,1,0:T(1,128)S(1)} %bitcast.21), custom_call_target="tpu_custom_call" | custom-call | flops 2644999936 | bytes 1048576 | tf_op jit(solution)/shard_map/inner_conv/pallas_call | solution.py:86
  9.4 1.5 %arrange.1 = (bf16[1536,384]{1,0:T(8,128)(2,1)S(1)}, bf16[1536,384]{1,0:T(8,128)(2,1)S(1)}, bf16[384,1536]{1,0:T(8,128)(2,1)S(1)}, f32[1536,128]{1,0:T(8,128)S(1)}) custom-call(bf16[1536,384]{1,0:T(8,128)(2,1)S(1)} %bitcast.19, bf16[1536,384]{1,0:T(8,128)(2,1)S(1)} %bitcast.20, f32[1,1536]{1,0:T(1,128)S(1)} %copy-done.6), custom_call_target="tpu_custom_call" | custom-call | flops 1724999936 | bytes 1048576 | tf_op jit(solution)/shard_map/arrange/pallas_call | solution.py:351
  11.0 1.9 %collective-permute-start.3 = (bf16[3,48,384]{2,1,0:T(8,128)(2,1)S(1)}, bf16[3,48,384]{2,1,0:T(8,128)(2,1)S(1)}, u32[]{:S(2)}, u32[]{:S(2)}) collective-permute-start(bf16[3,48,384]{2,1,0:T(8,128)(2,1)S(1)} %get-tuple-element.77), channel_id=1, source_target_pairs={{0,112},{16,0},{32,16},{48,32},{64,48},{80,64},{96,80},{112,96},{1... | collective-permute-start | bytes 331784 | tf_op jit(solution)/shard_map/ppermute | solution.py:786
  12.9 4.4 %inner_conv.5 = (f32[1024,128]{1,0:T(8,128)S(1)}, f32[1024,128]{1,0:T(8,128)S(1)}) custom-call(f32[1024,384]{1,0:T(8,128)S(1)} %bitcast.13, f32[49,1,384]{2,1,0:T(1,128)S(1)} %bitcast.22), custom_call_target="tpu_custom_call" | custom-call | flops 5289999872 | bytes 1048576 | tf_op jit(solution)/shard_map/inner_conv/pallas_call | solution.py:86
  17.3 1.0 %collective-permute-done.2.top_ref = bf16[3,48,384]{2,1,0:T(8,128)(2,1)S(1)} collective-permute-done((bf16[3,48,384]{2,1,0:T(8,128)(2,1)S(1)}, bf16[3,48,384]{2,1,0:T(8,128)(2,1)S(1)}, u32[]{:S(2)}, u32[]{:S(2)}) %collective-permute-start.2) | collective-permute-done | bytes 110624 | tf_op jit(solution)/shard_map/ppermute | solution.py:785
  18.3 2.0 %normalise.1 = (f32[1024,384]{1,0:T(8,128)S(1)}, f32[1024,128]{1,0:T(8,128)S(1)}, bf16[1024,384]{1,0:T(8,128)(2,1)S(1)}) custom-call(f32[1024,128]{1,0:T(8,128)S(1)} %inner_conv.4.conv0_ref, f32[1024,128]{1,0:T(8,128)S(1)} %get-tuple-element.80.conv1_ref, f32[1024,128]{1,0:T(8,128)S(1)} %get-tuple-element.81.conv2_ref, f32[49,1,384]{2,1,0:T(1,128)S(1)} %bitcast.23, ...), custom_call_target="tpu_custom_call" | custom-call | flops 3220000000 | bytes 1048576 | tf_op jit(solution)/shard_map/normalise/pallas_call | solution.py:264
  20.3 5.2 %hidden_far.1 = (bf16[768,768]{1,0:T(8,128)(2,1)S(1)}, bf16[768,1024]{1,0:T(8,128)(2,1)S(1)}) custom-call(bf16[1024,384]{1,0:T(8,128)(2,1)S(1)} %get-tuple-element.82.refs_0_, bf16[1024,384]{1,0:T(8,128)(2,1)S(1)} %mask_rows.1.refs_1_, bf16[1536,384]{1,0:T(8,128)(2,1)S(1)} %get-tuple-element.83.refs_2_, bf16[1536,384]{1,0:T(8,128)(2,1)S(1)} %get-tuple-element.84.refs_3_, ...), custom_call_target="tpu_custom_call" | custom-call | flops 6670000128 | bytes 1048576 | tf_op jit(solution)/shard_map/hidden_far/pallas_call | solution.py:440
  25.7 2.7 %near_first.1 = (f32[384,768]{1,0:T(8,128)S(1)}, bf16[768,1024]{1,0:T(8,128)(2,1)S(1)}) custom-call(bf16[1024,384]{1,0:T(8,128)(2,1)S(1)} %get-tuple-element.82.refs_0_, bf16[1024,384]{1,0:T(8,128)(2,1)S(1)} %mask_rows.1.refs_1_, bf16[1536,384]{1,0:T(8,128)(2,1)S(1)} %get-tuple-element.83.refs_2_, bf16[1536,384]{1,0:T(8,128)(2,1)S(1)} %get-tuple-element.84.refs_3_, ...), custom_call_target="tpu_custom_call" | custom-call | flops 3449999872 | bytes 1048576 | tf_op jit(solution)/shard_map/near_first/pallas_call | solution.py:470
  29.1 3.4 %collective-permute-start.6 = (bf16[192,768]{1,0:T(8,128)(2,1)S(1)}, bf16[192,768]{1,0:T(8,128)(2,1)S(1)}, u32[]{:S(2)}, u32[]{:S(2)}) collective-permute-start(bf16[192,768]{1,0:T(8,128)(2,1)S(1)} %get-tuple-element.89), channel_id=1, source_target_pairs={{0,64},{1,65},{2,66},{3,67},{4,68},{5,69},{6,70},{7,71},{8,72},{9,... | collective-permute-start | bytes 884744 | tf_op jit(solution)/shard_map/ppermute | solution.py:821
  32.5 2.7 %near_last.1 = (f32[192,768]{1,0:T(8,128)S(1)}, bf16[192,768]{1,0:T(8,128)(2,1)S(1)}, bf16[768,1024]{1,0:T(8,128)(2,1)S(1)}) custom-call(bf16[1024,384]{1,0:T(8,128)(2,1)S(1)} %get-tuple-element.82.refs_0_, bf16[1024,384]{1,0:T(8,128)(2,1)S(1)} %mask_rows.1.refs_1_, ...), custom_call_target="tpu_custom_call", output_to_operand_aliasing={{2}: (6, {})} | custom-call | flops 3449999872 | bytes 1048576 | tf_op jit(solution)/shard_map/near_last/pallas_call | solution.py:527
  35.2 0.6 collective-permute-start.7
  35.8 0.8 %collective-permute-done.5.first_ref = bf16[192,768]{1,0:T(8,128)(2,1)S(1)} collective-permute-done((bf16[192,768]{1,0:T(8,128)(2,1)S(1)}, bf16[192,768]{1,0:T(8,128)(2,1)S(1)}, u32[]{:S(2)}, u32[]{:S(2)}) %collective-permute-start.5) | collective-permute-done | bytes 294944 | tf_op jit(solution)/shard_map/ppermute | solution.py:820
  36.7 3.7 %collective-permute-done.6.second_ref = bf16[192,768]{1,0:T(8,128)(2,1)S(1)} collective-permute-done((bf16[192,768]{1,0:T(8,128)(2,1)S(1)}, bf16[192,768]{1,0:T(8,128)(2,1)S(1)}, u32[]{:S(2)}, u32[]{:S(2)}) %collective-permute-start.6) | collective-permute-done | bytes 294944 | tf_op jit(solution)/shard_map/ppermute | solution.py:821
  40.3 2.0 %norm_back.1 = (f32[32,32,384]{2,1,0:T(8,128)S(1)}, bf16[3,32,384]{2,1,0:T(8,128)(2,1)S(1)}, bf16[3,32,384]{2,1,0:T(8,128)(2,1)S(1)}) custom-call(bf16[384,1536]{1,0:T(8,128)(2,1)S(1)} %get-tuple-element.70.turned_ref, bf16[768,1024]{1,0:T(8,128)(2,1)S(1)} %get-tuple-element.93.other_ref, bf16[768,1024]{1,0:T(8,128)(2,1)S(1)} %get-tuple-element.94.mine_ref, ...), custom_call_target="tpu_custom_call" | custom-call | flops 230000000 | bytes 1048576 | tf_op jit(solution)/shard_map/norm_back/pallas_call | solution.py:574
  42.7 1.7 %collective-permute-start.11 = (bf16[3,32,384]{2,1,0:T(8,128)(2,1)S(1)}, bf16[3,32,384]{2,1,0:T(8,128)(2,1)S(1)}, u32[]{:S(2)}, u32[]{:S(2)}) collective-permute-start(bf16[3,32,384]{2,1,0:T(8,128)(2,1)S(1)} %get-tuple-element.102), channel_id=1, source_target_pairs={{0,1},{1,2},{2,3},{3,4},{4,5},{5,6},{6,7},{7,8},{8,9},{9,10},{10,1... | collective-permute-start | bytes 221192 | tf_op jit(solution)/shard_map/ppermute | solution.py:779
  44.6 1.7 %collective-permute-start.8 = (bf16[48,768]{1,0:T(8,128)(2,1)S(1)}, bf16[48,768]{1,0:T(8,128)(2,1)S(1)}, u32[]{:S(2)}, u32[]{:S(2)}) collective-permute-start(bf16[48,768]{1,0:T(8,128)(2,1)S(1)} %get-tuple-element.107), channel_id=1, source_target_pairs={{0,1},{1,128},{2,3},{3,130},{4,5},{5,132},{6,7},{7,134},{8,9},{9,1... | collective-permute-start | bytes 221192 | tf_op jit(solution)/shard_map/ppermute | solution.py:830
  46.3 3.0 %collective-permute-start.9 = (bf16[48,768]{1,0:T(8,128)(2,1)S(1)}, bf16[48,768]{1,0:T(8,128)(2,1)S(1)}, u32[]{:S(2)}, u32[]{:S(2)}) collective-permute-start(bf16[48,768]{1,0:T(8,128)(2,1)S(1)} %get-tuple-element.108), channel_id=1, source_target_pairs={{0,128},{1,129},{2,130},{3,131},{4,132},{5,133},{6,134},{7,135},{8... | collective-permute-start | bytes 221192 | tf_op jit(solution)/shard_map/ppermute | solution.py:830
  49.4 1.0 %collective-permute-start.10 = (bf16[48,768]{1,0:T(8,128)(2,1)S(1)}, bf16[48,768]{1,0:T(8,128)(2,1)S(1)}, u32[]{:S(2)}, u32[]{:S(2)}) collective-permute-start(bf16[48,768]{1,0:T(8,128)(2,1)S(1)} %get-tuple-element.109), channel_id=1, source_target_pairs={{0,129},{1,0},{2,131},{3,2},{4,133},{5,4},{6,135},{7,6},{8,137},{9... | collective-permute-start | bytes 221192 | tf_op jit(solution)/shard_map/ppermute | solution.py:830
  50.4 4.4 %inner_conv.6 = (f32[1024,128]{1,0:T(8,128)S(1)}, f32[1024,128]{1,0:T(8,128)S(1)}) custom-call(f32[1024,384]{1,0:T(8,128)S(1)} %bitcast.16, f32[49,1,384]{2,1,0:T(1,128)S(1)} %bitcast.24), custom_call_target="tpu_custom_call" | custom-call | flops 5289999872 | bytes 1048576 | tf_op jit(solution)/shard_map/inner_conv/pallas_call | solution.py:86
  54.9 5.1 %collective-permute-start.15 = (f32[12,768]{1,0:T(8,128)S(1)}, f32[12,768]{1,0:T(8,128)S(1)}, u32[]{:S(2)}, u32[]{:S(2)}) collective-permute-start(f32[12,768]{1,0:T(8,128)S(1)} %get-tuple-element.123), channel_id=1, source_target_pairs={{0,4},{1,5},{2,6},{3,7},{4,8},{5,9},{6,10},{7,11},{8,12},{9,13},{1... | collective-permute-start | bytes 110600 | tf_op jit(solution)/shard_map/ppermute | solution.py:835
  60.0 2.7 %collective-permute-start.16 = (f32[12,768]{1,0:T(8,128)S(1)}, f32[12,768]{1,0:T(8,128)S(1)}, u32[]{:S(2)}, u32[]{:S(2)}) collective-permute-start(f32[12,768]{1,0:T(8,128)S(1)} %get-tuple-element.124), channel_id=1, source_target_pairs={{0,8},{1,9},{2,10},{3,11},{4,12},{5,13},{6,14},{7,15},{8,0},{9,1},... | collective-permute-start | bytes 110600 | tf_op jit(solution)/shard_map/ppermute | solution.py:835
  62.8 2.7 %collective-permute-start.17 = (f32[12,768]{1,0:T(8,128)S(1)}, f32[12,768]{1,0:T(8,128)S(1)}, u32[]{:S(2)}, u32[]{:S(2)}) collective-permute-start(f32[12,768]{1,0:T(8,128)S(1)} %get-tuple-element.125), channel_id=1, source_target_pairs={{0,12},{1,13},{2,14},{3,15},{4,0},{5,1},{6,2},{7,3},{8,4},{9,5},{1... | collective-permute-start | bytes 110600 | tf_op jit(solution)/shard_map/ppermute | solution.py:835
  65.5 0.5 collective-permute-start.13
  66.0 2.2 %inner_conv.7.conv2_ref = f32[1024,128]{1,0:T(8,128)S(1)} custom-call(f32[1024,384]{1,0:T(8,128)S(1)} %bitcast.18, f32[49,1,384]{2,1,0:T(1,128)S(1)} %bitcast.25), custom_call_target="tpu_custom_call" | custom-call | flops 2644999936 | bytes 1048576 | tf_op jit(solution)/shard_map/inner_conv/pallas_call | solution.py:86
  68.4 2.5 %collective-permute-done.13.top_ref = bf16[3,48,384]{2,1,0:T(8,128)(2,1)S(1)} collective-permute-done((bf16[3,48,384]{2,1,0:T(8,128)(2,1)S(1)}, bf16[3,48,384]{2,1,0:T(8,128)(2,1)S(1)}, u32[]{:S(2)}, u32[]{:S(2)}) %collective-permute-start.13) | collective-permute-done | bytes 110624 | tf_op jit(solution)/shard_map/ppermute | solution.py:785
  70.9 2.3 %collective-permute-start.18 = (f32[6,768]{1,0:T(8,128)S(1)}, f32[6,768]{1,0:T(8,128)S(1)}, u32[]{:S(2)}, u32[]{:S(2)}) collective-permute-start(f32[6,768]{1,0:T(8,128)S(1)} %get-tuple-element.132), channel_id=1, source_target_pairs={{0,2},{1,3},{2,0},{3,1},{4,6},{5,7},{6,4},{7,5},{8,10},{9,11},{10,... | collective-permute-start | bytes 55304 | tf_op jit(solution)/shard_map/ppermute | solution.py:840
  73.2 3.4 %finish.1 = f32[1024,384]{1,0:T(8,128)} custom-call(s32[4,4]{1,0:T(4,128)S(1)} %copy-done.7, f32[1024,128]{1,0:T(8,128)S(1)} %get-tuple-element.111.conv0_ref, f32[1024,128]{1,0:T(8,128)S(1)} %get-tuple-element.112.conv1_ref, f32[1024,128]{1,0:T(8,128)S(1)} %inner_conv.7.conv2_ref, f32[49,1,384]{2,1,0:T(1,128)S(1)} %bitcast.26, ...), custom_call_target="tpu_custom_call" | custom-call | flops 2529999872 | bytes 1048576 | tf_op jit(solution)/shard_map/finish/pallas_call | solution.py:625
  76.5 0.6 last_sum.1
  (46 shorter events, 2.4 us)
Async XLA Ops:
  0.6 5.1 %copy-start.2 = (f32[1,32,32,384]{3,2,1,0:T(8,128)S(1)}, f32[1,32,32,384]{3,2,1,0:T(8,128)}, u32[]{:S(2)}) copy-start(f32[1,32,32,384]{3,2,1,0:T(8,128)} %param.11) | copy-start | bytes 4718596
  0.6 5.1 %copy-start.7 = (s32[4,4]{1,0:T(4,128)S(1)}, s32[4,4]{1,0:T(4,128)}, u32[]{:S(2)}) copy-start(s32[4,4]{1,0:T(4,128)} %counts_ref.3) | copy-start | bytes 196
  2.7 8.2 %collective-permute-start = (bf16[3,32,384]{2,1,0:T(8,128)(2,1)}, bf16[3,32,384]{2,1,0:T(8,128)(2,1)S(1)}, u32[]{:S(2)}, u32[]{:S(2)}) collective-permute-start(bf16[3,32,384]{2,1,0:T(8,128)(2,1)} %get-tuple-element.72), channel_id=1, source_target_pairs={{0,1},{1,2},{2,3},{3,4},{4,5},{5,6},{6,7},{7,8},{8,9},{9,10},{10,1... | collective-permute-start | bytes 221192 | tf_op jit(solution)/shard_map/ppermute | solution.py:779
  4.3 6.6 %collective-permute-start.1 = (bf16[3,32,384]{2,1,0:T(8,128)(2,1)}, bf16[3,32,384]{2,1,0:T(8,128)(2,1)S(1)}, u32[]{:S(2)}, u32[]{:S(2)}) collective-permute-start(bf16[3,32,384]{2,1,0:T(8,128)(2,1)} %get-tuple-element.73), channel_id=1, source_target_pairs={{0,15},{1,0},{2,1},{3,2},{4,3},{5,4},{6,5},{7,6},{8,7},{9,8},{10,9... | collective-permute-start | bytes 221192 | tf_op jit(solution)/shard_map/ppermute | solution.py:780
  5.7 1.4 %copy-start.1 = (f32[1,32,32,384]{3,2,1,0:T(8,128)S(1)}, f32[1,32,32,384]{3,2,1,0:T(8,128)}, u32[]{:S(2)}) copy-start(f32[1,32,32,384]{3,2,1,0:T(8,128)} %param.10) | copy-start | bytes 4718596
  5.7 1.4 %copy-start.5 = (f32[1,49,384]{2,0,1:T(1,128)S(1)}, f32[1,49,384]{2,0,1:T(1,128)}, u32[]{:S(2)}) copy-start(f32[1,49,384]{2,0,1:T(1,128)} %param.13) | copy-start | bytes 225796
  7.1 2.2 %copy-start.3 = (bf16[1,1536,384]{2,1,0:T(8,128)(2,1)S(1)}, bf16[1,1536,384]{2,1,0:T(8,128)(2,1)}, u32[]{:S(2)}) copy-start(bf16[1,1536,384]{2,1,0:T(8,128)(2,1)} %param.17) | copy-start | bytes 3538948
  7.1 2.2 %copy-start.4 = (bf16[1,1536,384]{2,1,0:T(8,128)(2,1)S(1)}, bf16[1,1536,384]{2,1,0:T(8,128)(2,1)}, u32[]{:S(2)}) copy-start(bf16[1,1536,384]{2,1,0:T(8,128)(2,1)} %param.19) | copy-start | bytes 3538948
  7.1 2.2 %copy-start.6 = (f32[1,1536]{1,0:T(1,128)S(1)}, f32[1,1536]{1,0:T(1,128)}, u32[]{:S(2)}) copy-start(f32[1,1536]{1,0:T(1,128)} %bias_ref.2) | copy-start | bytes 18436
  11.0 6.3 %collective-permute-start.3 = (bf16[3,48,384]{2,1,0:T(8,128)(2,1)S(1)}, bf16[3,48,384]{2,1,0:T(8,128)(2,1)S(1)}, u32[]{:S(2)}, u32[]{:S(2)}) collective-permute-start(bf16[3,48,384]{2,1,0:T(8,128)(2,1)S(1)} %get-tuple-element.77), channel_id=1, source_target_pairs={{0,112},{16,0},{32,16},{48,32},{64,48},{80,64},{96,80},{112,96},{1... | collective-permute-start | bytes 331784 | tf_op jit(solution)/shard_map/ppermute | solution.py:786
  12.9 5.4 %copy-start = (f32[1,384]{1,0:T(1,128)S(1)}, f32[1,384]{1,0:T(1,128)}, u32[]{:S(2)}) copy-start(f32[1,384]{1,0:T(1,128)} %gain_ref.3) | copy-start | bytes 4612
  12.9 5.4 %copy-start.8 = (f32[1,384]{1,0:T(1,128)S(1)}, f32[1,384]{1,0:T(1,128)}, u32[]{:S(2)}) copy-start(f32[1,384]{1,0:T(1,128)} %bias_ref.3) | copy-start | bytes 4612
  12.9 5.4 %copy-start.9 = (f32[1,384]{1,0:T(1,128)S(1)}, f32[1,384]{1,0:T(1,128)}, u32[]{:S(2)}) copy-start(f32[1,384]{1,0:T(1,128)} %shift_ref.1) | copy-start | bytes 4612
  12.9 5.4 %collective-permute-start.2 = (bf16[3,48,384]{2,1,0:T(8,128)(2,1)S(1)}, bf16[3,48,384]{2,1,0:T(8,128)(2,1)S(1)}, u32[]{:S(2)}, u32[]{:S(2)}) collective-permute-start(bf16[3,48,384]{2,1,0:T(8,128)(2,1)S(1)} %get-tuple-element.78), channel_id=1, source_target_pairs={{0,16},{16,32},{32,48},{48,64},{64,80},{80,96},{96,112},{112,0},{1... | collective-permute-start | bytes 331784 | tf_op jit(solution)/shard_map/ppermute | solution.py:785
  25.4 3.1 %collective-permute-start.4 = (bf16[768,768]{1,0:T(8,128)(2,1)S(1)}, bf16[768,768]{1,0:T(8,128)(2,1)S(1)}, u32[]{:S(2)}, u32[]{:S(2)}) collective-permute-start(bf16[768,768]{1,0:T(8,128)(2,1)S(1)} %get-tuple-element.87), channel_id=1, source_target_pairs={{0,16},{16,0},{32,48},{48,32},{64,80},{80,64},{96,112},{112,96},{1... | collective-permute-start | bytes 3538952 | tf_op jit(solution)/shard_map/ppermute | solution.py:817
  28.7 8.0 %collective-permute-start.5 = (bf16[192,768]{1,0:T(8,128)(2,1)S(1)}, bf16[192,768]{1,0:T(8,128)(2,1)S(1)}, u32[]{:S(2)}, u32[]{:S(2)}) collective-permute-start(bf16[192,768]{1,0:T(8,128)(2,1)S(1)} %get-tuple-element.88), channel_id=1, source_target_pairs={{0,32},{1,33},{2,34},{3,35},{4,36},{5,37},{6,38},{7,39},{8,40},{9,... | collective-permute-start | bytes 884744 | tf_op jit(solution)/shard_map/ppermute | solution.py:820
  29.1 11.3 %collective-permute-start.6 = (bf16[192,768]{1,0:T(8,128)(2,1)S(1)}, bf16[192,768]{1,0:T(8,128)(2,1)S(1)}, u32[]{:S(2)}, u32[]{:S(2)}) collective-permute-start(bf16[192,768]{1,0:T(8,128)(2,1)S(1)} %get-tuple-element.89), channel_id=1, source_target_pairs={{0,64},{1,65},{2,66},{3,67},{4,68},{5,69},{6,70},{7,71},{8,72},{9,... | collective-permute-start | bytes 884744 | tf_op jit(solution)/shard_map/ppermute | solution.py:821
  35.2 9.3 %collective-permute-start.7 = (bf16[192,768]{1,0:T(8,128)(2,1)S(1)}, bf16[192,768]{1,0:T(8,128)(2,1)S(1)}, u32[]{:S(2)}, u32[]{:S(2)}) collective-permute-start(bf16[192,768]{1,0:T(8,128)(2,1)S(1)} %get-tuple-element.92), channel_id=1, source_target_pairs={{0,96},{1,97},{2,98},{3,99},{4,100},{5,101},{6,102},{7,103},{8,104... | collective-permute-start | bytes 884744 | tf_op jit(solution)/shard_map/ppermute | solution.py:823
  42.4 12.4 %collective-permute-start.12 = (bf16[3,32,384]{2,1,0:T(8,128)(2,1)S(1)}, bf16[3,32,384]{2,1,0:T(8,128)(2,1)S(1)}, u32[]{:S(2)}, u32[]{:S(2)}) collective-permute-start(bf16[3,32,384]{2,1,0:T(8,128)(2,1)S(1)} %get-tuple-element.101), channel_id=1, source_target_pairs={{0,15},{1,0},{2,1},{3,2},{4,3},{5,4},{6,5},{7,6},{8,7},{9,8},{10,9... | collective-permute-start | bytes 221192 | tf_op jit(solution)/shard_map/ppermute | solution.py:780
  42.7 12.0 %collective-permute-start.11 = (bf16[3,32,384]{2,1,0:T(8,128)(2,1)S(1)}, bf16[3,32,384]{2,1,0:T(8,128)(2,1)S(1)}, u32[]{:S(2)}, u32[]{:S(2)}) collective-permute-start(bf16[3,32,384]{2,1,0:T(8,128)(2,1)S(1)} %get-tuple-element.102), channel_id=1, source_target_pairs={{0,1},{1,2},{2,3},{3,4},{4,5},{5,6},{6,7},{7,8},{8,9},{9,10},{10,1... | collective-permute-start | bytes 221192 | tf_op jit(solution)/shard_map/ppermute | solution.py:779
  44.6 10.2 %collective-permute-start.8 = (bf16[48,768]{1,0:T(8,128)(2,1)S(1)}, bf16[48,768]{1,0:T(8,128)(2,1)S(1)}, u32[]{:S(2)}, u32[]{:S(2)}) collective-permute-start(bf16[48,768]{1,0:T(8,128)(2,1)S(1)} %get-tuple-element.107), channel_id=1, source_target_pairs={{0,1},{1,128},{2,3},{3,130},{4,5},{5,132},{6,7},{7,134},{8,9},{9,1... | collective-permute-start | bytes 221192 | tf_op jit(solution)/shard_map/ppermute | solution.py:830
  46.3 8.5 %collective-permute-start.9 = (bf16[48,768]{1,0:T(8,128)(2,1)S(1)}, bf16[48,768]{1,0:T(8,128)(2,1)S(1)}, u32[]{:S(2)}, u32[]{:S(2)}) collective-permute-start(bf16[48,768]{1,0:T(8,128)(2,1)S(1)} %get-tuple-element.108), channel_id=1, source_target_pairs={{0,128},{1,129},{2,130},{3,131},{4,132},{5,133},{6,134},{7,135},{8... | collective-permute-start | bytes 221192 | tf_op jit(solution)/shard_map/ppermute | solution.py:830
  49.4 5.5 %collective-permute-start.10 = (bf16[48,768]{1,0:T(8,128)(2,1)S(1)}, bf16[48,768]{1,0:T(8,128)(2,1)S(1)}, u32[]{:S(2)}, u32[]{:S(2)}) collective-permute-start(bf16[48,768]{1,0:T(8,128)(2,1)S(1)} %get-tuple-element.109), channel_id=1, source_target_pairs={{0,129},{1,0},{2,131},{3,2},{4,133},{5,4},{6,135},{7,6},{8,137},{9... | collective-permute-start | bytes 221192 | tf_op jit(solution)/shard_map/ppermute | solution.py:830
  54.9 13.2 %collective-permute-start.15 = (f32[12,768]{1,0:T(8,128)S(1)}, f32[12,768]{1,0:T(8,128)S(1)}, u32[]{:S(2)}, u32[]{:S(2)}) collective-permute-start(f32[12,768]{1,0:T(8,128)S(1)} %get-tuple-element.123), channel_id=1, source_target_pairs={{0,4},{1,5},{2,6},{3,7},{4,8},{5,9},{6,10},{7,11},{8,12},{9,13},{1... | collective-permute-start | bytes 110600 | tf_op jit(solution)/shard_map/ppermute | solution.py:835
  60.0 8.2 %collective-permute-start.16 = (f32[12,768]{1,0:T(8,128)S(1)}, f32[12,768]{1,0:T(8,128)S(1)}, u32[]{:S(2)}, u32[]{:S(2)}) collective-permute-start(f32[12,768]{1,0:T(8,128)S(1)} %get-tuple-element.124), channel_id=1, source_target_pairs={{0,8},{1,9},{2,10},{3,11},{4,12},{5,13},{6,14},{7,15},{8,0},{9,1},... | collective-permute-start | bytes 110600 | tf_op jit(solution)/shard_map/ppermute | solution.py:835
  62.8 5.6 %collective-permute-start.17 = (f32[12,768]{1,0:T(8,128)S(1)}, f32[12,768]{1,0:T(8,128)S(1)}, u32[]{:S(2)}, u32[]{:S(2)}) collective-permute-start(f32[12,768]{1,0:T(8,128)S(1)} %get-tuple-element.125), channel_id=1, source_target_pairs={{0,12},{1,13},{2,14},{3,15},{4,0},{5,1},{6,2},{7,3},{8,4},{9,5},{1... | collective-permute-start | bytes 110600 | tf_op jit(solution)/shard_map/ppermute | solution.py:835
  65.5 2.9 %collective-permute-start.14 = (bf16[3,48,384]{2,1,0:T(8,128)(2,1)S(1)}, bf16[3,48,384]{2,1,0:T(8,128)(2,1)S(1)}, u32[]{:S(2)}, u32[]{:S(2)}) collective-permute-start(bf16[3,48,384]{2,1,0:T(8,128)(2,1)S(1)} %get-tuple-element.117), channel_id=1, source_target_pairs={{0,112},{16,0},{32,16},{48,32},{64,48},{80,64},{96,80},{112,96},{1... | collective-permute-start | bytes 331784 | tf_op jit(solution)/shard_map/ppermute | solution.py:786
  65.5 5.4 %collective-permute-start.13 = (bf16[3,48,384]{2,1,0:T(8,128)(2,1)S(1)}, bf16[3,48,384]{2,1,0:T(8,128)(2,1)S(1)}, u32[]{:S(2)}, u32[]{:S(2)}) collective-permute-start(bf16[3,48,384]{2,1,0:T(8,128)(2,1)S(1)} %get-tuple-element.118), channel_id=1, source_target_pairs={{0,16},{16,32},{32,48},{48,64},{64,80},{80,96},{96,112},{112,0},{1... | collective-permute-start | bytes 331784 | tf_op jit(solution)/shard_map/ppermute | solution.py:785
  70.9 5.7 %collective-permute-start.18 = (f32[6,768]{1,0:T(8,128)S(1)}, f32[6,768]{1,0:T(8,128)S(1)}, u32[]{:S(2)}, u32[]{:S(2)}) collective-permute-start(f32[6,768]{1,0:T(8,128)S(1)} %get-tuple-element.132), channel_id=1, source_target_pairs={{0,2},{1,3},{2,0},{3,1},{4,6},{5,7},{6,4},{7,5},{8,10},{9,11},{10,... | collective-permute-start | bytes 55304 | tf_op jit(solution)/shard_map/ppermute | solution.py:840

commit v7 on v6

--- a/solution.py
+++ b/solution.py
@@ -49,7 +49,7 @@
     return jnp.concatenate([first, turned[8:]], axis=0)
 
 
-def inner_conv_body(flipped, parts, cells_ref, kernel_ref, *refs):
+def inner_conv_body(parts, cells_ref, kernel_ref, *refs):
     outs, padded = refs[:-1], refs[-1]
     edge = reach * side
     total = side * side
@@ -66,7 +66,7 @@
             for q in range(7):
                 sums = [None, None]
                 for p in range(7):
-                    tap = tap_row(kernel_ref, flipped, p, q, cols)
+                    tap = tap_row(kernel_ref, False, p, q, cols)
                     for g in range(2):
                         term = tap * rows[p + g]
                         sums[g] = term if sums[g] is None else sums[g] + term
@@ -80,18 +80,71 @@
         lax.fori_loop(0, side // 2, two_rows, 0)
 
 
-def inner_conv(cells, kernel, flipped, parts):
+def inner_conv(cells, kernel, parts):
     total = cells.shape[0]
     shape = jax.ShapeDtypeStruct((total, lanes), f32)
     return pl.pallas_call(
-        functools.partial(inner_conv_body, flipped, parts),
+        functools.partial(inner_conv_body, parts),
         out_shape=(shape,) * len(parts),
         in_specs=[whole] * 2,
         out_specs=[whole] * len(parts),
         scratch_shapes=[pltpu.VMEM((total + 2 * reach * side, lanes), f32)],
         compiler_params=params(6),
-        cost_estimate=cost(2.3 * len(parts)),
+        cost_estimate=cost(2.2 * len(parts)),
         name="inner_conv",
+    )(cells, kernel)
+
+
+def back_conv_body(parts, cells_ref, kernel_ref, *refs):
+    outs, (padded, taps) = refs[:-2], refs[-2:]
+    edge = reach * side
+    total = side * side
+    group = 4
+    padded[0:edge] = jnp.zeros((edge, lanes), bf16)
+    padded[edge + total : 2 * edge + total] = jnp.zeros((edge, lanes), bf16)
+    for part, out_ref in zip(parts, outs):
+        cols = slice(part * lanes, (part + 1) * lanes)
+        padded[edge : edge + total] = cells_ref[:, cols].astype(bf16)
+        for p, q in itertools.product(range(7), range(7)):
+            tap = jnp.broadcast_to(tap_row(kernel_ref, True, p, q, cols), (16, lanes))
+            taps[7 * p + q] = tap.astype(bf16)
+
+        def some_rows(i, carry):
+            base = pl.multiple_of(i * (group * side), group * side)
+            rows = [padded[pl.ds(base + p * side, side), :] for p in range(6 + group)]
+            results = [None] * group
+            for q in range(7):
+                sums = [None] * group
+                for p in range(7):
+                    tap = jnp.concatenate([taps[7 * p + q]] * (side // 16), axis=0)
+                    for g in range(group):
+                        term = tap * rows[p + g]
+                        sums[g] = term if sums[g] is None else sums[g] + term
+                for g in range(group):
+                    moved = shift_cols(sums[g].astype(f32), q - reach)
+                    results[g] = moved if results[g] is None else results[g] + moved
+            for g in range(group):
+                out_ref[pl.ds(base + g * side, side), :] = results[g]
+            return carry
+
+        lax.fori_loop(0, side // group, some_rows, 0)
+
+
+def back_conv(cells, kernel, parts):
+    total = cells.shape[0]
+    shape = jax.ShapeDtypeStruct((total, lanes), f32)
+    return pl.pallas_call(
+        functools.partial(back_conv_body, parts),
+        out_shape=(shape,) * len(parts),
+        in_specs=[whole] * 2,
+        out_specs=[whole] * len(parts),
+        scratch_shapes=[
+            pltpu.VMEM((total + 2 * reach * side, lanes), bf16),
+            pltpu.VMEM((49, 16, lanes), bf16),
+        ],
+        compiler_params=params(6),
+        cost_estimate=cost(1.5 * len(parts)),
+        name="back_conv",
     )(cells, kernel)
 
 
@@ -457,7 +510,7 @@
     channels = refs[0].shape[1]
     size = half // 4
     core, place = own_place()[0], phase_place(False)
-    chunks = [pl.multiple_of(lax.rem(place + step, 4) * size, size) for step in (1, 2)]
+    chunks = [pl.multiple_of(lax.rem(place + step, 4) * size, size) for step in (2, 1)]
     sources = [pl.multiple_of(core * half + chunk, size) for chunk in chunks]
     expand, reduce = hidden_rows(cells, sources, size, grad_pre_ref, chunks)
     sums_ref[:, :channels] = expand
@@ -484,10 +537,10 @@
 def near_sends_body(sums_ref, arrived_ref, *sent_refs):
     size = sent_refs[0].shape[0]
     place = phase_place(False)
-    for step in (1, 2):
+    for n, step in enumerate((2, 1)):
         chunk = pl.multiple_of(lax.rem(place + step, 4) * size, size)
-        total = sums_ref[(step - 1) * size : step * size] + arrived_ref[pl.ds(chunk, size), :].astype(f32)
-        sent_refs[step - 1][...] = total.astype(bf16)
+        total = sums_ref[n * size : (n + 1) * size] + arrived_ref[pl.ds(chunk, size), :].astype(f32)
+        sent_refs[n][...] = total.astype(bf16)
 
 
 def near_sends(sums, arrived):
@@ -585,52 +638,39 @@
 
 def finish_body(
     counts_ref, conv0_ref, conv1_ref, conv2_ref, kernel_ref, left_ref, right_ref, top_ref, bottom_ref,
-    grad_ref, out_ref, rows_sum, cols_sum,
+    grad_ref, out_ref, rows_sum, cols_sum, done, sems,
 ):
     conv_refs = (conv0_ref, conv1_ref, conv2_ref)
-    rows = out_ref.shape[0] // side
-    steps = side // rows
-    block = pl.program_id(0)
-
-    @pl.when(block == 0)
-    def _():
-        add_edges(True, kernel_ref, left_ref, right_ref, top_ref, bottom_ref, rows_sum, cols_sum)
-
-    def write(outer_of):
-        for r in range(rows):
-            i = block * rows + r
-            at = pl.ds(pl.multiple_of(i * side, side), side)
+    add_edges(True, kernel_ref, left_ref, right_ref, top_ref, bottom_ref, rows_sum, cols_sum)
+    rows = 8
+    copies = []
+    for block in range(side // rows):
+        for i in range(block * rows, (block + 1) * rows):
+            at = slice(i * side, (i + 1) * side)
             value = edged_row(i, conv_rows(conv_refs, at), cols_sum)
-            outer = outer_of(r)
-            if outer is not None:
-                value = value + rows_sum[outer]
-            out_ref[r * side : (r + 1) * side, :] = value + masked_row(i, grad_ref[at, :], counts_ref)
-
-    @pl.when(block == 0)
-    def _():
-        write(lambda r: r if r < reach else None)
-
-    @pl.when(jnp.logical_and(block > 0, block < steps - 1))
-    def _():
-        write(lambda r: None)
-
-    @pl.when(block == steps - 1)
-    def _():
-        write(lambda r: r - (rows - 2 * reach) if r >= rows - reach else None)
+            if i < reach:
+                value = value + rows_sum[i]
+            if i >= side - reach:
+                value = value + rows_sum[i - (side - 2 * reach)]
+            done[at, :] = value + masked_row(i, grad_ref[at, :], counts_ref)
+        part = pl.ds(block * rows * side, rows * side)
+        copies.append(pltpu.make_async_copy(done.at[part, :], out_ref.at[part, :], sems.at[block]))
+        copies[-1].start()
+    for copy in copies:
+        copy.wait()
 
 
 def finish(counts, conv, kernel, left, right, top, bottom, grad):
     total, channels = grad.shape
-    rows = 8
     return pl.pallas_call(
         finish_body,
         out_shape=jax.ShapeDtypeStruct((total, channels), f32),
-        grid=(side // rows,),
         in_specs=[pl.BlockSpec(memory_space=pltpu.SMEM)] + [whole] * 9,
-        out_specs=pl.BlockSpec((rows * side, channels), lambda b: (b, 0)),
-        scratch_shapes=[pltpu.VMEM((2 * reach, side, channels), f32)] * 2,
+        out_specs=pl.BlockSpec(memory_space=pltpu.HBM),
+        scratch_shapes=[pltpu.VMEM((2 * reach, side, channels), f32)] * 2
+        + [pltpu.VMEM((total, channels), f32), pltpu.SemaphoreType.DMA((4,))],
         compiler_params=params(12),
-        cost_estimate=cost(2.2),
+        cost_estimate=cost(2.5),
         name="finish",
     )(counts, *conv, kernel, left, right, top, bottom, grad)
 
@@ -800,14 +840,16 @@
     total = cells.shape[0]
     kernel = dw_kernel.transpose(1, 0, 2)
 
-    left, right = lon_halo(*side_cols(cells))
+    first, last = side_cols(cells)
+    left, right = lon_halo(first, last)
+    grad, w_expand, w_reduce = after((grad, w_expand, w_reduce), first, last)
     rows = mask_rows(counts, grad)
     expand, reduce, expand_t, bias = arrange(w_expand[0], w_reduce[0], b_expand)
-    conv = inner_conv(after(cells, rows), kernel, False, (0,))
+    conv = inner_conv(after(cells, rows), kernel, (0,))
     left, right = after((left, right), rows, bias, conv)
     up, down = side_rows(cells, left, right)
     top, bottom = lat_halo(up, down)
-    conv += inner_conv(after(cells, up, down), kernel, False, (1, 2))
+    conv += inner_conv(after(cells, up, down), kernel, (1, 2))
     unit, spread, normed = normalise(
         conv, kernel, left, right, top, bottom, dw_bias, norm_gain, norm_bias
     )
@@ -816,25 +858,26 @@
     sent, far_pre = hidden_far(*inputs)
     arrived = lax.ppermute(sent, "lat", [(i, i ^ 1) for i in range(8)])
     sums, near_pre = near_first(*inputs)
-    one, two = near_sends(sums, arrived)
+    two, one = near_sends(sums, arrived)
+    part_two = lax.ppermute(two, every_axis, plane_pairs(2, True))
     part_one = lax.ppermute(one, every_axis, plane_pairs(1, True))
-    part_two = lax.ppermute(two, every_axis, plane_pairs(2, True))
     own, three, near_pre = near_last(*inputs, arrived, after(near_pre, one, two))
     part_three = lax.ppermute(three, every_axis, plane_pairs(3, True))
 
-    far_pre, part_one, part_two = after((far_pre, part_one, part_two), three)
+    far_pre, part_one = after((far_pre, part_one), three)
     conv_grad, first, last = norm_back(expand_t, far_pre, near_pre, unit, spread, norm_gain)
+    first, last, part_two = after((first, last, part_two))
     left, right = lon_halo(first, last)
     own, parts = after((own, (part_one, part_two, part_three)), first, last)
     own, *sent = split_four(own, parts)
     parts = [lax.ppermute(s, every_axis, plane_pairs(i + 1, False)) for i, s in enumerate(sent)]
-    back = inner_conv(after(conv_grad, sent), kernel, True, (0, 1))
+    back = back_conv(after(conv_grad, sent), kernel, (0, 1))
     up, down = side_rows(*after((conv_grad, left, right), back))
 
     own, *sent = split_ring(*after((own, parts), up, down))
     parts = [lax.ppermute(s, every_axis, ring_pairs(i + 1)) for i, s in enumerate(sent)]
     top, bottom = lat_halo(up, down)
-    back += inner_conv(after(conv_grad, sent), kernel, True, (2,))
+    back += back_conv(after(conv_grad, sent), kernel, (2,))
 
     own, sent = split_two(*after((own, parts), back, top, bottom))
     arrived = lax.ppermute(sent, every_axis, last_pairs())

time: 77.3 us -> 72.9 us (0.943)
  Pallas kernels: 36.7 us -> 33.5 us
  starting transfers between devices: 30.8 us -> 29.4 us
    ppermute x3, waiting for transfers between devices: 0.19 us -> 3.51 us  [local(): lax.ppermute(s, every_axis, ring_pairs(i + 1))]
    pallas_call x4, Pallas kernels: 13.2 us -> 10.6 us  [the longest x2 6.6 us: inner_conv(): pl.pallas_call(functools.partial(inner_conv_body, parts), out_shape=(shap...]
    ppermute x2, waiting for transfers between devices: 3.42 us -> 0.96 us  [lat_halo(): top = lax.ppermute(down, 'lat', shifted('lat', 1))]
    ppermute x2, starting transfers between devices: 1.8 us -> 4.2 us  [lon_halo(): right = lax.ppermute(first, 'lon', shifted('lon', -1))]
    ppermute x2, starting transfers between devices: 3.31 us -> 0.99 us  [lon_halo(): left = lax.ppermute(last, 'lon', shifted('lon', 1))]
    ppermute x1, waiting for transfers between devices: 3.66 us -> 1.6 us  [local(): part_two = lax.ppermute(two, every_axis, plane_pairs(2, True))]
    ppermute x3, waiting for transfers between devices: 0.01 us -> 1.2 us  [local(): lax.ppermute(s, every_axis, plane_pairs(i + 1, False))]
    ppermute x1, starting transfers between devices: 2.3 us -> 1.11 us  [local(): arrived = lax.ppermute(sent, every_axis, last_pairs())]
  transfers between devices with their start and end apart: 19 -> 19, of which waited for: 6 -> 8; matrix products, arithmetic and copies ran while one was open for 0% -> 0% of each run, Pallas kernels for 35% -> 32%
where the time goes in v7:
time: 72.9 us; the launch traced here: 72.6 us
  Pallas kernels  33.5 us (46%)
  starting transfers between devices  29.4 us (40%)
  waiting for transfers between devices  8.37 us (11%)
  between operations  0.89 us (1%)
    ppermute x3, starting transfers between devices, local(): lax.ppermute(s, every_axis, ring_pairs(i + 1))  10.5 us
    pallas_call x2, Pallas kernels, inner_conv(): pl.pallas_call(functools.partial(inner_conv_body, parts), out_shape=(shap...  6.6 us
    ppermute x3, starting transfers between devices, local(): lax.ppermute(s, every_axis, plane_pairs(i + 1, False))  5.44 us
    pallas_call x1, Pallas kernels, hidden_far(): pl.pallas_call(far_body, out_shape=(jax.ShapeDtypeStruct((half, 2 * chann...  5.17 us
    ppermute x2, starting transfers between devices, lon_halo(): right = lax.ppermute(first, 'lon', shifted('lon', -1))  4.2 us
    pallas_call x2, Pallas kernels, back_conv(): pl.pallas_call(functools.partial(back_conv_body, parts), out_shape=(shape...  4 us
    ppermute x3, waiting for transfers between devices, local(): lax.ppermute(s, every_axis, ring_pairs(i + 1))  3.51 us
    ppermute x1, starting transfers between devices, local(): part_two = lax.ppermute(two, every_axis, plane_pairs(2, True))  3.37 us
  transfers between devices with their start and end apart: 19, of which 8 were waited for; matrix products, arithmetic and copies ran while one was open for 0% of the time, Pallas kernels for 32%

profile of v7, /device:TPU:32, one launch (start us, length us, event | category | flops | bytes accessed | tf_op | source)
XLA Modules:
  0.0 72.6 jit_solution(16176925331851027011)
XLA Ops:
  0.7 2.1 %side_cols.1 = (bf16[3,32,384]{2,1,0:T(8,128)(2,1)}, bf16[3,32,384]{2,1,0:T(8,128)(2,1)}) custom-call(f32[32,32,384]{2,1,0:T(8,128)} %bitcast.10), custom_call_target="tpu_custom_call" | custom-call | flops 1150000000 | bytes 1048576 | tf_op jit(solution)/shard_map/side_cols/pallas_call | solution.py:169
  2.7 1.1 %collective-permute-start.1 = (bf16[3,32,384]{2,1,0:T(8,128)(2,1)}, bf16[3,32,384]{2,1,0:T(8,128)(2,1)S(1)}, u32[]{:S(2)}, u32[]{:S(2)}) collective-permute-start(bf16[3,32,384]{2,1,0:T(8,128)(2,1)} %get-tuple-element.75), channel_id=1, source_target_pairs={{0,15},{1,0},{2,1},{3,2},{4,3},{5,4},{6,5},{7,6},{8,7},{9,8},{10,9... | collective-permute-start | bytes 221192 | tf_op jit(solution)/shard_map/ppermute | solution.py:820
  3.8 1.0 %collective-permute-start = (bf16[3,32,384]{2,1,0:T(8,128)(2,1)}, bf16[3,32,384]{2,1,0:T(8,128)(2,1)S(1)}, u32[]{:S(2)}, u32[]{:S(2)}) collective-permute-start(bf16[3,32,384]{2,1,0:T(8,128)(2,1)} %get-tuple-element.76), channel_id=1, source_target_pairs={{0,1},{1,2},{2,3},{3,4},{4,5},{5,6},{6,7},{7,8},{8,9},{9,10},{10,1... | collective-permute-start | bytes 221192 | tf_op jit(solution)/shard_map/ppermute | solution.py:819
  4.8 1.0 %mask_rows.1.refs_1_ = bf16[1024,384]{1,0:T(8,128)(2,1)S(1)} custom-call(s32[4,4]{1,0:T(4,128)S(1)} %copy-done.7, f32[1024,384]{1,0:T(8,128)S(1)} %bitcast.14), custom_call_target="tpu_custom_call" | custom-call | flops 1035000000 | bytes 1048576 | tf_op jit(solution)/shard_map/mask_rows/pallas_call | solution.py:369
  6.2 2.2 %inner_conv.2.conv0_ref = f32[1024,128]{1,0:T(8,128)S(1)} custom-call(f32[1024,384]{1,0:T(8,128)S(1)} %bitcast.11, f32[49,1,384]{2,1,0:T(1,128)S(1)} %bitcast.21), custom_call_target="tpu_custom_call" | custom-call | flops 2529999872 | bytes 1048576 | tf_op jit(solution)/shard_map/inner_conv/pallas_call | solution.py:86
  8.5 1.5 %arrange.1 = (bf16[1536,384]{1,0:T(8,128)(2,1)S(1)}, bf16[1536,384]{1,0:T(8,128)(2,1)S(1)}, bf16[384,1536]{1,0:T(8,128)(2,1)S(1)}, f32[1536,128]{1,0:T(8,128)S(1)}) custom-call(bf16[1536,384]{1,0:T(8,128)(2,1)S(1)} %bitcast.19, bf16[1536,384]{1,0:T(8,128)(2,1)S(1)} %bitcast.20, f32[1,1536]{1,0:T(1,128)S(1)} %copy-done.6), custom_call_target="tpu_custom_call" | custom-call | flops 1724999936 | bytes 1048576 | tf_op jit(solution)/shard_map/arrange/pallas_call | solution.py:404
  10.1 1.9 %collective-permute-start.3 = (bf16[3,48,384]{2,1,0:T(8,128)(2,1)S(1)}, bf16[3,48,384]{2,1,0:T(8,128)(2,1)S(1)}, u32[]{:S(2)}, u32[]{:S(2)}) collective-permute-start(bf16[3,48,384]{2,1,0:T(8,128)(2,1)S(1)} %get-tuple-element.85), channel_id=1, source_target_pairs={{0,112},{16,0},{32,16},{48,32},{64,48},{80,64},{96,80},{112,96},{1... | collective-permute-start | bytes 331784 | tf_op jit(solution)/shard_map/ppermute | solution.py:826
  12.0 4.4 %inner_conv.3 = (f32[1024,128]{1,0:T(8,128)S(1)}, f32[1024,128]{1,0:T(8,128)S(1)}) custom-call(f32[1024,384]{1,0:T(8,128)S(1)} %bitcast.13, f32[49,1,384]{2,1,0:T(1,128)S(1)} %bitcast.22), custom_call_target="tpu_custom_call" | custom-call | flops 5059999744 | bytes 1048576 | tf_op jit(solution)/shard_map/inner_conv/pallas_call | solution.py:86
  16.4 1.0 %collective-permute-done.2.top_ref = bf16[3,48,384]{2,1,0:T(8,128)(2,1)S(1)} collective-permute-done((bf16[3,48,384]{2,1,0:T(8,128)(2,1)S(1)}, bf16[3,48,384]{2,1,0:T(8,128)(2,1)S(1)}, u32[]{:S(2)}, u32[]{:S(2)}) %collective-permute-start.2) | collective-permute-done | bytes 110624 | tf_op jit(solution)/shard_map/ppermute | solution.py:825
  17.4 2.0 %normalise.1 = (f32[1024,384]{1,0:T(8,128)S(1)}, f32[1024,128]{1,0:T(8,128)S(1)}, bf16[1024,384]{1,0:T(8,128)(2,1)S(1)}) custom-call(f32[1024,128]{1,0:T(8,128)S(1)} %inner_conv.2.conv0_ref, f32[1024,128]{1,0:T(8,128)S(1)} %get-tuple-element.88.conv1_ref, f32[1024,128]{1,0:T(8,128)S(1)} %get-tuple-element.89.conv2_ref, f32[49,1,384]{2,1,0:T(1,128)S(1)} %bitcast.23, ...), custom_call_target="tpu_custom_call" | custom-call | flops 3220000000 | bytes 1048576 | tf_op jit(solution)/shard_map/normalise/pallas_call | solution.py:317
  19.4 5.2 %hidden_far.1 = (bf16[768,768]{1,0:T(8,128)(2,1)S(1)}, bf16[768,1024]{1,0:T(8,128)(2,1)S(1)}) custom-call(bf16[1024,384]{1,0:T(8,128)(2,1)S(1)} %get-tuple-element.90.refs_0_, bf16[1024,384]{1,0:T(8,128)(2,1)S(1)} %mask_rows.1.refs_1_, bf16[1536,384]{1,0:T(8,128)(2,1)S(1)} %get-tuple-element.91.refs_2_, bf16[1536,384]{1,0:T(8,128)(2,1)S(1)} %get-tuple-element.92.refs_3_, ...), custom_call_target="tpu_custom_call" | custom-call | flops 6670000128 | bytes 1048576 | tf_op jit(solution)/shard_map/hidden_far/pallas_call | solution.py:493
  24.8 2.7 %near_first.1 = (f32[384,768]{1,0:T(8,128)S(1)}, bf16[768,1024]{1,0:T(8,128)(2,1)S(1)}) custom-call(bf16[1024,384]{1,0:T(8,128)(2,1)S(1)} %get-tuple-element.90.refs_0_, bf16[1024,384]{1,0:T(8,128)(2,1)S(1)} %mask_rows.1.refs_1_, bf16[1536,384]{1,0:T(8,128)(2,1)S(1)} %get-tuple-element.91.refs_2_, bf16[1536,384]{1,0:T(8,128)(2,1)S(1)} %get-tuple-element.92.refs_3_, ...), custom_call_target="tpu_custom_call" | custom-call | flops 3449999872 | bytes 1048576 | tf_op jit(solution)/shard_map/near_first/pallas_call | solution.py:523
  28.2 3.4 %collective-permute-start.6 = (bf16[192,768]{1,0:T(8,128)(2,1)S(1)}, bf16[192,768]{1,0:T(8,128)(2,1)S(1)}, u32[]{:S(2)}, u32[]{:S(2)}) collective-permute-start(bf16[192,768]{1,0:T(8,128)(2,1)S(1)} %get-tuple-element.98), channel_id=1, source_target_pairs={{0,64},{1,65},{2,66},{3,67},{4,68},{5,69},{6,70},{7,71},{8,72},{9,... | collective-permute-start | bytes 884744 | tf_op jit(solution)/shard_map/ppermute | solution.py:862
  31.6 2.7 %near_last.1 = (f32[192,768]{1,0:T(8,128)S(1)}, bf16[192,768]{1,0:T(8,128)(2,1)S(1)}, bf16[768,1024]{1,0:T(8,128)(2,1)S(1)}) custom-call(bf16[1024,384]{1,0:T(8,128)(2,1)S(1)} %get-tuple-element.90.refs_0_, bf16[1024,384]{1,0:T(8,128)(2,1)S(1)} %mask_rows.1.refs_1_, ...), custom_call_target="tpu_custom_call", output_to_operand_aliasing={{2}: (6, {})} | custom-call | flops 3449999872 | bytes 1048576 | tf_op jit(solution)/shard_map/near_last/pallas_call | solution.py:580
  34.3 0.7 collective-permute-start.7
  34.9 0.8 %collective-permute-done.5.first_ref = bf16[192,768]{1,0:T(8,128)(2,1)S(1)} collective-permute-done((bf16[192,768]{1,0:T(8,128)(2,1)S(1)}, bf16[192,768]{1,0:T(8,128)(2,1)S(1)}, u32[]{:S(2)}, u32[]{:S(2)}) %collective-permute-start.5) | collective-permute-done | bytes 294944 | tf_op jit(solution)/shard_map/ppermute | solution.py:863
  35.8 2.0 %norm_back.1 = (f32[32,32,384]{2,1,0:T(8,128)S(1)}, bf16[3,32,384]{2,1,0:T(8,128)(2,1)S(1)}, bf16[3,32,384]{2,1,0:T(8,128)(2,1)S(1)}) custom-call(bf16[384,1536]{1,0:T(8,128)(2,1)S(1)} %get-tuple-element.79.turned_ref, bf16[768,1024]{1,0:T(8,128)(2,1)S(1)} %get-tuple-element.101.other_ref, bf16[768,1024]{1,0:T(8,128)(2,1)S(1)} %get-tuple-element.102.mine_ref, ...), custom_call_target="tpu_custom_call" | custom-call | flops 230000000 | bytes 1048576 | tf_op jit(solution)/shard_map/norm_back/pallas_call | solution.py:627
  37.8 1.6 %collective-permute-done.6.second_ref = bf16[192,768]{1,0:T(8,128)(2,1)S(1)} collective-permute-done((bf16[192,768]{1,0:T(8,128)(2,1)S(1)}, bf16[192,768]{1,0:T(8,128)(2,1)S(1)}, u32[]{:S(2)}, u32[]{:S(2)}) %collective-permute-start.6) | collective-permute-done | bytes 294944 | tf_op jit(solution)/shard_map/ppermute | solution.py:862
  39.4 3.1 %collective-permute-start.12 = (bf16[3,32,384]{2,1,0:T(8,128)(2,1)S(1)}, bf16[3,32,384]{2,1,0:T(8,128)(2,1)S(1)}, u32[]{:S(2)}, u32[]{:S(2)}) collective-permute-start(bf16[3,32,384]{2,1,0:T(8,128)(2,1)S(1)} %get-tuple-element.111), channel_id=1, source_target_pairs={{0,15},{1,0},{2,1},{3,2},{4,3},{5,4},{6,5},{7,6},{8,7},{9,8},{10,9... | collective-permute-start | bytes 221192 | tf_op jit(solution)/shard_map/ppermute | solution.py:820
  42.7 2.3 %collective-permute-start.8 = (bf16[48,768]{1,0:T(8,128)(2,1)S(1)}, bf16[48,768]{1,0:T(8,128)(2,1)S(1)}, u32[]{:S(2)}, u32[]{:S(2)}) collective-permute-start(bf16[48,768]{1,0:T(8,128)(2,1)S(1)} %get-tuple-element.117), channel_id=1, source_target_pairs={{0,1},{1,128},{2,3},{3,130},{4,5},{5,132},{6,7},{7,134},{8,9},{9,1... | collective-permute-start | bytes 221192 | tf_op jit(solution)/shard_map/ppermute | solution.py:873
  45.0 2.7 %collective-permute-start.9 = (bf16[48,768]{1,0:T(8,128)(2,1)S(1)}, bf16[48,768]{1,0:T(8,128)(2,1)S(1)}, u32[]{:S(2)}, u32[]{:S(2)}) collective-permute-start(bf16[48,768]{1,0:T(8,128)(2,1)S(1)} %get-tuple-element.118), channel_id=1, source_target_pairs={{0,128},{1,129},{2,130},{3,131},{4,132},{5,133},{6,134},{7,135},{8... | collective-permute-start | bytes 221192 | tf_op jit(solution)/shard_map/ppermute | solution.py:873
  48.1 2.7 %back_conv.2 = (f32[1024,128]{1,0:T(8,128)S(1)}, f32[1024,128]{1,0:T(8,128)S(1)}) custom-call(f32[1024,384]{1,0:T(8,128)S(1)} %bitcast.16, f32[49,1,384]{2,1,0:T(1,128)S(1)} %bitcast.24), custom_call_target="tpu_custom_call" | custom-call | flops 3449999872 | bytes 1048576 | tf_op jit(solution)/shard_map/back_conv/pallas_call | solution.py:136
  50.9 1.2 %collective-permute-done.10.third_ref = bf16[48,768]{1,0:T(8,128)(2,1)S(1)} collective-permute-done((bf16[48,768]{1,0:T(8,128)(2,1)S(1)}, bf16[48,768]{1,0:T(8,128)(2,1)S(1)}, u32[]{:S(2)}, u32[]{:S(2)}) %collective-permute-start.10) | collective-permute-done | bytes 73760 | tf_op jit(solution)/shard_map/ppermute | solution.py:873
  52.2 5.8 %collective-permute-start.15 = (f32[12,768]{1,0:T(8,128)S(1)}, f32[12,768]{1,0:T(8,128)S(1)}, u32[]{:S(2)}, u32[]{:S(2)}) collective-permute-start(f32[12,768]{1,0:T(8,128)S(1)} %get-tuple-element.133), channel_id=1, source_target_pairs={{0,4},{1,5},{2,6},{3,7},{4,8},{5,9},{6,10},{7,11},{8,12},{9,13},{1... | collective-permute-start | bytes 110600 | tf_op jit(solution)/shard_map/ppermute | solution.py:878
  57.9 4.5 %collective-permute-start.16 = (f32[12,768]{1,0:T(8,128)S(1)}, f32[12,768]{1,0:T(8,128)S(1)}, u32[]{:S(2)}, u32[]{:S(2)}) collective-permute-start(f32[12,768]{1,0:T(8,128)S(1)} %get-tuple-element.134), channel_id=1, source_target_pairs={{0,8},{1,9},{2,10},{3,11},{4,12},{5,13},{6,14},{7,15},{8,0},{9,1},... | collective-permute-start | bytes 110600 | tf_op jit(solution)/shard_map/ppermute | solution.py:878
  62.7 0.5 collective-permute-start.13
  63.2 1.3 %back_conv.3.conv2_ref = f32[1024,128]{1,0:T(8,128)S(1)} custom-call(f32[1024,384]{1,0:T(8,128)S(1)} %bitcast.18, f32[49,1,384]{2,1,0:T(1,128)S(1)} %bitcast.25), custom_call_target="tpu_custom_call" | custom-call | flops 1724999936 | bytes 1048576 | tf_op jit(solution)/shard_map/back_conv/pallas_call | solution.py:136
  64.5 2.5 %collective-permute-done.16.refs_1_ = f32[12,768]{1,0:T(8,128)S(1)} collective-permute-done((f32[12,768]{1,0:T(8,128)S(1)}, f32[12,768]{1,0:T(8,128)S(1)}, u32[]{:S(2)}, u32[]{:S(2)}) %collective-permute-start.16) | collective-permute-done | bytes 36896 | tf_op jit(solution)/shard_map/ppermute | solution.py:878
  67.0 1.0 %collective-permute-done.17.refs_2_ = f32[12,768]{1,0:T(8,128)S(1)} collective-permute-done((f32[12,768]{1,0:T(8,128)S(1)}, f32[12,768]{1,0:T(8,128)S(1)}, u32[]{:S(2)}, u32[]{:S(2)}) %collective-permute-start.17) | collective-permute-done | bytes 36896 | tf_op jit(solution)/shard_map/ppermute | solution.py:878
  68.1 1.1 %collective-permute-start.18 = (f32[6,768]{1,0:T(8,128)S(1)}, f32[6,768]{1,0:T(8,128)S(1)}, u32[]{:S(2)}, u32[]{:S(2)}) collective-permute-start(f32[6,768]{1,0:T(8,128)S(1)} %get-tuple-element.142), channel_id=1, source_target_pairs={{0,2},{1,3},{2,0},{3,1},{4,6},{5,7},{6,4},{7,5},{8,10},{9,11},{10,... | collective-permute-start | bytes 55304 | tf_op jit(solution)/shard_map/ppermute | solution.py:883
  69.2 2.7 %finish.1 = f32[1024,384]{1,0:T(8,128)} custom-call(s32[4,4]{1,0:T(4,128)S(1)} %copy-done.7, f32[1024,128]{1,0:T(8,128)S(1)} %get-tuple-element.121.conv0_ref, f32[1024,128]{1,0:T(8,128)S(1)} %get-tuple-element.122.conv1_ref, f32[1024,128]{1,0:T(8,128)S(1)} %back_conv.3.conv2_ref, f32[49,1,384]{2,1,0:T(1,128)S(1)} %bitcast.26, ...), custom_call_target="tpu_custom_call" | custom-call | flops 2875000064 | bytes 1048576 | tf_op jit(solution)/shard_map/finish/pallas_call | solution.py:665
  72.0 0.6 last_sum.1
  (46 shorter events, 2.5 us)
Async XLA Ops:
  0.6 4.2 %copy-start.2 = (f32[1,32,32,384]{3,2,1,0:T(8,128)S(1)}, f32[1,32,32,384]{3,2,1,0:T(8,128)}, u32[]{:S(2)}) copy-start(f32[1,32,32,384]{3,2,1,0:T(8,128)} %param.11) | copy-start | bytes 4718596
  0.6 4.2 %copy-start.7 = (s32[4,4]{1,0:T(4,128)S(1)}, s32[4,4]{1,0:T(4,128)}, u32[]{:S(2)}) copy-start(s32[4,4]{1,0:T(4,128)} %counts_ref.3) | copy-start | bytes 196
  2.7 7.3 %collective-permute-start.1 = (bf16[3,32,384]{2,1,0:T(8,128)(2,1)}, bf16[3,32,384]{2,1,0:T(8,128)(2,1)S(1)}, u32[]{:S(2)}, u32[]{:S(2)}) collective-permute-start(bf16[3,32,384]{2,1,0:T(8,128)(2,1)} %get-tuple-element.75), channel_id=1, source_target_pairs={{0,15},{1,0},{2,1},{3,2},{4,3},{5,4},{6,5},{7,6},{8,7},{9,8},{10,9... | collective-permute-start | bytes 221192 | tf_op jit(solution)/shard_map/ppermute | solution.py:820
  3.8 6.2 %collective-permute-start = (bf16[3,32,384]{2,1,0:T(8,128)(2,1)}, bf16[3,32,384]{2,1,0:T(8,128)(2,1)S(1)}, u32[]{:S(2)}, u32[]{:S(2)}) collective-permute-start(bf16[3,32,384]{2,1,0:T(8,128)(2,1)} %get-tuple-element.76), channel_id=1, source_target_pairs={{0,1},{1,2},{2,3},{3,4},{4,5},{5,6},{6,7},{7,8},{8,9},{9,10},{10,1... | collective-permute-start | bytes 221192 | tf_op jit(solution)/shard_map/ppermute | solution.py:819
  4.8 1.4 %copy-start.1 = (f32[1,32,32,384]{3,2,1,0:T(8,128)S(1)}, f32[1,32,32,384]{3,2,1,0:T(8,128)}, u32[]{:S(2)}) copy-start(f32[1,32,32,384]{3,2,1,0:T(8,128)} %param.10) | copy-start | bytes 4718596
  4.8 1.4 %copy-start.5 = (f32[1,49,384]{2,0,1:T(1,128)S(1)}, f32[1,49,384]{2,0,1:T(1,128)}, u32[]{:S(2)}) copy-start(f32[1,49,384]{2,0,1:T(1,128)} %param.13) | copy-start | bytes 225796
  6.2 2.2 %copy-start.3 = (bf16[1,1536,384]{2,1,0:T(8,128)(2,1)S(1)}, bf16[1,1536,384]{2,1,0:T(8,128)(2,1)}, u32[]{:S(2)}) copy-start(bf16[1,1536,384]{2,1,0:T(8,128)(2,1)} %param.17) | copy-start | bytes 3538948
  6.2 2.2 %copy-start.4 = (bf16[1,1536,384]{2,1,0:T(8,128)(2,1)S(1)}, bf16[1,1536,384]{2,1,0:T(8,128)(2,1)}, u32[]{:S(2)}) copy-start(bf16[1,1536,384]{2,1,0:T(8,128)(2,1)} %param.19) | copy-start | bytes 3538948
  6.2 2.2 %copy-start.6 = (f32[1,1536]{1,0:T(1,128)S(1)}, f32[1,1536]{1,0:T(1,128)}, u32[]{:S(2)}) copy-start(f32[1,1536]{1,0:T(1,128)} %bias_ref.2) | copy-start | bytes 18436
  10.1 6.3 %collective-permute-start.3 = (bf16[3,48,384]{2,1,0:T(8,128)(2,1)S(1)}, bf16[3,48,384]{2,1,0:T(8,128)(2,1)S(1)}, u32[]{:S(2)}, u32[]{:S(2)}) collective-permute-start(bf16[3,48,384]{2,1,0:T(8,128)(2,1)S(1)} %get-tuple-element.85), channel_id=1, source_target_pairs={{0,112},{16,0},{32,16},{48,32},{64,48},{80,64},{96,80},{112,96},{1... | collective-permute-start | bytes 331784 | tf_op jit(solution)/shard_map/ppermute | solution.py:826
  12.0 5.4 %copy-start = (f32[1,384]{1,0:T(1,128)S(1)}, f32[1,384]{1,0:T(1,128)}, u32[]{:S(2)}) copy-start(f32[1,384]{1,0:T(1,128)} %gain_ref.3) | copy-start | bytes 4612
  12.0 5.4 %copy-start.8 = (f32[1,384]{1,0:T(1,128)S(1)}, f32[1,384]{1,0:T(1,128)}, u32[]{:S(2)}) copy-start(f32[1,384]{1,0:T(1,128)} %bias_ref.3) | copy-start | bytes 4612
  12.0 5.4 %copy-start.9 = (f32[1,384]{1,0:T(1,128)S(1)}, f32[1,384]{1,0:T(1,128)}, u32[]{:S(2)}) copy-start(f32[1,384]{1,0:T(1,128)} %shift_ref.1) | copy-start | bytes 4612
  12.0 5.4 %collective-permute-start.2 = (bf16[3,48,384]{2,1,0:T(8,128)(2,1)S(1)}, bf16[3,48,384]{2,1,0:T(8,128)(2,1)S(1)}, u32[]{:S(2)}, u32[]{:S(2)}) collective-permute-start(bf16[3,48,384]{2,1,0:T(8,128)(2,1)S(1)} %get-tuple-element.86), channel_id=1, source_target_pairs={{0,16},{16,32},{32,48},{48,64},{64,80},{80,96},{96,112},{112,0},{1... | collective-permute-start | bytes 331784 | tf_op jit(solution)/shard_map/ppermute | solution.py:825
  24.5 3.1 %collective-permute-start.4 = (bf16[768,768]{1,0:T(8,128)(2,1)S(1)}, bf16[768,768]{1,0:T(8,128)(2,1)S(1)}, u32[]{:S(2)}, u32[]{:S(2)}) collective-permute-start(bf16[768,768]{1,0:T(8,128)(2,1)S(1)} %get-tuple-element.95), channel_id=1, source_target_pairs={{0,16},{16,0},{32,48},{48,32},{64,80},{80,64},{96,112},{112,96},{1... | collective-permute-start | bytes 3538952 | tf_op jit(solution)/shard_map/ppermute | solution.py:859
  27.8 8.0 %collective-permute-start.5 = (bf16[192,768]{1,0:T(8,128)(2,1)S(1)}, bf16[192,768]{1,0:T(8,128)(2,1)S(1)}, u32[]{:S(2)}, u32[]{:S(2)}) collective-permute-start(bf16[192,768]{1,0:T(8,128)(2,1)S(1)} %get-tuple-element.96), channel_id=1, source_target_pairs={{0,32},{1,33},{2,34},{3,35},{4,36},{5,37},{6,38},{7,39},{8,40},{9,... | collective-permute-start | bytes 884744 | tf_op jit(solution)/shard_map/ppermute | solution.py:863
  28.2 11.2 %collective-permute-start.6 = (bf16[192,768]{1,0:T(8,128)(2,1)S(1)}, bf16[192,768]{1,0:T(8,128)(2,1)S(1)}, u32[]{:S(2)}, u32[]{:S(2)}) collective-permute-start(bf16[192,768]{1,0:T(8,128)(2,1)S(1)} %get-tuple-element.98), channel_id=1, source_target_pairs={{0,64},{1,65},{2,66},{3,67},{4,68},{5,69},{6,70},{7,71},{8,72},{9,... | collective-permute-start | bytes 884744 | tf_op jit(solution)/shard_map/ppermute | solution.py:862
  34.3 8.2 %collective-permute-start.7 = (bf16[192,768]{1,0:T(8,128)(2,1)S(1)}, bf16[192,768]{1,0:T(8,128)(2,1)S(1)}, u32[]{:S(2)}, u32[]{:S(2)}) collective-permute-start(bf16[192,768]{1,0:T(8,128)(2,1)S(1)} %get-tuple-element.100), channel_id=1, source_target_pairs={{0,96},{1,97},{2,98},{3,99},{4,100},{5,101},{6,102},{7,103},{8,104... | collective-permute-start | bytes 884744 | tf_op jit(solution)/shard_map/ppermute | solution.py:865
  39.4 11.3 %collective-permute-start.12 = (bf16[3,32,384]{2,1,0:T(8,128)(2,1)S(1)}, bf16[3,32,384]{2,1,0:T(8,128)(2,1)S(1)}, u32[]{:S(2)}, u32[]{:S(2)}) collective-permute-start(bf16[3,32,384]{2,1,0:T(8,128)(2,1)S(1)} %get-tuple-element.111), channel_id=1, source_target_pairs={{0,15},{1,0},{2,1},{3,2},{4,3},{5,4},{6,5},{7,6},{8,7},{9,8},{10,9... | collective-permute-start | bytes 221192 | tf_op jit(solution)/shard_map/ppermute | solution.py:820
  42.5 8.3 %collective-permute-start.11 = (bf16[3,32,384]{2,1,0:T(8,128)(2,1)S(1)}, bf16[3,32,384]{2,1,0:T(8,128)(2,1)S(1)}, u32[]{:S(2)}, u32[]{:S(2)}) collective-permute-start(bf16[3,32,384]{2,1,0:T(8,128)(2,1)S(1)} %get-tuple-element.112), channel_id=1, source_target_pairs={{0,1},{1,2},{2,3},{3,4},{4,5},{5,6},{6,7},{7,8},{8,9},{9,10},{10,1... | collective-permute-start | bytes 221192 | tf_op jit(solution)/shard_map/ppermute | solution.py:819
  42.7 8.2 %collective-permute-start.8 = (bf16[48,768]{1,0:T(8,128)(2,1)S(1)}, bf16[48,768]{1,0:T(8,128)(2,1)S(1)}, u32[]{:S(2)}, u32[]{:S(2)}) collective-permute-start(bf16[48,768]{1,0:T(8,128)(2,1)S(1)} %get-tuple-element.117), channel_id=1, source_target_pairs={{0,1},{1,128},{2,3},{3,130},{4,5},{5,132},{6,7},{7,134},{8,9},{9,1... | collective-permute-start | bytes 221192 | tf_op jit(solution)/shard_map/ppermute | solution.py:873
  45.0 5.9 %collective-permute-start.9 = (bf16[48,768]{1,0:T(8,128)(2,1)S(1)}, bf16[48,768]{1,0:T(8,128)(2,1)S(1)}, u32[]{:S(2)}, u32[]{:S(2)}) collective-permute-start(bf16[48,768]{1,0:T(8,128)(2,1)S(1)} %get-tuple-element.118), channel_id=1, source_target_pairs={{0,128},{1,129},{2,130},{3,131},{4,132},{5,133},{6,134},{7,135},{8... | collective-permute-start | bytes 221192 | tf_op jit(solution)/shard_map/ppermute | solution.py:873
  47.7 4.4 %collective-permute-start.10 = (bf16[48,768]{1,0:T(8,128)(2,1)S(1)}, bf16[48,768]{1,0:T(8,128)(2,1)S(1)}, u32[]{:S(2)}, u32[]{:S(2)}) collective-permute-start(bf16[48,768]{1,0:T(8,128)(2,1)S(1)} %get-tuple-element.119), channel_id=1, source_target_pairs={{0,129},{1,0},{2,131},{3,2},{4,133},{5,4},{6,135},{7,6},{8,137},{9... | collective-permute-start | bytes 221192 | tf_op jit(solution)/shard_map/ppermute | solution.py:873
  52.2 12.4 %collective-permute-start.15 = (f32[12,768]{1,0:T(8,128)S(1)}, f32[12,768]{1,0:T(8,128)S(1)}, u32[]{:S(2)}, u32[]{:S(2)}) collective-permute-start(f32[12,768]{1,0:T(8,128)S(1)} %get-tuple-element.133), channel_id=1, source_target_pairs={{0,4},{1,5},{2,6},{3,7},{4,8},{5,9},{6,10},{7,11},{8,12},{9,13},{1... | collective-permute-start | bytes 110600 | tf_op jit(solution)/shard_map/ppermute | solution.py:878
  57.9 9.1 %collective-permute-start.16 = (f32[12,768]{1,0:T(8,128)S(1)}, f32[12,768]{1,0:T(8,128)S(1)}, u32[]{:S(2)}, u32[]{:S(2)}) collective-permute-start(f32[12,768]{1,0:T(8,128)S(1)} %get-tuple-element.134), channel_id=1, source_target_pairs={{0,8},{1,9},{2,10},{3,11},{4,12},{5,13},{6,14},{7,15},{8,0},{9,1},... | collective-permute-start | bytes 110600 | tf_op jit(solution)/shard_map/ppermute | solution.py:878
  62.4 5.6 %collective-permute-start.17 = (f32[12,768]{1,0:T(8,128)S(1)}, f32[12,768]{1,0:T(8,128)S(1)}, u32[]{:S(2)}, u32[]{:S(2)}) collective-permute-start(f32[12,768]{1,0:T(8,128)S(1)} %get-tuple-element.135), channel_id=1, source_target_pairs={{0,12},{1,13},{2,14},{3,15},{4,0},{5,1},{6,2},{7,3},{8,4},{9,5},{1... | collective-permute-start | bytes 110600 | tf_op jit(solution)/shard_map/ppermute | solution.py:878
  62.6 5.4 %collective-permute-start.14 = (bf16[3,48,384]{2,1,0:T(8,128)(2,1)S(1)}, bf16[3,48,384]{2,1,0:T(8,128)(2,1)S(1)}, u32[]{:S(2)}, u32[]{:S(2)}) collective-permute-start(bf16[3,48,384]{2,1,0:T(8,128)(2,1)S(1)} %get-tuple-element.127), channel_id=1, source_target_pairs={{0,112},{16,0},{32,16},{48,32},{64,48},{80,64},{96,80},{112,96},{1... | collective-permute-start | bytes 331784 | tf_op jit(solution)/shard_map/ppermute | solution.py:826
  62.7 5.4 %collective-permute-start.13 = (bf16[3,48,384]{2,1,0:T(8,128)(2,1)S(1)}, bf16[3,48,384]{2,1,0:T(8,128)(2,1)S(1)}, u32[]{:S(2)}, u32[]{:S(2)}) collective-permute-start(bf16[3,48,384]{2,1,0:T(8,128)(2,1)S(1)} %get-tuple-element.128), channel_id=1, source_target_pairs={{0,16},{16,32},{32,48},{48,64},{64,80},{80,96},{96,112},{112,0},{1... | collective-permute-start | bytes 331784 | tf_op jit(solution)/shard_map/ppermute | solution.py:825
  68.1 3.9 %collective-permute-start.18 = (f32[6,768]{1,0:T(8,128)S(1)}, f32[6,768]{1,0:T(8,128)S(1)}, u32[]{:S(2)}, u32[]{:S(2)}) collective-permute-start(f32[6,768]{1,0:T(8,128)S(1)} %get-tuple-element.142), channel_id=1, source_target_pairs={{0,2},{1,3},{2,0},{3,1},{4,6},{5,7},{6,4},{7,5},{8,10},{9,11},{10,... | collective-permute-start | bytes 55304 | tf_op jit(solution)/shard_map/ppermute | solution.py:883

commit v8 on v7

--- a/solution.py
+++ b/solution.py
@@ -53,31 +53,32 @@
     outs, padded = refs[:-1], refs[-1]
     edge = reach * side
     total = side * side
+    group = 4
     padded[0:edge] = jnp.zeros((edge, lanes), f32)
     padded[edge + total : 2 * edge + total] = jnp.zeros((edge, lanes), f32)
     for part, out_ref in zip(parts, outs):
         cols = slice(part * lanes, (part + 1) * lanes)
         padded[edge : edge + total] = cells_ref[:, cols]
 
-        def two_rows(i, carry):
-            base = pl.multiple_of(i * (2 * side), 2 * side)
-            rows = [padded[pl.ds(base + p * side, side), :] for p in range(8)]
-            results = [None, None]
+        def some_rows(i, carry):
+            base = pl.multiple_of(i * (group * side), group * side)
+            rows = [padded[pl.ds(base + p * side, side), :] for p in range(6 + group)]
+            results = [None] * group
             for q in range(7):
-                sums = [None, None]
+                sums = [None] * group
                 for p in range(7):
                     tap = tap_row(kernel_ref, False, p, q, cols)
-                    for g in range(2):
+                    for g in range(group):
                         term = tap * rows[p + g]
                         sums[g] = term if sums[g] is None else sums[g] + term
-                for g in range(2):
+                for g in range(group):
                     moved = shift_cols(sums[g], q - reach)
                     results[g] = moved if results[g] is None else results[g] + moved
-            for g in range(2):
+            for g in range(group):
                 out_ref[pl.ds(base + g * side, side), :] = results[g]
             return carry
 
-        lax.fori_loop(0, side // 2, two_rows, 0)
+        lax.fori_loop(0, side // group, some_rows, 0)
 
 
 def inner_conv(cells, kernel, parts):
@@ -361,7 +362,7 @@
         rows_ref[at, :] = masked_row(i, grad_ref[at, :], counts_ref).astype(bf16)
         return carry
 
-    lax.fori_loop(0, side, step, 0, unroll=2)
+    lax.fori_loop(0, side, step, 0, unroll=side)
 
 
 def mask_rows(counts, grad):
@@ -378,23 +379,27 @@
 
 
 def arrange_body(expand_ref, reduce_ref, bias_ref, expand_out, reduce_out, turned_out, bias_out):
-    unit_row = lax.broadcasted_iota(jnp.int32, (48, 96), 0)
-    unit_col = lax.broadcasted_iota(jnp.int32, (48, 96), 1)
-    picks = [unit_col == (unit_row // 6) * 12 + lo * 6 + unit_row % 6 for lo in range(2)]
-    chosen = [pick.astype(f32).astype(bf16) for pick in picks]
+    channels = expand_ref.shape[1]
+    new = lax.broadcasted_iota(jnp.int32, (96, 96), 0)
+    old = lax.broadcasted_iota(jnp.int32, (96, 96), 1)
+    lo, rest = new // 48, new % 48
+    pick = old == (rest // 6) * 12 + lo * 6 + rest % 6
+    chosen = pick.astype(f32).astype(bf16)
     for hi, y, core in itertools.product(range(2), range(4), range(2)):
         unit = (hi * 4 + y) * 2 + core
         at = slice(unit * 96, (unit + 1) * 96)
-        expand, reduce = expand_ref[at, :], reduce_ref[at, :]
-        bias = bias_ref[:, at]
-        for lo in range(2):
-            x = 2 * hi + lo
+        both = jnp.concatenate([expand_ref[at, :], reduce_ref[at, :]], axis=1)
+        moved = jnp.dot(chosen, both, preferred_element_type=f32).astype(bf16)
+        column = jnp.sum(jnp.where(pick, bias_ref[:, at], 0.0), axis=1, keepdims=True)
+        column = jnp.broadcast_to(column, (96, lanes))
+        for lo_place in range(2):
+            x = 2 * hi + lo_place
             place = core * 16 + (y * 4 + x if core == 0 else x * 4 + y)
             to = slice(place * 48, (place + 1) * 48)
-            expand_out[to, :] = jnp.dot(chosen[lo], expand, preferred_element_type=f32).astype(bf16)
-            reduce_out[to, :] = jnp.dot(chosen[lo], reduce, preferred_element_type=f32).astype(bf16)
-            column = jnp.sum(jnp.where(picks[lo], bias, 0.0), axis=1, keepdims=True)
-            bias_out[to, :] = jnp.broadcast_to(column, (48, lanes))
+            half = slice(lo_place * 48, (lo_place + 1) * 48)
+            expand_out[to, :] = moved[half, :channels]
+            reduce_out[to, :] = moved[half, channels:]
+            bias_out[to, :] = column[half]
     turn(expand_out, turned_out)
 
 
@@ -452,39 +457,75 @@
     return lax.dot_general(left, right, (((1,), (1,)), ((), ())), preferred_element_type=f32)
 
 
-def hidden_rows(cells, sources, rows, grad_pre_ref, places):
-    normed_ref, grad_ref, expand_ref, reduce_ref, bias_ref = cells
-    total = normed_ref.shape[0]
-
-    def gather(ref):
-        return jnp.concatenate([ref[pl.ds(source, rows), :] for source in sources], axis=0)
-
-    preact = dot_rows(gather(expand_ref), normed_ref[...])
-    grad_hidden = dot_rows(gather(reduce_ref), grad_ref[...])
-    bias = jnp.concatenate([gather(bias_ref)] * (total // lanes), axis=1)
-    value, slope = gelu_pair(preact + bias)
-    hidden = value.astype(bf16)
-    grad_pre = (grad_hidden * slope).astype(bf16)
-    for n, place in enumerate(places):
-        grad_pre_ref[pl.ds(place, rows), :] = grad_pre[n * rows : (n + 1) * rows]
-    return (
-        jnp.dot(grad_pre, normed_ref[...], preferred_element_type=f32),
-        jnp.dot(hidden, grad_ref[...], preferred_element_type=f32),
-    )
+class HiddenBlock:
+
+    def __init__(self, cells, sources, rows, grad_pre_ref, places, scratch):
+        self.normed, self.grad, self.expand, self.reduce, self.bias = cells
+        self.sources, self.rows, self.places = sources, rows, places
+        self.grad_pre = grad_pre_ref
+        self.preact, self.grad_hidden, self.hidden, self.terms = scratch
+        self.total = self.normed.shape[0]
+
+    def gather(self, ref):
+        return jnp.concatenate([ref[pl.ds(s, self.rows), :] for s in self.sources], axis=0)
+
+    def dots(self, at):
+        self.preact[:, at] = dot_rows(self.gather(self.expand), self.normed[at, :])
+        self.grad_hidden[:, at] = dot_rows(self.gather(self.reduce), self.grad[at, :])
+
+    def activate(self, at):
+        bias = jnp.concatenate([self.gather(self.bias)] * ((at.stop - at.start) // lanes), axis=1)
+        value, slope = gelu_pair(self.preact[:, at] + bias)
+        self.hidden[:, at] = value.astype(bf16)
+        grad_pre = (self.grad_hidden[:, at] * slope).astype(bf16)
+        self.terms[:, at] = grad_pre
+        for n, place in enumerate(self.places):
+            self.grad_pre[pl.ds(place, self.rows), at] = grad_pre[n * self.rows : (n + 1) * self.rows]
+
+    def expand_sum(self):
+        return jnp.dot(self.terms[...], self.normed[...], preferred_element_type=f32)
+
+    def reduce_sum(self):
+        return jnp.dot(self.hidden[...], self.grad[...], preferred_element_type=f32)
+
+
+def hidden_scratch(rows, total):
+    return [
+        pltpu.VMEM((rows, total), f32),
+        pltpu.VMEM((rows, total), f32),
+        pltpu.VMEM((rows, total), bf16),
+        pltpu.VMEM((rows, total), bf16),
+    ]
 
 
 def far_body(*refs):
-    cells, (sent_ref, grad_pre_ref) = refs[:5], refs[5:]
-    half = grad_pre_ref.shape[0]
+    cells, (sent_ref, grad_pre_ref), scratch = refs[:5], refs[5:7], refs[7:]
+    half, total = grad_pre_ref.shape
     channels = refs[0].shape[1]
     base = (1 - own_place()[0]) * half
     rows = half // 2
-    for b in range(half // rows):
-        source = pl.multiple_of(base + b * rows, rows)
-        expand, reduce = hidden_rows(cells, [source], rows, grad_pre_ref, [b * rows])
-        at = slice(b * rows, (b + 1) * rows)
-        sent_ref[at, :channels] = expand.astype(bf16)
-        sent_ref[at, channels:] = reduce.astype(bf16)
+    blocks = [
+        HiddenBlock(
+            cells, [pl.multiple_of(base + b * rows, rows)], rows, grad_pre_ref, [b * rows],
+            scratch[4 * b : 4 * b + 4],
+        )
+        for b in range(2)
+    ]
+    first, second = blocks
+    pieces = [slice(c, c + 256) for c in range(0, total, 256)]
+    for at in pieces:
+        first.dots(at)
+    for at in pieces:
+        first.activate(at)
+        second.dots(at)
+    second.activate(pieces[0])
+    sent_ref[:rows, :channels] = first.expand_sum().astype(bf16)
+    second.activate(pieces[1])
+    sent_ref[:rows, channels:] = first.reduce_sum().astype(bf16)
+    for at in pieces[2:]:
+        second.activate(at)
+    sent_ref[rows:, :channels] = second.expand_sum().astype(bf16)
+    sent_ref[rows:, channels:] = second.reduce_sum().astype(bf16)
 
 
 def hidden_far(*cells):
@@ -498,23 +539,26 @@
         ),
         in_specs=[whole] * 5,
         out_specs=[whole] * 2,
-        compiler_params=params(16),
-        cost_estimate=cost(5.8),
+        scratch_shapes=hidden_scratch(half // 2, total) * 2,
+        compiler_params=params(20),
+        cost_estimate=cost(5.0),
         name="hidden_far",
     )(*cells)
 
 
 def near_first_body(*refs):
-    cells, (sums_ref, grad_pre_ref) = refs[:5], refs[5:]
+    cells, (sums_ref, grad_pre_ref), scratch = refs[:5], refs[5:7], refs[7:]
     half = grad_pre_ref.shape[0]
     channels = refs[0].shape[1]
     size = half // 4
     core, place = own_place()[0], phase_place(False)
     chunks = [pl.multiple_of(lax.rem(place + step, 4) * size, size) for step in (2, 1)]
     sources = [pl.multiple_of(core * half + chunk, size) for chunk in chunks]
-    expand, reduce = hidden_rows(cells, sources, size, grad_pre_ref, chunks)
-    sums_ref[:, :channels] = expand
-    sums_ref[:, channels:] = reduce
+    block = HiddenBlock(cells, sources, size, grad_pre_ref, chunks, scratch)
+    block.dots(slice(0, block.total))
+    block.activate(slice(0, block.total))
+    sums_ref[:, :channels] = block.expand_sum()
+    sums_ref[:, channels:] = block.reduce_sum()
 
 
 def near_first(*cells):
@@ -528,6 +572,7 @@
         ),
         in_specs=[whole] * 5,
         out_specs=[whole] * 2,
+        scratch_shapes=hidden_scratch(half // 2, total),
         compiler_params=params(16),
         cost_estimate=cost(3.0),
         name="near_first",
@@ -558,14 +603,17 @@
 
 
 def near_last_body(*refs):
-    cells, (arrived_ref, _, own_ref, sent_ref, grad_pre_ref) = refs[:5], refs[5:]
+    cells, (arrived_ref, _, own_ref, sent_ref, grad_pre_ref) = refs[:5], refs[5:10]
     half = grad_pre_ref.shape[0]
     channels = refs[0].shape[1]
     size = half // 4
     core, place = own_place()[0], phase_place(False)
     chunks = [pl.multiple_of(lax.rem(place + step, 4) * size, size) for step in (3, 0)]
     sources = [pl.multiple_of(core * half + chunk, size) for chunk in chunks]
-    expand, reduce = hidden_rows(cells, sources, size, grad_pre_ref, chunks)
+    block = HiddenBlock(cells, sources, size, grad_pre_ref, chunks, refs[10:])
+    block.dots(slice(0, block.total))
+    block.activate(slice(0, block.total))
+    expand, reduce = block.expand_sum(), block.reduce_sum()
     for n, (chunk, ref) in enumerate(zip(chunks, (sent_ref, own_ref))):
         at = slice(n * size, (n + 1) * size)
         other = arrived_ref[pl.ds(chunk, size), :].astype(f32)
@@ -587,6 +635,7 @@
         in_specs=[whole] * 7,
         out_specs=[whole] * 3,
         input_output_aliases={6: 2},
+        scratch_shapes=hidden_scratch(2 * size, cells[0].shape[0]),
         compiler_params=params(16),
         cost_estimate=cost(3.0),
         name="near_last",
@@ -842,10 +891,10 @@
 
     first, last = side_cols(cells)
     left, right = lon_halo(first, last)
+    conv = inner_conv(cells, kernel, (0,))
     grad, w_expand, w_reduce = after((grad, w_expand, w_reduce), first, last)
     rows = mask_rows(counts, grad)
     expand, reduce, expand_t, bias = arrange(w_expand[0], w_reduce[0], b_expand)
-    conv = inner_conv(after(cells, rows), kernel, (0,))
     left, right = after((left, right), rows, bias, conv)
     up, down = side_rows(cells, left, right)
     top, bottom = lat_halo(up, down)
@@ -870,12 +919,12 @@
     left, right = lon_halo(first, last)
     own, parts = after((own, (part_one, part_two, part_three)), first, last)
     own, *sent = split_four(own, parts)
-    parts = [lax.ppermute(s, every_axis, plane_pairs(i + 1, False)) for i, s in enumerate(sent)]
+    parts = [lax.ppermute(sent[i], every_axis, plane_pairs(i + 1, False)) for i in (1, 0, 2)]
     back = back_conv(after(conv_grad, sent), kernel, (0, 1))
     up, down = side_rows(*after((conv_grad, left, right), back))
 
     own, *sent = split_ring(*after((own, parts), up, down))
-    parts = [lax.ppermute(s, every_axis, ring_pairs(i + 1)) for i, s in enumerate(sent)]
+    parts = [lax.ppermute(sent[i], every_axis, ring_pairs(i + 1)) for i in (1, 0, 2)]
     top, bottom = lat_halo(up, down)
     back += back_conv(after(conv_grad, sent), kernel, (2,))
 

time: 72.9 us -> 71.3 us (0.978)
  Pallas kernels: 33.5 us -> 32.1 us
where the time goes in v8:
time: 71.3 us; the launch traced here: 71 us
  Pallas kernels  32.1 us (45%)
  starting transfers between devices  29.7 us (42%)
  waiting for transfers between devices  8.19 us (11%)
  between operations  0.94 us (1%)
    ppermute x3, starting transfers between devices, local(): lax.ppermute(sent[i], every_axis, ring_pairs(i + 1))  10.5 us
    pallas_call x2, Pallas kernels, inner_conv(): pl.pallas_call(functools.partial(inner_conv_body, parts), out_shape=(shap...  6.22 us
    ppermute x3, starting transfers between devices, local(): lax.ppermute(sent[i], every_axis, plane_pairs(i + 1, False))  5.44 us
    ppermute x2, starting transfers between devices, lon_halo(): right = lax.ppermute(first, 'lon', shifted('lon', -1))  4.91 us
    pallas_call x1, Pallas kernels, hidden_far(): pl.pallas_call(far_body, out_shape=(jax.ShapeDtypeStruct((half, 2 * chann...  4.69 us
    pallas_call x2, Pallas kernels, back_conv(): pl.pallas_call(functools.partial(back_conv_body, parts), out_shape=(shape...  4 us
    ppermute x3, waiting for transfers between devices, local(): lax.ppermute(sent[i], every_axis, ring_pairs(i + 1))  3.5 us
    ppermute x1, starting transfers between devices, local(): part_two = lax.ppermute(two, every_axis, plane_pairs(2, True))  3.3 us
  transfers between devices with their start and end apart: 19, of which 8 were waited for; matrix products, arithmetic and copies ran while one was open for 0% of the time, Pallas kernels for 32%

profile of v8, /device:TPU:32, one launch (start us, length us, event | category | flops | bytes accessed | tf_op | source)
XLA Modules:
  0.0 71.0 jit_solution(5113314460005507095)
XLA Ops:
  0.6 2.1 %side_cols.1 = (bf16[3,32,384]{2,1,0:T(8,128)(2,1)}, bf16[3,32,384]{2,1,0:T(8,128)(2,1)}) custom-call(f32[32,32,384]{2,1,0:T(8,128)} %bitcast.10), custom_call_target="tpu_custom_call" | custom-call | flops 1150000000 | bytes 1048576 | tf_op jit(solution)/shard_map/side_cols/pallas_call | solution.py:170
  2.7 1.1 %collective-permute-start.1 = (bf16[3,32,384]{2,1,0:T(8,128)(2,1)}, bf16[3,32,384]{2,1,0:T(8,128)(2,1)S(1)}, u32[]{:S(2)}, u32[]{:S(2)}) collective-permute-start(bf16[3,32,384]{2,1,0:T(8,128)(2,1)} %get-tuple-element.74), channel_id=1, source_target_pairs={{0,15},{1,0},{2,1},{3,2},{4,3},{5,4},{6,5},{7,6},{8,7},{9,8},{10,9... | collective-permute-start | bytes 221192 | tf_op jit(solution)/shard_map/ppermute | solution.py:869
  3.8 1.0 %collective-permute-start = (bf16[3,32,384]{2,1,0:T(8,128)(2,1)}, bf16[3,32,384]{2,1,0:T(8,128)(2,1)S(1)}, u32[]{:S(2)}, u32[]{:S(2)}) collective-permute-start(bf16[3,32,384]{2,1,0:T(8,128)(2,1)} %get-tuple-element.75), channel_id=1, source_target_pairs={{0,1},{1,2},{2,3},{3,4},{4,5},{5,6},{6,7},{7,8},{8,9},{9,10},{10,1... | collective-permute-start | bytes 221192 | tf_op jit(solution)/shard_map/ppermute | solution.py:868
  4.8 2.1 %inner_conv.2.conv0_ref = f32[1024,128]{1,0:T(8,128)S(1)} custom-call(f32[1024,384]{1,0:T(8,128)S(1)} %bitcast.11, f32[49,1,384]{2,1,0:T(1,128)S(1)} %bitcast.21), custom_call_target="tpu_custom_call" | custom-call | flops 2529999872 | bytes 1048576 | tf_op jit(solution)/shard_map/inner_conv/pallas_call | solution.py:87
  7.0 1.6 %arrange.1 = (bf16[1536,384]{1,0:T(8,128)(2,1)S(1)}, bf16[1536,384]{1,0:T(8,128)(2,1)S(1)}, bf16[384,1536]{1,0:T(8,128)(2,1)S(1)}, f32[1536,128]{1,0:T(8,128)S(1)}) custom-call(bf16[1536,384]{1,0:T(8,128)(2,1)S(1)} %bitcast.19, bf16[1536,384]{1,0:T(8,128)(2,1)S(1)} %bitcast.20, f32[1,1536]{1,0:T(1,128)S(1)} %copy-done.6), custom_call_target="tpu_custom_call" | custom-call | flops 1724999936 | bytes 1048576 | tf_op jit(solution)/shard_map/arrange/pallas_call | solution.py:409
  8.6 0.7 mask_rows.1.refs_1_
  9.4 1.9 %collective-permute-start.3 = (bf16[3,48,384]{2,1,0:T(8,128)(2,1)S(1)}, bf16[3,48,384]{2,1,0:T(8,128)(2,1)S(1)}, u32[]{:S(2)}, u32[]{:S(2)}) collective-permute-start(bf16[3,48,384]{2,1,0:T(8,128)(2,1)S(1)} %get-tuple-element.83), channel_id=1, source_target_pairs={{0,112},{16,0},{32,16},{48,32},{64,48},{80,64},{96,80},{112,96},{1... | collective-permute-start | bytes 331784 | tf_op jit(solution)/shard_map/ppermute | solution.py:875
  11.3 4.1 %inner_conv.3 = (f32[1024,128]{1,0:T(8,128)S(1)}, f32[1024,128]{1,0:T(8,128)S(1)}) custom-call(f32[1024,384]{1,0:T(8,128)S(1)} %bitcast.13, f32[49,1,384]{2,1,0:T(1,128)S(1)} %bitcast.22), custom_call_target="tpu_custom_call" | custom-call | flops 5059999744 | bytes 1048576 | tf_op jit(solution)/shard_map/inner_conv/pallas_call | solution.py:87
  15.4 1.2 %collective-permute-done.2.top_ref = bf16[3,48,384]{2,1,0:T(8,128)(2,1)S(1)} collective-permute-done((bf16[3,48,384]{2,1,0:T(8,128)(2,1)S(1)}, bf16[3,48,384]{2,1,0:T(8,128)(2,1)S(1)}, u32[]{:S(2)}, u32[]{:S(2)}) %collective-permute-start.2) | collective-permute-done | bytes 110624 | tf_op jit(solution)/shard_map/ppermute | solution.py:874
  16.7 1.9 %normalise.1 = (f32[1024,384]{1,0:T(8,128)S(1)}, f32[1024,128]{1,0:T(8,128)S(1)}, bf16[1024,384]{1,0:T(8,128)(2,1)S(1)}) custom-call(f32[1024,128]{1,0:T(8,128)S(1)} %inner_conv.2.conv0_ref, f32[1024,128]{1,0:T(8,128)S(1)} %get-tuple-element.86.conv1_ref, f32[1024,128]{1,0:T(8,128)S(1)} %get-tuple-element.87.conv2_ref, f32[49,1,384]{2,1,0:T(1,128)S(1)} %bitcast.23, ...), custom_call_target="tpu_custom_call" | custom-call | flops 3220000000 | bytes 1048576 | tf_op jit(solution)/shard_map/normalise/pallas_call | solution.py:318
  18.6 4.7 %hidden_far.1 = (bf16[768,768]{1,0:T(8,128)(2,1)S(1)}, bf16[768,1024]{1,0:T(8,128)(2,1)S(1)}) custom-call(bf16[1024,384]{1,0:T(8,128)(2,1)S(1)} %get-tuple-element.88.refs_0_, bf16[1024,384]{1,0:T(8,128)(2,1)S(1)} %mask_rows.1.refs_1_, bf16[1536,384]{1,0:T(8,128)(2,1)S(1)} %get-tuple-element.89.refs_2_, bf16[1536,384]{1,0:T(8,128)(2,1)S(1)} %get-tuple-element.90.refs_3_, ...), custom_call_target="tpu_custom_call" | custom-call | flops 5750000128 | bytes 1048576 | tf_op jit(solution)/shard_map/hidden_far/pallas_call | solution.py:534
  23.6 2.5 %near_first.1 = (f32[384,768]{1,0:T(8,128)S(1)}, bf16[768,1024]{1,0:T(8,128)(2,1)S(1)}) custom-call(bf16[1024,384]{1,0:T(8,128)(2,1)S(1)} %get-tuple-element.88.refs_0_, bf16[1024,384]{1,0:T(8,128)(2,1)S(1)} %mask_rows.1.refs_1_, bf16[1536,384]{1,0:T(8,128)(2,1)S(1)} %get-tuple-element.89.refs_2_, bf16[1536,384]{1,0:T(8,128)(2,1)S(1)} %get-tuple-element.90.refs_3_, ...), custom_call_target="tpu_custom_call" | custom-call | flops 3449999872 | bytes 1048576 | tf_op jit(solution)/shard_map/near_first/pallas_call | solution.py:567
  26.6 3.3 %collective-permute-start.6 = (bf16[192,768]{1,0:T(8,128)(2,1)S(1)}, bf16[192,768]{1,0:T(8,128)(2,1)S(1)}, u32[]{:S(2)}, u32[]{:S(2)}) collective-permute-start(bf16[192,768]{1,0:T(8,128)(2,1)S(1)} %get-tuple-element.96), channel_id=1, source_target_pairs={{0,64},{1,65},{2,66},{3,67},{4,68},{5,69},{6,70},{7,71},{8,72},{9,... | collective-permute-start | bytes 884744 | tf_op jit(solution)/shard_map/ppermute | solution.py:911
  29.9 2.6 %near_last.1 = (f32[192,768]{1,0:T(8,128)S(1)}, bf16[192,768]{1,0:T(8,128)(2,1)S(1)}, bf16[768,1024]{1,0:T(8,128)(2,1)S(1)}) custom-call(bf16[1024,384]{1,0:T(8,128)(2,1)S(1)} %get-tuple-element.88.refs_0_, bf16[1024,384]{1,0:T(8,128)(2,1)S(1)} %mask_rows.1.refs_1_, ...), custom_call_target="tpu_custom_call", output_to_operand_aliasing={{2}: (6, {})} | custom-call | flops 3449999872 | bytes 1048576 | tf_op jit(solution)/shard_map/near_last/pallas_call | solution.py:628
  32.5 0.7 collective-permute-start.7
  33.2 1.4 %collective-permute-done.5.first_ref = bf16[192,768]{1,0:T(8,128)(2,1)S(1)} collective-permute-done((bf16[192,768]{1,0:T(8,128)(2,1)S(1)}, bf16[192,768]{1,0:T(8,128)(2,1)S(1)}, u32[]{:S(2)}, u32[]{:S(2)}) %collective-permute-start.5) | collective-permute-done | bytes 294944 | tf_op jit(solution)/shard_map/ppermute | solution.py:912
  34.5 2.1 %norm_back.1 = (f32[32,32,384]{2,1,0:T(8,128)S(1)}, bf16[3,32,384]{2,1,0:T(8,128)(2,1)S(1)}, bf16[3,32,384]{2,1,0:T(8,128)(2,1)S(1)}) custom-call(bf16[384,1536]{1,0:T(8,128)(2,1)S(1)} %get-tuple-element.78.turned_ref, bf16[768,1024]{1,0:T(8,128)(2,1)S(1)} %get-tuple-element.99.other_ref, bf16[768,1024]{1,0:T(8,128)(2,1)S(1)} %get-tuple-element.100.mine_ref, ...), custom_call_target="tpu_custom_call" | custom-call | flops 230000000 | bytes 1048576 | tf_op jit(solution)/shard_map/norm_back/pallas_call | solution.py:676
  36.6 1.2 %collective-permute-done.6.second_ref = bf16[192,768]{1,0:T(8,128)(2,1)S(1)} collective-permute-done((bf16[192,768]{1,0:T(8,128)(2,1)S(1)}, bf16[192,768]{1,0:T(8,128)(2,1)S(1)}, u32[]{:S(2)}, u32[]{:S(2)}) %collective-permute-start.6) | collective-permute-done | bytes 294944 | tf_op jit(solution)/shard_map/ppermute | solution.py:911
  37.8 3.8 %collective-permute-start.12 = (bf16[3,32,384]{2,1,0:T(8,128)(2,1)S(1)}, bf16[3,32,384]{2,1,0:T(8,128)(2,1)S(1)}, u32[]{:S(2)}, u32[]{:S(2)}) collective-permute-start(bf16[3,32,384]{2,1,0:T(8,128)(2,1)S(1)} %get-tuple-element.109), channel_id=1, source_target_pairs={{0,15},{1,0},{2,1},{3,2},{4,3},{5,4},{6,5},{7,6},{8,7},{9,8},{10,9... | collective-permute-start | bytes 221192 | tf_op jit(solution)/shard_map/ppermute | solution.py:869
  41.7 1.6 %collective-permute-start.9 = (bf16[48,768]{1,0:T(8,128)(2,1)S(1)}, bf16[48,768]{1,0:T(8,128)(2,1)S(1)}, u32[]{:S(2)}, u32[]{:S(2)}) collective-permute-start(bf16[48,768]{1,0:T(8,128)(2,1)S(1)} %get-tuple-element.115), channel_id=1, source_target_pairs={{0,1},{1,128},{2,3},{3,130},{4,5},{5,132},{6,7},{7,134},{8,9},{9,1... | collective-permute-start | bytes 221192 | tf_op jit(solution)/shard_map/ppermute | solution.py:922
  43.3 2.7 %collective-permute-start.8 = (bf16[48,768]{1,0:T(8,128)(2,1)S(1)}, bf16[48,768]{1,0:T(8,128)(2,1)S(1)}, u32[]{:S(2)}, u32[]{:S(2)}) collective-permute-start(bf16[48,768]{1,0:T(8,128)(2,1)S(1)} %get-tuple-element.116), channel_id=1, source_target_pairs={{0,128},{1,129},{2,130},{3,131},{4,132},{5,133},{6,134},{7,135},{8... | collective-permute-start | bytes 221192 | tf_op jit(solution)/shard_map/ppermute | solution.py:922
  46.1 1.1 %collective-permute-start.10 = (bf16[48,768]{1,0:T(8,128)(2,1)S(1)}, bf16[48,768]{1,0:T(8,128)(2,1)S(1)}, u32[]{:S(2)}, u32[]{:S(2)}) collective-permute-start(bf16[48,768]{1,0:T(8,128)(2,1)S(1)} %get-tuple-element.117), channel_id=1, source_target_pairs={{0,129},{1,0},{2,131},{3,2},{4,133},{5,4},{6,135},{7,6},{8,137},{9... | collective-permute-start | bytes 221192 | tf_op jit(solution)/shard_map/ppermute | solution.py:922
  47.2 2.7 %back_conv.2 = (f32[1024,128]{1,0:T(8,128)S(1)}, f32[1024,128]{1,0:T(8,128)S(1)}) custom-call(f32[1024,384]{1,0:T(8,128)S(1)} %bitcast.16, f32[49,1,384]{2,1,0:T(1,128)S(1)} %bitcast.24), custom_call_target="tpu_custom_call" | custom-call | flops 3449999872 | bytes 1048576 | tf_op jit(solution)/shard_map/back_conv/pallas_call | solution.py:137
  50.5 5.8 %collective-permute-start.16 = (f32[12,768]{1,0:T(8,128)S(1)}, f32[12,768]{1,0:T(8,128)S(1)}, u32[]{:S(2)}, u32[]{:S(2)}) collective-permute-start(f32[12,768]{1,0:T(8,128)S(1)} %get-tuple-element.131), channel_id=1, source_target_pairs={{0,4},{1,5},{2,6},{3,7},{4,8},{5,9},{6,10},{7,11},{8,12},{9,13},{1... | collective-permute-start | bytes 110600 | tf_op jit(solution)/shard_map/ppermute | solution.py:927
  56.3 4.5 %collective-permute-start.15 = (f32[12,768]{1,0:T(8,128)S(1)}, f32[12,768]{1,0:T(8,128)S(1)}, u32[]{:S(2)}, u32[]{:S(2)}) collective-permute-start(f32[12,768]{1,0:T(8,128)S(1)} %get-tuple-element.132), channel_id=1, source_target_pairs={{0,8},{1,9},{2,10},{3,11},{4,12},{5,13},{6,14},{7,15},{8,0},{9,1},... | collective-permute-start | bytes 110600 | tf_op jit(solution)/shard_map/ppermute | solution.py:927
  61.0 0.5 collective-permute-start.13
  61.5 1.3 %back_conv.3.conv2_ref = f32[1024,128]{1,0:T(8,128)S(1)} custom-call(f32[1024,384]{1,0:T(8,128)S(1)} %bitcast.18, f32[49,1,384]{2,1,0:T(1,128)S(1)} %bitcast.25), custom_call_target="tpu_custom_call" | custom-call | flops 1724999936 | bytes 1048576 | tf_op jit(solution)/shard_map/back_conv/pallas_call | solution.py:137
  62.9 2.4 %collective-permute-done.15.refs_0_ = f32[12,768]{1,0:T(8,128)S(1)} collective-permute-done((f32[12,768]{1,0:T(8,128)S(1)}, f32[12,768]{1,0:T(8,128)S(1)}, u32[]{:S(2)}, u32[]{:S(2)}) %collective-permute-start.15) | collective-permute-done | bytes 36896 | tf_op jit(solution)/shard_map/ppermute | solution.py:927
  65.3 1.0 %collective-permute-done.17.refs_2_ = f32[12,768]{1,0:T(8,128)S(1)} collective-permute-done((f32[12,768]{1,0:T(8,128)S(1)}, f32[12,768]{1,0:T(8,128)S(1)}, u32[]{:S(2)}, u32[]{:S(2)}) %collective-permute-start.17) | collective-permute-done | bytes 36896 | tf_op jit(solution)/shard_map/ppermute | solution.py:927
  66.4 1.1 %collective-permute-start.18 = (f32[6,768]{1,0:T(8,128)S(1)}, f32[6,768]{1,0:T(8,128)S(1)}, u32[]{:S(2)}, u32[]{:S(2)}) collective-permute-start(f32[6,768]{1,0:T(8,128)S(1)} %get-tuple-element.140), channel_id=1, source_target_pairs={{0,2},{1,3},{2,0},{3,1},{4,6},{5,7},{6,4},{7,5},{8,10},{9,11},{10,... | collective-permute-start | bytes 55304 | tf_op jit(solution)/shard_map/ppermute | solution.py:932
  67.5 2.7 %finish.1 = f32[1024,384]{1,0:T(8,128)} custom-call(s32[4,4]{1,0:T(4,128)S(1)} %copy-done.7, f32[1024,128]{1,0:T(8,128)S(1)} %get-tuple-element.119.conv0_ref, f32[1024,128]{1,0:T(8,128)S(1)} %get-tuple-element.120.conv1_ref, f32[1024,128]{1,0:T(8,128)S(1)} %back_conv.3.conv2_ref, f32[49,1,384]{2,1,0:T(1,128)S(1)} %bitcast.26, ...), custom_call_target="tpu_custom_call" | custom-call | flops 2875000064 | bytes 1048576 | tf_op jit(solution)/shard_map/finish/pallas_call | solution.py:714
  70.3 0.6 last_sum.1
  (46 shorter events, 2.1 us)
Async XLA Ops:
  0.6 4.2 %copy-start.1 = (f32[1,32,32,384]{3,2,1,0:T(8,128)S(1)}, f32[1,32,32,384]{3,2,1,0:T(8,128)}, u32[]{:S(2)}) copy-start(f32[1,32,32,384]{3,2,1,0:T(8,128)} %param.10) | copy-start | bytes 4718596
  0.6 4.2 %copy-start.5 = (f32[1,49,384]{2,0,1:T(1,128)S(1)}, f32[1,49,384]{2,0,1:T(1,128)}, u32[]{:S(2)}) copy-start(f32[1,49,384]{2,0,1:T(1,128)} %param.13) | copy-start | bytes 225796
  2.7 6.6 %collective-permute-start.1 = (bf16[3,32,384]{2,1,0:T(8,128)(2,1)}, bf16[3,32,384]{2,1,0:T(8,128)(2,1)S(1)}, u32[]{:S(2)}, u32[]{:S(2)}) collective-permute-start(bf16[3,32,384]{2,1,0:T(8,128)(2,1)} %get-tuple-element.74), channel_id=1, source_target_pairs={{0,15},{1,0},{2,1},{3,2},{4,3},{5,4},{6,5},{7,6},{8,7},{9,8},{10,9... | collective-permute-start | bytes 221192 | tf_op jit(solution)/shard_map/ppermute | solution.py:869
  3.8 5.5 %collective-permute-start = (bf16[3,32,384]{2,1,0:T(8,128)(2,1)}, bf16[3,32,384]{2,1,0:T(8,128)(2,1)S(1)}, u32[]{:S(2)}, u32[]{:S(2)}) collective-permute-start(bf16[3,32,384]{2,1,0:T(8,128)(2,1)} %get-tuple-element.75), channel_id=1, source_target_pairs={{0,1},{1,2},{2,3},{3,4},{4,5},{5,6},{6,7},{7,8},{8,9},{9,10},{10,1... | collective-permute-start | bytes 221192 | tf_op jit(solution)/shard_map/ppermute | solution.py:868
  4.8 2.1 %copy-start.3 = (bf16[1,1536,384]{2,1,0:T(8,128)(2,1)S(1)}, bf16[1,1536,384]{2,1,0:T(8,128)(2,1)}, u32[]{:S(2)}) copy-start(bf16[1,1536,384]{2,1,0:T(8,128)(2,1)} %param.17) | copy-start | bytes 3538948
  4.8 2.1 %copy-start.4 = (bf16[1,1536,384]{2,1,0:T(8,128)(2,1)S(1)}, bf16[1,1536,384]{2,1,0:T(8,128)(2,1)}, u32[]{:S(2)}) copy-start(bf16[1,1536,384]{2,1,0:T(8,128)(2,1)} %param.19) | copy-start | bytes 3538948
  4.8 2.1 %copy-start.6 = (f32[1,1536]{1,0:T(1,128)S(1)}, f32[1,1536]{1,0:T(1,128)}, u32[]{:S(2)}) copy-start(f32[1,1536]{1,0:T(1,128)} %bias_ref.2) | copy-start | bytes 18436
  7.0 1.6 %copy-start.2 = (f32[1,32,32,384]{3,2,1,0:T(8,128)S(1)}, f32[1,32,32,384]{3,2,1,0:T(8,128)}, u32[]{:S(2)}) copy-start(f32[1,32,32,384]{3,2,1,0:T(8,128)} %param.11) | copy-start | bytes 4718596
  7.0 1.6 %copy-start.7 = (s32[4,4]{1,0:T(4,128)S(1)}, s32[4,4]{1,0:T(4,128)}, u32[]{:S(2)}) copy-start(s32[4,4]{1,0:T(4,128)} %counts_ref.3) | copy-start | bytes 196
  9.4 6.1 %collective-permute-start.3 = (bf16[3,48,384]{2,1,0:T(8,128)(2,1)S(1)}, bf16[3,48,384]{2,1,0:T(8,128)(2,1)S(1)}, u32[]{:S(2)}, u32[]{:S(2)}) collective-permute-start(bf16[3,48,384]{2,1,0:T(8,128)(2,1)S(1)} %get-tuple-element.83), channel_id=1, source_target_pairs={{0,112},{16,0},{32,16},{48,32},{64,48},{80,64},{96,80},{112,96},{1... | collective-permute-start | bytes 331784 | tf_op jit(solution)/shard_map/ppermute | solution.py:875
  11.3 5.4 %copy-start = (f32[1,384]{1,0:T(1,128)S(1)}, f32[1,384]{1,0:T(1,128)}, u32[]{:S(2)}) copy-start(f32[1,384]{1,0:T(1,128)} %gain_ref.3) | copy-start | bytes 4612
  11.3 5.4 %copy-start.8 = (f32[1,384]{1,0:T(1,128)S(1)}, f32[1,384]{1,0:T(1,128)}, u32[]{:S(2)}) copy-start(f32[1,384]{1,0:T(1,128)} %bias_ref.3) | copy-start | bytes 4612
  11.3 5.4 %copy-start.9 = (f32[1,384]{1,0:T(1,128)S(1)}, f32[1,384]{1,0:T(1,128)}, u32[]{:S(2)}) copy-start(f32[1,384]{1,0:T(1,128)} %shift_ref.1) | copy-start | bytes 4612
  11.3 5.4 %collective-permute-start.2 = (bf16[3,48,384]{2,1,0:T(8,128)(2,1)S(1)}, bf16[3,48,384]{2,1,0:T(8,128)(2,1)S(1)}, u32[]{:S(2)}, u32[]{:S(2)}) collective-permute-start(bf16[3,48,384]{2,1,0:T(8,128)(2,1)S(1)} %get-tuple-element.84), channel_id=1, source_target_pairs={{0,16},{16,32},{32,48},{48,64},{64,80},{80,96},{96,112},{112,0},{1... | collective-permute-start | bytes 331784 | tf_op jit(solution)/shard_map/ppermute | solution.py:874
  23.3 3.1 %collective-permute-start.4 = (bf16[768,768]{1,0:T(8,128)(2,1)S(1)}, bf16[768,768]{1,0:T(8,128)(2,1)S(1)}, u32[]{:S(2)}, u32[]{:S(2)}) collective-permute-start(bf16[768,768]{1,0:T(8,128)(2,1)S(1)} %get-tuple-element.93), channel_id=1, source_target_pairs={{0,16},{16,0},{32,48},{48,32},{64,80},{80,64},{96,112},{112,96},{1... | collective-permute-start | bytes 3538952 | tf_op jit(solution)/shard_map/ppermute | solution.py:908
  26.5 8.0 %collective-permute-start.5 = (bf16[192,768]{1,0:T(8,128)(2,1)S(1)}, bf16[192,768]{1,0:T(8,128)(2,1)S(1)}, u32[]{:S(2)}, u32[]{:S(2)}) collective-permute-start(bf16[192,768]{1,0:T(8,128)(2,1)S(1)} %get-tuple-element.94), channel_id=1, source_target_pairs={{0,32},{1,33},{2,34},{3,35},{4,36},{5,37},{6,38},{7,39},{8,40},{9,... | collective-permute-start | bytes 884744 | tf_op jit(solution)/shard_map/ppermute | solution.py:912
  26.6 11.2 %collective-permute-start.6 = (bf16[192,768]{1,0:T(8,128)(2,1)S(1)}, bf16[192,768]{1,0:T(8,128)(2,1)S(1)}, u32[]{:S(2)}, u32[]{:S(2)}) collective-permute-start(bf16[192,768]{1,0:T(8,128)(2,1)S(1)} %get-tuple-element.96), channel_id=1, source_target_pairs={{0,64},{1,65},{2,66},{3,67},{4,68},{5,69},{6,70},{7,71},{8,72},{9,... | collective-permute-start | bytes 884744 | tf_op jit(solution)/shard_map/ppermute | solution.py:911
  32.5 9.1 %collective-permute-start.7 = (bf16[192,768]{1,0:T(8,128)(2,1)S(1)}, bf16[192,768]{1,0:T(8,128)(2,1)S(1)}, u32[]{:S(2)}, u32[]{:S(2)}) collective-permute-start(bf16[192,768]{1,0:T(8,128)(2,1)S(1)} %get-tuple-element.98), channel_id=1, source_target_pairs={{0,96},{1,97},{2,98},{3,99},{4,100},{5,101},{6,102},{7,103},{8,104... | collective-permute-start | bytes 884744 | tf_op jit(solution)/shard_map/ppermute | solution.py:914
  37.8 12.0 %collective-permute-start.12 = (bf16[3,32,384]{2,1,0:T(8,128)(2,1)S(1)}, bf16[3,32,384]{2,1,0:T(8,128)(2,1)S(1)}, u32[]{:S(2)}, u32[]{:S(2)}) collective-permute-start(bf16[3,32,384]{2,1,0:T(8,128)(2,1)S(1)} %get-tuple-element.109), channel_id=1, source_target_pairs={{0,15},{1,0},{2,1},{3,2},{4,3},{5,4},{6,5},{7,6},{8,7},{9,8},{10,9... | collective-permute-start | bytes 221192 | tf_op jit(solution)/shard_map/ppermute | solution.py:869
  41.6 8.3 %collective-permute-start.11 = (bf16[3,32,384]{2,1,0:T(8,128)(2,1)S(1)}, bf16[3,32,384]{2,1,0:T(8,128)(2,1)S(1)}, u32[]{:S(2)}, u32[]{:S(2)}) collective-permute-start(bf16[3,32,384]{2,1,0:T(8,128)(2,1)S(1)} %get-tuple-element.110), channel_id=1, source_target_pairs={{0,1},{1,2},{2,3},{3,4},{4,5},{5,6},{6,7},{7,8},{8,9},{9,10},{10,1... | collective-permute-start | bytes 221192 | tf_op jit(solution)/shard_map/ppermute | solution.py:868
  41.7 8.2 %collective-permute-start.9 = (bf16[48,768]{1,0:T(8,128)(2,1)S(1)}, bf16[48,768]{1,0:T(8,128)(2,1)S(1)}, u32[]{:S(2)}, u32[]{:S(2)}) collective-permute-start(bf16[48,768]{1,0:T(8,128)(2,1)S(1)} %get-tuple-element.115), channel_id=1, source_target_pairs={{0,1},{1,128},{2,3},{3,130},{4,5},{5,132},{6,7},{7,134},{8,9},{9,1... | collective-permute-start | bytes 221192 | tf_op jit(solution)/shard_map/ppermute | solution.py:922
  43.3 6.6 %collective-permute-start.8 = (bf16[48,768]{1,0:T(8,128)(2,1)S(1)}, bf16[48,768]{1,0:T(8,128)(2,1)S(1)}, u32[]{:S(2)}, u32[]{:S(2)}) collective-permute-start(bf16[48,768]{1,0:T(8,128)(2,1)S(1)} %get-tuple-element.116), channel_id=1, source_target_pairs={{0,128},{1,129},{2,130},{3,131},{4,132},{5,133},{6,134},{7,135},{8... | collective-permute-start | bytes 221192 | tf_op jit(solution)/shard_map/ppermute | solution.py:922
  46.1 4.4 %collective-permute-start.10 = (bf16[48,768]{1,0:T(8,128)(2,1)S(1)}, bf16[48,768]{1,0:T(8,128)(2,1)S(1)}, u32[]{:S(2)}, u32[]{:S(2)}) collective-permute-start(bf16[48,768]{1,0:T(8,128)(2,1)S(1)} %get-tuple-element.117), channel_id=1, source_target_pairs={{0,129},{1,0},{2,131},{3,2},{4,133},{5,4},{6,135},{7,6},{8,137},{9... | collective-permute-start | bytes 221192 | tf_op jit(solution)/shard_map/ppermute | solution.py:922
  50.5 12.4 %collective-permute-start.16 = (f32[12,768]{1,0:T(8,128)S(1)}, f32[12,768]{1,0:T(8,128)S(1)}, u32[]{:S(2)}, u32[]{:S(2)}) collective-permute-start(f32[12,768]{1,0:T(8,128)S(1)} %get-tuple-element.131), channel_id=1, source_target_pairs={{0,4},{1,5},{2,6},{3,7},{4,8},{5,9},{6,10},{7,11},{8,12},{9,13},{1... | collective-permute-start | bytes 110600 | tf_op jit(solution)/shard_map/ppermute | solution.py:927
  56.3 9.1 %collective-permute-start.15 = (f32[12,768]{1,0:T(8,128)S(1)}, f32[12,768]{1,0:T(8,128)S(1)}, u32[]{:S(2)}, u32[]{:S(2)}) collective-permute-start(f32[12,768]{1,0:T(8,128)S(1)} %get-tuple-element.132), channel_id=1, source_target_pairs={{0,8},{1,9},{2,10},{3,11},{4,12},{5,13},{6,14},{7,15},{8,0},{9,1},... | collective-permute-start | bytes 110600 | tf_op jit(solution)/shard_map/ppermute | solution.py:927
  60.8 5.6 %collective-permute-start.17 = (f32[12,768]{1,0:T(8,128)S(1)}, f32[12,768]{1,0:T(8,128)S(1)}, u32[]{:S(2)}, u32[]{:S(2)}) collective-permute-start(f32[12,768]{1,0:T(8,128)S(1)} %get-tuple-element.133), channel_id=1, source_target_pairs={{0,12},{1,13},{2,14},{3,15},{4,0},{5,1},{6,2},{7,3},{8,4},{9,5},{1... | collective-permute-start | bytes 110600 | tf_op jit(solution)/shard_map/ppermute | solution.py:927
  61.0 5.4 %collective-permute-start.14 = (bf16[3,48,384]{2,1,0:T(8,128)(2,1)S(1)}, bf16[3,48,384]{2,1,0:T(8,128)(2,1)S(1)}, u32[]{:S(2)}, u32[]{:S(2)}) collective-permute-start(bf16[3,48,384]{2,1,0:T(8,128)(2,1)S(1)} %get-tuple-element.125), channel_id=1, source_target_pairs={{0,112},{16,0},{32,16},{48,32},{64,48},{80,64},{96,80},{112,96},{1... | collective-permute-start | bytes 331784 | tf_op jit(solution)/shard_map/ppermute | solution.py:875
  61.0 5.4 %collective-permute-start.13 = (bf16[3,48,384]{2,1,0:T(8,128)(2,1)S(1)}, bf16[3,48,384]{2,1,0:T(8,128)(2,1)S(1)}, u32[]{:S(2)}, u32[]{:S(2)}) collective-permute-start(bf16[3,48,384]{2,1,0:T(8,128)(2,1)S(1)} %get-tuple-element.126), channel_id=1, source_target_pairs={{0,16},{16,32},{32,48},{48,64},{64,80},{80,96},{96,112},{112,0},{1... | collective-permute-start | bytes 331784 | tf_op jit(solution)/shard_map/ppermute | solution.py:874
  66.4 3.9 %collective-permute-start.18 = (f32[6,768]{1,0:T(8,128)S(1)}, f32[6,768]{1,0:T(8,128)S(1)}, u32[]{:S(2)}, u32[]{:S(2)}) collective-permute-start(f32[6,768]{1,0:T(8,128)S(1)} %get-tuple-element.140), channel_id=1, source_target_pairs={{0,2},{1,3},{2,0},{3,1},{4,6},{5,7},{6,4},{7,5},{8,10},{9,11},{10,... | collective-permute-start | bytes 55304 | tf_op jit(solution)/shard_map/ppermute | solution.py:932

commit v9 on v8

--- a/solution.py
+++ b/solution.py
@@ -209,7 +209,13 @@
     )(cells, left, right)
 
 
-def add_edges(flipped, kernel_ref, left_ref, right_ref, top_ref, bottom_ref, rows_sum, cols_sum):
+def beyond_steps(low, r):
+    if low:
+        return [(h, h - r) for h in range(r, reach)]
+    return [(h, 6 + h - r) for h in range(0, r + 1)]
+
+
+def add_rows(flipped, kernel_ref, top_ref, bottom_ref, rows_sum):
     lat = lax.axis_index("lat")
     channels = kernel_ref.shape[2]
     for c in range(channels // lanes):
@@ -221,27 +227,27 @@
             ]
             for r in range(reach):
                 result = None
-                steps = [(h, h - r) for h in range(r, reach)] if low else [
-                    (h, 6 + h - r) for h in range(0, r + 1)
-                ]
                 for q in range(7):
                     summed = None
-                    for h, p in steps:
+                    for h, p in beyond_steps(low, r):
                         term = tap_row(kernel_ref, flipped, p, q, cols) * beyond[h]
                         summed = term if summed is None else summed + term
                     summed = pltpu.roll(summed, (reach - q) % (side + 8), 0) if q != reach else summed
                     result = summed if result is None else result + summed
                 rows_sum[r if low else reach + r, :, cols] = result[:side]
+
+
+def add_cols(flipped, kernel_ref, left_ref, right_ref, cols_sum):
+    channels = kernel_ref.shape[2]
+    for c in range(channels // lanes):
+        cols = slice(c * lanes, (c + 1) * lanes)
         for low, ref in ((True, left_ref), (False, right_ref)):
             beyond = [ref[h, :, cols].astype(f32) for h in range(reach)]
             for r in range(reach):
-                steps = [(h, h - r) for h in range(r, reach)] if low else [
-                    (h, 6 + h - r) for h in range(0, r + 1)
-                ]
                 result = None
                 for p in range(7):
                     summed = None
-                    for h, q in steps:
+                    for h, q in beyond_steps(low, r):
                         term = tap_row(kernel_ref, flipped, p, q, cols) * beyond[h]
                         summed = term if summed is None else summed + term
                     summed = shift_cols(summed, p - reach)
@@ -287,7 +293,8 @@
 ):
     channels = kernel_ref.shape[2]
     conv_refs = (conv0_ref, conv1_ref, conv2_ref)
-    add_edges(False, kernel_ref, left_ref, right_ref, top_ref, bottom_ref, rows_sum, cols_sum)
+    add_rows(False, kernel_ref, top_ref, bottom_ref, rows_sum)
+    add_cols(False, kernel_ref, left_ref, right_ref, cols_sum)
     share = 1.0 / channels
 
     def step(i, outer):
@@ -552,7 +559,7 @@
     channels = refs[0].shape[1]
     size = half // 4
     core, place = own_place()[0], phase_place(False)
-    chunks = [pl.multiple_of(lax.rem(place + step, 4) * size, size) for step in (2, 1)]
+    chunks = [pl.multiple_of(lax.rem(place + step, 4) * size, size) for step in (3, 2)]
     sources = [pl.multiple_of(core * half + chunk, size) for chunk in chunks]
     block = HiddenBlock(cells, sources, size, grad_pre_ref, chunks, scratch)
     block.dots(slice(0, block.total))
@@ -582,7 +589,7 @@
 def near_sends_body(sums_ref, arrived_ref, *sent_refs):
     size = sent_refs[0].shape[0]
     place = phase_place(False)
-    for n, step in enumerate((2, 1)):
+    for n, step in enumerate((3, 2)):
         chunk = pl.multiple_of(lax.rem(place + step, 4) * size, size)
         total = sums_ref[n * size : (n + 1) * size] + arrived_ref[pl.ds(chunk, size), :].astype(f32)
         sent_refs[n][...] = total.astype(bf16)
@@ -608,7 +615,7 @@
     channels = refs[0].shape[1]
     size = half // 4
     core, place = own_place()[0], phase_place(False)
-    chunks = [pl.multiple_of(lax.rem(place + step, 4) * size, size) for step in (3, 0)]
+    chunks = [pl.multiple_of(lax.rem(place + step, 4) * size, size) for step in (1, 0)]
     sources = [pl.multiple_of(core * half + chunk, size) for chunk in chunks]
     block = HiddenBlock(cells, sources, size, grad_pre_ref, chunks, refs[10:])
     block.dots(slice(0, block.total))
@@ -685,43 +692,82 @@
     return found.reshape(total, channels), first, last
 
 
-def finish_body(
-    counts_ref, conv0_ref, conv1_ref, conv2_ref, kernel_ref, left_ref, right_ref, top_ref, bottom_ref,
-    grad_ref, out_ref, rows_sum, cols_sum, done, sems,
+def finish_inner_body(
+    counts_ref, conv0_ref, conv1_ref, conv2_ref, kernel_ref, left_ref, right_ref, grad_ref,
+    out_ref, cols_sum, done, sems,
 ):
     conv_refs = (conv0_ref, conv1_ref, conv2_ref)
-    add_edges(True, kernel_ref, left_ref, right_ref, top_ref, bottom_ref, rows_sum, cols_sum)
-    rows = 8
+    add_cols(True, kernel_ref, left_ref, right_ref, cols_sum)
+    bounds = [reach, 9, 16, 23, side - reach]
     copies = []
-    for block in range(side // rows):
-        for i in range(block * rows, (block + 1) * rows):
+    for n, (low, high) in enumerate(zip(bounds[:-1], bounds[1:])):
+        for i in range(low, high):
             at = slice(i * side, (i + 1) * side)
             value = edged_row(i, conv_rows(conv_refs, at), cols_sum)
-            if i < reach:
-                value = value + rows_sum[i]
-            if i >= side - reach:
-                value = value + rows_sum[i - (side - 2 * reach)]
             done[at, :] = value + masked_row(i, grad_ref[at, :], counts_ref)
-        part = pl.ds(block * rows * side, rows * side)
-        copies.append(pltpu.make_async_copy(done.at[part, :], out_ref.at[part, :], sems.at[block]))
+        part = pl.ds(low * side, (high - low) * side)
+        copies.append(pltpu.make_async_copy(done.at[part, :], out_ref.at[part, :], sems.at[n]))
         copies[-1].start()
     for copy in copies:
         copy.wait()
 
 
-def finish(counts, conv, kernel, left, right, top, bottom, grad):
+def finish_inner(counts, conv, kernel, left, right, grad):
     total, channels = grad.shape
     return pl.pallas_call(
-        finish_body,
-        out_shape=jax.ShapeDtypeStruct((total, channels), f32),
-        in_specs=[pl.BlockSpec(memory_space=pltpu.SMEM)] + [whole] * 9,
+        finish_inner_body,
+        out_shape=(
+            jax.ShapeDtypeStruct((total, channels), f32),
+            jax.ShapeDtypeStruct((2 * reach, side, channels), f32),
+        ),
+        in_specs=[pl.BlockSpec(memory_space=pltpu.SMEM)] + [whole] * 7,
+        out_specs=[pl.BlockSpec(memory_space=pltpu.HBM), whole],
+        scratch_shapes=[pltpu.VMEM((total, channels), f32), pltpu.SemaphoreType.DMA((4,))],
+        compiler_params=params(12),
+        cost_estimate=cost(2.2),
+        name="finish_inner",
+    )(counts, *conv, kernel, left, right, grad)
+
+
+def finish_outer_body(
+    counts_ref, conv0_ref, conv1_ref, conv2_ref, kernel_ref, top_ref, bottom_ref, cols_ref,
+    grad_ref, _, out_ref, rows_sum, done, sems,
+):
+    conv_refs = (conv0_ref, conv1_ref, conv2_ref)
+    add_rows(True, kernel_ref, top_ref, bottom_ref, rows_sum)
+    copies = []
+    for n, start in enumerate((0, side - reach)):
+        for r in range(reach):
+            i = start + r
+            at = slice(i * side, (i + 1) * side)
+            value = edged_row(i, conv_rows(conv_refs, at), cols_ref) + rows_sum[n * reach + r]
+            done[n, r * side : (r + 1) * side, :] = value + masked_row(i, grad_ref[at, :], counts_ref)
+        part = pl.ds(start * side, reach * side)
+        copies.append(pltpu.make_async_copy(done.at[n], out_ref.at[part, :], sems.at[n]))
+        copies[-1].start()
+    for copy in copies:
+        copy.wait()
+
+
+def finish_outer(counts, conv, kernel, top, bottom, cols_sum, grad, inner):
+    channels = grad.shape[1]
+    return pl.pallas_call(
+        finish_outer_body,
+        out_shape=jax.ShapeDtypeStruct(inner.shape, f32),
+        in_specs=[pl.BlockSpec(memory_space=pltpu.SMEM)]
+        + [whole] * 8
+        + [pl.BlockSpec(memory_space=pltpu.HBM)],
         out_specs=pl.BlockSpec(memory_space=pltpu.HBM),
-        scratch_shapes=[pltpu.VMEM((2 * reach, side, channels), f32)] * 2
-        + [pltpu.VMEM((total, channels), f32), pltpu.SemaphoreType.DMA((4,))],
+        input_output_aliases={9: 0},
+        scratch_shapes=[
+            pltpu.VMEM((2 * reach, side, channels), f32),
+            pltpu.VMEM((2, reach * side, channels), f32),
+            pltpu.SemaphoreType.DMA((2,)),
+        ],
         compiler_params=params(12),
-        cost_estimate=cost(2.5),
-        name="finish",
-    )(counts, *conv, kernel, left, right, top, bottom, grad)
+        cost_estimate=cost(1.0),
+        name="finish_outer",
+    )(counts, *conv, kernel, top, bottom, cols_sum, grad, inner)
 
 
 def split_four_body(own_ref, first_ref, second_ref, third_ref, kept_ref, *sent_refs):
@@ -907,31 +953,34 @@
     sent, far_pre = hidden_far(*inputs)
     arrived = lax.ppermute(sent, "lat", [(i, i ^ 1) for i in range(8)])
     sums, near_pre = near_first(*inputs)
-    two, one = near_sends(sums, arrived)
+    three, two = near_sends(sums, arrived)
+    part_three = lax.ppermute(three, every_axis, plane_pairs(3, True))
     part_two = lax.ppermute(two, every_axis, plane_pairs(2, True))
+    own, one, near_pre = near_last(*inputs, arrived, after(near_pre, three, two))
     part_one = lax.ppermute(one, every_axis, plane_pairs(1, True))
-    own, three, near_pre = near_last(*inputs, arrived, after(near_pre, one, two))
-    part_three = lax.ppermute(three, every_axis, plane_pairs(3, True))
-
-    far_pre, part_one = after((far_pre, part_one), three)
+
+    far_pre, part_three = after((far_pre, part_three), one)
     conv_grad, first, last = norm_back(expand_t, far_pre, near_pre, unit, spread, norm_gain)
-    first, last, part_two = after((first, last, part_two))
+    last, part_two = after((last, part_two))
     left, right = lon_halo(first, last)
     own, parts = after((own, (part_one, part_two, part_three)), first, last)
     own, *sent = split_four(own, parts)
     parts = [lax.ppermute(sent[i], every_axis, plane_pairs(i + 1, False)) for i in (1, 0, 2)]
     back = back_conv(after(conv_grad, sent), kernel, (0, 1))
-    up, down = side_rows(*after((conv_grad, left, right), back))
+    (conv_grad, left, right), parts = after(((conv_grad, left, right), parts), back)
+    up, down = side_rows(conv_grad, left, right)
 
     own, *sent = split_ring(*after((own, parts), up, down))
     parts = [lax.ppermute(sent[i], every_axis, ring_pairs(i + 1)) for i in (1, 0, 2)]
     top, bottom = lat_halo(up, down)
-    back += back_conv(after(conv_grad, sent), kernel, (2,))
-
-    own, sent = split_two(*after((own, parts), back, top, bottom))
+    back += back_conv(after(conv_grad, sent, top, bottom), kernel, (2,))
+
+    inner, cols_sum = finish_inner(counts, back, kernel, left, right, grad)
+
+    own, sent = split_two(*after((own, parts), inner))
     arrived = lax.ppermute(sent, every_axis, last_pairs())
-    grad = after(grad, sent)
-    gradient = finish(counts, back, kernel, left, right, top, bottom, grad)
+    inner = after(inner, sent)
+    gradient = finish_outer(counts, back, kernel, top, bottom, cols_sum, grad, inner)
 
     cells_all = lax.axis_size("dp") * lax.axis_size("lat") * lax.axis_size("lon") * total
     kept = last_sum(own, arrived, 1.0 / math.sqrt(cells_all))

time: 71.3 us -> 72.4 us (1.015)
  starting transfers between devices: 29.7 us -> 27.7 us
  waiting for transfers between devices: 8.19 us -> 9.59 us
  Pallas kernels: 32.1 us -> 33.3 us
    ppermute x1, waiting for transfers between devices: 0.01 us -> 3.8 us  [local(): part_three = lax.ppermute(three, every_axis, plane_pairs(3, True))]
    ppermute x1, starting transfers between devices: 3.3 us -> 0.16 us  [local(): part_two = lax.ppermute(two, every_axis, plane_pairs(2, True))]
    ppermute x1, waiting for transfers between devices: 0.12 us -> 1.98 us  [local(): arrived = lax.ppermute(sent, every_axis, last_pairs())]
    ppermute x3, waiting for transfers between devices: 3.5 us -> 1.72 us  [local(): lax.ppermute(sent[i], every_axis, ring_pairs(i + 1))]
    ppermute x1, waiting for transfers between devices: 1.35 us -> 0.01 us  [local(): part_one = lax.ppermute(one, every_axis, plane_pairs(1, True))]
    ppermute x1, starting transfers between devices: 0.66 us -> 1.93 us  [local(): part_three = lax.ppermute(three, every_axis, plane_pairs(3, True))]
    pallas_call x1 -> x2, Pallas kernels: 2.69 us -> 3.93 us  [the longest x1 2.1 us: finish_inner(): pl.pallas_call(finish_inner_body, out_shape=(jax.ShapeDtypeStruct((total,...]
    ppermute x1, waiting for transfers between devices: 1.17 us -> 0.01 us  [local(): part_two = lax.ppermute(two, every_axis, plane_pairs(2, True))]
  transfers between devices with their start and end apart: 19 -> 19, of which waited for: 8 -> 7; matrix products, arithmetic and copies ran while one was open for 0% -> 0% of each run, Pallas kernels for 32% -> 33%
where the time goes in v9:
time: 72.4 us; the launch traced here: 71.6 us
  Pallas kernels  33.3 us (46%)
  starting transfers between devices  27.7 us (38%)
  waiting for transfers between devices  9.59 us (13%)
  between operations  0.94 us (1%)
    ppermute x3, starting transfers between devices, local(): lax.ppermute(sent[i], every_axis, ring_pairs(i + 1))  10.5 us
    pallas_call x2, Pallas kernels, inner_conv(): pl.pallas_call(functools.partial(inner_conv_body, parts), out_shape=(shap...  6.22 us
    ppermute x3, starting transfers between devices, local(): lax.ppermute(sent[i], every_axis, plane_pairs(i + 1, False))  5.43 us
    ppermute x2, starting transfers between devices, lon_halo(): right = lax.ppermute(first, 'lon', shifted('lon', -1))  4.99 us
    pallas_call x1, Pallas kernels, hidden_far(): pl.pallas_call(far_body, out_shape=(jax.ShapeDtypeStruct((half, 2 * chann...  4.65 us
    pallas_call x2, Pallas kernels, back_conv(): pl.pallas_call(functools.partial(back_conv_body, parts), out_shape=(shape...  4 us
    ppermute x1, waiting for transfers between devices, local(): part_three = lax.ppermute(three, every_axis, plane_pairs(3, True))  3.8 us
    pallas_call x1, Pallas kernels, near_last(): pl.pallas_call(near_last_body, out_shape=(jax.ShapeDtypeStruct((size, 2 *...  2.59 us
  transfers between devices with their start and end apart: 19, of which 7 were waited for; matrix products, arithmetic and copies ran while one was open for 0% of the time, Pallas kernels for 33%

profile of v9, /device:TPU:32, one launch (start us, length us, event | category | flops | bytes accessed | tf_op | source)
XLA Modules:
  0.0 71.6 jit_solution(17067467012033796969)
XLA Ops:
  0.6 2.1 %side_cols.1 = (bf16[3,32,384]{2,1,0:T(8,128)(2,1)}, bf16[3,32,384]{2,1,0:T(8,128)(2,1)}) custom-call(f32[32,32,384]{2,1,0:T(8,128)} %bitcast.20), custom_call_target="tpu_custom_call" | custom-call | flops 1150000000 | bytes 1048576 | tf_op jit(solution)/shard_map/side_cols/pallas_call | solution.py:170
  2.7 1.1 %collective-permute-start.1 = (bf16[3,32,384]{2,1,0:T(8,128)(2,1)}, bf16[3,32,384]{2,1,0:T(8,128)(2,1)S(1)}, u32[]{:S(2)}, u32[]{:S(2)}) collective-permute-start(bf16[3,32,384]{2,1,0:T(8,128)(2,1)} %get-tuple-element.78), channel_id=1, source_target_pairs={{0,15},{1,0},{2,1},{3,2},{4,3},{5,4},{6,5},{7,6},{8,7},{9,8},{10,9... | collective-permute-start | bytes 221192 | tf_op jit(solution)/shard_map/ppermute | solution.py:915
  3.8 1.0 %collective-permute-start = (bf16[3,32,384]{2,1,0:T(8,128)(2,1)}, bf16[3,32,384]{2,1,0:T(8,128)(2,1)S(1)}, u32[]{:S(2)}, u32[]{:S(2)}) collective-permute-start(bf16[3,32,384]{2,1,0:T(8,128)(2,1)} %get-tuple-element.79), channel_id=1, source_target_pairs={{0,1},{1,2},{2,3},{3,4},{4,5},{5,6},{6,7},{7,8},{8,9},{9,10},{10,1... | collective-permute-start | bytes 221192 | tf_op jit(solution)/shard_map/ppermute | solution.py:914
  4.8 2.1 %inner_conv.2.conv0_ref = f32[1024,128]{1,0:T(8,128)S(1)} custom-call(f32[1024,384]{1,0:T(8,128)S(1)} %bitcast.21, f32[49,1,384]{2,1,0:T(1,128)S(1)} %bitcast.13), custom_call_target="tpu_custom_call" | custom-call | flops 2529999872 | bytes 1048576 | tf_op jit(solution)/shard_map/inner_conv/pallas_call | solution.py:87
  7.0 1.6 %arrange.1 = (bf16[1536,384]{1,0:T(8,128)(2,1)S(1)}, bf16[1536,384]{1,0:T(8,128)(2,1)S(1)}, bf16[384,1536]{1,0:T(8,128)(2,1)S(1)}, f32[1536,128]{1,0:T(8,128)S(1)}) custom-call(bf16[1536,384]{1,0:T(8,128)(2,1)S(1)} %bitcast.27, bf16[1536,384]{1,0:T(8,128)(2,1)S(1)} %bitcast.28, f32[1,1536]{1,0:T(1,128)S(1)} %copy-done.7), custom_call_target="tpu_custom_call" | custom-call | flops 1724999936 | bytes 1048576 | tf_op jit(solution)/shard_map/arrange/pallas_call | solution.py:416
  8.6 0.7 mask_rows.1.refs_1_
  9.4 1.9 %collective-permute-start.3 = (bf16[3,48,384]{2,1,0:T(8,128)(2,1)S(1)}, bf16[3,48,384]{2,1,0:T(8,128)(2,1)S(1)}, u32[]{:S(2)}, u32[]{:S(2)}) collective-permute-start(bf16[3,48,384]{2,1,0:T(8,128)(2,1)S(1)} %get-tuple-element.87), channel_id=1, source_target_pairs={{0,112},{16,0},{32,16},{48,32},{64,48},{80,64},{96,80},{112,96},{1... | collective-permute-start | bytes 331784 | tf_op jit(solution)/shard_map/ppermute | solution.py:921
  11.3 4.1 %inner_conv.3 = (f32[1024,128]{1,0:T(8,128)S(1)}, f32[1024,128]{1,0:T(8,128)S(1)}) custom-call(f32[1024,384]{1,0:T(8,128)S(1)} %bitcast.23, f32[49,1,384]{2,1,0:T(1,128)S(1)} %bitcast.14), custom_call_target="tpu_custom_call" | custom-call | flops 5059999744 | bytes 1048576 | tf_op jit(solution)/shard_map/inner_conv/pallas_call | solution.py:87
  15.4 1.2 %collective-permute-done.2.top_ref = bf16[3,48,384]{2,1,0:T(8,128)(2,1)S(1)} collective-permute-done((bf16[3,48,384]{2,1,0:T(8,128)(2,1)S(1)}, bf16[3,48,384]{2,1,0:T(8,128)(2,1)S(1)}, u32[]{:S(2)}, u32[]{:S(2)}) %collective-permute-start.2) | collective-permute-done | bytes 110624 | tf_op jit(solution)/shard_map/ppermute | solution.py:920
  16.7 1.9 %normalise.1 = (f32[1024,384]{1,0:T(8,128)S(1)}, f32[1024,128]{1,0:T(8,128)S(1)}, bf16[1024,384]{1,0:T(8,128)(2,1)S(1)}) custom-call(f32[1024,128]{1,0:T(8,128)S(1)} %inner_conv.2.conv0_ref, f32[1024,128]{1,0:T(8,128)S(1)} %get-tuple-element.90.conv1_ref, f32[1024,128]{1,0:T(8,128)S(1)} %get-tuple-element.91.conv2_ref, f32[49,1,384]{2,1,0:T(1,128)S(1)} %bitcast.15, ...), custom_call_target="tpu_custom_call" | custom-call | flops 3220000000 | bytes 1048576 | tf_op jit(solution)/shard_map/normalise/pallas_call | solution.py:325
  18.6 4.6 %hidden_far.1 = (bf16[768,768]{1,0:T(8,128)(2,1)S(1)}, bf16[768,1024]{1,0:T(8,128)(2,1)S(1)}) custom-call(bf16[1024,384]{1,0:T(8,128)(2,1)S(1)} %get-tuple-element.92.refs_0_, bf16[1024,384]{1,0:T(8,128)(2,1)S(1)} %mask_rows.1.refs_1_, bf16[1536,384]{1,0:T(8,128)(2,1)S(1)} %get-tuple-element.93.refs_2_, bf16[1536,384]{1,0:T(8,128)(2,1)S(1)} %get-tuple-element.94.refs_3_, ...), custom_call_target="tpu_custom_call" | custom-call | flops 5750000128 | bytes 1048576 | tf_op jit(solution)/shard_map/hidden_far/pallas_call | solution.py:541
  23.6 2.5 %near_first.1 = (f32[384,768]{1,0:T(8,128)S(1)}, bf16[768,1024]{1,0:T(8,128)(2,1)S(1)}) custom-call(bf16[1024,384]{1,0:T(8,128)(2,1)S(1)} %get-tuple-element.92.refs_0_, bf16[1024,384]{1,0:T(8,128)(2,1)S(1)} %mask_rows.1.refs_1_, bf16[1536,384]{1,0:T(8,128)(2,1)S(1)} %get-tuple-element.93.refs_2_, bf16[1536,384]{1,0:T(8,128)(2,1)S(1)} %get-tuple-element.94.refs_3_, ...), custom_call_target="tpu_custom_call" | custom-call | flops 3449999872 | bytes 1048576 | tf_op jit(solution)/shard_map/near_first/pallas_call | solution.py:574
  26.5 1.9 %collective-permute-start.5 = (bf16[192,768]{1,0:T(8,128)(2,1)S(1)}, bf16[192,768]{1,0:T(8,128)(2,1)S(1)}, u32[]{:S(2)}, u32[]{:S(2)}) collective-permute-start(bf16[192,768]{1,0:T(8,128)(2,1)S(1)} %get-tuple-element.98), channel_id=1, source_target_pairs={{0,96},{1,97},{2,98},{3,99},{4,100},{5,101},{6,102},{7,103},{8,104... | collective-permute-start | bytes 884744 | tf_op jit(solution)/shard_map/ppermute | solution.py:957
  28.6 2.6 %near_last.1 = (f32[192,768]{1,0:T(8,128)S(1)}, bf16[192,768]{1,0:T(8,128)(2,1)S(1)}, bf16[768,1024]{1,0:T(8,128)(2,1)S(1)}) custom-call(bf16[1024,384]{1,0:T(8,128)(2,1)S(1)} %get-tuple-element.92.refs_0_, bf16[1024,384]{1,0:T(8,128)(2,1)S(1)} %mask_rows.1.refs_1_, ...), custom_call_target="tpu_custom_call", output_to_operand_aliasing={{2}: (6, {})} | custom-call | flops 3449999872 | bytes 1048576 | tf_op jit(solution)/shard_map/near_last/pallas_call | solution.py:635
  31.2 0.9 %collective-permute-start.6 = (bf16[192,768]{1,0:T(8,128)(2,1)S(1)}, bf16[192,768]{1,0:T(8,128)(2,1)S(1)}, u32[]{:S(2)}, u32[]{:S(2)}) collective-permute-start(bf16[192,768]{1,0:T(8,128)(2,1)S(1)} %get-tuple-element.102), channel_id=1, source_target_pairs={{0,32},{1,33},{2,34},{3,35},{4,36},{5,37},{6,38},{7,39},{8,40},{9,... | collective-permute-start | bytes 884744 | tf_op jit(solution)/shard_map/ppermute | solution.py:960
  32.1 3.8 %collective-permute-done.5.third_ref = bf16[192,768]{1,0:T(8,128)(2,1)S(1)} collective-permute-done((bf16[192,768]{1,0:T(8,128)(2,1)S(1)}, bf16[192,768]{1,0:T(8,128)(2,1)S(1)}, u32[]{:S(2)}, u32[]{:S(2)}) %collective-permute-start.5) | collective-permute-done | bytes 294944 | tf_op jit(solution)/shard_map/ppermute | solution.py:957
  35.9 2.1 %norm_back.1 = (f32[32,32,384]{2,1,0:T(8,128)S(1)}, bf16[3,32,384]{2,1,0:T(8,128)(2,1)S(1)}, bf16[3,32,384]{2,1,0:T(8,128)(2,1)S(1)}) custom-call(bf16[384,1536]{1,0:T(8,128)(2,1)S(1)} %get-tuple-element.82.turned_ref, bf16[768,1024]{1,0:T(8,128)(2,1)S(1)} %get-tuple-element.103.other_ref, bf16[768,1024]{1,0:T(8,128)(2,1)S(1)} %get-tuple-element.104.mine_ref, ...), custom_call_target="tpu_custom_call" | custom-call | flops 230000000 | bytes 1048576 | tf_op jit(solution)/shard_map/norm_back/pallas_call | solution.py:683
  38.0 3.9 %collective-permute-start.9 = (bf16[3,32,384]{2,1,0:T(8,128)(2,1)S(1)}, bf16[3,32,384]{2,1,0:T(8,128)(2,1)S(1)}, u32[]{:S(2)}, u32[]{:S(2)}) collective-permute-start(bf16[3,32,384]{2,1,0:T(8,128)(2,1)S(1)} %get-tuple-element.112), channel_id=1, source_target_pairs={{0,15},{1,0},{2,1},{3,2},{4,3},{5,4},{6,5},{7,6},{8,7},{9,8},{10,9... | collective-permute-start | bytes 221192 | tf_op jit(solution)/shard_map/ppermute | solution.py:915
  42.0 1.6 %collective-permute-start.11 = (bf16[48,768]{1,0:T(8,128)(2,1)S(1)}, bf16[48,768]{1,0:T(8,128)(2,1)S(1)}, u32[]{:S(2)}, u32[]{:S(2)}) collective-permute-start(bf16[48,768]{1,0:T(8,128)(2,1)S(1)} %get-tuple-element.118), channel_id=1, source_target_pairs={{0,1},{1,128},{2,3},{3,130},{4,5},{5,132},{6,7},{7,134},{8,9},{9,1... | collective-permute-start | bytes 221192 | tf_op jit(solution)/shard_map/ppermute | solution.py:968
  43.6 2.7 %collective-permute-start.10 = (bf16[48,768]{1,0:T(8,128)(2,1)S(1)}, bf16[48,768]{1,0:T(8,128)(2,1)S(1)}, u32[]{:S(2)}, u32[]{:S(2)}) collective-permute-start(bf16[48,768]{1,0:T(8,128)(2,1)S(1)} %get-tuple-element.119), channel_id=1, source_target_pairs={{0,128},{1,129},{2,130},{3,131},{4,132},{5,133},{6,134},{7,135},{8... | collective-permute-start | bytes 221192 | tf_op jit(solution)/shard_map/ppermute | solution.py:968
  46.3 1.1 %collective-permute-start.12 = (bf16[48,768]{1,0:T(8,128)(2,1)S(1)}, bf16[48,768]{1,0:T(8,128)(2,1)S(1)}, u32[]{:S(2)}, u32[]{:S(2)}) collective-permute-start(bf16[48,768]{1,0:T(8,128)(2,1)S(1)} %get-tuple-element.120), channel_id=1, source_target_pairs={{0,129},{1,0},{2,131},{3,2},{4,133},{5,4},{6,135},{7,6},{8,137},{9... | collective-permute-start | bytes 221192 | tf_op jit(solution)/shard_map/ppermute | solution.py:968
  47.5 2.7 %back_conv.2 = (f32[1024,128]{1,0:T(8,128)S(1)}, f32[1024,128]{1,0:T(8,128)S(1)}) custom-call(f32[1024,384]{1,0:T(8,128)S(1)} %bitcast.24, f32[49,1,384]{2,1,0:T(1,128)S(1)} %bitcast.16), custom_call_target="tpu_custom_call" | custom-call | flops 3449999872 | bytes 1048576 | tf_op jit(solution)/shard_map/back_conv/pallas_call | solution.py:137
  50.1 0.5 collective-permute-done.12.third_ref
  50.8 0.5 collective-permute-start.13
  51.4 5.8 %collective-permute-start.16 = (f32[12,768]{1,0:T(8,128)S(1)}, f32[12,768]{1,0:T(8,128)S(1)}, u32[]{:S(2)}, u32[]{:S(2)}) collective-permute-start(f32[12,768]{1,0:T(8,128)S(1)} %get-tuple-element.137), channel_id=1, source_target_pairs={{0,4},{1,5},{2,6},{3,7},{4,8},{5,9},{6,10},{7,11},{8,12},{9,13},{1... | collective-permute-start | bytes 110600 | tf_op jit(solution)/shard_map/ppermute | solution.py:974
  57.1 4.5 %collective-permute-start.15 = (f32[12,768]{1,0:T(8,128)S(1)}, f32[12,768]{1,0:T(8,128)S(1)}, u32[]{:S(2)}, u32[]{:S(2)}) collective-permute-start(f32[12,768]{1,0:T(8,128)S(1)} %get-tuple-element.138), channel_id=1, source_target_pairs={{0,8},{1,9},{2,10},{3,11},{4,12},{5,13},{6,14},{7,15},{8,0},{9,1},... | collective-permute-start | bytes 110600 | tf_op jit(solution)/shard_map/ppermute | solution.py:974
  61.9 1.3 %back_conv.3.conv2_ref = f32[1024,128]{1,0:T(8,128)S(1)} custom-call(f32[1024,384]{1,0:T(8,128)S(1)} %bitcast.26, f32[49,1,384]{2,1,0:T(1,128)S(1)} %bitcast.17), custom_call_target="tpu_custom_call" | custom-call | flops 1724999936 | bytes 1048576 | tf_op jit(solution)/shard_map/back_conv/pallas_call | solution.py:137
  63.2 2.1 %finish_inner.1 = (f32[1024,384]{1,0:T(8,128)}, f32[6,32,384]{2,1,0:T(8,128)S(1)}) custom-call(s32[4,4]{1,0:T(4,128)S(1)} %copy-done.2, f32[1024,128]{1,0:T(8,128)S(1)} %get-tuple-element.122.conv0_ref, f32[1024,128]{1,0:T(8,128)S(1)} %get-tuple-element.123.conv1_ref, f32[1024,128]{1,0:T(8,128)S(1)} %back_conv.3.conv2_ref, f32[49,1,384]{2,1,0:T(1,128)S(1)} %bitcast.18, ...), custom_call_target="tpu_custom_call" | custom-call | flops 2529999872 | bytes 1048576 | tf_op jit(solution)/shard_map/finish_inner/pallas_call | solution.py:717
  65.3 1.4 %collective-permute-done.15.refs_0_ = f32[12,768]{1,0:T(8,128)S(1)} collective-permute-done((f32[12,768]{1,0:T(8,128)S(1)}, f32[12,768]{1,0:T(8,128)S(1)}, u32[]{:S(2)}, u32[]{:S(2)}) %collective-permute-start.15) | collective-permute-done | bytes 36896 | tf_op jit(solution)/shard_map/ppermute | solution.py:974
  67.2 1.8 %finish_outer.1 = f32[1024,384]{1,0:T(8,128)} custom-call(s32[4,4]{1,0:T(4,128)S(1)} %copy-done.2, f32[1024,128]{1,0:T(8,128)S(1)} %get-tuple-element.122.conv0_ref, f32[1024,128]{1,0:T(8,128)S(1)} %get-tuple-element.123.conv1_ref, f32[1024,128]{1,0:T(8,128)S(1)} %back_conv.3.conv2_ref, f32[49,1,384]{2,1,0:T(1,128)S(1)} %bitcast.19, ...), custom_call_target="tpu_custom_call", output_to_operand_aliasing={{}: (9, {})} | custom-call | flops 1150000000 | bytes 1048576 | tf_op jit(solution)/shard_map/finish_outer/pallas_call | solution.py:754
  69.0 2.0 %collective-permute-done.18.arrived_ref = f32[6,768]{1,0:T(8,128)S(1)} collective-permute-done((f32[6,768]{1,0:T(8,128)S(1)}, f32[6,768]{1,0:T(8,128)S(1)}, u32[]{:S(2)}, u32[]{:S(2)}) %collective-permute-start.18) | collective-permute-done | bytes 18464 | tf_op jit(solution)/shard_map/ppermute | solution.py:981
  71.0 0.6 last_sum.1
  (47 shorter events, 1.9 us)
Async XLA Ops:
  0.6 4.2 %copy-start.1 = (f32[1,49,384]{2,0,1:T(1,128)S(1)}, f32[1,49,384]{2,0,1:T(1,128)}, u32[]{:S(2)}) copy-start(f32[1,49,384]{2,0,1:T(1,128)} %param.13) | copy-start | bytes 225796
  0.6 4.2 %copy-start.4 = (f32[1,32,32,384]{3,2,1,0:T(8,128)S(1)}, f32[1,32,32,384]{3,2,1,0:T(8,128)}, u32[]{:S(2)}) copy-start(f32[1,32,32,384]{3,2,1,0:T(8,128)} %param.10) | copy-start | bytes 4718596
  2.7 6.6 %collective-permute-start.1 = (bf16[3,32,384]{2,1,0:T(8,128)(2,1)}, bf16[3,32,384]{2,1,0:T(8,128)(2,1)S(1)}, u32[]{:S(2)}, u32[]{:S(2)}) collective-permute-start(bf16[3,32,384]{2,1,0:T(8,128)(2,1)} %get-tuple-element.78), channel_id=1, source_target_pairs={{0,15},{1,0},{2,1},{3,2},{4,3},{5,4},{6,5},{7,6},{8,7},{9,8},{10,9... | collective-permute-start | bytes 221192 | tf_op jit(solution)/shard_map/ppermute | solution.py:915
  3.8 5.5 %collective-permute-start = (bf16[3,32,384]{2,1,0:T(8,128)(2,1)}, bf16[3,32,384]{2,1,0:T(8,128)(2,1)S(1)}, u32[]{:S(2)}, u32[]{:S(2)}) collective-permute-start(bf16[3,32,384]{2,1,0:T(8,128)(2,1)} %get-tuple-element.79), channel_id=1, source_target_pairs={{0,1},{1,2},{2,3},{3,4},{4,5},{5,6},{6,7},{7,8},{8,9},{9,10},{10,1... | collective-permute-start | bytes 221192 | tf_op jit(solution)/shard_map/ppermute | solution.py:914
  4.8 2.1 %copy-start.5 = (bf16[1,1536,384]{2,1,0:T(8,128)(2,1)S(1)}, bf16[1,1536,384]{2,1,0:T(8,128)(2,1)}, u32[]{:S(2)}) copy-start(bf16[1,1536,384]{2,1,0:T(8,128)(2,1)} %param.17) | copy-start | bytes 3538948
  4.8 2.1 %copy-start.6 = (bf16[1,1536,384]{2,1,0:T(8,128)(2,1)S(1)}, bf16[1,1536,384]{2,1,0:T(8,128)(2,1)}, u32[]{:S(2)}) copy-start(bf16[1,1536,384]{2,1,0:T(8,128)(2,1)} %param.19) | copy-start | bytes 3538948
  4.8 2.1 %copy-start.7 = (f32[1,1536]{1,0:T(1,128)S(1)}, f32[1,1536]{1,0:T(1,128)}, u32[]{:S(2)}) copy-start(f32[1,1536]{1,0:T(1,128)} %bias_ref.2) | copy-start | bytes 18436
  7.0 1.6 %copy-start = (f32[1,32,32,384]{3,2,1,0:T(8,128)S(1)}, f32[1,32,32,384]{3,2,1,0:T(8,128)}, u32[]{:S(2)}) copy-start(f32[1,32,32,384]{3,2,1,0:T(8,128)} %param.11) | copy-start | bytes 4718596
  7.0 1.6 %copy-start.2 = (s32[4,4]{1,0:T(4,128)S(1)}, s32[4,4]{1,0:T(4,128)}, u32[]{:S(2)}) copy-start(s32[4,4]{1,0:T(4,128)} %counts_ref.5) | copy-start | bytes 196
  9.4 6.1 %collective-permute-start.3 = (bf16[3,48,384]{2,1,0:T(8,128)(2,1)S(1)}, bf16[3,48,384]{2,1,0:T(8,128)(2,1)S(1)}, u32[]{:S(2)}, u32[]{:S(2)}) collective-permute-start(bf16[3,48,384]{2,1,0:T(8,128)(2,1)S(1)} %get-tuple-element.87), channel_id=1, source_target_pairs={{0,112},{16,0},{32,16},{48,32},{64,48},{80,64},{96,80},{112,96},{1... | collective-permute-start | bytes 331784 | tf_op jit(solution)/shard_map/ppermute | solution.py:921
  11.3 5.4 %copy-start.3 = (f32[1,384]{1,0:T(1,128)S(1)}, f32[1,384]{1,0:T(1,128)}, u32[]{:S(2)}) copy-start(f32[1,384]{1,0:T(1,128)} %gain_ref.3) | copy-start | bytes 4612
  11.3 5.4 %copy-start.8 = (f32[1,384]{1,0:T(1,128)S(1)}, f32[1,384]{1,0:T(1,128)}, u32[]{:S(2)}) copy-start(f32[1,384]{1,0:T(1,128)} %bias_ref.3) | copy-start | bytes 4612
  11.3 5.4 %copy-start.9 = (f32[1,384]{1,0:T(1,128)S(1)}, f32[1,384]{1,0:T(1,128)}, u32[]{:S(2)}) copy-start(f32[1,384]{1,0:T(1,128)} %shift_ref.1) | copy-start | bytes 4612
  11.3 5.4 %collective-permute-start.2 = (bf16[3,48,384]{2,1,0:T(8,128)(2,1)S(1)}, bf16[3,48,384]{2,1,0:T(8,128)(2,1)S(1)}, u32[]{:S(2)}, u32[]{:S(2)}) collective-permute-start(bf16[3,48,384]{2,1,0:T(8,128)(2,1)S(1)} %get-tuple-element.88), channel_id=1, source_target_pairs={{0,16},{16,32},{32,48},{48,64},{64,80},{80,96},{96,112},{112,0},{1... | collective-permute-start | bytes 331784 | tf_op jit(solution)/shard_map/ppermute | solution.py:920
  23.3 3.1 %collective-permute-start.4 = (bf16[768,768]{1,0:T(8,128)(2,1)S(1)}, bf16[768,768]{1,0:T(8,128)(2,1)S(1)}, u32[]{:S(2)}, u32[]{:S(2)}) collective-permute-start(bf16[768,768]{1,0:T(8,128)(2,1)S(1)} %get-tuple-element.97), channel_id=1, source_target_pairs={{0,16},{16,0},{32,48},{48,32},{64,80},{80,64},{96,112},{112,96},{1... | collective-permute-start | bytes 3538952 | tf_op jit(solution)/shard_map/ppermute | solution.py:954
  26.5 9.4 %collective-permute-start.5 = (bf16[192,768]{1,0:T(8,128)(2,1)S(1)}, bf16[192,768]{1,0:T(8,128)(2,1)S(1)}, u32[]{:S(2)}, u32[]{:S(2)}) collective-permute-start(bf16[192,768]{1,0:T(8,128)(2,1)S(1)} %get-tuple-element.98), channel_id=1, source_target_pairs={{0,96},{1,97},{2,98},{3,99},{4,100},{5,101},{6,102},{7,103},{8,104... | collective-permute-start | bytes 884744 | tf_op jit(solution)/shard_map/ppermute | solution.py:957
  28.4 13.4 %collective-permute-start.7 = (bf16[192,768]{1,0:T(8,128)(2,1)S(1)}, bf16[192,768]{1,0:T(8,128)(2,1)S(1)}, u32[]{:S(2)}, u32[]{:S(2)}) collective-permute-start(bf16[192,768]{1,0:T(8,128)(2,1)S(1)} %get-tuple-element.100), channel_id=1, source_target_pairs={{0,64},{1,65},{2,66},{3,67},{4,68},{5,69},{6,70},{7,71},{8,72},{9,... | collective-permute-start | bytes 884744 | tf_op jit(solution)/shard_map/ppermute | solution.py:958
  31.2 10.7 %collective-permute-start.6 = (bf16[192,768]{1,0:T(8,128)(2,1)S(1)}, bf16[192,768]{1,0:T(8,128)(2,1)S(1)}, u32[]{:S(2)}, u32[]{:S(2)}) collective-permute-start(bf16[192,768]{1,0:T(8,128)(2,1)S(1)} %get-tuple-element.102), channel_id=1, source_target_pairs={{0,32},{1,33},{2,34},{3,35},{4,36},{5,37},{6,38},{7,39},{8,40},{9,... | collective-permute-start | bytes 884744 | tf_op jit(solution)/shard_map/ppermute | solution.py:960
  38.0 12.1 %collective-permute-start.9 = (bf16[3,32,384]{2,1,0:T(8,128)(2,1)S(1)}, bf16[3,32,384]{2,1,0:T(8,128)(2,1)S(1)}, u32[]{:S(2)}, u32[]{:S(2)}) collective-permute-start(bf16[3,32,384]{2,1,0:T(8,128)(2,1)S(1)} %get-tuple-element.112), channel_id=1, source_target_pairs={{0,15},{1,0},{2,1},{3,2},{4,3},{5,4},{6,5},{7,6},{8,7},{9,8},{10,9... | collective-permute-start | bytes 221192 | tf_op jit(solution)/shard_map/ppermute | solution.py:915
  41.9 8.8 %collective-permute-start.8 = (bf16[3,32,384]{2,1,0:T(8,128)(2,1)S(1)}, bf16[3,32,384]{2,1,0:T(8,128)(2,1)S(1)}, u32[]{:S(2)}, u32[]{:S(2)}) collective-permute-start(bf16[3,32,384]{2,1,0:T(8,128)(2,1)S(1)} %get-tuple-element.113), channel_id=1, source_target_pairs={{0,1},{1,2},{2,3},{3,4},{4,5},{5,6},{6,7},{7,8},{8,9},{9,10},{10,1... | collective-permute-start | bytes 221192 | tf_op jit(solution)/shard_map/ppermute | solution.py:914
  42.0 8.1 %collective-permute-start.11 = (bf16[48,768]{1,0:T(8,128)(2,1)S(1)}, bf16[48,768]{1,0:T(8,128)(2,1)S(1)}, u32[]{:S(2)}, u32[]{:S(2)}) collective-permute-start(bf16[48,768]{1,0:T(8,128)(2,1)S(1)} %get-tuple-element.118), channel_id=1, source_target_pairs={{0,1},{1,128},{2,3},{3,130},{4,5},{5,132},{6,7},{7,134},{8,9},{9,1... | collective-permute-start | bytes 221192 | tf_op jit(solution)/shard_map/ppermute | solution.py:968
  43.6 6.5 %collective-permute-start.10 = (bf16[48,768]{1,0:T(8,128)(2,1)S(1)}, bf16[48,768]{1,0:T(8,128)(2,1)S(1)}, u32[]{:S(2)}, u32[]{:S(2)}) collective-permute-start(bf16[48,768]{1,0:T(8,128)(2,1)S(1)} %get-tuple-element.119), channel_id=1, source_target_pairs={{0,128},{1,129},{2,130},{3,131},{4,132},{5,133},{6,134},{7,135},{8... | collective-permute-start | bytes 221192 | tf_op jit(solution)/shard_map/ppermute | solution.py:968
  46.3 4.4 %collective-permute-start.12 = (bf16[48,768]{1,0:T(8,128)(2,1)S(1)}, bf16[48,768]{1,0:T(8,128)(2,1)S(1)}, u32[]{:S(2)}, u32[]{:S(2)}) collective-permute-start(bf16[48,768]{1,0:T(8,128)(2,1)S(1)} %get-tuple-element.120), channel_id=1, source_target_pairs={{0,129},{1,0},{2,131},{3,2},{4,133},{5,4},{6,135},{7,6},{8,137},{9... | collective-permute-start | bytes 221192 | tf_op jit(solution)/shard_map/ppermute | solution.py:968
  50.8 11.1 %collective-permute-start.14 = (bf16[3,48,384]{2,1,0:T(8,128)(2,1)S(1)}, bf16[3,48,384]{2,1,0:T(8,128)(2,1)S(1)}, u32[]{:S(2)}, u32[]{:S(2)}) collective-permute-start(bf16[3,48,384]{2,1,0:T(8,128)(2,1)S(1)} %get-tuple-element.131), channel_id=1, source_target_pairs={{0,112},{16,0},{32,16},{48,32},{64,48},{80,64},{96,80},{112,96},{1... | collective-permute-start | bytes 331784 | tf_op jit(solution)/shard_map/ppermute | solution.py:921
  50.8 11.1 %collective-permute-start.13 = (bf16[3,48,384]{2,1,0:T(8,128)(2,1)S(1)}, bf16[3,48,384]{2,1,0:T(8,128)(2,1)S(1)}, u32[]{:S(2)}, u32[]{:S(2)}) collective-permute-start(bf16[3,48,384]{2,1,0:T(8,128)(2,1)S(1)} %get-tuple-element.132), channel_id=1, source_target_pairs={{0,16},{16,32},{32,48},{48,64},{64,80},{80,96},{96,112},{112,0},{1... | collective-permute-start | bytes 331784 | tf_op jit(solution)/shard_map/ppermute | solution.py:920
  51.4 14.0 %collective-permute-start.16 = (f32[12,768]{1,0:T(8,128)S(1)}, f32[12,768]{1,0:T(8,128)S(1)}, u32[]{:S(2)}, u32[]{:S(2)}) collective-permute-start(f32[12,768]{1,0:T(8,128)S(1)} %get-tuple-element.137), channel_id=1, source_target_pairs={{0,4},{1,5},{2,6},{3,7},{4,8},{5,9},{6,10},{7,11},{8,12},{9,13},{1... | collective-permute-start | bytes 110600 | tf_op jit(solution)/shard_map/ppermute | solution.py:974
  57.1 9.7 %collective-permute-start.15 = (f32[12,768]{1,0:T(8,128)S(1)}, f32[12,768]{1,0:T(8,128)S(1)}, u32[]{:S(2)}, u32[]{:S(2)}) collective-permute-start(f32[12,768]{1,0:T(8,128)S(1)} %get-tuple-element.138), channel_id=1, source_target_pairs={{0,8},{1,9},{2,10},{3,11},{4,12},{5,13},{6,14},{7,15},{8,0},{9,1},... | collective-permute-start | bytes 110600 | tf_op jit(solution)/shard_map/ppermute | solution.py:974
  61.6 5.4 %collective-permute-start.17 = (f32[12,768]{1,0:T(8,128)S(1)}, f32[12,768]{1,0:T(8,128)S(1)}, u32[]{:S(2)}, u32[]{:S(2)}) collective-permute-start(f32[12,768]{1,0:T(8,128)S(1)} %get-tuple-element.139), channel_id=1, source_target_pairs={{0,12},{1,13},{2,14},{3,15},{4,0},{5,1},{6,2},{7,3},{8,4},{9,5},{1... | collective-permute-start | bytes 110600 | tf_op jit(solution)/shard_map/ppermute | solution.py:974
  67.1 3.9 %collective-permute-start.18 = (f32[6,768]{1,0:T(8,128)S(1)}, f32[6,768]{1,0:T(8,128)S(1)}, u32[]{:S(2)}, u32[]{:S(2)}) collective-permute-start(f32[6,768]{1,0:T(8,128)S(1)} %get-tuple-element.148), channel_id=1, source_target_pairs={{0,2},{1,3},{2,0},{3,1},{4,6},{5,7},{6,4},{7,5},{8,10},{9,11},{10,... | collective-permute-start | bytes 55304 | tf_op jit(solution)/shard_map/ppermute | solution.py:981

commit v10 on v9

--- a/solution.py
+++ b/solution.py
@@ -559,7 +559,7 @@
     channels = refs[0].shape[1]
     size = half // 4
     core, place = own_place()[0], phase_place(False)
-    chunks = [pl.multiple_of(lax.rem(place + step, 4) * size, size) for step in (3, 2)]
+    chunks = [pl.multiple_of(lax.rem(place + step, 4) * size, size) for step in (1, 2)]
     sources = [pl.multiple_of(core * half + chunk, size) for chunk in chunks]
     block = HiddenBlock(cells, sources, size, grad_pre_ref, chunks, scratch)
     block.dots(slice(0, block.total))
@@ -589,7 +589,7 @@
 def near_sends_body(sums_ref, arrived_ref, *sent_refs):
     size = sent_refs[0].shape[0]
     place = phase_place(False)
-    for n, step in enumerate((3, 2)):
+    for n, step in enumerate((1, 2)):
         chunk = pl.multiple_of(lax.rem(place + step, 4) * size, size)
         total = sums_ref[n * size : (n + 1) * size] + arrived_ref[pl.ds(chunk, size), :].astype(f32)
         sent_refs[n][...] = total.astype(bf16)
@@ -615,7 +615,7 @@
     channels = refs[0].shape[1]
     size = half // 4
     core, place = own_place()[0], phase_place(False)
-    chunks = [pl.multiple_of(lax.rem(place + step, 4) * size, size) for step in (1, 0)]
+    chunks = [pl.multiple_of(lax.rem(place + step, 4) * size, size) for step in (3, 0)]
     sources = [pl.multiple_of(core * half + chunk, size) for chunk in chunks]
     block = HiddenBlock(cells, sources, size, grad_pre_ref, chunks, refs[10:])
     block.dots(slice(0, block.total))
@@ -835,14 +835,15 @@
         found = chunks[0]
         for c in range(1, 4):
             found = jnp.where(wanted == c, chunks[c], found)
-        ref[...] = found
+        ref[...] = found.astype(ref.dtype)
 
 
 def split_ring(own, parts):
-    shape = jax.ShapeDtypeStruct((own.shape[0] // 4, own.shape[1]), f32)
+    size, width = own.shape[0] // 4, own.shape[1]
+    sent = jax.ShapeDtypeStruct((size, width), bf16)
     return pl.pallas_call(
         split_ring_body,
-        out_shape=(shape,) * 4,
+        out_shape=(jax.ShapeDtypeStruct((size, width), f32), sent, sent, sent),
         in_specs=[whole] * 4,
         out_specs=[whole] * 4,
         compiler_params=params(4),
@@ -953,13 +954,13 @@
     sent, far_pre = hidden_far(*inputs)
     arrived = lax.ppermute(sent, "lat", [(i, i ^ 1) for i in range(8)])
     sums, near_pre = near_first(*inputs)
-    three, two = near_sends(sums, arrived)
+    one, two = near_sends(sums, arrived)
+    part_one = lax.ppermute(one, every_axis, plane_pairs(1, True))
+    part_two = lax.ppermute(two, every_axis, plane_pairs(2, True))
+    own, three, near_pre = near_last(*inputs, arrived, after(near_pre, one, two))
     part_three = lax.ppermute(three, every_axis, plane_pairs(3, True))
-    part_two = lax.ppermute(two, every_axis, plane_pairs(2, True))
-    own, one, near_pre = near_last(*inputs, arrived, after(near_pre, three, two))
-    part_one = lax.ppermute(one, every_axis, plane_pairs(1, True))
-
-    far_pre, part_three = after((far_pre, part_three), one)
+
+    far_pre, part_one = after((far_pre, part_one), three)
     conv_grad, first, last = norm_back(expand_t, far_pre, near_pre, unit, spread, norm_gain)
     last, part_two = after((last, part_two))
     left, right = lon_halo(first, last)

time: 72.4 us -> 69.6 us (0.961); the launches traced: 71.6 us -> 69.5 us
  waiting for transfers between devices: 9.59 us -> 6.41 us
  starting transfers between devices: 27.7 us -> 28.8 us
    ppermute x1, waiting for transfers between devices: 3.8 us -> 0.01 us  [local(): part_three = lax.ppermute(three, every_axis, plane_pairs(3, True))]
    ppermute x1, starting transfers between devices: 0.16 us -> 3.31 us  [local(): part_two = lax.ppermute(two, every_axis, plane_pairs(2, True))]
    ppermute x2, starting transfers between devices: 1.92 us -> 4.68 us  [lat_halo(): bottom = lax.ppermute(up, 'lat', shifted('lat', -1))]
    ppermute x3, starting transfers between devices: 10.5 us -> 8.25 us  [local(): lax.ppermute(sent[i], every_axis, ring_pairs(i + 1))]
    ppermute x1, waiting for transfers between devices: 0.01 us -> 1.36 us  [local(): part_one = lax.ppermute(one, every_axis, plane_pairs(1, True))]
    ppermute x1, starting transfers between devices: 1.93 us -> 0.66 us  [local(): part_three = lax.ppermute(three, every_axis, plane_pairs(3, True))]
    ppermute x1, starting transfers between devices: 0.88 us -> 0.08 us  [local(): part_one = lax.ppermute(one, every_axis, plane_pairs(1, True))]
  transfers between devices with their start and end apart: 19 -> 19, of which waited for: 7 -> 6; matrix products, arithmetic and copies ran while one was open for 0% -> 0% of each run, Pallas kernels for 33% -> 34%
where the time goes in v10:
time: 69.6 us; the launch traced here: 69.5 us
  Pallas kernels  33.4 us (48%)
  starting transfers between devices  28.8 us (41%)
  waiting for transfers between devices  6.41 us (9%)
  between operations  0.94 us (1%)
    ppermute x3, starting transfers between devices, local(): lax.ppermute(sent[i], every_axis, ring_pairs(i + 1))  8.25 us
    pallas_call x2, Pallas kernels, inner_conv(): pl.pallas_call(functools.partial(inner_conv_body, parts), out_shape=(shap...  6.22 us
    ppermute x3, starting transfers between devices, local(): lax.ppermute(sent[i], every_axis, plane_pairs(i + 1, False))  5.44 us
    ppermute x2, starting transfers between devices, lon_halo(): right = lax.ppermute(first, 'lon', shifted('lon', -1))  4.98 us
    ppermute x2, starting transfers between devices, lat_halo(): bottom = lax.ppermute(up, 'lat', shifted('lat', -1))  4.68 us
    pallas_call x1, Pallas kernels, hidden_far(): pl.pallas_call(far_body, out_shape=(jax.ShapeDtypeStruct((half, 2 * chann...  4.65 us
    pallas_call x2, Pallas kernels, back_conv(): pl.pallas_call(functools.partial(back_conv_body, parts), out_shape=(shape...  4 us
    ppermute x1, starting transfers between devices, local(): part_two = lax.ppermute(two, every_axis, plane_pairs(2, True))  3.31 us
  transfers between devices with their start and end apart: 19, of which 6 were waited for; matrix products, arithmetic and copies ran while one was open for 0% of the time, Pallas kernels for 34%

profile of v10, /device:TPU:32, one launch (start us, length us, event | category | flops | bytes accessed | tf_op | source)
XLA Modules:
  0.0 69.5 jit_solution(519416383130108608)
XLA Ops:
  0.6 2.1 %side_cols.1 = (bf16[3,32,384]{2,1,0:T(8,128)(2,1)}, bf16[3,32,384]{2,1,0:T(8,128)(2,1)}) custom-call(f32[32,32,384]{2,1,0:T(8,128)} %bitcast.20), custom_call_target="tpu_custom_call" | custom-call | flops 1150000000 | bytes 1048576 | tf_op jit(solution)/shard_map/side_cols/pallas_call | solution.py:170
  2.7 1.1 %collective-permute-start.1 = (bf16[3,32,384]{2,1,0:T(8,128)(2,1)}, bf16[3,32,384]{2,1,0:T(8,128)(2,1)S(1)}, u32[]{:S(2)}, u32[]{:S(2)}) collective-permute-start(bf16[3,32,384]{2,1,0:T(8,128)(2,1)} %get-tuple-element.78), channel_id=1, source_target_pairs={{0,15},{1,0},{2,1},{3,2},{4,3},{5,4},{6,5},{7,6},{8,7},{9,8},{10,9... | collective-permute-start | bytes 221192 | tf_op jit(solution)/shard_map/ppermute | solution.py:916
  3.8 1.0 %collective-permute-start = (bf16[3,32,384]{2,1,0:T(8,128)(2,1)}, bf16[3,32,384]{2,1,0:T(8,128)(2,1)S(1)}, u32[]{:S(2)}, u32[]{:S(2)}) collective-permute-start(bf16[3,32,384]{2,1,0:T(8,128)(2,1)} %get-tuple-element.79), channel_id=1, source_target_pairs={{0,1},{1,2},{2,3},{3,4},{4,5},{5,6},{6,7},{7,8},{8,9},{9,10},{10,1... | collective-permute-start | bytes 221192 | tf_op jit(solution)/shard_map/ppermute | solution.py:915
  4.8 2.1 %inner_conv.2.conv0_ref = f32[1024,128]{1,0:T(8,128)S(1)} custom-call(f32[1024,384]{1,0:T(8,128)S(1)} %bitcast.21, f32[49,1,384]{2,1,0:T(1,128)S(1)} %bitcast.13), custom_call_target="tpu_custom_call" | custom-call | flops 2529999872 | bytes 1048576 | tf_op jit(solution)/shard_map/inner_conv/pallas_call | solution.py:87
  7.0 1.6 %arrange.1 = (bf16[1536,384]{1,0:T(8,128)(2,1)S(1)}, bf16[1536,384]{1,0:T(8,128)(2,1)S(1)}, bf16[384,1536]{1,0:T(8,128)(2,1)S(1)}, f32[1536,128]{1,0:T(8,128)S(1)}) custom-call(bf16[1536,384]{1,0:T(8,128)(2,1)S(1)} %bitcast.27, bf16[1536,384]{1,0:T(8,128)(2,1)S(1)} %bitcast.28, f32[1,1536]{1,0:T(1,128)S(1)} %copy-done.7), custom_call_target="tpu_custom_call" | custom-call | flops 1724999936 | bytes 1048576 | tf_op jit(solution)/shard_map/arrange/pallas_call | solution.py:416
  8.6 0.7 mask_rows.1.refs_1_
  9.4 1.9 %collective-permute-start.3 = (bf16[3,48,384]{2,1,0:T(8,128)(2,1)S(1)}, bf16[3,48,384]{2,1,0:T(8,128)(2,1)S(1)}, u32[]{:S(2)}, u32[]{:S(2)}) collective-permute-start(bf16[3,48,384]{2,1,0:T(8,128)(2,1)S(1)} %get-tuple-element.87), channel_id=1, source_target_pairs={{0,112},{16,0},{32,16},{48,32},{64,48},{80,64},{96,80},{112,96},{1... | collective-permute-start | bytes 331784 | tf_op jit(solution)/shard_map/ppermute | solution.py:922
  11.3 4.1 %inner_conv.3 = (f32[1024,128]{1,0:T(8,128)S(1)}, f32[1024,128]{1,0:T(8,128)S(1)}) custom-call(f32[1024,384]{1,0:T(8,128)S(1)} %bitcast.23, f32[49,1,384]{2,1,0:T(1,128)S(1)} %bitcast.14), custom_call_target="tpu_custom_call" | custom-call | flops 5059999744 | bytes 1048576 | tf_op jit(solution)/shard_map/inner_conv/pallas_call | solution.py:87
  15.4 1.2 %collective-permute-done.2.top_ref = bf16[3,48,384]{2,1,0:T(8,128)(2,1)S(1)} collective-permute-done((bf16[3,48,384]{2,1,0:T(8,128)(2,1)S(1)}, bf16[3,48,384]{2,1,0:T(8,128)(2,1)S(1)}, u32[]{:S(2)}, u32[]{:S(2)}) %collective-permute-start.2) | collective-permute-done | bytes 110624 | tf_op jit(solution)/shard_map/ppermute | solution.py:921
  16.7 1.9 %normalise.1 = (f32[1024,384]{1,0:T(8,128)S(1)}, f32[1024,128]{1,0:T(8,128)S(1)}, bf16[1024,384]{1,0:T(8,128)(2,1)S(1)}) custom-call(f32[1024,128]{1,0:T(8,128)S(1)} %inner_conv.2.conv0_ref, f32[1024,128]{1,0:T(8,128)S(1)} %get-tuple-element.90.conv1_ref, f32[1024,128]{1,0:T(8,128)S(1)} %get-tuple-element.91.conv2_ref, f32[49,1,384]{2,1,0:T(1,128)S(1)} %bitcast.15, ...), custom_call_target="tpu_custom_call" | custom-call | flops 3220000000 | bytes 1048576 | tf_op jit(solution)/shard_map/normalise/pallas_call | solution.py:325
  18.6 4.6 %hidden_far.1 = (bf16[768,768]{1,0:T(8,128)(2,1)S(1)}, bf16[768,1024]{1,0:T(8,128)(2,1)S(1)}) custom-call(bf16[1024,384]{1,0:T(8,128)(2,1)S(1)} %get-tuple-element.92.refs_0_, bf16[1024,384]{1,0:T(8,128)(2,1)S(1)} %mask_rows.1.refs_1_, bf16[1536,384]{1,0:T(8,128)(2,1)S(1)} %get-tuple-element.93.refs_2_, bf16[1536,384]{1,0:T(8,128)(2,1)S(1)} %get-tuple-element.94.refs_3_, ...), custom_call_target="tpu_custom_call" | custom-call | flops 5750000128 | bytes 1048576 | tf_op jit(solution)/shard_map/hidden_far/pallas_call | solution.py:541
  23.6 2.5 %near_first.1 = (f32[384,768]{1,0:T(8,128)S(1)}, bf16[768,1024]{1,0:T(8,128)(2,1)S(1)}) custom-call(bf16[1024,384]{1,0:T(8,128)(2,1)S(1)} %get-tuple-element.92.refs_0_, bf16[1024,384]{1,0:T(8,128)(2,1)S(1)} %mask_rows.1.refs_1_, bf16[1536,384]{1,0:T(8,128)(2,1)S(1)} %get-tuple-element.93.refs_2_, bf16[1536,384]{1,0:T(8,128)(2,1)S(1)} %get-tuple-element.94.refs_3_, ...), custom_call_target="tpu_custom_call" | custom-call | flops 3449999872 | bytes 1048576 | tf_op jit(solution)/shard_map/near_first/pallas_call | solution.py:574
  26.6 3.3 %collective-permute-start.6 = (bf16[192,768]{1,0:T(8,128)(2,1)S(1)}, bf16[192,768]{1,0:T(8,128)(2,1)S(1)}, u32[]{:S(2)}, u32[]{:S(2)}) collective-permute-start(bf16[192,768]{1,0:T(8,128)(2,1)S(1)} %get-tuple-element.100), channel_id=1, source_target_pairs={{0,64},{1,65},{2,66},{3,67},{4,68},{5,69},{6,70},{7,71},{8,72},{9,... | collective-permute-start | bytes 884744 | tf_op jit(solution)/shard_map/ppermute | solution.py:959
  29.9 2.6 %near_last.1 = (f32[192,768]{1,0:T(8,128)S(1)}, bf16[192,768]{1,0:T(8,128)(2,1)S(1)}, bf16[768,1024]{1,0:T(8,128)(2,1)S(1)}) custom-call(bf16[1024,384]{1,0:T(8,128)(2,1)S(1)} %get-tuple-element.92.refs_0_, bf16[1024,384]{1,0:T(8,128)(2,1)S(1)} %mask_rows.1.refs_1_, ...), custom_call_target="tpu_custom_call", output_to_operand_aliasing={{2}: (6, {})} | custom-call | flops 3449999872 | bytes 1048576 | tf_op jit(solution)/shard_map/near_last/pallas_call | solution.py:635
  32.5 0.7 collective-permute-start.7
  33.1 1.4 %collective-permute-done.5.first_ref = bf16[192,768]{1,0:T(8,128)(2,1)S(1)} collective-permute-done((bf16[192,768]{1,0:T(8,128)(2,1)S(1)}, bf16[192,768]{1,0:T(8,128)(2,1)S(1)}, u32[]{:S(2)}, u32[]{:S(2)}) %collective-permute-start.5) | collective-permute-done | bytes 294944 | tf_op jit(solution)/shard_map/ppermute | solution.py:958
  34.5 2.1 %norm_back.1 = (f32[32,32,384]{2,1,0:T(8,128)S(1)}, bf16[3,32,384]{2,1,0:T(8,128)(2,1)S(1)}, bf16[3,32,384]{2,1,0:T(8,128)(2,1)S(1)}) custom-call(bf16[384,1536]{1,0:T(8,128)(2,1)S(1)} %get-tuple-element.82.turned_ref, bf16[768,1024]{1,0:T(8,128)(2,1)S(1)} %get-tuple-element.103.other_ref, bf16[768,1024]{1,0:T(8,128)(2,1)S(1)} %get-tuple-element.104.mine_ref, ...), custom_call_target="tpu_custom_call" | custom-call | flops 230000000 | bytes 1048576 | tf_op jit(solution)/shard_map/norm_back/pallas_call | solution.py:683
  36.6 3.9 %collective-permute-start.9 = (bf16[3,32,384]{2,1,0:T(8,128)(2,1)S(1)}, bf16[3,32,384]{2,1,0:T(8,128)(2,1)S(1)}, u32[]{:S(2)}, u32[]{:S(2)}) collective-permute-start(bf16[3,32,384]{2,1,0:T(8,128)(2,1)S(1)} %get-tuple-element.112), channel_id=1, source_target_pairs={{0,15},{1,0},{2,1},{3,2},{4,3},{5,4},{6,5},{7,6},{8,7},{9,8},{10,9... | collective-permute-start | bytes 221192 | tf_op jit(solution)/shard_map/ppermute | solution.py:916
  40.7 1.6 %collective-permute-start.11 = (bf16[48,768]{1,0:T(8,128)(2,1)S(1)}, bf16[48,768]{1,0:T(8,128)(2,1)S(1)}, u32[]{:S(2)}, u32[]{:S(2)}) collective-permute-start(bf16[48,768]{1,0:T(8,128)(2,1)S(1)} %get-tuple-element.118), channel_id=1, source_target_pairs={{0,1},{1,128},{2,3},{3,130},{4,5},{5,132},{6,7},{7,134},{8,9},{9,1... | collective-permute-start | bytes 221192 | tf_op jit(solution)/shard_map/ppermute | solution.py:969
  42.2 2.7 %collective-permute-start.10 = (bf16[48,768]{1,0:T(8,128)(2,1)S(1)}, bf16[48,768]{1,0:T(8,128)(2,1)S(1)}, u32[]{:S(2)}, u32[]{:S(2)}) collective-permute-start(bf16[48,768]{1,0:T(8,128)(2,1)S(1)} %get-tuple-element.119), channel_id=1, source_target_pairs={{0,128},{1,129},{2,130},{3,131},{4,132},{5,133},{6,134},{7,135},{8... | collective-permute-start | bytes 221192 | tf_op jit(solution)/shard_map/ppermute | solution.py:969
  45.0 1.1 %collective-permute-start.12 = (bf16[48,768]{1,0:T(8,128)(2,1)S(1)}, bf16[48,768]{1,0:T(8,128)(2,1)S(1)}, u32[]{:S(2)}, u32[]{:S(2)}) collective-permute-start(bf16[48,768]{1,0:T(8,128)(2,1)S(1)} %get-tuple-element.120), channel_id=1, source_target_pairs={{0,129},{1,0},{2,131},{3,2},{4,133},{5,4},{6,135},{7,6},{8,137},{9... | collective-permute-start | bytes 221192 | tf_op jit(solution)/shard_map/ppermute | solution.py:969
  46.1 2.7 %back_conv.2 = (f32[1024,128]{1,0:T(8,128)S(1)}, f32[1024,128]{1,0:T(8,128)S(1)}) custom-call(f32[1024,384]{1,0:T(8,128)S(1)} %bitcast.24, f32[49,1,384]{2,1,0:T(1,128)S(1)} %bitcast.16), custom_call_target="tpu_custom_call" | custom-call | flops 3449999872 | bytes 1048576 | tf_op jit(solution)/shard_map/back_conv/pallas_call | solution.py:137
  48.8 0.5 collective-permute-done.12.third_ref
  49.4 2.8 %collective-permute-start.14 = (bf16[3,48,384]{2,1,0:T(8,128)(2,1)S(1)}, bf16[3,48,384]{2,1,0:T(8,128)(2,1)S(1)}, u32[]{:S(2)}, u32[]{:S(2)}) collective-permute-start(bf16[3,48,384]{2,1,0:T(8,128)(2,1)S(1)} %get-tuple-element.131), channel_id=1, source_target_pairs={{0,112},{16,0},{32,16},{48,32},{64,48},{80,64},{96,80},{112,96},{1... | collective-permute-start | bytes 331784 | tf_op jit(solution)/shard_map/ppermute | solution.py:922
  52.3 3.5 %collective-permute-start.16 = (bf16[12,768]{1,0:T(8,128)(2,1)S(1)}, bf16[12,768]{1,0:T(8,128)(2,1)S(1)}, u32[]{:S(2)}, u32[]{:S(2)}) collective-permute-start(bf16[12,768]{1,0:T(8,128)(2,1)S(1)} %get-tuple-element.137), channel_id=1, source_target_pairs={{0,4},{1,5},{2,6},{3,7},{4,8},{5,9},{6,10},{7,11},{8,12},{9,13},{1... | collective-permute-start | bytes 55304 | tf_op jit(solution)/shard_map/ppermute | solution.py:975
  55.8 4.5 %collective-permute-start.15 = (bf16[12,768]{1,0:T(8,128)(2,1)S(1)}, bf16[12,768]{1,0:T(8,128)(2,1)S(1)}, u32[]{:S(2)}, u32[]{:S(2)}) collective-permute-start(bf16[12,768]{1,0:T(8,128)(2,1)S(1)} %get-tuple-element.138), channel_id=1, source_target_pairs={{0,8},{1,9},{2,10},{3,11},{4,12},{5,13},{6,14},{7,15},{8,0},{9,1},... | collective-permute-start | bytes 55304 | tf_op jit(solution)/shard_map/ppermute | solution.py:975
  60.5 1.3 %back_conv.3.conv2_ref = f32[1024,128]{1,0:T(8,128)S(1)} custom-call(f32[1024,384]{1,0:T(8,128)S(1)} %bitcast.26, f32[49,1,384]{2,1,0:T(1,128)S(1)} %bitcast.17), custom_call_target="tpu_custom_call" | custom-call | flops 1724999936 | bytes 1048576 | tf_op jit(solution)/shard_map/back_conv/pallas_call | solution.py:137
  61.9 2.1 %finish_inner.1 = (f32[1024,384]{1,0:T(8,128)}, f32[6,32,384]{2,1,0:T(8,128)S(1)}) custom-call(s32[4,4]{1,0:T(4,128)S(1)} %copy-done.2, f32[1024,128]{1,0:T(8,128)S(1)} %get-tuple-element.122.conv0_ref, f32[1024,128]{1,0:T(8,128)S(1)} %get-tuple-element.123.conv1_ref, f32[1024,128]{1,0:T(8,128)S(1)} %back_conv.3.conv2_ref, f32[49,1,384]{2,1,0:T(1,128)S(1)} %bitcast.18, ...), custom_call_target="tpu_custom_call" | custom-call | flops 2529999872 | bytes 1048576 | tf_op jit(solution)/shard_map/finish_inner/pallas_call | solution.py:717
  64.0 1.0 %collective-permute-done.17.refs_2_ = bf16[12,768]{1,0:T(8,128)(2,1)S(1)} collective-permute-done((bf16[12,768]{1,0:T(8,128)(2,1)S(1)}, bf16[12,768]{1,0:T(8,128)(2,1)S(1)}, u32[]{:S(2)}, u32[]{:S(2)}) %collective-permute-start.17) | collective-permute-done | bytes 18464 | tf_op jit(solution)/shard_map/ppermute | solution.py:975
  65.1 1.8 %finish_outer.1 = f32[1024,384]{1,0:T(8,128)} custom-call(s32[4,4]{1,0:T(4,128)S(1)} %copy-done.2, f32[1024,128]{1,0:T(8,128)S(1)} %get-tuple-element.122.conv0_ref, f32[1024,128]{1,0:T(8,128)S(1)} %get-tuple-element.123.conv1_ref, f32[1024,128]{1,0:T(8,128)S(1)} %back_conv.3.conv2_ref, f32[49,1,384]{2,1,0:T(1,128)S(1)} %bitcast.19, ...), custom_call_target="tpu_custom_call", output_to_operand_aliasing={{}: (9, {})} | custom-call | flops 1150000000 | bytes 1048576 | tf_op jit(solution)/shard_map/finish_outer/pallas_call | solution.py:754
  67.0 2.0 %collective-permute-done.18.arrived_ref = f32[6,768]{1,0:T(8,128)S(1)} collective-permute-done((f32[6,768]{1,0:T(8,128)S(1)}, f32[6,768]{1,0:T(8,128)S(1)}, u32[]{:S(2)}, u32[]{:S(2)}) %collective-permute-start.18) | collective-permute-done | bytes 18464 | tf_op jit(solution)/shard_map/ppermute | solution.py:982
  68.9 0.6 last_sum.1
  (47 shorter events, 1.6 us)
Async XLA Ops:
  0.6 4.2 %copy-start.1 = (f32[1,49,384]{2,0,1:T(1,128)S(1)}, f32[1,49,384]{2,0,1:T(1,128)}, u32[]{:S(2)}) copy-start(f32[1,49,384]{2,0,1:T(1,128)} %param.13) | copy-start | bytes 225796
  0.6 4.2 %copy-start.4 = (f32[1,32,32,384]{3,2,1,0:T(8,128)S(1)}, f32[1,32,32,384]{3,2,1,0:T(8,128)}, u32[]{:S(2)}) copy-start(f32[1,32,32,384]{3,2,1,0:T(8,128)} %param.10) | copy-start | bytes 4718596
  2.7 6.6 %collective-permute-start.1 = (bf16[3,32,384]{2,1,0:T(8,128)(2,1)}, bf16[3,32,384]{2,1,0:T(8,128)(2,1)S(1)}, u32[]{:S(2)}, u32[]{:S(2)}) collective-permute-start(bf16[3,32,384]{2,1,0:T(8,128)(2,1)} %get-tuple-element.78), channel_id=1, source_target_pairs={{0,15},{1,0},{2,1},{3,2},{4,3},{5,4},{6,5},{7,6},{8,7},{9,8},{10,9... | collective-permute-start | bytes 221192 | tf_op jit(solution)/shard_map/ppermute | solution.py:916
  3.8 5.5 %collective-permute-start = (bf16[3,32,384]{2,1,0:T(8,128)(2,1)}, bf16[3,32,384]{2,1,0:T(8,128)(2,1)S(1)}, u32[]{:S(2)}, u32[]{:S(2)}) collective-permute-start(bf16[3,32,384]{2,1,0:T(8,128)(2,1)} %get-tuple-element.79), channel_id=1, source_target_pairs={{0,1},{1,2},{2,3},{3,4},{4,5},{5,6},{6,7},{7,8},{8,9},{9,10},{10,1... | collective-permute-start | bytes 221192 | tf_op jit(solution)/shard_map/ppermute | solution.py:915
  4.8 2.1 %copy-start.5 = (bf16[1,1536,384]{2,1,0:T(8,128)(2,1)S(1)}, bf16[1,1536,384]{2,1,0:T(8,128)(2,1)}, u32[]{:S(2)}) copy-start(bf16[1,1536,384]{2,1,0:T(8,128)(2,1)} %param.17) | copy-start | bytes 3538948
  4.8 2.1 %copy-start.6 = (bf16[1,1536,384]{2,1,0:T(8,128)(2,1)S(1)}, bf16[1,1536,384]{2,1,0:T(8,128)(2,1)}, u32[]{:S(2)}) copy-start(bf16[1,1536,384]{2,1,0:T(8,128)(2,1)} %param.19) | copy-start | bytes 3538948
  4.8 2.1 %copy-start.7 = (f32[1,1536]{1,0:T(1,128)S(1)}, f32[1,1536]{1,0:T(1,128)}, u32[]{:S(2)}) copy-start(f32[1,1536]{1,0:T(1,128)} %bias_ref.2) | copy-start | bytes 18436
  7.0 1.6 %copy-start = (f32[1,32,32,384]{3,2,1,0:T(8,128)S(1)}, f32[1,32,32,384]{3,2,1,0:T(8,128)}, u32[]{:S(2)}) copy-start(f32[1,32,32,384]{3,2,1,0:T(8,128)} %param.11) | copy-start | bytes 4718596
  7.0 1.6 %copy-start.2 = (s32[4,4]{1,0:T(4,128)S(1)}, s32[4,4]{1,0:T(4,128)}, u32[]{:S(2)}) copy-start(s32[4,4]{1,0:T(4,128)} %counts_ref.5) | copy-start | bytes 196
  9.4 6.1 %collective-permute-start.3 = (bf16[3,48,384]{2,1,0:T(8,128)(2,1)S(1)}, bf16[3,48,384]{2,1,0:T(8,128)(2,1)S(1)}, u32[]{:S(2)}, u32[]{:S(2)}) collective-permute-start(bf16[3,48,384]{2,1,0:T(8,128)(2,1)S(1)} %get-tuple-element.87), channel_id=1, source_target_pairs={{0,112},{16,0},{32,16},{48,32},{64,48},{80,64},{96,80},{112,96},{1... | collective-permute-start | bytes 331784 | tf_op jit(solution)/shard_map/ppermute | solution.py:922
  11.3 5.4 %copy-start.3 = (f32[1,384]{1,0:T(1,128)S(1)}, f32[1,384]{1,0:T(1,128)}, u32[]{:S(2)}) copy-start(f32[1,384]{1,0:T(1,128)} %gain_ref.3) | copy-start | bytes 4612
  11.3 5.4 %copy-start.8 = (f32[1,384]{1,0:T(1,128)S(1)}, f32[1,384]{1,0:T(1,128)}, u32[]{:S(2)}) copy-start(f32[1,384]{1,0:T(1,128)} %bias_ref.3) | copy-start | bytes 4612
  11.3 5.4 %copy-start.9 = (f32[1,384]{1,0:T(1,128)S(1)}, f32[1,384]{1,0:T(1,128)}, u32[]{:S(2)}) copy-start(f32[1,384]{1,0:T(1,128)} %shift_ref.1) | copy-start | bytes 4612
  11.3 5.4 %collective-permute-start.2 = (bf16[3,48,384]{2,1,0:T(8,128)(2,1)S(1)}, bf16[3,48,384]{2,1,0:T(8,128)(2,1)S(1)}, u32[]{:S(2)}, u32[]{:S(2)}) collective-permute-start(bf16[3,48,384]{2,1,0:T(8,128)(2,1)S(1)} %get-tuple-element.88), channel_id=1, source_target_pairs={{0,16},{16,32},{32,48},{48,64},{64,80},{80,96},{96,112},{112,0},{1... | collective-permute-start | bytes 331784 | tf_op jit(solution)/shard_map/ppermute | solution.py:921
  23.3 3.1 %collective-permute-start.4 = (bf16[768,768]{1,0:T(8,128)(2,1)S(1)}, bf16[768,768]{1,0:T(8,128)(2,1)S(1)}, u32[]{:S(2)}, u32[]{:S(2)}) collective-permute-start(bf16[768,768]{1,0:T(8,128)(2,1)S(1)} %get-tuple-element.97), channel_id=1, source_target_pairs={{0,16},{16,0},{32,48},{48,32},{64,80},{80,64},{96,112},{112,96},{1... | collective-permute-start | bytes 3538952 | tf_op jit(solution)/shard_map/ppermute | solution.py:955
  26.5 8.0 %collective-permute-start.5 = (bf16[192,768]{1,0:T(8,128)(2,1)S(1)}, bf16[192,768]{1,0:T(8,128)(2,1)S(1)}, u32[]{:S(2)}, u32[]{:S(2)}) collective-permute-start(bf16[192,768]{1,0:T(8,128)(2,1)S(1)} %get-tuple-element.98), channel_id=1, source_target_pairs={{0,32},{1,33},{2,34},{3,35},{4,36},{5,37},{6,38},{7,39},{8,40},{9,... | collective-permute-start | bytes 884744 | tf_op jit(solution)/shard_map/ppermute | solution.py:958
  26.6 13.9 %collective-permute-start.6 = (bf16[192,768]{1,0:T(8,128)(2,1)S(1)}, bf16[192,768]{1,0:T(8,128)(2,1)S(1)}, u32[]{:S(2)}, u32[]{:S(2)}) collective-permute-start(bf16[192,768]{1,0:T(8,128)(2,1)S(1)} %get-tuple-element.100), channel_id=1, source_target_pairs={{0,64},{1,65},{2,66},{3,67},{4,68},{5,69},{6,70},{7,71},{8,72},{9,... | collective-permute-start | bytes 884744 | tf_op jit(solution)/shard_map/ppermute | solution.py:959
  32.5 8.0 %collective-permute-start.7 = (bf16[192,768]{1,0:T(8,128)(2,1)S(1)}, bf16[192,768]{1,0:T(8,128)(2,1)S(1)}, u32[]{:S(2)}, u32[]{:S(2)}) collective-permute-start(bf16[192,768]{1,0:T(8,128)(2,1)S(1)} %get-tuple-element.102), channel_id=1, source_target_pairs={{0,96},{1,97},{2,98},{3,99},{4,100},{5,101},{6,102},{7,103},{8,104... | collective-permute-start | bytes 884744 | tf_op jit(solution)/shard_map/ppermute | solution.py:961
  36.6 12.1 %collective-permute-start.9 = (bf16[3,32,384]{2,1,0:T(8,128)(2,1)S(1)}, bf16[3,32,384]{2,1,0:T(8,128)(2,1)S(1)}, u32[]{:S(2)}, u32[]{:S(2)}) collective-permute-start(bf16[3,32,384]{2,1,0:T(8,128)(2,1)S(1)} %get-tuple-element.112), channel_id=1, source_target_pairs={{0,15},{1,0},{2,1},{3,2},{4,3},{5,4},{6,5},{7,6},{8,7},{9,8},{10,9... | collective-permute-start | bytes 221192 | tf_op jit(solution)/shard_map/ppermute | solution.py:916
  40.5 8.8 %collective-permute-start.8 = (bf16[3,32,384]{2,1,0:T(8,128)(2,1)S(1)}, bf16[3,32,384]{2,1,0:T(8,128)(2,1)S(1)}, u32[]{:S(2)}, u32[]{:S(2)}) collective-permute-start(bf16[3,32,384]{2,1,0:T(8,128)(2,1)S(1)} %get-tuple-element.113), channel_id=1, source_target_pairs={{0,1},{1,2},{2,3},{3,4},{4,5},{5,6},{6,7},{7,8},{8,9},{9,10},{10,1... | collective-permute-start | bytes 221192 | tf_op jit(solution)/shard_map/ppermute | solution.py:915
  40.7 8.1 %collective-permute-start.11 = (bf16[48,768]{1,0:T(8,128)(2,1)S(1)}, bf16[48,768]{1,0:T(8,128)(2,1)S(1)}, u32[]{:S(2)}, u32[]{:S(2)}) collective-permute-start(bf16[48,768]{1,0:T(8,128)(2,1)S(1)} %get-tuple-element.118), channel_id=1, source_target_pairs={{0,1},{1,128},{2,3},{3,130},{4,5},{5,132},{6,7},{7,134},{8,9},{9,1... | collective-permute-start | bytes 221192 | tf_op jit(solution)/shard_map/ppermute | solution.py:969
  42.2 6.5 %collective-permute-start.10 = (bf16[48,768]{1,0:T(8,128)(2,1)S(1)}, bf16[48,768]{1,0:T(8,128)(2,1)S(1)}, u32[]{:S(2)}, u32[]{:S(2)}) collective-permute-start(bf16[48,768]{1,0:T(8,128)(2,1)S(1)} %get-tuple-element.119), channel_id=1, source_target_pairs={{0,128},{1,129},{2,130},{3,131},{4,132},{5,133},{6,134},{7,135},{8... | collective-permute-start | bytes 221192 | tf_op jit(solution)/shard_map/ppermute | solution.py:969
  45.0 4.4 %collective-permute-start.12 = (bf16[48,768]{1,0:T(8,128)(2,1)S(1)}, bf16[48,768]{1,0:T(8,128)(2,1)S(1)}, u32[]{:S(2)}, u32[]{:S(2)}) collective-permute-start(bf16[48,768]{1,0:T(8,128)(2,1)S(1)} %get-tuple-element.120), channel_id=1, source_target_pairs={{0,129},{1,0},{2,131},{3,2},{4,133},{5,4},{6,135},{7,6},{8,137},{9... | collective-permute-start | bytes 221192 | tf_op jit(solution)/shard_map/ppermute | solution.py:969
  49.4 11.1 %collective-permute-start.14 = (bf16[3,48,384]{2,1,0:T(8,128)(2,1)S(1)}, bf16[3,48,384]{2,1,0:T(8,128)(2,1)S(1)}, u32[]{:S(2)}, u32[]{:S(2)}) collective-permute-start(bf16[3,48,384]{2,1,0:T(8,128)(2,1)S(1)} %get-tuple-element.131), channel_id=1, source_target_pairs={{0,112},{16,0},{32,16},{48,32},{64,48},{80,64},{96,80},{112,96},{1... | collective-permute-start | bytes 331784 | tf_op jit(solution)/shard_map/ppermute | solution.py:922
  52.2 8.4 %collective-permute-start.13 = (bf16[3,48,384]{2,1,0:T(8,128)(2,1)S(1)}, bf16[3,48,384]{2,1,0:T(8,128)(2,1)S(1)}, u32[]{:S(2)}, u32[]{:S(2)}) collective-permute-start(bf16[3,48,384]{2,1,0:T(8,128)(2,1)S(1)} %get-tuple-element.132), channel_id=1, source_target_pairs={{0,16},{16,32},{32,48},{48,64},{64,80},{80,96},{96,112},{112,0},{1... | collective-permute-start | bytes 331784 | tf_op jit(solution)/shard_map/ppermute | solution.py:921
  52.3 11.7 %collective-permute-start.16 = (bf16[12,768]{1,0:T(8,128)(2,1)S(1)}, bf16[12,768]{1,0:T(8,128)(2,1)S(1)}, u32[]{:S(2)}, u32[]{:S(2)}) collective-permute-start(bf16[12,768]{1,0:T(8,128)(2,1)S(1)} %get-tuple-element.137), channel_id=1, source_target_pairs={{0,4},{1,5},{2,6},{3,7},{4,8},{5,9},{6,10},{7,11},{8,12},{9,13},{1... | collective-permute-start | bytes 55304 | tf_op jit(solution)/shard_map/ppermute | solution.py:975
  55.8 8.2 %collective-permute-start.15 = (bf16[12,768]{1,0:T(8,128)(2,1)S(1)}, bf16[12,768]{1,0:T(8,128)(2,1)S(1)}, u32[]{:S(2)}, u32[]{:S(2)}) collective-permute-start(bf16[12,768]{1,0:T(8,128)(2,1)S(1)} %get-tuple-element.138), channel_id=1, source_target_pairs={{0,8},{1,9},{2,10},{3,11},{4,12},{5,13},{6,14},{7,15},{8,0},{9,1},... | collective-permute-start | bytes 55304 | tf_op jit(solution)/shard_map/ppermute | solution.py:975
  60.3 4.7 %collective-permute-start.17 = (bf16[12,768]{1,0:T(8,128)(2,1)S(1)}, bf16[12,768]{1,0:T(8,128)(2,1)S(1)}, u32[]{:S(2)}, u32[]{:S(2)}) collective-permute-start(bf16[12,768]{1,0:T(8,128)(2,1)S(1)} %get-tuple-element.139), channel_id=1, source_target_pairs={{0,12},{1,13},{2,14},{3,15},{4,0},{5,1},{6,2},{7,3},{8,4},{9,5},{1... | collective-permute-start | bytes 55304 | tf_op jit(solution)/shard_map/ppermute | solution.py:975
  65.0 3.9 %collective-permute-start.18 = (f32[6,768]{1,0:T(8,128)S(1)}, f32[6,768]{1,0:T(8,128)S(1)}, u32[]{:S(2)}, u32[]{:S(2)}) collective-permute-start(f32[6,768]{1,0:T(8,128)S(1)} %get-tuple-element.148), channel_id=1, source_target_pairs={{0,2},{1,3},{2,0},{3,1},{4,6},{5,7},{6,4},{7,5},{8,10},{9,11},{10,... | collective-permute-start | bytes 55304 | tf_op jit(solution)/shard_map/ppermute | solution.py:982

commit v11 on v10

--- a/solution.py
+++ b/solution.py
@@ -559,7 +559,7 @@
     channels = refs[0].shape[1]
     size = half // 4
     core, place = own_place()[0], phase_place(False)
-    chunks = [pl.multiple_of(lax.rem(place + step, 4) * size, size) for step in (1, 2)]
+    chunks = [pl.multiple_of(lax.rem(place + step, 4) * size, size) for step in (2, 3)]
     sources = [pl.multiple_of(core * half + chunk, size) for chunk in chunks]
     block = HiddenBlock(cells, sources, size, grad_pre_ref, chunks, scratch)
     block.dots(slice(0, block.total))
@@ -589,7 +589,7 @@
 def near_sends_body(sums_ref, arrived_ref, *sent_refs):
     size = sent_refs[0].shape[0]
     place = phase_place(False)
-    for n, step in enumerate((1, 2)):
+    for n, step in enumerate((2, 3)):
         chunk = pl.multiple_of(lax.rem(place + step, 4) * size, size)
         total = sums_ref[n * size : (n + 1) * size] + arrived_ref[pl.ds(chunk, size), :].astype(f32)
         sent_refs[n][...] = total.astype(bf16)
@@ -610,22 +610,22 @@
 
 
 def near_last_body(*refs):
-    cells, (arrived_ref, _, own_ref, sent_ref, grad_pre_ref) = refs[:5], refs[5:10]
+    cells, (arrived_ref, _, own_ref, next_ref, grad_pre_ref) = refs[:5], refs[5:10]
     half = grad_pre_ref.shape[0]
     channels = refs[0].shape[1]
     size = half // 4
     core, place = own_place()[0], phase_place(False)
-    chunks = [pl.multiple_of(lax.rem(place + step, 4) * size, size) for step in (3, 0)]
+    chunks = [pl.multiple_of(lax.rem(place + step, 4) * size, size) for step in (1, 0)]
     sources = [pl.multiple_of(core * half + chunk, size) for chunk in chunks]
     block = HiddenBlock(cells, sources, size, grad_pre_ref, chunks, refs[10:])
     block.dots(slice(0, block.total))
     block.activate(slice(0, block.total))
     expand, reduce = block.expand_sum(), block.reduce_sum()
-    for n, (chunk, ref) in enumerate(zip(chunks, (sent_ref, own_ref))):
+    for n, (chunk, ref) in enumerate(zip(chunks, (next_ref, own_ref))):
         at = slice(n * size, (n + 1) * size)
         other = arrived_ref[pl.ds(chunk, size), :].astype(f32)
-        ref[:, :channels] = (expand[at] + other[:, :channels]).astype(ref.dtype)
-        ref[:, channels:] = (reduce[at] + other[:, channels:]).astype(ref.dtype)
+        ref[:, :channels] = expand[at] + other[:, :channels]
+        ref[:, channels:] = reduce[at] + other[:, channels:]
 
 
 def near_last(*inputs):
@@ -636,7 +636,7 @@
         near_last_body,
         out_shape=(
             jax.ShapeDtypeStruct((size, 2 * channels), f32),
-            jax.ShapeDtypeStruct((size, 2 * channels), bf16),
+            jax.ShapeDtypeStruct((size, 2 * channels), f32),
             jax.ShapeDtypeStruct(grad_pre.shape, bf16),
         ),
         in_specs=[whole] * 7,
@@ -770,13 +770,29 @@
     )(counts, *conv, kernel, top, bottom, cols_sum, grad, inner)
 
 
-def split_four_body(own_ref, first_ref, second_ref, third_ref, kept_ref, *sent_refs):
+def relay_body(own_ref, passed_ref, sent_ref):
+    sent_ref[...] = (own_ref[...] + passed_ref[...].astype(f32)).astype(bf16)
+
+
+def relay(own, passed):
+    return pl.pallas_call(
+        relay_body,
+        out_shape=jax.ShapeDtypeStruct(own.shape, bf16),
+        in_specs=[whole] * 2,
+        out_specs=whole,
+        compiler_params=params(6),
+        cost_estimate=cost(0.2),
+        name="relay",
+    )(own, passed)
+
+
+def split_four_body(own_ref, first_ref, second_ref, kept_ref, *sent_refs):
     size = kept_ref.shape[0]
     place = phase_place(True)
     for step in range(4):
         at = pl.ds(pl.multiple_of(lax.rem(place + step, 4) * size, size), size)
         total = own_ref[at, :]
-        for ref in (first_ref, second_ref, third_ref):
+        for ref in (first_ref, second_ref):
             total = total + ref[at, :].astype(f32)
         if step == 0:
             kept_ref[...] = total
@@ -790,7 +806,7 @@
     return pl.pallas_call(
         split_four_body,
         out_shape=(jax.ShapeDtypeStruct((size, width), f32), sent, sent, sent),
-        in_specs=[whole] * 4,
+        in_specs=[whole] * 3,
         out_specs=[whole] * 4,
         compiler_params=params(4),
         cost_estimate=cost(0.3),
@@ -954,17 +970,18 @@
     sent, far_pre = hidden_far(*inputs)
     arrived = lax.ppermute(sent, "lat", [(i, i ^ 1) for i in range(8)])
     sums, near_pre = near_first(*inputs)
-    one, two = near_sends(sums, arrived)
-    part_one = lax.ppermute(one, every_axis, plane_pairs(1, True))
-    part_two = lax.ppermute(two, every_axis, plane_pairs(2, True))
-    own, three, near_pre = near_last(*inputs, arrived, after(near_pre, one, two))
-    part_three = lax.ppermute(three, every_axis, plane_pairs(3, True))
-
-    far_pre, part_one = after((far_pre, part_one), three)
+    two, three = near_sends(sums, arrived)
+    passed = lax.ppermute(two, every_axis, plane_pairs(1, True))
+    part_before = lax.ppermute(three, every_axis, plane_pairs(3, True))
+    own, following, near_pre = near_last(*inputs, arrived, after(near_pre, two, three))
+    one = relay(following, passed)
+    part_after = lax.ppermute(one, every_axis, plane_pairs(1, True))
+
+    far_pre = after(far_pre, one)
     conv_grad, first, last = norm_back(expand_t, far_pre, near_pre, unit, spread, norm_gain)
-    last, part_two = after((last, part_two))
+    last, part_before = after((last, part_before))
     left, right = lon_halo(first, last)
-    own, parts = after((own, (part_one, part_two, part_three)), first, last)
+    own, parts = after((own, (part_before, part_after)), first, last)
     own, *sent = split_four(own, parts)
     parts = [lax.ppermute(sent[i], every_axis, plane_pairs(i + 1, False)) for i in (1, 0, 2)]
     back = back_conv(after(conv_grad, sent), kernel, (0, 1))

time: 69.6 us -> 71.6 us (1.029)
  waiting for transfers between devices: 6.41 us -> 7.82 us
    ppermute x2, starting transfers between devices: 4.68 us -> 1.92 us  [lat_halo(): bottom = lax.ppermute(up, 'lat', shifted('lat', -1))]
    ppermute x3, waiting for transfers between devices: 1.36 us -> 4.04 us  [the longest x1 2.12 us: local(): passed = lax.ppermute(two, every_axis, plane_pairs(1, True))]
    ppermute x3, starting transfers between devices: 8.25 us -> 10.5 us  [local(): lax.ppermute(sent[i], every_axis, ring_pairs(i + 1))]
    ppermute x3, waiting for transfers between devices: 1.01 us -> 0.06 us  [local(): lax.ppermute(sent[i], every_axis, ring_pairs(i + 1))]
    ppermute x1, starting transfers between devices: 0.12 us -> 1.06 us  [local(): arrived = lax.ppermute(sent, every_axis, last_pairs())]
    ppermute x1, waiting for transfers between devices: 1.96 us -> 1.03 us  [local(): arrived = lax.ppermute(sent, every_axis, last_pairs())]
  transfers between devices with their start and end apart: 19 -> 19, of which waited for: 6 -> 8; matrix products, arithmetic and copies ran while one was open for 0% -> 0% of each run, Pallas kernels for 34% -> 33%
where the time goes in v11:
time: 71.6 us; the launch traced here: 71.5 us
  Pallas kernels  33.3 us (47%)
  starting transfers between devices  29.4 us (41%)
  waiting for transfers between devices  7.82 us (11%)
  between operations  0.96 us (1%)
    ppermute x3, starting transfers between devices, local(): lax.ppermute(sent[i], every_axis, ring_pairs(i + 1))  10.5 us
    pallas_call x2, Pallas kernels, inner_conv(): pl.pallas_call(functools.partial(inner_conv_body, parts), out_shape=(shap...  6.22 us
    ppermute x3, starting transfers between devices, local(): lax.ppermute(sent[i], every_axis, plane_pairs(i + 1, False))  5.75 us
    ppermute x2, starting transfers between devices, lon_halo(): right = lax.ppermute(first, 'lon', shifted('lon', -1))  4.98 us
    pallas_call x1, Pallas kernels, hidden_far(): pl.pallas_call(far_body, out_shape=(jax.ShapeDtypeStruct((half, 2 * chann...  4.62 us
    pallas_call x2, Pallas kernels, back_conv(): pl.pallas_call(functools.partial(back_conv_body, parts), out_shape=(shape...  4 us
    ppermute x1, starting transfers between devices, local(): part_before = lax.ppermute(three, every_axis, plane_pairs(3, True))  3.22 us
    pallas_call x1, Pallas kernels, near_last(): pl.pallas_call(near_last_body, out_shape=(jax.ShapeDtypeStruct((size, 2 *...  2.57 us
  transfers between devices with their start and end apart: 19, of which 8 were waited for; matrix products, arithmetic and copies ran while one was open for 0% of the time, Pallas kernels for 33%

profile of v11, /device:TPU:32, one launch (start us, length us, event | category | flops | bytes accessed | tf_op | source)
XLA Modules:
  0.0 71.5 jit_solution(4520596748956778641)
XLA Ops:
  0.6 2.1 %side_cols.1 = (bf16[3,32,384]{2,1,0:T(8,128)(2,1)}, bf16[3,32,384]{2,1,0:T(8,128)(2,1)}) custom-call(f32[32,32,384]{2,1,0:T(8,128)} %bitcast.20), custom_call_target="tpu_custom_call" | custom-call | flops 1150000000 | bytes 1048576 | tf_op jit(solution)/shard_map/side_cols/pallas_call | solution.py:170
  2.7 1.1 %collective-permute-start.1 = (bf16[3,32,384]{2,1,0:T(8,128)(2,1)}, bf16[3,32,384]{2,1,0:T(8,128)(2,1)S(1)}, u32[]{:S(2)}, u32[]{:S(2)}) collective-permute-start(bf16[3,32,384]{2,1,0:T(8,128)(2,1)} %get-tuple-element.76), channel_id=1, source_target_pairs={{0,15},{1,0},{2,1},{3,2},{4,3},{5,4},{6,5},{7,6},{8,7},{9,8},{10,9... | collective-permute-start | bytes 221192 | tf_op jit(solution)/shard_map/ppermute | solution.py:932
  3.8 1.0 %collective-permute-start = (bf16[3,32,384]{2,1,0:T(8,128)(2,1)}, bf16[3,32,384]{2,1,0:T(8,128)(2,1)S(1)}, u32[]{:S(2)}, u32[]{:S(2)}) collective-permute-start(bf16[3,32,384]{2,1,0:T(8,128)(2,1)} %get-tuple-element.77), channel_id=1, source_target_pairs={{0,1},{1,2},{2,3},{3,4},{4,5},{5,6},{6,7},{7,8},{8,9},{9,10},{10,1... | collective-permute-start | bytes 221192 | tf_op jit(solution)/shard_map/ppermute | solution.py:931
  4.8 2.1 %inner_conv.2.conv0_ref = f32[1024,128]{1,0:T(8,128)S(1)} custom-call(f32[1024,384]{1,0:T(8,128)S(1)} %bitcast.21, f32[49,1,384]{2,1,0:T(1,128)S(1)} %bitcast.13), custom_call_target="tpu_custom_call" | custom-call | flops 2529999872 | bytes 1048576 | tf_op jit(solution)/shard_map/inner_conv/pallas_call | solution.py:87
  7.0 1.6 %arrange.1 = (bf16[1536,384]{1,0:T(8,128)(2,1)S(1)}, bf16[1536,384]{1,0:T(8,128)(2,1)S(1)}, bf16[384,1536]{1,0:T(8,128)(2,1)S(1)}, f32[1536,128]{1,0:T(8,128)S(1)}) custom-call(bf16[1536,384]{1,0:T(8,128)(2,1)S(1)} %bitcast.27, bf16[1536,384]{1,0:T(8,128)(2,1)S(1)} %bitcast.28, f32[1,1536]{1,0:T(1,128)S(1)} %copy-done.7), custom_call_target="tpu_custom_call" | custom-call | flops 1724999936 | bytes 1048576 | tf_op jit(solution)/shard_map/arrange/pallas_call | solution.py:416
  8.6 0.7 mask_rows.1.refs_1_
  9.4 1.9 %collective-permute-start.3 = (bf16[3,48,384]{2,1,0:T(8,128)(2,1)S(1)}, bf16[3,48,384]{2,1,0:T(8,128)(2,1)S(1)}, u32[]{:S(2)}, u32[]{:S(2)}) collective-permute-start(bf16[3,48,384]{2,1,0:T(8,128)(2,1)S(1)} %get-tuple-element.85), channel_id=1, source_target_pairs={{0,112},{16,0},{32,16},{48,32},{64,48},{80,64},{96,80},{112,96},{1... | collective-permute-start | bytes 331784 | tf_op jit(solution)/shard_map/ppermute | solution.py:938
  11.3 4.1 %inner_conv.3 = (f32[1024,128]{1,0:T(8,128)S(1)}, f32[1024,128]{1,0:T(8,128)S(1)}) custom-call(f32[1024,384]{1,0:T(8,128)S(1)} %bitcast.23, f32[49,1,384]{2,1,0:T(1,128)S(1)} %bitcast.14), custom_call_target="tpu_custom_call" | custom-call | flops 5059999744 | bytes 1048576 | tf_op jit(solution)/shard_map/inner_conv/pallas_call | solution.py:87
  15.4 1.2 %collective-permute-done.2.top_ref = bf16[3,48,384]{2,1,0:T(8,128)(2,1)S(1)} collective-permute-done((bf16[3,48,384]{2,1,0:T(8,128)(2,1)S(1)}, bf16[3,48,384]{2,1,0:T(8,128)(2,1)S(1)}, u32[]{:S(2)}, u32[]{:S(2)}) %collective-permute-start.2) | collective-permute-done | bytes 110624 | tf_op jit(solution)/shard_map/ppermute | solution.py:937
  16.7 1.9 %normalise.1 = (f32[1024,384]{1,0:T(8,128)S(1)}, f32[1024,128]{1,0:T(8,128)S(1)}, bf16[1024,384]{1,0:T(8,128)(2,1)S(1)}) custom-call(f32[1024,128]{1,0:T(8,128)S(1)} %inner_conv.2.conv0_ref, f32[1024,128]{1,0:T(8,128)S(1)} %get-tuple-element.88.conv1_ref, f32[1024,128]{1,0:T(8,128)S(1)} %get-tuple-element.89.conv2_ref, f32[49,1,384]{2,1,0:T(1,128)S(1)} %bitcast.15, ...), custom_call_target="tpu_custom_call" | custom-call | flops 3220000000 | bytes 1048576 | tf_op jit(solution)/shard_map/normalise/pallas_call | solution.py:325
  18.6 4.6 %hidden_far.1 = (bf16[768,768]{1,0:T(8,128)(2,1)S(1)}, bf16[768,1024]{1,0:T(8,128)(2,1)S(1)}) custom-call(bf16[1024,384]{1,0:T(8,128)(2,1)S(1)} %get-tuple-element.90.refs_0_, bf16[1024,384]{1,0:T(8,128)(2,1)S(1)} %mask_rows.1.refs_1_, bf16[1536,384]{1,0:T(8,128)(2,1)S(1)} %get-tuple-element.91.refs_2_, bf16[1536,384]{1,0:T(8,128)(2,1)S(1)} %get-tuple-element.92.refs_3_, ...), custom_call_target="tpu_custom_call" | custom-call | flops 5750000128 | bytes 1048576 | tf_op jit(solution)/shard_map/hidden_far/pallas_call | solution.py:541
  23.5 2.5 %near_first.1 = (f32[384,768]{1,0:T(8,128)S(1)}, bf16[768,1024]{1,0:T(8,128)(2,1)S(1)}) custom-call(bf16[1024,384]{1,0:T(8,128)(2,1)S(1)} %get-tuple-element.90.refs_0_, bf16[1024,384]{1,0:T(8,128)(2,1)S(1)} %mask_rows.1.refs_1_, bf16[1536,384]{1,0:T(8,128)(2,1)S(1)} %get-tuple-element.91.refs_2_, bf16[1536,384]{1,0:T(8,128)(2,1)S(1)} %get-tuple-element.92.refs_3_, ...), custom_call_target="tpu_custom_call" | custom-call | flops 3449999872 | bytes 1048576 | tf_op jit(solution)/shard_map/near_first/pallas_call | solution.py:574
  26.6 3.2 %collective-permute-start.6 = (bf16[192,768]{1,0:T(8,128)(2,1)S(1)}, bf16[192,768]{1,0:T(8,128)(2,1)S(1)}, u32[]{:S(2)}, u32[]{:S(2)}) collective-permute-start(bf16[192,768]{1,0:T(8,128)(2,1)S(1)} %get-tuple-element.98), channel_id=1, source_target_pairs={{0,96},{1,97},{2,98},{3,99},{4,100},{5,101},{6,102},{7,103},{8,104... | collective-permute-start | bytes 884744 | tf_op jit(solution)/shard_map/ppermute | solution.py:975
  29.8 2.6 %near_last.1 = (f32[192,768]{1,0:T(8,128)S(1)}, f32[192,768]{1,0:T(8,128)S(1)}, bf16[768,1024]{1,0:T(8,128)(2,1)S(1)}) custom-call(bf16[1024,384]{1,0:T(8,128)(2,1)S(1)} %get-tuple-element.90.refs_0_, bf16[1024,384]{1,0:T(8,128)(2,1)S(1)} %mask_rows.1.refs_1_, bf16[1536,384]{1,0:T(8,128)(2,1)S(1)} %get-tuple-element.91.refs_2_, ...), custom_call_target="tpu_custom_call", output_to_operand_aliasing={{2}: (6, {})} | custom-call | flops 3449999872 | bytes 1048576 | tf_op jit(solution)/shard_map/near_last/pallas_call | solution.py:635
  32.4 2.1 %collective-permute-done.5.passed_ref = bf16[192,768]{1,0:T(8,128)(2,1)S(1)} collective-permute-done((bf16[192,768]{1,0:T(8,128)(2,1)S(1)}, bf16[192,768]{1,0:T(8,128)(2,1)S(1)}, u32[]{:S(2)}, u32[]{:S(2)}) %collective-permute-start.5) | collective-permute-done | bytes 294944 | tf_op jit(solution)/shard_map/ppermute | solution.py:974
  34.6 2.1 %norm_back.1 = (f32[32,32,384]{2,1,0:T(8,128)S(1)}, bf16[3,32,384]{2,1,0:T(8,128)(2,1)S(1)}, bf16[3,32,384]{2,1,0:T(8,128)(2,1)S(1)}) custom-call(bf16[384,1536]{1,0:T(8,128)(2,1)S(1)} %get-tuple-element.80.turned_ref, bf16[768,1024]{1,0:T(8,128)(2,1)S(1)} %get-tuple-element.101.other_ref, bf16[768,1024]{1,0:T(8,128)(2,1)S(1)} %get-tuple-element.102.mine_ref, ...), custom_call_target="tpu_custom_call" | custom-call | flops 230000000 | bytes 1048576 | tf_op jit(solution)/shard_map/norm_back/pallas_call | solution.py:683
  36.7 3.9 %collective-permute-start.9 = (bf16[3,32,384]{2,1,0:T(8,128)(2,1)S(1)}, bf16[3,32,384]{2,1,0:T(8,128)(2,1)S(1)}, u32[]{:S(2)}, u32[]{:S(2)}) collective-permute-start(bf16[3,32,384]{2,1,0:T(8,128)(2,1)S(1)} %get-tuple-element.109), channel_id=1, source_target_pairs={{0,15},{1,0},{2,1},{3,2},{4,3},{5,4},{6,5},{7,6},{8,7},{9,8},{10,9... | collective-permute-start | bytes 221192 | tf_op jit(solution)/shard_map/ppermute | solution.py:932
  40.6 1.9 %collective-permute-done.7.second_ref = bf16[192,768]{1,0:T(8,128)(2,1)S(1)} collective-permute-done((bf16[192,768]{1,0:T(8,128)(2,1)S(1)}, bf16[192,768]{1,0:T(8,128)(2,1)S(1)}, u32[]{:S(2)}, u32[]{:S(2)}) %collective-permute-start.7) | collective-permute-done | bytes 294944 | tf_op jit(solution)/shard_map/ppermute | solution.py:978
  42.6 2.7 %collective-permute-start.11 = (bf16[48,768]{1,0:T(8,128)(2,1)S(1)}, bf16[48,768]{1,0:T(8,128)(2,1)S(1)}, u32[]{:S(2)}, u32[]{:S(2)}) collective-permute-start(bf16[48,768]{1,0:T(8,128)(2,1)S(1)} %get-tuple-element.114), channel_id=1, source_target_pairs={{0,1},{1,128},{2,3},{3,130},{4,5},{5,132},{6,7},{7,134},{8,9},{9,1... | collective-permute-start | bytes 221192 | tf_op jit(solution)/shard_map/ppermute | solution.py:986
  45.3 2.6 %collective-permute-start.10 = (bf16[48,768]{1,0:T(8,128)(2,1)S(1)}, bf16[48,768]{1,0:T(8,128)(2,1)S(1)}, u32[]{:S(2)}, u32[]{:S(2)}) collective-permute-start(bf16[48,768]{1,0:T(8,128)(2,1)S(1)} %get-tuple-element.115), channel_id=1, source_target_pairs={{0,128},{1,129},{2,130},{3,131},{4,132},{5,133},{6,134},{7,135},{8... | collective-permute-start | bytes 221192 | tf_op jit(solution)/shard_map/ppermute | solution.py:986
  47.8 0.5 collective-permute-start.12
  48.4 2.7 %back_conv.2 = (f32[1024,128]{1,0:T(8,128)S(1)}, f32[1024,128]{1,0:T(8,128)S(1)}) custom-call(f32[1024,384]{1,0:T(8,128)S(1)} %bitcast.24, f32[49,1,384]{2,1,0:T(1,128)S(1)} %bitcast.16), custom_call_target="tpu_custom_call" | custom-call | flops 3449999872 | bytes 1048576 | tf_op jit(solution)/shard_map/back_conv/pallas_call | solution.py:137
  51.2 1.0 %collective-permute-done.12.third_ref = bf16[48,768]{1,0:T(8,128)(2,1)S(1)} collective-permute-done((bf16[48,768]{1,0:T(8,128)(2,1)S(1)}, bf16[48,768]{1,0:T(8,128)(2,1)S(1)}, u32[]{:S(2)}, u32[]{:S(2)}) %collective-permute-start.12) | collective-permute-done | bytes 73760 | tf_op jit(solution)/shard_map/ppermute | solution.py:986
  52.9 4.5 %collective-permute-start.16 = (bf16[12,768]{1,0:T(8,128)(2,1)S(1)}, bf16[12,768]{1,0:T(8,128)(2,1)S(1)}, u32[]{:S(2)}, u32[]{:S(2)}) collective-permute-start(bf16[12,768]{1,0:T(8,128)(2,1)S(1)} %get-tuple-element.133), channel_id=1, source_target_pairs={{0,4},{1,5},{2,6},{3,7},{4,8},{5,9},{6,10},{7,11},{8,12},{9,13},{1... | collective-permute-start | bytes 55304 | tf_op jit(solution)/shard_map/ppermute | solution.py:992
  57.4 4.5 %collective-permute-start.15 = (bf16[12,768]{1,0:T(8,128)(2,1)S(1)}, bf16[12,768]{1,0:T(8,128)(2,1)S(1)}, u32[]{:S(2)}, u32[]{:S(2)}) collective-permute-start(bf16[12,768]{1,0:T(8,128)(2,1)S(1)} %get-tuple-element.134), channel_id=1, source_target_pairs={{0,8},{1,9},{2,10},{3,11},{4,12},{5,13},{6,14},{7,15},{8,0},{9,1},... | collective-permute-start | bytes 55304 | tf_op jit(solution)/shard_map/ppermute | solution.py:992
  61.9 1.5 %collective-permute-start.17 = (bf16[12,768]{1,0:T(8,128)(2,1)S(1)}, bf16[12,768]{1,0:T(8,128)(2,1)S(1)}, u32[]{:S(2)}, u32[]{:S(2)}) collective-permute-start(bf16[12,768]{1,0:T(8,128)(2,1)S(1)} %get-tuple-element.135), channel_id=1, source_target_pairs={{0,12},{1,13},{2,14},{3,15},{4,0},{5,1},{6,2},{7,3},{8,4},{9,5},{1... | collective-permute-start | bytes 55304 | tf_op jit(solution)/shard_map/ppermute | solution.py:992
  63.4 1.3 %back_conv.3.conv2_ref = f32[1024,128]{1,0:T(8,128)S(1)} custom-call(f32[1024,384]{1,0:T(8,128)S(1)} %bitcast.26, f32[49,1,384]{2,1,0:T(1,128)S(1)} %bitcast.17), custom_call_target="tpu_custom_call" | custom-call | flops 1724999936 | bytes 1048576 | tf_op jit(solution)/shard_map/back_conv/pallas_call | solution.py:137
  64.7 2.1 %finish_inner.1 = (f32[1024,384]{1,0:T(8,128)}, f32[6,32,384]{2,1,0:T(8,128)S(1)}) custom-call(s32[4,4]{1,0:T(4,128)S(1)} %copy-done.2, f32[1024,128]{1,0:T(8,128)S(1)} %get-tuple-element.118.conv0_ref, f32[1024,128]{1,0:T(8,128)S(1)} %get-tuple-element.119.conv1_ref, f32[1024,128]{1,0:T(8,128)S(1)} %back_conv.3.conv2_ref, f32[49,1,384]{2,1,0:T(1,128)S(1)} %bitcast.18, ...), custom_call_target="tpu_custom_call" | custom-call | flops 2529999872 | bytes 1048576 | tf_op jit(solution)/shard_map/finish_inner/pallas_call | solution.py:717
  66.9 1.1 %collective-permute-start.18 = (f32[6,768]{1,0:T(8,128)S(1)}, f32[6,768]{1,0:T(8,128)S(1)}, u32[]{:S(2)}, u32[]{:S(2)}) collective-permute-start(f32[6,768]{1,0:T(8,128)S(1)} %get-tuple-element.144), channel_id=1, source_target_pairs={{0,2},{1,3},{2,0},{3,1},{4,6},{5,7},{6,4},{7,5},{8,10},{9,11},{10,... | collective-permute-start | bytes 55304 | tf_op jit(solution)/shard_map/ppermute | solution.py:999
  68.0 1.8 %finish_outer.1 = f32[1024,384]{1,0:T(8,128)} custom-call(s32[4,4]{1,0:T(4,128)S(1)} %copy-done.2, f32[1024,128]{1,0:T(8,128)S(1)} %get-tuple-element.118.conv0_ref, f32[1024,128]{1,0:T(8,128)S(1)} %get-tuple-element.119.conv1_ref, f32[1024,128]{1,0:T(8,128)S(1)} %back_conv.3.conv2_ref, f32[49,1,384]{2,1,0:T(1,128)S(1)} %bitcast.19, ...), custom_call_target="tpu_custom_call", output_to_operand_aliasing={{}: (9, {})} | custom-call | flops 1150000000 | bytes 1048576 | tf_op jit(solution)/shard_map/finish_outer/pallas_call | solution.py:754
  69.8 1.0 %collective-permute-done.18.arrived_ref = f32[6,768]{1,0:T(8,128)S(1)} collective-permute-done((f32[6,768]{1,0:T(8,128)S(1)}, f32[6,768]{1,0:T(8,128)S(1)}, u32[]{:S(2)}, u32[]{:S(2)}) %collective-permute-start.18) | collective-permute-done | bytes 18464 | tf_op jit(solution)/shard_map/ppermute | solution.py:999
  70.9 0.6 last_sum.1
  (48 shorter events, 2.0 us)
Async XLA Ops:
  0.6 4.2 %copy-start.1 = (f32[1,49,384]{2,0,1:T(1,128)S(1)}, f32[1,49,384]{2,0,1:T(1,128)}, u32[]{:S(2)}) copy-start(f32[1,49,384]{2,0,1:T(1,128)} %param.13) | copy-start | bytes 225796
  0.6 4.2 %copy-start.4 = (f32[1,32,32,384]{3,2,1,0:T(8,128)S(1)}, f32[1,32,32,384]{3,2,1,0:T(8,128)}, u32[]{:S(2)}) copy-start(f32[1,32,32,384]{3,2,1,0:T(8,128)} %param.10) | copy-start | bytes 4718596
  2.7 6.6 %collective-permute-start.1 = (bf16[3,32,384]{2,1,0:T(8,128)(2,1)}, bf16[3,32,384]{2,1,0:T(8,128)(2,1)S(1)}, u32[]{:S(2)}, u32[]{:S(2)}) collective-permute-start(bf16[3,32,384]{2,1,0:T(8,128)(2,1)} %get-tuple-element.76), channel_id=1, source_target_pairs={{0,15},{1,0},{2,1},{3,2},{4,3},{5,4},{6,5},{7,6},{8,7},{9,8},{10,9... | collective-permute-start | bytes 221192 | tf_op jit(solution)/shard_map/ppermute | solution.py:932
  3.8 5.5 %collective-permute-start = (bf16[3,32,384]{2,1,0:T(8,128)(2,1)}, bf16[3,32,384]{2,1,0:T(8,128)(2,1)S(1)}, u32[]{:S(2)}, u32[]{:S(2)}) collective-permute-start(bf16[3,32,384]{2,1,0:T(8,128)(2,1)} %get-tuple-element.77), channel_id=1, source_target_pairs={{0,1},{1,2},{2,3},{3,4},{4,5},{5,6},{6,7},{7,8},{8,9},{9,10},{10,1... | collective-permute-start | bytes 221192 | tf_op jit(solution)/shard_map/ppermute | solution.py:931
  4.8 2.1 %copy-start.5 = (bf16[1,1536,384]{2,1,0:T(8,128)(2,1)S(1)}, bf16[1,1536,384]{2,1,0:T(8,128)(2,1)}, u32[]{:S(2)}) copy-start(bf16[1,1536,384]{2,1,0:T(8,128)(2,1)} %param.17) | copy-start | bytes 3538948
  4.8 2.1 %copy-start.6 = (bf16[1,1536,384]{2,1,0:T(8,128)(2,1)S(1)}, bf16[1,1536,384]{2,1,0:T(8,128)(2,1)}, u32[]{:S(2)}) copy-start(bf16[1,1536,384]{2,1,0:T(8,128)(2,1)} %param.19) | copy-start | bytes 3538948
  4.8 2.1 %copy-start.7 = (f32[1,1536]{1,0:T(1,128)S(1)}, f32[1,1536]{1,0:T(1,128)}, u32[]{:S(2)}) copy-start(f32[1,1536]{1,0:T(1,128)} %bias_ref.2) | copy-start | bytes 18436
  7.0 1.6 %copy-start = (f32[1,32,32,384]{3,2,1,0:T(8,128)S(1)}, f32[1,32,32,384]{3,2,1,0:T(8,128)}, u32[]{:S(2)}) copy-start(f32[1,32,32,384]{3,2,1,0:T(8,128)} %param.11) | copy-start | bytes 4718596
  7.0 1.6 %copy-start.2 = (s32[4,4]{1,0:T(4,128)S(1)}, s32[4,4]{1,0:T(4,128)}, u32[]{:S(2)}) copy-start(s32[4,4]{1,0:T(4,128)} %counts_ref.5) | copy-start | bytes 196
  9.4 6.1 %collective-permute-start.3 = (bf16[3,48,384]{2,1,0:T(8,128)(2,1)S(1)}, bf16[3,48,384]{2,1,0:T(8,128)(2,1)S(1)}, u32[]{:S(2)}, u32[]{:S(2)}) collective-permute-start(bf16[3,48,384]{2,1,0:T(8,128)(2,1)S(1)} %get-tuple-element.85), channel_id=1, source_target_pairs={{0,112},{16,0},{32,16},{48,32},{64,48},{80,64},{96,80},{112,96},{1... | collective-permute-start | bytes 331784 | tf_op jit(solution)/shard_map/ppermute | solution.py:938
  11.3 5.4 %copy-start.3 = (f32[1,384]{1,0:T(1,128)S(1)}, f32[1,384]{1,0:T(1,128)}, u32[]{:S(2)}) copy-start(f32[1,384]{1,0:T(1,128)} %gain_ref.3) | copy-start | bytes 4612
  11.3 5.4 %copy-start.8 = (f32[1,384]{1,0:T(1,128)S(1)}, f32[1,384]{1,0:T(1,128)}, u32[]{:S(2)}) copy-start(f32[1,384]{1,0:T(1,128)} %bias_ref.3) | copy-start | bytes 4612
  11.3 5.4 %copy-start.9 = (f32[1,384]{1,0:T(1,128)S(1)}, f32[1,384]{1,0:T(1,128)}, u32[]{:S(2)}) copy-start(f32[1,384]{1,0:T(1,128)} %shift_ref.1) | copy-start | bytes 4612
  11.3 5.4 %collective-permute-start.2 = (bf16[3,48,384]{2,1,0:T(8,128)(2,1)S(1)}, bf16[3,48,384]{2,1,0:T(8,128)(2,1)S(1)}, u32[]{:S(2)}, u32[]{:S(2)}) collective-permute-start(bf16[3,48,384]{2,1,0:T(8,128)(2,1)S(1)} %get-tuple-element.86), channel_id=1, source_target_pairs={{0,16},{16,32},{32,48},{48,64},{64,80},{80,96},{96,112},{112,0},{1... | collective-permute-start | bytes 331784 | tf_op jit(solution)/shard_map/ppermute | solution.py:937
  23.2 3.1 %collective-permute-start.4 = (bf16[768,768]{1,0:T(8,128)(2,1)S(1)}, bf16[768,768]{1,0:T(8,128)(2,1)S(1)}, u32[]{:S(2)}, u32[]{:S(2)}) collective-permute-start(bf16[768,768]{1,0:T(8,128)(2,1)S(1)} %get-tuple-element.94), channel_id=1, source_target_pairs={{0,16},{16,0},{32,48},{48,32},{64,80},{80,64},{96,112},{112,96},{1... | collective-permute-start | bytes 3538952 | tf_op jit(solution)/shard_map/ppermute | solution.py:971
  26.5 8.0 %collective-permute-start.5 = (bf16[192,768]{1,0:T(8,128)(2,1)S(1)}, bf16[192,768]{1,0:T(8,128)(2,1)S(1)}, u32[]{:S(2)}, u32[]{:S(2)}) collective-permute-start(bf16[192,768]{1,0:T(8,128)(2,1)S(1)} %get-tuple-element.97), channel_id=1, source_target_pairs={{0,32},{1,33},{2,34},{3,35},{4,36},{5,37},{6,38},{7,39},{8,40},{9,... | collective-permute-start | bytes 884744 | tf_op jit(solution)/shard_map/ppermute | solution.py:974
  26.6 14.1 %collective-permute-start.6 = (bf16[192,768]{1,0:T(8,128)(2,1)S(1)}, bf16[192,768]{1,0:T(8,128)(2,1)S(1)}, u32[]{:S(2)}, u32[]{:S(2)}) collective-permute-start(bf16[192,768]{1,0:T(8,128)(2,1)S(1)} %get-tuple-element.98), channel_id=1, source_target_pairs={{0,96},{1,97},{2,98},{3,99},{4,100},{5,101},{6,102},{7,103},{8,104... | collective-permute-start | bytes 884744 | tf_op jit(solution)/shard_map/ppermute | solution.py:975
  34.5 8.0 %collective-permute-start.7 = (bf16[192,768]{1,0:T(8,128)(2,1)S(1)}, bf16[192,768]{1,0:T(8,128)(2,1)S(1)}, u32[]{:S(2)}, u32[]{:S(2)}) collective-permute-start(bf16[192,768]{1,0:T(8,128)(2,1)S(1)} %relay.1), channel_id=1, source_target_pairs={{0,32},{1,33},{2,34},{3,35},{4,36},{5,37},{6,38},{7,39},{8,40},{9,... | collective-permute-start | bytes 884744 | tf_op jit(solution)/shard_map/ppermute | solution.py:978
  36.7 14.3 %collective-permute-start.9 = (bf16[3,32,384]{2,1,0:T(8,128)(2,1)S(1)}, bf16[3,32,384]{2,1,0:T(8,128)(2,1)S(1)}, u32[]{:S(2)}, u32[]{:S(2)}) collective-permute-start(bf16[3,32,384]{2,1,0:T(8,128)(2,1)S(1)} %get-tuple-element.109), channel_id=1, source_target_pairs={{0,15},{1,0},{2,1},{3,2},{4,3},{5,4},{6,5},{7,6},{8,7},{9,8},{10,9... | collective-permute-start | bytes 221192 | tf_op jit(solution)/shard_map/ppermute | solution.py:932
  40.6 10.4 %collective-permute-start.8 = (bf16[3,32,384]{2,1,0:T(8,128)(2,1)S(1)}, bf16[3,32,384]{2,1,0:T(8,128)(2,1)S(1)}, u32[]{:S(2)}, u32[]{:S(2)}) collective-permute-start(bf16[3,32,384]{2,1,0:T(8,128)(2,1)S(1)} %get-tuple-element.110), channel_id=1, source_target_pairs={{0,1},{1,2},{2,3},{3,4},{4,5},{5,6},{6,7},{7,8},{8,9},{9,10},{10,1... | collective-permute-start | bytes 221192 | tf_op jit(solution)/shard_map/ppermute | solution.py:931
  42.6 8.4 %collective-permute-start.11 = (bf16[48,768]{1,0:T(8,128)(2,1)S(1)}, bf16[48,768]{1,0:T(8,128)(2,1)S(1)}, u32[]{:S(2)}, u32[]{:S(2)}) collective-permute-start(bf16[48,768]{1,0:T(8,128)(2,1)S(1)} %get-tuple-element.114), channel_id=1, source_target_pairs={{0,1},{1,128},{2,3},{3,130},{4,5},{5,132},{6,7},{7,134},{8,9},{9,1... | collective-permute-start | bytes 221192 | tf_op jit(solution)/shard_map/ppermute | solution.py:986
  45.3 5.9 %collective-permute-start.10 = (bf16[48,768]{1,0:T(8,128)(2,1)S(1)}, bf16[48,768]{1,0:T(8,128)(2,1)S(1)}, u32[]{:S(2)}, u32[]{:S(2)}) collective-permute-start(bf16[48,768]{1,0:T(8,128)(2,1)S(1)} %get-tuple-element.115), channel_id=1, source_target_pairs={{0,128},{1,129},{2,130},{3,131},{4,132},{5,133},{6,134},{7,135},{8... | collective-permute-start | bytes 221192 | tf_op jit(solution)/shard_map/ppermute | solution.py:986
  47.8 4.4 %collective-permute-start.12 = (bf16[48,768]{1,0:T(8,128)(2,1)S(1)}, bf16[48,768]{1,0:T(8,128)(2,1)S(1)}, u32[]{:S(2)}, u32[]{:S(2)}) collective-permute-start(bf16[48,768]{1,0:T(8,128)(2,1)S(1)} %get-tuple-element.116), channel_id=1, source_target_pairs={{0,129},{1,0},{2,131},{3,2},{4,133},{5,4},{6,135},{7,6},{8,137},{9... | collective-permute-start | bytes 221192 | tf_op jit(solution)/shard_map/ppermute | solution.py:986
  52.3 11.1 %collective-permute-start.14 = (bf16[3,48,384]{2,1,0:T(8,128)(2,1)S(1)}, bf16[3,48,384]{2,1,0:T(8,128)(2,1)S(1)}, u32[]{:S(2)}, u32[]{:S(2)}) collective-permute-start(bf16[3,48,384]{2,1,0:T(8,128)(2,1)S(1)} %get-tuple-element.127), channel_id=1, source_target_pairs={{0,112},{16,0},{32,16},{48,32},{64,48},{80,64},{96,80},{112,96},{1... | collective-permute-start | bytes 331784 | tf_op jit(solution)/shard_map/ppermute | solution.py:938
  52.3 11.1 %collective-permute-start.13 = (bf16[3,48,384]{2,1,0:T(8,128)(2,1)S(1)}, bf16[3,48,384]{2,1,0:T(8,128)(2,1)S(1)}, u32[]{:S(2)}, u32[]{:S(2)}) collective-permute-start(bf16[3,48,384]{2,1,0:T(8,128)(2,1)S(1)} %get-tuple-element.128), channel_id=1, source_target_pairs={{0,16},{16,32},{32,48},{48,64},{64,80},{80,96},{96,112},{112,0},{1... | collective-permute-start | bytes 331784 | tf_op jit(solution)/shard_map/ppermute | solution.py:937
  52.9 14.0 %collective-permute-start.16 = (bf16[12,768]{1,0:T(8,128)(2,1)S(1)}, bf16[12,768]{1,0:T(8,128)(2,1)S(1)}, u32[]{:S(2)}, u32[]{:S(2)}) collective-permute-start(bf16[12,768]{1,0:T(8,128)(2,1)S(1)} %get-tuple-element.133), channel_id=1, source_target_pairs={{0,4},{1,5},{2,6},{3,7},{4,8},{5,9},{6,10},{7,11},{8,12},{9,13},{1... | collective-permute-start | bytes 55304 | tf_op jit(solution)/shard_map/ppermute | solution.py:992
  57.4 9.4 %collective-permute-start.15 = (bf16[12,768]{1,0:T(8,128)(2,1)S(1)}, bf16[12,768]{1,0:T(8,128)(2,1)S(1)}, u32[]{:S(2)}, u32[]{:S(2)}) collective-permute-start(bf16[12,768]{1,0:T(8,128)(2,1)S(1)} %get-tuple-element.134), channel_id=1, source_target_pairs={{0,8},{1,9},{2,10},{3,11},{4,12},{5,13},{6,14},{7,15},{8,0},{9,1},... | collective-permute-start | bytes 55304 | tf_op jit(solution)/shard_map/ppermute | solution.py:992
  61.9 5.0 %collective-permute-start.17 = (bf16[12,768]{1,0:T(8,128)(2,1)S(1)}, bf16[12,768]{1,0:T(8,128)(2,1)S(1)}, u32[]{:S(2)}, u32[]{:S(2)}) collective-permute-start(bf16[12,768]{1,0:T(8,128)(2,1)S(1)} %get-tuple-element.135), channel_id=1, source_target_pairs={{0,12},{1,13},{2,14},{3,15},{4,0},{5,1},{6,2},{7,3},{8,4},{9,5},{1... | collective-permute-start | bytes 55304 | tf_op jit(solution)/shard_map/ppermute | solution.py:992
  66.9 3.9 %collective-permute-start.18 = (f32[6,768]{1,0:T(8,128)S(1)}, f32[6,768]{1,0:T(8,128)S(1)}, u32[]{:S(2)}, u32[]{:S(2)}) collective-permute-start(f32[6,768]{1,0:T(8,128)S(1)} %get-tuple-element.144), channel_id=1, source_target_pairs={{0,2},{1,3},{2,0},{3,1},{4,6},{5,7},{6,4},{7,5},{8,10},{9,11},{10,... | collective-permute-start | bytes 55304 | tf_op jit(solution)/shard_map/ppermute | solution.py:999

commit v12 on v10

--- a/solution.py
+++ b/solution.py
@@ -149,19 +149,10 @@
     )(cells, kernel)
 
 
-def side_cols_body(cells_ref, first_ref, last_ref, low, high, sems):
-    copies = [
-        pltpu.make_async_copy(cells_ref.at[:, pl.ds(0, 8), :], low, sems.at[0]),
-        pltpu.make_async_copy(cells_ref.at[:, pl.ds(side - 8, 8), :], high, sems.at[1]),
-    ]
-    for copy in copies:
-        copy.start()
-    copies[0].wait()
+def side_cols_body(cells_ref, first_ref, last_ref):
     for j in range(reach):
-        first_ref[j] = low[:, j, :].astype(bf16)
-    copies[1].wait()
-    for j in range(reach):
-        last_ref[j] = high[:, 8 - reach + j, :].astype(bf16)
+        first_ref[j] = cells_ref[:, j, :].astype(bf16)
+        last_ref[j] = cells_ref[:, side - reach + j, :].astype(bf16)
 
 
 def side_cols(cells):
@@ -170,11 +161,10 @@
     return pl.pallas_call(
         side_cols_body,
         out_shape=(shape, shape),
-        in_specs=[pl.BlockSpec(memory_space=pltpu.HBM)],
+        in_specs=[whole],
         out_specs=[whole] * 2,
-        scratch_shapes=[pltpu.VMEM((side, 8, channels), f32)] * 2 + [pltpu.SemaphoreType.DMA((2,))],
-        compiler_params=params(58),
-        cost_estimate=cost(1.0),
+        compiler_params=params(4),
+        cost_estimate=cost(0.3),
         name="side_cols",
     )(cells.reshape(side, side, channels))
 
@@ -966,13 +956,13 @@
     left, right = lon_halo(first, last)
     own, parts = after((own, (part_one, part_two, part_three)), first, last)
     own, *sent = split_four(own, parts)
-    parts = [lax.ppermute(sent[i], every_axis, plane_pairs(i + 1, False)) for i in (1, 0, 2)]
+    parts = [lax.ppermute(sent[i], every_axis, plane_pairs(i + 1, False)) for i in (0, 2, 1)]
     back = back_conv(after(conv_grad, sent), kernel, (0, 1))
     (conv_grad, left, right), parts = after(((conv_grad, left, right), parts), back)
     up, down = side_rows(conv_grad, left, right)
 
     own, *sent = split_ring(*after((own, parts), up, down))
-    parts = [lax.ppermute(sent[i], every_axis, ring_pairs(i + 1)) for i in (1, 0, 2)]
+    parts = [lax.ppermute(sent[i], every_axis, ring_pairs(i + 1)) for i in (0, 2, 1)]
     top, bottom = lat_halo(up, down)
     back += back_conv(after(conv_grad, sent, top, bottom), kernel, (2,))
 

time: 69.6 us -> 70.3 us (1.010)
  local copies, waits for them, and re-layouts: 0.05 us -> 2.33 us
  Pallas kernels: 33.4 us -> 31.6 us
    unnamed x20 -> x24, local copies, waits for them, and re-layouts: 0.05 us -> 2.33 us
    pallas_call x1, Pallas kernels: 2.06 us -> 0.3 us  [side_cols(): pl.pallas_call(side_cols_body, out_shape=(shape, shape), in_specs=[whole]...]
    ppermute x3, starting transfers between devices: 8.25 us -> 9.33 us  [local(): lax.ppermute(sent[i], every_axis, ring_pairs(i + 1))]
    ppermute x2, starting transfers between devices: 4.98 us -> 3.89 us  [lon_halo(): right = lax.ppermute(first, 'lon', shifted('lon', -1))]
    ppermute x2, starting transfers between devices: 4.68 us -> 3.6 us  [lat_halo(): bottom = lax.ppermute(up, 'lat', shifted('lat', -1))]
    ppermute x2, starting transfers between devices: 0.99 us -> 1.73 us  [lon_halo(): left = lax.ppermute(last, 'lon', shifted('lon', 1))]
where the time goes in v12:
time: 70.3 us; the launch traced here: 70.1 us
  Pallas kernels  31.6 us (45%)
  starting transfers between devices  28.4 us (40%)
  waiting for transfers between devices  6.8 us (10%)
  local copies, waits for them, and re-layouts  2.33 us (3%)
  between operations  0.93 us (1%)
    ppermute x3, starting transfers between devices, local(): lax.ppermute(sent[i], every_axis, ring_pairs(i + 1))  9.33 us
    pallas_call x2, Pallas kernels, inner_conv(): pl.pallas_call(functools.partial(inner_conv_body, parts), out_shape=(shap...  6.22 us
    ppermute x3, starting transfers between devices, local(): lax.ppermute(sent[i], every_axis, plane_pairs(i + 1, False))  5.43 us
    pallas_call x1, Pallas kernels, hidden_far(): pl.pallas_call(far_body, out_shape=(jax.ShapeDtypeStruct((half, 2 * chann...  4.68 us
    pallas_call x2, Pallas kernels, back_conv(): pl.pallas_call(functools.partial(back_conv_body, parts), out_shape=(shape...  4 us
    ppermute x2, starting transfers between devices, lon_halo(): right = lax.ppermute(first, 'lon', shifted('lon', -1))  3.89 us
    ppermute x2, starting transfers between devices, lat_halo(): bottom = lax.ppermute(up, 'lat', shifted('lat', -1))  3.6 us
    ppermute x1, starting transfers between devices, local(): part_two = lax.ppermute(two, every_axis, plane_pairs(2, True))  3.32 us
  transfers between devices with their start and end apart: 19, of which 6 were waited for; matrix products, arithmetic and copies ran while one was open for 0% of the time, Pallas kernels for 34%

profile of v12, /device:TPU:32, one launch (start us, length us, event | category | flops | bytes accessed | tf_op | source)
XLA Modules:
  0.0 70.1 jit_solution(4919594062629426403)
XLA Ops:
  0.6 1.4 %copy-done = f32[1,32,32,384]{3,2,1,0:T(8,128)S(1)} copy-done((f32[1,32,32,384]{3,2,1,0:T(8,128)S(1)}, f32[1,32,32,384]{3,2,1,0:T(8,128)}, u32[]{:S(2)}) %copy-start) | copy-done | bytes 1572888
  2.3 1.1 %collective-permute-start.1 = (bf16[3,32,384]{2,1,0:T(8,128)(2,1)S(1)}, bf16[3,32,384]{2,1,0:T(8,128)(2,1)S(1)}, u32[]{:S(2)}, u32[]{:S(2)}) collective-permute-start(bf16[3,32,384]{2,1,0:T(8,128)(2,1)S(1)} %get-tuple-element.78), channel_id=1, source_target_pairs={{0,15},{1,0},{2,1},{3,2},{4,3},{5,4},{6,5},{7,6},{8,7},{9,8},{10,9... | collective-permute-start | bytes 221192 | tf_op jit(solution)/shard_map/ppermute | solution.py:906
  3.5 1.0 %collective-permute-start = (bf16[3,32,384]{2,1,0:T(8,128)(2,1)S(1)}, bf16[3,32,384]{2,1,0:T(8,128)(2,1)S(1)}, u32[]{:S(2)}, u32[]{:S(2)}) collective-permute-start(bf16[3,32,384]{2,1,0:T(8,128)(2,1)S(1)} %get-tuple-element.79), channel_id=1, source_target_pairs={{0,1},{1,2},{2,3},{3,4},{4,5},{5,6},{6,7},{7,8},{8,9},{9,10},{10,1... | collective-permute-start | bytes 221192 | tf_op jit(solution)/shard_map/ppermute | solution.py:905
  4.4 0.9 %copy-done.3 = f32[1,49,384]{2,0,1:T(1,128)S(1)} copy-done((f32[1,49,384]{2,0,1:T(1,128)S(1)}, f32[1,49,384]{2,0,1:T(1,128)}, u32[]{:S(2)}) %copy-start.3) | copy-done | bytes 75288
  5.3 2.1 %inner_conv.2.conv0_ref = f32[1024,128]{1,0:T(8,128)S(1)} custom-call(f32[1024,384]{1,0:T(8,128)S(1)} %bitcast.11, f32[49,1,384]{2,1,0:T(1,128)S(1)} %bitcast.17), custom_call_target="tpu_custom_call" | custom-call | flops 2529999872 | bytes 1048576 | tf_op jit(solution)/shard_map/inner_conv/pallas_call | solution.py:87
  7.5 1.6 %arrange.1 = (bf16[1536,384]{1,0:T(8,128)(2,1)S(1)}, bf16[1536,384]{1,0:T(8,128)(2,1)S(1)}, bf16[384,1536]{1,0:T(8,128)(2,1)S(1)}, f32[1536,128]{1,0:T(8,128)S(1)}) custom-call(bf16[1536,384]{1,0:T(8,128)(2,1)S(1)} %bitcast.27, bf16[1536,384]{1,0:T(8,128)(2,1)S(1)} %bitcast.28, f32[1,1536]{1,0:T(1,128)S(1)} %copy-done.9), custom_call_target="tpu_custom_call" | custom-call | flops 1724999936 | bytes 1048576 | tf_op jit(solution)/shard_map/arrange/pallas_call | solution.py:406
  9.1 0.7 mask_rows.1.refs_1_
  9.9 1.9 %collective-permute-start.3 = (bf16[3,48,384]{2,1,0:T(8,128)(2,1)S(1)}, bf16[3,48,384]{2,1,0:T(8,128)(2,1)S(1)}, u32[]{:S(2)}, u32[]{:S(2)}) collective-permute-start(bf16[3,48,384]{2,1,0:T(8,128)(2,1)S(1)} %get-tuple-element.87), channel_id=1, source_target_pairs={{0,112},{16,0},{32,16},{48,32},{64,48},{80,64},{96,80},{112,96},{1... | collective-permute-start | bytes 331784 | tf_op jit(solution)/shard_map/ppermute | solution.py:912
  11.8 4.1 %inner_conv.3 = (f32[1024,128]{1,0:T(8,128)S(1)}, f32[1024,128]{1,0:T(8,128)S(1)}) custom-call(f32[1024,384]{1,0:T(8,128)S(1)} %bitcast.13, f32[49,1,384]{2,1,0:T(1,128)S(1)} %bitcast.18), custom_call_target="tpu_custom_call" | custom-call | flops 5059999744 | bytes 1048576 | tf_op jit(solution)/shard_map/inner_conv/pallas_call | solution.py:87
  16.0 1.2 %collective-permute-done.2.top_ref = bf16[3,48,384]{2,1,0:T(8,128)(2,1)S(1)} collective-permute-done((bf16[3,48,384]{2,1,0:T(8,128)(2,1)S(1)}, bf16[3,48,384]{2,1,0:T(8,128)(2,1)S(1)}, u32[]{:S(2)}, u32[]{:S(2)}) %collective-permute-start.2) | collective-permute-done | bytes 110624 | tf_op jit(solution)/shard_map/ppermute | solution.py:911
  17.2 1.9 %normalise.1 = (f32[1024,384]{1,0:T(8,128)S(1)}, f32[1024,128]{1,0:T(8,128)S(1)}, bf16[1024,384]{1,0:T(8,128)(2,1)S(1)}) custom-call(f32[1024,128]{1,0:T(8,128)S(1)} %inner_conv.2.conv0_ref, f32[1024,128]{1,0:T(8,128)S(1)} %get-tuple-element.90.conv1_ref, f32[1024,128]{1,0:T(8,128)S(1)} %get-tuple-element.91.conv2_ref, f32[49,1,384]{2,1,0:T(1,128)S(1)} %bitcast.19, ...), custom_call_target="tpu_custom_call" | custom-call | flops 3220000000 | bytes 1048576 | tf_op jit(solution)/shard_map/normalise/pallas_call | solution.py:315
  19.1 4.7 %hidden_far.1 = (bf16[768,768]{1,0:T(8,128)(2,1)S(1)}, bf16[768,1024]{1,0:T(8,128)(2,1)S(1)}) custom-call(bf16[1024,384]{1,0:T(8,128)(2,1)S(1)} %get-tuple-element.92.refs_0_, bf16[1024,384]{1,0:T(8,128)(2,1)S(1)} %mask_rows.1.refs_1_, bf16[1536,384]{1,0:T(8,128)(2,1)S(1)} %get-tuple-element.93.refs_2_, bf16[1536,384]{1,0:T(8,128)(2,1)S(1)} %get-tuple-element.94.refs_3_, ...), custom_call_target="tpu_custom_call" | custom-call | flops 5750000128 | bytes 1048576 | tf_op jit(solution)/shard_map/hidden_far/pallas_call | solution.py:531
  24.1 2.5 %near_first.1 = (f32[384,768]{1,0:T(8,128)S(1)}, bf16[768,1024]{1,0:T(8,128)(2,1)S(1)}) custom-call(bf16[1024,384]{1,0:T(8,128)(2,1)S(1)} %get-tuple-element.92.refs_0_, bf16[1024,384]{1,0:T(8,128)(2,1)S(1)} %mask_rows.1.refs_1_, bf16[1536,384]{1,0:T(8,128)(2,1)S(1)} %get-tuple-element.93.refs_2_, bf16[1536,384]{1,0:T(8,128)(2,1)S(1)} %get-tuple-element.94.refs_3_, ...), custom_call_target="tpu_custom_call" | custom-call | flops 3449999872 | bytes 1048576 | tf_op jit(solution)/shard_map/near_first/pallas_call | solution.py:564
  27.1 3.3 %collective-permute-start.6 = (bf16[192,768]{1,0:T(8,128)(2,1)S(1)}, bf16[192,768]{1,0:T(8,128)(2,1)S(1)}, u32[]{:S(2)}, u32[]{:S(2)}) collective-permute-start(bf16[192,768]{1,0:T(8,128)(2,1)S(1)} %get-tuple-element.100), channel_id=1, source_target_pairs={{0,64},{1,65},{2,66},{3,67},{4,68},{5,69},{6,70},{7,71},{8,72},{9,... | collective-permute-start | bytes 884744 | tf_op jit(solution)/shard_map/ppermute | solution.py:949
  30.4 2.6 %near_last.1 = (f32[192,768]{1,0:T(8,128)S(1)}, bf16[192,768]{1,0:T(8,128)(2,1)S(1)}, bf16[768,1024]{1,0:T(8,128)(2,1)S(1)}) custom-call(bf16[1024,384]{1,0:T(8,128)(2,1)S(1)} %get-tuple-element.92.refs_0_, bf16[1024,384]{1,0:T(8,128)(2,1)S(1)} %mask_rows.1.refs_1_, ...), custom_call_target="tpu_custom_call", output_to_operand_aliasing={{2}: (6, {})} | custom-call | flops 3449999872 | bytes 1048576 | tf_op jit(solution)/shard_map/near_last/pallas_call | solution.py:625
  33.7 1.4 %collective-permute-done.5.first_ref = bf16[192,768]{1,0:T(8,128)(2,1)S(1)} collective-permute-done((bf16[192,768]{1,0:T(8,128)(2,1)S(1)}, bf16[192,768]{1,0:T(8,128)(2,1)S(1)}, u32[]{:S(2)}, u32[]{:S(2)}) %collective-permute-start.5) | collective-permute-done | bytes 294944 | tf_op jit(solution)/shard_map/ppermute | solution.py:948
  35.0 2.1 %norm_back.1 = (f32[32,32,384]{2,1,0:T(8,128)S(1)}, bf16[3,32,384]{2,1,0:T(8,128)(2,1)S(1)}, bf16[3,32,384]{2,1,0:T(8,128)(2,1)S(1)}) custom-call(bf16[384,1536]{1,0:T(8,128)(2,1)S(1)} %get-tuple-element.82.turned_ref, bf16[768,1024]{1,0:T(8,128)(2,1)S(1)} %get-tuple-element.103.other_ref, bf16[768,1024]{1,0:T(8,128)(2,1)S(1)} %get-tuple-element.104.mine_ref, ...), custom_call_target="tpu_custom_call" | custom-call | flops 230000000 | bytes 1048576 | tf_op jit(solution)/shard_map/norm_back/pallas_call | solution.py:673
  37.2 2.8 %collective-permute-start.9 = (bf16[3,32,384]{2,1,0:T(8,128)(2,1)S(1)}, bf16[3,32,384]{2,1,0:T(8,128)(2,1)S(1)}, u32[]{:S(2)}, u32[]{:S(2)}) collective-permute-start(bf16[3,32,384]{2,1,0:T(8,128)(2,1)S(1)} %get-tuple-element.112), channel_id=1, source_target_pairs={{0,15},{1,0},{2,1},{3,2},{4,3},{5,4},{6,5},{7,6},{8,7},{9,8},{10,9... | collective-permute-start | bytes 221192 | tf_op jit(solution)/shard_map/ppermute | solution.py:906
  40.0 0.7 %collective-permute-start.8 = (bf16[3,32,384]{2,1,0:T(8,128)(2,1)S(1)}, bf16[3,32,384]{2,1,0:T(8,128)(2,1)S(1)}, u32[]{:S(2)}, u32[]{:S(2)}) collective-permute-start(bf16[3,32,384]{2,1,0:T(8,128)(2,1)S(1)} %get-tuple-element.113), channel_id=1, source_target_pairs={{0,1},{1,2},{2,3},{3,4},{4,5},{5,6},{6,7},{7,8},{8,9},{9,10},{10,1... | collective-permute-start | bytes 221192 | tf_op jit(solution)/shard_map/ppermute | solution.py:905
  40.8 2.0 %collective-permute-start.10 = (bf16[48,768]{1,0:T(8,128)(2,1)S(1)}, bf16[48,768]{1,0:T(8,128)(2,1)S(1)}, u32[]{:S(2)}, u32[]{:S(2)}) collective-permute-start(bf16[48,768]{1,0:T(8,128)(2,1)S(1)} %get-tuple-element.118), channel_id=1, source_target_pairs={{0,1},{1,128},{2,3},{3,130},{4,5},{5,132},{6,7},{7,134},{8,9},{9,1... | collective-permute-start | bytes 221192 | tf_op jit(solution)/shard_map/ppermute | solution.py:959
  42.8 2.7 %collective-permute-start.12 = (bf16[48,768]{1,0:T(8,128)(2,1)S(1)}, bf16[48,768]{1,0:T(8,128)(2,1)S(1)}, u32[]{:S(2)}, u32[]{:S(2)}) collective-permute-start(bf16[48,768]{1,0:T(8,128)(2,1)S(1)} %get-tuple-element.119), channel_id=1, source_target_pairs={{0,128},{1,129},{2,130},{3,131},{4,132},{5,133},{6,134},{7,135},{8... | collective-permute-start | bytes 221192 | tf_op jit(solution)/shard_map/ppermute | solution.py:959
  45.5 0.7 %collective-permute-start.11 = (bf16[48,768]{1,0:T(8,128)(2,1)S(1)}, bf16[48,768]{1,0:T(8,128)(2,1)S(1)}, u32[]{:S(2)}, u32[]{:S(2)}) collective-permute-start(bf16[48,768]{1,0:T(8,128)(2,1)S(1)} %get-tuple-element.120), channel_id=1, source_target_pairs={{0,129},{1,0},{2,131},{3,2},{4,133},{5,4},{6,135},{7,6},{8,137},{9... | collective-permute-start | bytes 221192 | tf_op jit(solution)/shard_map/ppermute | solution.py:959
  46.3 2.7 %back_conv.2 = (f32[1024,128]{1,0:T(8,128)S(1)}, f32[1024,128]{1,0:T(8,128)S(1)}) custom-call(f32[1024,384]{1,0:T(8,128)S(1)} %bitcast.24, f32[49,1,384]{2,1,0:T(1,128)S(1)} %bitcast.20), custom_call_target="tpu_custom_call" | custom-call | flops 3449999872 | bytes 1048576 | tf_op jit(solution)/shard_map/back_conv/pallas_call | solution.py:137
  48.9 0.9 %collective-permute-done.11.second_ref = bf16[48,768]{1,0:T(8,128)(2,1)S(1)} collective-permute-done((bf16[48,768]{1,0:T(8,128)(2,1)S(1)}, bf16[48,768]{1,0:T(8,128)(2,1)S(1)}, u32[]{:S(2)}, u32[]{:S(2)}) %collective-permute-start.11) | collective-permute-done | bytes 73760 | tf_op jit(solution)/shard_map/ppermute | solution.py:959
  49.9 1.7 %collective-permute-start.14 = (bf16[3,48,384]{2,1,0:T(8,128)(2,1)S(1)}, bf16[3,48,384]{2,1,0:T(8,128)(2,1)S(1)}, u32[]{:S(2)}, u32[]{:S(2)}) collective-permute-start(bf16[3,48,384]{2,1,0:T(8,128)(2,1)S(1)} %get-tuple-element.131), channel_id=1, source_target_pairs={{0,112},{16,0},{32,16},{48,32},{64,48},{80,64},{96,80},{112,96},{1... | collective-permute-start | bytes 331784 | tf_op jit(solution)/shard_map/ppermute | solution.py:912
  51.7 4.6 %collective-permute-start.15 = (bf16[12,768]{1,0:T(8,128)(2,1)S(1)}, bf16[12,768]{1,0:T(8,128)(2,1)S(1)}, u32[]{:S(2)}, u32[]{:S(2)}) collective-permute-start(bf16[12,768]{1,0:T(8,128)(2,1)S(1)} %get-tuple-element.137), channel_id=1, source_target_pairs={{0,4},{1,5},{2,6},{3,7},{4,8},{5,9},{6,10},{7,11},{8,12},{9,13},{1... | collective-permute-start | bytes 55304 | tf_op jit(solution)/shard_map/ppermute | solution.py:965
  56.3 4.5 %collective-permute-start.17 = (bf16[12,768]{1,0:T(8,128)(2,1)S(1)}, bf16[12,768]{1,0:T(8,128)(2,1)S(1)}, u32[]{:S(2)}, u32[]{:S(2)}) collective-permute-start(bf16[12,768]{1,0:T(8,128)(2,1)S(1)} %get-tuple-element.138), channel_id=1, source_target_pairs={{0,8},{1,9},{2,10},{3,11},{4,12},{5,13},{6,14},{7,15},{8,0},{9,1},... | collective-permute-start | bytes 55304 | tf_op jit(solution)/shard_map/ppermute | solution.py:965
  61.1 1.3 %back_conv.3.conv2_ref = f32[1024,128]{1,0:T(8,128)S(1)} custom-call(f32[1024,384]{1,0:T(8,128)S(1)} %bitcast.26, f32[49,1,384]{2,1,0:T(1,128)S(1)} %bitcast.21), custom_call_target="tpu_custom_call" | custom-call | flops 1724999936 | bytes 1048576 | tf_op jit(solution)/shard_map/back_conv/pallas_call | solution.py:137
  62.4 2.1 %finish_inner.1 = (f32[1024,384]{1,0:T(8,128)}, f32[6,32,384]{2,1,0:T(8,128)S(1)}) custom-call(s32[4,4]{1,0:T(4,128)S(1)} %copy-done.5, f32[1024,128]{1,0:T(8,128)S(1)} %get-tuple-element.122.conv0_ref, f32[1024,128]{1,0:T(8,128)S(1)} %get-tuple-element.123.conv1_ref, f32[1024,128]{1,0:T(8,128)S(1)} %back_conv.3.conv2_ref, f32[49,1,384]{2,1,0:T(1,128)S(1)} %bitcast.22, ...), custom_call_target="tpu_custom_call" | custom-call | flops 2529999872 | bytes 1048576 | tf_op jit(solution)/shard_map/finish_inner/pallas_call | solution.py:707
  64.5 1.0 %collective-permute-done.16.refs_1_ = bf16[12,768]{1,0:T(8,128)(2,1)S(1)} collective-permute-done((bf16[12,768]{1,0:T(8,128)(2,1)S(1)}, bf16[12,768]{1,0:T(8,128)(2,1)S(1)}, u32[]{:S(2)}, u32[]{:S(2)}) %collective-permute-start.16) | collective-permute-done | bytes 18464 | tf_op jit(solution)/shard_map/ppermute | solution.py:965
  65.7 1.8 %finish_outer.1 = f32[1024,384]{1,0:T(8,128)} custom-call(s32[4,4]{1,0:T(4,128)S(1)} %copy-done.5, f32[1024,128]{1,0:T(8,128)S(1)} %get-tuple-element.122.conv0_ref, f32[1024,128]{1,0:T(8,128)S(1)} %get-tuple-element.123.conv1_ref, f32[1024,128]{1,0:T(8,128)S(1)} %back_conv.3.conv2_ref, f32[49,1,384]{2,1,0:T(1,128)S(1)} %bitcast.23, ...), custom_call_target="tpu_custom_call", output_to_operand_aliasing={{}: (9, {})} | custom-call | flops 1150000000 | bytes 1048576 | tf_op jit(solution)/shard_map/finish_outer/pallas_call | solution.py:744
  67.5 2.0 %collective-permute-done.18.arrived_ref = f32[6,768]{1,0:T(8,128)S(1)} collective-permute-done((f32[6,768]{1,0:T(8,128)S(1)}, f32[6,768]{1,0:T(8,128)S(1)}, u32[]{:S(2)}, u32[]{:S(2)}) %collective-permute-start.18) | collective-permute-done | bytes 18464 | tf_op jit(solution)/shard_map/ppermute | solution.py:972
  (51 shorter events, 3.1 us)
Async XLA Ops:
  0.6 1.4 %copy-start = (f32[1,32,32,384]{3,2,1,0:T(8,128)S(1)}, f32[1,32,32,384]{3,2,1,0:T(8,128)}, u32[]{:S(2)}) copy-start(f32[1,32,32,384]{3,2,1,0:T(8,128)} %param.10) | copy-start | bytes 4718596
  2.0 2.4 %copy-start.1 = (f32[1,32,32,384]{3,2,1,0:T(8,128)S(1)}, f32[1,32,32,384]{3,2,1,0:T(8,128)}, u32[]{:S(2)}) copy-start(f32[1,32,32,384]{3,2,1,0:T(8,128)} %param.10) | copy-start | bytes 4718596
  2.3 7.4 %collective-permute-start.1 = (bf16[3,32,384]{2,1,0:T(8,128)(2,1)S(1)}, bf16[3,32,384]{2,1,0:T(8,128)(2,1)S(1)}, u32[]{:S(2)}, u32[]{:S(2)}) collective-permute-start(bf16[3,32,384]{2,1,0:T(8,128)(2,1)S(1)} %get-tuple-element.78), channel_id=1, source_target_pairs={{0,15},{1,0},{2,1},{3,2},{4,3},{5,4},{6,5},{7,6},{8,7},{9,8},{10,9... | collective-permute-start | bytes 221192 | tf_op jit(solution)/shard_map/ppermute | solution.py:906
  3.5 6.3 %collective-permute-start = (bf16[3,32,384]{2,1,0:T(8,128)(2,1)S(1)}, bf16[3,32,384]{2,1,0:T(8,128)(2,1)S(1)}, u32[]{:S(2)}, u32[]{:S(2)}) collective-permute-start(bf16[3,32,384]{2,1,0:T(8,128)(2,1)S(1)} %get-tuple-element.79), channel_id=1, source_target_pairs={{0,1},{1,2},{2,3},{3,4},{4,5},{5,6},{6,7},{7,8},{8,9},{9,10},{10,1... | collective-permute-start | bytes 221192 | tf_op jit(solution)/shard_map/ppermute | solution.py:905
  4.4 0.9 %copy-start.3 = (f32[1,49,384]{2,0,1:T(1,128)S(1)}, f32[1,49,384]{2,0,1:T(1,128)}, u32[]{:S(2)}) copy-start(f32[1,49,384]{2,0,1:T(1,128)} %param.13) | copy-start | bytes 225796
  5.3 2.1 %copy-start.7 = (bf16[1,1536,384]{2,1,0:T(8,128)(2,1)S(1)}, bf16[1,1536,384]{2,1,0:T(8,128)(2,1)}, u32[]{:S(2)}) copy-start(bf16[1,1536,384]{2,1,0:T(8,128)(2,1)} %param.17) | copy-start | bytes 3538948
  5.3 2.1 %copy-start.8 = (bf16[1,1536,384]{2,1,0:T(8,128)(2,1)S(1)}, bf16[1,1536,384]{2,1,0:T(8,128)(2,1)}, u32[]{:S(2)}) copy-start(bf16[1,1536,384]{2,1,0:T(8,128)(2,1)} %param.19) | copy-start | bytes 3538948
  5.3 2.1 %copy-start.9 = (f32[1,1536]{1,0:T(1,128)S(1)}, f32[1,1536]{1,0:T(1,128)}, u32[]{:S(2)}) copy-start(f32[1,1536]{1,0:T(1,128)} %bias_ref.2) | copy-start | bytes 18436
  7.4 1.6 %copy-start.2 = (f32[1,32,32,384]{3,2,1,0:T(8,128)S(1)}, f32[1,32,32,384]{3,2,1,0:T(8,128)}, u32[]{:S(2)}) copy-start(f32[1,32,32,384]{3,2,1,0:T(8,128)} %param.11) | copy-start | bytes 4718596
  7.5 1.6 %copy-start.5 = (s32[4,4]{1,0:T(4,128)S(1)}, s32[4,4]{1,0:T(4,128)}, u32[]{:S(2)}) copy-start(s32[4,4]{1,0:T(4,128)} %counts_ref.5) | copy-start | bytes 196
  9.8 2.0 %copy-start.4 = (f32[1,49,384]{2,0,1:T(1,128)S(1)}, f32[1,49,384]{2,0,1:T(1,128)}, u32[]{:S(2)}) copy-start(f32[1,49,384]{2,0,1:T(1,128)} %param.13) | copy-start | bytes 225796
  9.9 6.1 %collective-permute-start.3 = (bf16[3,48,384]{2,1,0:T(8,128)(2,1)S(1)}, bf16[3,48,384]{2,1,0:T(8,128)(2,1)S(1)}, u32[]{:S(2)}, u32[]{:S(2)}) collective-permute-start(bf16[3,48,384]{2,1,0:T(8,128)(2,1)S(1)} %get-tuple-element.87), channel_id=1, source_target_pairs={{0,112},{16,0},{32,16},{48,32},{64,48},{80,64},{96,80},{112,96},{1... | collective-permute-start | bytes 331784 | tf_op jit(solution)/shard_map/ppermute | solution.py:912
  11.8 5.4 %copy-start.6 = (f32[1,384]{1,0:T(1,128)S(1)}, f32[1,384]{1,0:T(1,128)}, u32[]{:S(2)}) copy-start(f32[1,384]{1,0:T(1,128)} %gain_ref.3) | copy-start | bytes 4612
  11.8 5.4 %copy-start.10 = (f32[1,384]{1,0:T(1,128)S(1)}, f32[1,384]{1,0:T(1,128)}, u32[]{:S(2)}) copy-start(f32[1,384]{1,0:T(1,128)} %bias_ref.3) | copy-start | bytes 4612
  11.8 5.4 %copy-start.11 = (f32[1,384]{1,0:T(1,128)S(1)}, f32[1,384]{1,0:T(1,128)}, u32[]{:S(2)}) copy-start(f32[1,384]{1,0:T(1,128)} %shift_ref.1) | copy-start | bytes 4612
  11.8 5.4 %collective-permute-start.2 = (bf16[3,48,384]{2,1,0:T(8,128)(2,1)S(1)}, bf16[3,48,384]{2,1,0:T(8,128)(2,1)S(1)}, u32[]{:S(2)}, u32[]{:S(2)}) collective-permute-start(bf16[3,48,384]{2,1,0:T(8,128)(2,1)S(1)} %get-tuple-element.88), channel_id=1, source_target_pairs={{0,16},{16,32},{32,48},{48,64},{64,80},{80,96},{96,112},{112,0},{1... | collective-permute-start | bytes 331784 | tf_op jit(solution)/shard_map/ppermute | solution.py:911
  23.8 3.1 %collective-permute-start.4 = (bf16[768,768]{1,0:T(8,128)(2,1)S(1)}, bf16[768,768]{1,0:T(8,128)(2,1)S(1)}, u32[]{:S(2)}, u32[]{:S(2)}) collective-permute-start(bf16[768,768]{1,0:T(8,128)(2,1)S(1)} %get-tuple-element.97), channel_id=1, source_target_pairs={{0,16},{16,0},{32,48},{48,32},{64,80},{80,64},{96,112},{112,96},{1... | collective-permute-start | bytes 3538952 | tf_op jit(solution)/shard_map/ppermute | solution.py:945
  27.0 8.0 %collective-permute-start.5 = (bf16[192,768]{1,0:T(8,128)(2,1)S(1)}, bf16[192,768]{1,0:T(8,128)(2,1)S(1)}, u32[]{:S(2)}, u32[]{:S(2)}) collective-permute-start(bf16[192,768]{1,0:T(8,128)(2,1)S(1)} %get-tuple-element.98), channel_id=1, source_target_pairs={{0,32},{1,33},{2,34},{3,35},{4,36},{5,37},{6,38},{7,39},{8,40},{9,... | collective-permute-start | bytes 884744 | tf_op jit(solution)/shard_map/ppermute | solution.py:948
  27.1 12.8 %collective-permute-start.6 = (bf16[192,768]{1,0:T(8,128)(2,1)S(1)}, bf16[192,768]{1,0:T(8,128)(2,1)S(1)}, u32[]{:S(2)}, u32[]{:S(2)}) collective-permute-start(bf16[192,768]{1,0:T(8,128)(2,1)S(1)} %get-tuple-element.100), channel_id=1, source_target_pairs={{0,64},{1,65},{2,66},{3,67},{4,68},{5,69},{6,70},{7,71},{8,72},{9,... | collective-permute-start | bytes 884744 | tf_op jit(solution)/shard_map/ppermute | solution.py:949
  33.1 7.6 %collective-permute-start.7 = (bf16[192,768]{1,0:T(8,128)(2,1)S(1)}, bf16[192,768]{1,0:T(8,128)(2,1)S(1)}, u32[]{:S(2)}, u32[]{:S(2)}) collective-permute-start(bf16[192,768]{1,0:T(8,128)(2,1)S(1)} %get-tuple-element.102), channel_id=1, source_target_pairs={{0,96},{1,97},{2,98},{3,99},{4,100},{5,101},{6,102},{7,103},{8,104... | collective-permute-start | bytes 884744 | tf_op jit(solution)/shard_map/ppermute | solution.py:951
  37.2 11.8 %collective-permute-start.9 = (bf16[3,32,384]{2,1,0:T(8,128)(2,1)S(1)}, bf16[3,32,384]{2,1,0:T(8,128)(2,1)S(1)}, u32[]{:S(2)}, u32[]{:S(2)}) collective-permute-start(bf16[3,32,384]{2,1,0:T(8,128)(2,1)S(1)} %get-tuple-element.112), channel_id=1, source_target_pairs={{0,15},{1,0},{2,1},{3,2},{4,3},{5,4},{6,5},{7,6},{8,7},{9,8},{10,9... | collective-permute-start | bytes 221192 | tf_op jit(solution)/shard_map/ppermute | solution.py:906
  40.0 9.9 %collective-permute-start.8 = (bf16[3,32,384]{2,1,0:T(8,128)(2,1)S(1)}, bf16[3,32,384]{2,1,0:T(8,128)(2,1)S(1)}, u32[]{:S(2)}, u32[]{:S(2)}) collective-permute-start(bf16[3,32,384]{2,1,0:T(8,128)(2,1)S(1)} %get-tuple-element.113), channel_id=1, source_target_pairs={{0,1},{1,2},{2,3},{3,4},{4,5},{5,6},{6,7},{7,8},{8,9},{9,10},{10,1... | collective-permute-start | bytes 221192 | tf_op jit(solution)/shard_map/ppermute | solution.py:905
  40.8 8.1 %collective-permute-start.10 = (bf16[48,768]{1,0:T(8,128)(2,1)S(1)}, bf16[48,768]{1,0:T(8,128)(2,1)S(1)}, u32[]{:S(2)}, u32[]{:S(2)}) collective-permute-start(bf16[48,768]{1,0:T(8,128)(2,1)S(1)} %get-tuple-element.118), channel_id=1, source_target_pairs={{0,1},{1,128},{2,3},{3,130},{4,5},{5,132},{6,7},{7,134},{8,9},{9,1... | collective-permute-start | bytes 221192 | tf_op jit(solution)/shard_map/ppermute | solution.py:959
  42.8 6.2 %collective-permute-start.12 = (bf16[48,768]{1,0:T(8,128)(2,1)S(1)}, bf16[48,768]{1,0:T(8,128)(2,1)S(1)}, u32[]{:S(2)}, u32[]{:S(2)}) collective-permute-start(bf16[48,768]{1,0:T(8,128)(2,1)S(1)} %get-tuple-element.119), channel_id=1, source_target_pairs={{0,128},{1,129},{2,130},{3,131},{4,132},{5,133},{6,134},{7,135},{8... | collective-permute-start | bytes 221192 | tf_op jit(solution)/shard_map/ppermute | solution.py:959
  45.5 4.4 %collective-permute-start.11 = (bf16[48,768]{1,0:T(8,128)(2,1)S(1)}, bf16[48,768]{1,0:T(8,128)(2,1)S(1)}, u32[]{:S(2)}, u32[]{:S(2)}) collective-permute-start(bf16[48,768]{1,0:T(8,128)(2,1)S(1)} %get-tuple-element.120), channel_id=1, source_target_pairs={{0,129},{1,0},{2,131},{3,2},{4,133},{5,4},{6,135},{7,6},{8,137},{9... | collective-permute-start | bytes 221192 | tf_op jit(solution)/shard_map/ppermute | solution.py:959
  49.9 11.1 %collective-permute-start.14 = (bf16[3,48,384]{2,1,0:T(8,128)(2,1)S(1)}, bf16[3,48,384]{2,1,0:T(8,128)(2,1)S(1)}, u32[]{:S(2)}, u32[]{:S(2)}) collective-permute-start(bf16[3,48,384]{2,1,0:T(8,128)(2,1)S(1)} %get-tuple-element.131), channel_id=1, source_target_pairs={{0,112},{16,0},{32,16},{48,32},{64,48},{80,64},{96,80},{112,96},{1... | collective-permute-start | bytes 331784 | tf_op jit(solution)/shard_map/ppermute | solution.py:912
  51.6 9.4 %collective-permute-start.13 = (bf16[3,48,384]{2,1,0:T(8,128)(2,1)S(1)}, bf16[3,48,384]{2,1,0:T(8,128)(2,1)S(1)}, u32[]{:S(2)}, u32[]{:S(2)}) collective-permute-start(bf16[3,48,384]{2,1,0:T(8,128)(2,1)S(1)} %get-tuple-element.132), channel_id=1, source_target_pairs={{0,16},{16,32},{32,48},{48,64},{64,80},{80,96},{96,112},{112,0},{1... | collective-permute-start | bytes 331784 | tf_op jit(solution)/shard_map/ppermute | solution.py:911
  51.7 12.8 %collective-permute-start.15 = (bf16[12,768]{1,0:T(8,128)(2,1)S(1)}, bf16[12,768]{1,0:T(8,128)(2,1)S(1)}, u32[]{:S(2)}, u32[]{:S(2)}) collective-permute-start(bf16[12,768]{1,0:T(8,128)(2,1)S(1)} %get-tuple-element.137), channel_id=1, source_target_pairs={{0,4},{1,5},{2,6},{3,7},{4,8},{5,9},{6,10},{7,11},{8,12},{9,13},{1... | collective-permute-start | bytes 55304 | tf_op jit(solution)/shard_map/ppermute | solution.py:965
  56.3 8.2 %collective-permute-start.17 = (bf16[12,768]{1,0:T(8,128)(2,1)S(1)}, bf16[12,768]{1,0:T(8,128)(2,1)S(1)}, u32[]{:S(2)}, u32[]{:S(2)}) collective-permute-start(bf16[12,768]{1,0:T(8,128)(2,1)S(1)} %get-tuple-element.138), channel_id=1, source_target_pairs={{0,8},{1,9},{2,10},{3,11},{4,12},{5,13},{6,14},{7,15},{8,0},{9,1},... | collective-permute-start | bytes 55304 | tf_op jit(solution)/shard_map/ppermute | solution.py:965
  60.8 4.7 %collective-permute-start.16 = (bf16[12,768]{1,0:T(8,128)(2,1)S(1)}, bf16[12,768]{1,0:T(8,128)(2,1)S(1)}, u32[]{:S(2)}, u32[]{:S(2)}) collective-permute-start(bf16[12,768]{1,0:T(8,128)(2,1)S(1)} %get-tuple-element.139), channel_id=1, source_target_pairs={{0,12},{1,13},{2,14},{3,15},{4,0},{5,1},{6,2},{7,3},{8,4},{9,5},{1... | collective-permute-start | bytes 55304 | tf_op jit(solution)/shard_map/ppermute | solution.py:965
  65.6 3.9 %collective-permute-start.18 = (f32[6,768]{1,0:T(8,128)S(1)}, f32[6,768]{1,0:T(8,128)S(1)}, u32[]{:S(2)}, u32[]{:S(2)}) collective-permute-start(f32[6,768]{1,0:T(8,128)S(1)} %get-tuple-element.148), channel_id=1, source_target_pairs={{0,2},{1,3},{2,0},{3,1},{4,6},{5,7},{6,4},{7,5},{8,10},{9,11},{10,... | collective-permute-start | bytes 55304 | tf_op jit(solution)/shard_map/ppermute | solution.py:972

commit v13 on v10

--- a/solution.py
+++ b/solution.py
@@ -823,14 +823,14 @@
     )(own, *parts)
 
 
-def split_ring_body(own_ref, first_ref, second_ref, third_ref, kept_ref, *sent_refs):
+def split_ring_body(own_ref, first_ref, second_ref, third_ref, kept_ref, following_ref, *sent_refs):
     size = kept_ref.shape[0]
     total = own_ref[...]
     for ref in (first_ref, second_ref, third_ref):
         total = total + ref[...].astype(f32)
     chunks = [total[c * size : (c + 1) * size] for c in range(4)]
     place = own_place()[3] >> 1
-    for step, ref in enumerate((kept_ref, *sent_refs)):
+    for step, ref in enumerate((kept_ref, following_ref, *sent_refs)):
         wanted = (place + step) & 3
         found = chunks[0]
         for c in range(1, 4):
@@ -840,16 +840,33 @@
 
 def split_ring(own, parts):
     size, width = own.shape[0] // 4, own.shape[1]
+    kept = jax.ShapeDtypeStruct((size, width), f32)
     sent = jax.ShapeDtypeStruct((size, width), bf16)
     return pl.pallas_call(
         split_ring_body,
-        out_shape=(jax.ShapeDtypeStruct((size, width), f32), sent, sent, sent),
+        out_shape=(kept, kept, sent, sent),
         in_specs=[whole] * 4,
         out_specs=[whole] * 4,
         compiler_params=params(4),
         cost_estimate=cost(0.2),
         name="split_ring",
     )(own, *parts)
+
+
+def relay_body(own_ref, passed_ref, sent_ref):
+    sent_ref[...] = (own_ref[...] + passed_ref[...].astype(f32)).astype(bf16)
+
+
+def relay(own, passed):
+    return pl.pallas_call(
+        relay_body,
+        out_shape=jax.ShapeDtypeStruct(own.shape, bf16),
+        in_specs=[whole] * 2,
+        out_specs=whole,
+        compiler_params=params(4),
+        cost_estimate=cost(0.1),
+        name="relay",
+    )(own, passed)
 
 
 def last_sum_body(scale, own_ref, arrived_ref, expand_ref, reduce_ref):
@@ -971,12 +988,16 @@
     (conv_grad, left, right), parts = after(((conv_grad, left, right), parts), back)
     up, down = side_rows(conv_grad, left, right)
 
-    own, *sent = split_ring(*after((own, parts), up, down))
-    parts = [lax.ppermute(sent[i], every_axis, ring_pairs(i + 1)) for i in (1, 0, 2)]
+    own, following, two, three = split_ring(*after((own, parts), up, down))
+    passed = lax.ppermute(two, every_axis, ring_pairs(1))
+    part_before = lax.ppermute(three, every_axis, ring_pairs(3))
     top, bottom = lat_halo(up, down)
-    back += back_conv(after(conv_grad, sent, top, bottom), kernel, (2,))
-
-    inner, cols_sum = finish_inner(counts, back, kernel, left, right, grad)
+    back += back_conv(after(conv_grad, two, three, top, bottom), kernel, (2,))
+    passed, part_before = after((passed, part_before), back)
+    one = relay(following, passed)
+    part_after = lax.ppermute(one, every_axis, ring_pairs(1))
+    parts = [part_before, part_after]
+    inner, cols_sum = finish_inner(counts, back, kernel, left, right, after(grad, one))
 
     own, sent = split_two(*after((own, parts), inner))
     arrived = lax.ppermute(sent, every_axis, last_pairs())

time: 69.6 us -> 71.6 us (1.029)
  starting transfers between devices: 28.8 us -> 30.1 us
    ppermute x3, waiting for transfers between devices: 1.01 us -> 2.64 us  [the longest x1 1.47 us: local(): part_after = lax.ppermute(one, every_axis, ring_pairs(1))]
    ppermute x1, waiting for transfers between devices: 1.96 us -> 0.54 us  [local(): arrived = lax.ppermute(sent, every_axis, last_pairs())]
    ppermute x1, starting transfers between devices: 0.12 us -> 1.54 us  [local(): arrived = lax.ppermute(sent, every_axis, last_pairs())]
  transfers between devices with their start and end apart: 19 -> 19, of which waited for: 6 -> 8; matrix products, arithmetic and copies ran while one was open for 0% -> 0% of each run, Pallas kernels for 34% -> 34%
where the time goes in v13:
time: 71.6 us; the launch traced here: 71.1 us
  Pallas kernels  33.4 us (47%)
  starting transfers between devices  30.1 us (42%)
  waiting for transfers between devices  6.62 us (9%)
  between operations  0.93 us (1%)
    pallas_call x2, Pallas kernels, inner_conv(): pl.pallas_call(functools.partial(inner_conv_body, parts), out_shape=(shap...  6.22 us
    ppermute x3, starting transfers between devices, local(): lax.ppermute(sent[i], every_axis, plane_pairs(i + 1, False))  5.44 us
    ppermute x2, starting transfers between devices, lon_halo(): right = lax.ppermute(first, 'lon', shifted('lon', -1))  4.98 us
    ppermute x2, starting transfers between devices, lat_halo(): bottom = lax.ppermute(up, 'lat', shifted('lat', -1))  4.68 us
    pallas_call x1, Pallas kernels, hidden_far(): pl.pallas_call(far_body, out_shape=(jax.ShapeDtypeStruct((half, 2 * chann...  4.65 us
    pallas_call x2, Pallas kernels, back_conv(): pl.pallas_call(functools.partial(back_conv_body, parts), out_shape=(shape...  4 us
    ppermute x1, starting transfers between devices, local(): passed = lax.ppermute(two, every_axis, ring_pairs(1))  3.51 us
    ppermute x1, starting transfers between devices, local(): part_two = lax.ppermute(two, every_axis, plane_pairs(2, True))  3.31 us
  transfers between devices with their start and end apart: 19, of which 8 were waited for; matrix products, arithmetic and copies ran while one was open for 0% of the time, Pallas kernels for 34%

profile of v13, /device:TPU:32, one launch (start us, length us, event | category | flops | bytes accessed | tf_op | source)
XLA Modules:
  0.0 71.1 jit_solution(4916708257698530277)
XLA Ops:
  0.6 2.1 %side_cols.1 = (bf16[3,32,384]{2,1,0:T(8,128)(2,1)}, bf16[3,32,384]{2,1,0:T(8,128)(2,1)}) custom-call(f32[32,32,384]{2,1,0:T(8,128)} %bitcast.20), custom_call_target="tpu_custom_call" | custom-call | flops 1150000000 | bytes 1048576 | tf_op jit(solution)/shard_map/side_cols/pallas_call | solution.py:170
  2.7 1.1 %collective-permute-start.1 = (bf16[3,32,384]{2,1,0:T(8,128)(2,1)}, bf16[3,32,384]{2,1,0:T(8,128)(2,1)S(1)}, u32[]{:S(2)}, u32[]{:S(2)}) collective-permute-start(bf16[3,32,384]{2,1,0:T(8,128)(2,1)} %get-tuple-element.80), channel_id=1, source_target_pairs={{0,15},{1,0},{2,1},{3,2},{4,3},{5,4},{6,5},{7,6},{8,7},{9,8},{10,9... | collective-permute-start | bytes 221192 | tf_op jit(solution)/shard_map/ppermute | solution.py:933
  3.8 1.0 %collective-permute-start = (bf16[3,32,384]{2,1,0:T(8,128)(2,1)}, bf16[3,32,384]{2,1,0:T(8,128)(2,1)S(1)}, u32[]{:S(2)}, u32[]{:S(2)}) collective-permute-start(bf16[3,32,384]{2,1,0:T(8,128)(2,1)} %get-tuple-element.81), channel_id=1, source_target_pairs={{0,1},{1,2},{2,3},{3,4},{4,5},{5,6},{6,7},{7,8},{8,9},{9,10},{10,1... | collective-permute-start | bytes 221192 | tf_op jit(solution)/shard_map/ppermute | solution.py:932
  4.8 2.1 %inner_conv.2.conv0_ref = f32[1024,128]{1,0:T(8,128)S(1)} custom-call(f32[1024,384]{1,0:T(8,128)S(1)} %bitcast.21, f32[49,1,384]{2,1,0:T(1,128)S(1)} %bitcast.13), custom_call_target="tpu_custom_call" | custom-call | flops 2529999872 | bytes 1048576 | tf_op jit(solution)/shard_map/inner_conv/pallas_call | solution.py:87
  7.0 1.6 %arrange.1 = (bf16[1536,384]{1,0:T(8,128)(2,1)S(1)}, bf16[1536,384]{1,0:T(8,128)(2,1)S(1)}, bf16[384,1536]{1,0:T(8,128)(2,1)S(1)}, f32[1536,128]{1,0:T(8,128)S(1)}) custom-call(bf16[1536,384]{1,0:T(8,128)(2,1)S(1)} %bitcast.27, bf16[1536,384]{1,0:T(8,128)(2,1)S(1)} %bitcast.28, f32[1,1536]{1,0:T(1,128)S(1)} %copy-done.7), custom_call_target="tpu_custom_call" | custom-call | flops 1724999936 | bytes 1048576 | tf_op jit(solution)/shard_map/arrange/pallas_call | solution.py:416
  8.6 0.7 mask_rows.1.refs_1_
  9.4 1.9 %collective-permute-start.3 = (bf16[3,48,384]{2,1,0:T(8,128)(2,1)S(1)}, bf16[3,48,384]{2,1,0:T(8,128)(2,1)S(1)}, u32[]{:S(2)}, u32[]{:S(2)}) collective-permute-start(bf16[3,48,384]{2,1,0:T(8,128)(2,1)S(1)} %get-tuple-element.89), channel_id=1, source_target_pairs={{0,112},{16,0},{32,16},{48,32},{64,48},{80,64},{96,80},{112,96},{1... | collective-permute-start | bytes 331784 | tf_op jit(solution)/shard_map/ppermute | solution.py:939
  11.3 4.1 %inner_conv.3 = (f32[1024,128]{1,0:T(8,128)S(1)}, f32[1024,128]{1,0:T(8,128)S(1)}) custom-call(f32[1024,384]{1,0:T(8,128)S(1)} %bitcast.23, f32[49,1,384]{2,1,0:T(1,128)S(1)} %bitcast.14), custom_call_target="tpu_custom_call" | custom-call | flops 5059999744 | bytes 1048576 | tf_op jit(solution)/shard_map/inner_conv/pallas_call | solution.py:87
  15.4 1.2 %collective-permute-done.2.top_ref = bf16[3,48,384]{2,1,0:T(8,128)(2,1)S(1)} collective-permute-done((bf16[3,48,384]{2,1,0:T(8,128)(2,1)S(1)}, bf16[3,48,384]{2,1,0:T(8,128)(2,1)S(1)}, u32[]{:S(2)}, u32[]{:S(2)}) %collective-permute-start.2) | collective-permute-done | bytes 110624 | tf_op jit(solution)/shard_map/ppermute | solution.py:938
  16.7 1.9 %normalise.1 = (f32[1024,384]{1,0:T(8,128)S(1)}, f32[1024,128]{1,0:T(8,128)S(1)}, bf16[1024,384]{1,0:T(8,128)(2,1)S(1)}) custom-call(f32[1024,128]{1,0:T(8,128)S(1)} %inner_conv.2.conv0_ref, f32[1024,128]{1,0:T(8,128)S(1)} %get-tuple-element.92.conv1_ref, f32[1024,128]{1,0:T(8,128)S(1)} %get-tuple-element.93.conv2_ref, f32[49,1,384]{2,1,0:T(1,128)S(1)} %bitcast.15, ...), custom_call_target="tpu_custom_call" | custom-call | flops 3220000000 | bytes 1048576 | tf_op jit(solution)/shard_map/normalise/pallas_call | solution.py:325
  18.6 4.6 %hidden_far.1 = (bf16[768,768]{1,0:T(8,128)(2,1)S(1)}, bf16[768,1024]{1,0:T(8,128)(2,1)S(1)}) custom-call(bf16[1024,384]{1,0:T(8,128)(2,1)S(1)} %get-tuple-element.94.refs_0_, bf16[1024,384]{1,0:T(8,128)(2,1)S(1)} %mask_rows.1.refs_1_, bf16[1536,384]{1,0:T(8,128)(2,1)S(1)} %get-tuple-element.95.refs_2_, bf16[1536,384]{1,0:T(8,128)(2,1)S(1)} %get-tuple-element.96.refs_3_, ...), custom_call_target="tpu_custom_call" | custom-call | flops 5750000128 | bytes 1048576 | tf_op jit(solution)/shard_map/hidden_far/pallas_call | solution.py:541
  23.6 2.5 %near_first.1 = (f32[384,768]{1,0:T(8,128)S(1)}, bf16[768,1024]{1,0:T(8,128)(2,1)S(1)}) custom-call(bf16[1024,384]{1,0:T(8,128)(2,1)S(1)} %get-tuple-element.94.refs_0_, bf16[1024,384]{1,0:T(8,128)(2,1)S(1)} %mask_rows.1.refs_1_, bf16[1536,384]{1,0:T(8,128)(2,1)S(1)} %get-tuple-element.95.refs_2_, bf16[1536,384]{1,0:T(8,128)(2,1)S(1)} %get-tuple-element.96.refs_3_, ...), custom_call_target="tpu_custom_call" | custom-call | flops 3449999872 | bytes 1048576 | tf_op jit(solution)/shard_map/near_first/pallas_call | solution.py:574
  26.6 3.3 %collective-permute-start.6 = (bf16[192,768]{1,0:T(8,128)(2,1)S(1)}, bf16[192,768]{1,0:T(8,128)(2,1)S(1)}, u32[]{:S(2)}, u32[]{:S(2)}) collective-permute-start(bf16[192,768]{1,0:T(8,128)(2,1)S(1)} %get-tuple-element.102), channel_id=1, source_target_pairs={{0,64},{1,65},{2,66},{3,67},{4,68},{5,69},{6,70},{7,71},{8,72},{9,... | collective-permute-start | bytes 884744 | tf_op jit(solution)/shard_map/ppermute | solution.py:976
  29.9 2.6 %near_last.1 = (f32[192,768]{1,0:T(8,128)S(1)}, bf16[192,768]{1,0:T(8,128)(2,1)S(1)}, bf16[768,1024]{1,0:T(8,128)(2,1)S(1)}) custom-call(bf16[1024,384]{1,0:T(8,128)(2,1)S(1)} %get-tuple-element.94.refs_0_, bf16[1024,384]{1,0:T(8,128)(2,1)S(1)} %mask_rows.1.refs_1_, ...), custom_call_target="tpu_custom_call", output_to_operand_aliasing={{2}: (6, {})} | custom-call | flops 3449999872 | bytes 1048576 | tf_op jit(solution)/shard_map/near_last/pallas_call | solution.py:635
  32.5 0.7 collective-permute-start.7
  33.1 1.4 %collective-permute-done.5.first_ref = bf16[192,768]{1,0:T(8,128)(2,1)S(1)} collective-permute-done((bf16[192,768]{1,0:T(8,128)(2,1)S(1)}, bf16[192,768]{1,0:T(8,128)(2,1)S(1)}, u32[]{:S(2)}, u32[]{:S(2)}) %collective-permute-start.5) | collective-permute-done | bytes 294944 | tf_op jit(solution)/shard_map/ppermute | solution.py:975
  34.5 2.1 %norm_back.1 = (f32[32,32,384]{2,1,0:T(8,128)S(1)}, bf16[3,32,384]{2,1,0:T(8,128)(2,1)S(1)}, bf16[3,32,384]{2,1,0:T(8,128)(2,1)S(1)}) custom-call(bf16[384,1536]{1,0:T(8,128)(2,1)S(1)} %get-tuple-element.84.turned_ref, bf16[768,1024]{1,0:T(8,128)(2,1)S(1)} %get-tuple-element.105.other_ref, bf16[768,1024]{1,0:T(8,128)(2,1)S(1)} %get-tuple-element.106.mine_ref, ...), custom_call_target="tpu_custom_call" | custom-call | flops 230000000 | bytes 1048576 | tf_op jit(solution)/shard_map/norm_back/pallas_call | solution.py:683
  36.6 3.9 %collective-permute-start.9 = (bf16[3,32,384]{2,1,0:T(8,128)(2,1)S(1)}, bf16[3,32,384]{2,1,0:T(8,128)(2,1)S(1)}, u32[]{:S(2)}, u32[]{:S(2)}) collective-permute-start(bf16[3,32,384]{2,1,0:T(8,128)(2,1)S(1)} %get-tuple-element.114), channel_id=1, source_target_pairs={{0,15},{1,0},{2,1},{3,2},{4,3},{5,4},{6,5},{7,6},{8,7},{9,8},{10,9... | collective-permute-start | bytes 221192 | tf_op jit(solution)/shard_map/ppermute | solution.py:933
  40.7 1.6 %collective-permute-start.11 = (bf16[48,768]{1,0:T(8,128)(2,1)S(1)}, bf16[48,768]{1,0:T(8,128)(2,1)S(1)}, u32[]{:S(2)}, u32[]{:S(2)}) collective-permute-start(bf16[48,768]{1,0:T(8,128)(2,1)S(1)} %get-tuple-element.120), channel_id=1, source_target_pairs={{0,1},{1,128},{2,3},{3,130},{4,5},{5,132},{6,7},{7,134},{8,9},{9,1... | collective-permute-start | bytes 221192 | tf_op jit(solution)/shard_map/ppermute | solution.py:986
  42.2 2.7 %collective-permute-start.10 = (bf16[48,768]{1,0:T(8,128)(2,1)S(1)}, bf16[48,768]{1,0:T(8,128)(2,1)S(1)}, u32[]{:S(2)}, u32[]{:S(2)}) collective-permute-start(bf16[48,768]{1,0:T(8,128)(2,1)S(1)} %get-tuple-element.121), channel_id=1, source_target_pairs={{0,128},{1,129},{2,130},{3,131},{4,132},{5,133},{6,134},{7,135},{8... | collective-permute-start | bytes 221192 | tf_op jit(solution)/shard_map/ppermute | solution.py:986
  45.0 1.1 %collective-permute-start.12 = (bf16[48,768]{1,0:T(8,128)(2,1)S(1)}, bf16[48,768]{1,0:T(8,128)(2,1)S(1)}, u32[]{:S(2)}, u32[]{:S(2)}) collective-permute-start(bf16[48,768]{1,0:T(8,128)(2,1)S(1)} %get-tuple-element.122), channel_id=1, source_target_pairs={{0,129},{1,0},{2,131},{3,2},{4,133},{5,4},{6,135},{7,6},{8,137},{9... | collective-permute-start | bytes 221192 | tf_op jit(solution)/shard_map/ppermute | solution.py:986
  46.1 2.7 %back_conv.2 = (f32[1024,128]{1,0:T(8,128)S(1)}, f32[1024,128]{1,0:T(8,128)S(1)}) custom-call(f32[1024,384]{1,0:T(8,128)S(1)} %bitcast.24, f32[49,1,384]{2,1,0:T(1,128)S(1)} %bitcast.16), custom_call_target="tpu_custom_call" | custom-call | flops 3449999872 | bytes 1048576 | tf_op jit(solution)/shard_map/back_conv/pallas_call | solution.py:137
  49.4 2.8 %collective-permute-start.14 = (bf16[3,48,384]{2,1,0:T(8,128)(2,1)S(1)}, bf16[3,48,384]{2,1,0:T(8,128)(2,1)S(1)}, u32[]{:S(2)}, u32[]{:S(2)}) collective-permute-start(bf16[3,48,384]{2,1,0:T(8,128)(2,1)S(1)} %get-tuple-element.133), channel_id=1, source_target_pairs={{0,112},{16,0},{32,16},{48,32},{64,48},{80,64},{96,80},{112,96},{1... | collective-permute-start | bytes 331784 | tf_op jit(solution)/shard_map/ppermute | solution.py:939
  52.3 3.5 %collective-permute-start.15 = (bf16[12,768]{1,0:T(8,128)(2,1)S(1)}, bf16[12,768]{1,0:T(8,128)(2,1)S(1)}, u32[]{:S(2)}, u32[]{:S(2)}) collective-permute-start(bf16[12,768]{1,0:T(8,128)(2,1)S(1)} %get-tuple-element.139), channel_id=1, source_target_pairs={{0,4},{1,5},{2,6},{3,7},{4,8},{5,9},{6,10},{7,11},{8,12},{9,13},{1... | collective-permute-start | bytes 55304 | tf_op jit(solution)/shard_map/ppermute | solution.py:992
  55.8 2.2 %collective-permute-start.16 = (bf16[12,768]{1,0:T(8,128)(2,1)S(1)}, bf16[12,768]{1,0:T(8,128)(2,1)S(1)}, u32[]{:S(2)}, u32[]{:S(2)}) collective-permute-start(bf16[12,768]{1,0:T(8,128)(2,1)S(1)} %get-tuple-element.140), channel_id=1, source_target_pairs={{0,12},{1,13},{2,14},{3,15},{4,0},{5,1},{6,2},{7,3},{8,4},{9,5},{1... | collective-permute-start | bytes 55304 | tf_op jit(solution)/shard_map/ppermute | solution.py:993
  58.0 1.3 %back_conv.3.conv2_ref = f32[1024,128]{1,0:T(8,128)S(1)} custom-call(f32[1024,384]{1,0:T(8,128)S(1)} %bitcast.26, f32[49,1,384]{2,1,0:T(1,128)S(1)} %bitcast.17), custom_call_target="tpu_custom_call" | custom-call | flops 1724999936 | bytes 1048576 | tf_op jit(solution)/shard_map/back_conv/pallas_call | solution.py:137
  59.7 0.8 %collective-permute-done.16.refs_0_ = bf16[12,768]{1,0:T(8,128)(2,1)S(1)} collective-permute-done((bf16[12,768]{1,0:T(8,128)(2,1)S(1)}, bf16[12,768]{1,0:T(8,128)(2,1)S(1)}, u32[]{:S(2)}, u32[]{:S(2)}) %collective-permute-start.16) | collective-permute-done | bytes 18464 | tf_op jit(solution)/shard_map/ppermute | solution.py:993
  60.5 2.4 %collective-permute-start.17 = (bf16[12,768]{1,0:T(8,128)(2,1)S(1)}, bf16[12,768]{1,0:T(8,128)(2,1)S(1)}, u32[]{:S(2)}, u32[]{:S(2)}) collective-permute-start(bf16[12,768]{1,0:T(8,128)(2,1)S(1)} %relay.1), channel_id=1, source_target_pairs={{0,4},{1,5},{2,6},{3,7},{4,8},{5,9},{6,10},{7,11},{8,12},{9,13},{1... | collective-permute-start | bytes 55304 | tf_op jit(solution)/shard_map/ppermute | solution.py:998
  63.0 2.1 %finish_inner.1 = (f32[1024,384]{1,0:T(8,128)}, f32[6,32,384]{2,1,0:T(8,128)S(1)}) custom-call(s32[4,4]{1,0:T(4,128)S(1)} %copy-done.2, f32[1024,128]{1,0:T(8,128)S(1)} %get-tuple-element.124.conv0_ref, f32[1024,128]{1,0:T(8,128)S(1)} %get-tuple-element.125.conv1_ref, f32[1024,128]{1,0:T(8,128)S(1)} %back_conv.3.conv2_ref, f32[49,1,384]{2,1,0:T(1,128)S(1)} %bitcast.18, ...), custom_call_target="tpu_custom_call" | custom-call | flops 2529999872 | bytes 1048576 | tf_op jit(solution)/shard_map/finish_inner/pallas_call | solution.py:717
  65.1 1.5 %collective-permute-done.17.refs_1_ = bf16[12,768]{1,0:T(8,128)(2,1)S(1)} collective-permute-done((bf16[12,768]{1,0:T(8,128)(2,1)S(1)}, bf16[12,768]{1,0:T(8,128)(2,1)S(1)}, u32[]{:S(2)}, u32[]{:S(2)}) %collective-permute-start.17) | collective-permute-done | bytes 18464 | tf_op jit(solution)/shard_map/ppermute | solution.py:998
  66.6 1.5 %collective-permute-start.18 = (f32[6,768]{1,0:T(8,128)S(1)}, f32[6,768]{1,0:T(8,128)S(1)}, u32[]{:S(2)}, u32[]{:S(2)}) collective-permute-start(f32[6,768]{1,0:T(8,128)S(1)} %get-tuple-element.152), channel_id=1, source_target_pairs={{0,2},{1,3},{2,0},{3,1},{4,6},{5,7},{6,4},{7,5},{8,10},{9,11},{10,... | collective-permute-start | bytes 55304 | tf_op jit(solution)/shard_map/ppermute | solution.py:1003
  68.1 1.8 %finish_outer.1 = f32[1024,384]{1,0:T(8,128)} custom-call(s32[4,4]{1,0:T(4,128)S(1)} %copy-done.2, f32[1024,128]{1,0:T(8,128)S(1)} %get-tuple-element.124.conv0_ref, f32[1024,128]{1,0:T(8,128)S(1)} %get-tuple-element.125.conv1_ref, f32[1024,128]{1,0:T(8,128)S(1)} %back_conv.3.conv2_ref, f32[49,1,384]{2,1,0:T(1,128)S(1)} %bitcast.19, ...), custom_call_target="tpu_custom_call", output_to_operand_aliasing={{}: (9, {})} | custom-call | flops 1150000000 | bytes 1048576 | tf_op jit(solution)/shard_map/finish_outer/pallas_call | solution.py:754
  (48 shorter events, 3.3 us)
Async XLA Ops:
  0.6 4.2 %copy-start.1 = (f32[1,49,384]{2,0,1:T(1,128)S(1)}, f32[1,49,384]{2,0,1:T(1,128)}, u32[]{:S(2)}) copy-start(f32[1,49,384]{2,0,1:T(1,128)} %param.13) | copy-start | bytes 225796
  0.6 4.2 %copy-start.4 = (f32[1,32,32,384]{3,2,1,0:T(8,128)S(1)}, f32[1,32,32,384]{3,2,1,0:T(8,128)}, u32[]{:S(2)}) copy-start(f32[1,32,32,384]{3,2,1,0:T(8,128)} %param.10) | copy-start | bytes 4718596
  2.7 6.6 %collective-permute-start.1 = (bf16[3,32,384]{2,1,0:T(8,128)(2,1)}, bf16[3,32,384]{2,1,0:T(8,128)(2,1)S(1)}, u32[]{:S(2)}, u32[]{:S(2)}) collective-permute-start(bf16[3,32,384]{2,1,0:T(8,128)(2,1)} %get-tuple-element.80), channel_id=1, source_target_pairs={{0,15},{1,0},{2,1},{3,2},{4,3},{5,4},{6,5},{7,6},{8,7},{9,8},{10,9... | collective-permute-start | bytes 221192 | tf_op jit(solution)/shard_map/ppermute | solution.py:933
  3.8 5.5 %collective-permute-start = (bf16[3,32,384]{2,1,0:T(8,128)(2,1)}, bf16[3,32,384]{2,1,0:T(8,128)(2,1)S(1)}, u32[]{:S(2)}, u32[]{:S(2)}) collective-permute-start(bf16[3,32,384]{2,1,0:T(8,128)(2,1)} %get-tuple-element.81), channel_id=1, source_target_pairs={{0,1},{1,2},{2,3},{3,4},{4,5},{5,6},{6,7},{7,8},{8,9},{9,10},{10,1... | collective-permute-start | bytes 221192 | tf_op jit(solution)/shard_map/ppermute | solution.py:932
  4.8 2.1 %copy-start.5 = (bf16[1,1536,384]{2,1,0:T(8,128)(2,1)S(1)}, bf16[1,1536,384]{2,1,0:T(8,128)(2,1)}, u32[]{:S(2)}) copy-start(bf16[1,1536,384]{2,1,0:T(8,128)(2,1)} %param.17) | copy-start | bytes 3538948
  4.8 2.1 %copy-start.6 = (bf16[1,1536,384]{2,1,0:T(8,128)(2,1)S(1)}, bf16[1,1536,384]{2,1,0:T(8,128)(2,1)}, u32[]{:S(2)}) copy-start(bf16[1,1536,384]{2,1,0:T(8,128)(2,1)} %param.19) | copy-start | bytes 3538948
  4.8 2.1 %copy-start.7 = (f32[1,1536]{1,0:T(1,128)S(1)}, f32[1,1536]{1,0:T(1,128)}, u32[]{:S(2)}) copy-start(f32[1,1536]{1,0:T(1,128)} %bias_ref.2) | copy-start | bytes 18436
  7.0 1.6 %copy-start = (f32[1,32,32,384]{3,2,1,0:T(8,128)S(1)}, f32[1,32,32,384]{3,2,1,0:T(8,128)}, u32[]{:S(2)}) copy-start(f32[1,32,32,384]{3,2,1,0:T(8,128)} %param.11) | copy-start | bytes 4718596
  7.0 1.6 %copy-start.2 = (s32[4,4]{1,0:T(4,128)S(1)}, s32[4,4]{1,0:T(4,128)}, u32[]{:S(2)}) copy-start(s32[4,4]{1,0:T(4,128)} %counts_ref.5) | copy-start | bytes 196
  9.4 6.1 %collective-permute-start.3 = (bf16[3,48,384]{2,1,0:T(8,128)(2,1)S(1)}, bf16[3,48,384]{2,1,0:T(8,128)(2,1)S(1)}, u32[]{:S(2)}, u32[]{:S(2)}) collective-permute-start(bf16[3,48,384]{2,1,0:T(8,128)(2,1)S(1)} %get-tuple-element.89), channel_id=1, source_target_pairs={{0,112},{16,0},{32,16},{48,32},{64,48},{80,64},{96,80},{112,96},{1... | collective-permute-start | bytes 331784 | tf_op jit(solution)/shard_map/ppermute | solution.py:939
  11.3 5.4 %copy-start.3 = (f32[1,384]{1,0:T(1,128)S(1)}, f32[1,384]{1,0:T(1,128)}, u32[]{:S(2)}) copy-start(f32[1,384]{1,0:T(1,128)} %gain_ref.3) | copy-start | bytes 4612
  11.3 5.4 %copy-start.8 = (f32[1,384]{1,0:T(1,128)S(1)}, f32[1,384]{1,0:T(1,128)}, u32[]{:S(2)}) copy-start(f32[1,384]{1,0:T(1,128)} %bias_ref.3) | copy-start | bytes 4612
  11.3 5.4 %copy-start.9 = (f32[1,384]{1,0:T(1,128)S(1)}, f32[1,384]{1,0:T(1,128)}, u32[]{:S(2)}) copy-start(f32[1,384]{1,0:T(1,128)} %shift_ref.1) | copy-start | bytes 4612
  11.3 5.4 %collective-permute-start.2 = (bf16[3,48,384]{2,1,0:T(8,128)(2,1)S(1)}, bf16[3,48,384]{2,1,0:T(8,128)(2,1)S(1)}, u32[]{:S(2)}, u32[]{:S(2)}) collective-permute-start(bf16[3,48,384]{2,1,0:T(8,128)(2,1)S(1)} %get-tuple-element.90), channel_id=1, source_target_pairs={{0,16},{16,32},{32,48},{48,64},{64,80},{80,96},{96,112},{112,0},{1... | collective-permute-start | bytes 331784 | tf_op jit(solution)/shard_map/ppermute | solution.py:938
  23.3 3.1 %collective-permute-start.4 = (bf16[768,768]{1,0:T(8,128)(2,1)S(1)}, bf16[768,768]{1,0:T(8,128)(2,1)S(1)}, u32[]{:S(2)}, u32[]{:S(2)}) collective-permute-start(bf16[768,768]{1,0:T(8,128)(2,1)S(1)} %get-tuple-element.99), channel_id=1, source_target_pairs={{0,16},{16,0},{32,48},{48,32},{64,80},{80,64},{96,112},{112,96},{1... | collective-permute-start | bytes 3538952 | tf_op jit(solution)/shard_map/ppermute | solution.py:972
  26.5 8.0 %collective-permute-start.5 = (bf16[192,768]{1,0:T(8,128)(2,1)S(1)}, bf16[192,768]{1,0:T(8,128)(2,1)S(1)}, u32[]{:S(2)}, u32[]{:S(2)}) collective-permute-start(bf16[192,768]{1,0:T(8,128)(2,1)S(1)} %get-tuple-element.100), channel_id=1, source_target_pairs={{0,32},{1,33},{2,34},{3,35},{4,36},{5,37},{6,38},{7,39},{8,40},{9,... | collective-permute-start | bytes 884744 | tf_op jit(solution)/shard_map/ppermute | solution.py:975
  26.6 13.9 %collective-permute-start.6 = (bf16[192,768]{1,0:T(8,128)(2,1)S(1)}, bf16[192,768]{1,0:T(8,128)(2,1)S(1)}, u32[]{:S(2)}, u32[]{:S(2)}) collective-permute-start(bf16[192,768]{1,0:T(8,128)(2,1)S(1)} %get-tuple-element.102), channel_id=1, source_target_pairs={{0,64},{1,65},{2,66},{3,67},{4,68},{5,69},{6,70},{7,71},{8,72},{9,... | collective-permute-start | bytes 884744 | tf_op jit(solution)/shard_map/ppermute | solution.py:976
  32.5 8.0 %collective-permute-start.7 = (bf16[192,768]{1,0:T(8,128)(2,1)S(1)}, bf16[192,768]{1,0:T(8,128)(2,1)S(1)}, u32[]{:S(2)}, u32[]{:S(2)}) collective-permute-start(bf16[192,768]{1,0:T(8,128)(2,1)S(1)} %get-tuple-element.104), channel_id=1, source_target_pairs={{0,96},{1,97},{2,98},{3,99},{4,100},{5,101},{6,102},{7,103},{8,104... | collective-permute-start | bytes 884744 | tf_op jit(solution)/shard_map/ppermute | solution.py:978
  36.6 12.1 %collective-permute-start.9 = (bf16[3,32,384]{2,1,0:T(8,128)(2,1)S(1)}, bf16[3,32,384]{2,1,0:T(8,128)(2,1)S(1)}, u32[]{:S(2)}, u32[]{:S(2)}) collective-permute-start(bf16[3,32,384]{2,1,0:T(8,128)(2,1)S(1)} %get-tuple-element.114), channel_id=1, source_target_pairs={{0,15},{1,0},{2,1},{3,2},{4,3},{5,4},{6,5},{7,6},{8,7},{9,8},{10,9... | collective-permute-start | bytes 221192 | tf_op jit(solution)/shard_map/ppermute | solution.py:933
  40.5 8.8 %collective-permute-start.8 = (bf16[3,32,384]{2,1,0:T(8,128)(2,1)S(1)}, bf16[3,32,384]{2,1,0:T(8,128)(2,1)S(1)}, u32[]{:S(2)}, u32[]{:S(2)}) collective-permute-start(bf16[3,32,384]{2,1,0:T(8,128)(2,1)S(1)} %get-tuple-element.115), channel_id=1, source_target_pairs={{0,1},{1,2},{2,3},{3,4},{4,5},{5,6},{6,7},{7,8},{8,9},{9,10},{10,1... | collective-permute-start | bytes 221192 | tf_op jit(solution)/shard_map/ppermute | solution.py:932
  40.7 8.1 %collective-permute-start.11 = (bf16[48,768]{1,0:T(8,128)(2,1)S(1)}, bf16[48,768]{1,0:T(8,128)(2,1)S(1)}, u32[]{:S(2)}, u32[]{:S(2)}) collective-permute-start(bf16[48,768]{1,0:T(8,128)(2,1)S(1)} %get-tuple-element.120), channel_id=1, source_target_pairs={{0,1},{1,128},{2,3},{3,130},{4,5},{5,132},{6,7},{7,134},{8,9},{9,1... | collective-permute-start | bytes 221192 | tf_op jit(solution)/shard_map/ppermute | solution.py:986
  42.2 6.5 %collective-permute-start.10 = (bf16[48,768]{1,0:T(8,128)(2,1)S(1)}, bf16[48,768]{1,0:T(8,128)(2,1)S(1)}, u32[]{:S(2)}, u32[]{:S(2)}) collective-permute-start(bf16[48,768]{1,0:T(8,128)(2,1)S(1)} %get-tuple-element.121), channel_id=1, source_target_pairs={{0,128},{1,129},{2,130},{3,131},{4,132},{5,133},{6,134},{7,135},{8... | collective-permute-start | bytes 221192 | tf_op jit(solution)/shard_map/ppermute | solution.py:986
  45.0 4.4 %collective-permute-start.12 = (bf16[48,768]{1,0:T(8,128)(2,1)S(1)}, bf16[48,768]{1,0:T(8,128)(2,1)S(1)}, u32[]{:S(2)}, u32[]{:S(2)}) collective-permute-start(bf16[48,768]{1,0:T(8,128)(2,1)S(1)} %get-tuple-element.122), channel_id=1, source_target_pairs={{0,129},{1,0},{2,131},{3,2},{4,133},{5,4},{6,135},{7,6},{8,137},{9... | collective-permute-start | bytes 221192 | tf_op jit(solution)/shard_map/ppermute | solution.py:986
  49.4 8.6 %collective-permute-start.14 = (bf16[3,48,384]{2,1,0:T(8,128)(2,1)S(1)}, bf16[3,48,384]{2,1,0:T(8,128)(2,1)S(1)}, u32[]{:S(2)}, u32[]{:S(2)}) collective-permute-start(bf16[3,48,384]{2,1,0:T(8,128)(2,1)S(1)} %get-tuple-element.133), channel_id=1, source_target_pairs={{0,112},{16,0},{32,16},{48,32},{64,48},{80,64},{96,80},{112,96},{1... | collective-permute-start | bytes 331784 | tf_op jit(solution)/shard_map/ppermute | solution.py:939
  52.2 5.8 %collective-permute-start.13 = (bf16[3,48,384]{2,1,0:T(8,128)(2,1)S(1)}, bf16[3,48,384]{2,1,0:T(8,128)(2,1)S(1)}, u32[]{:S(2)}, u32[]{:S(2)}) collective-permute-start(bf16[3,48,384]{2,1,0:T(8,128)(2,1)S(1)} %get-tuple-element.134), channel_id=1, source_target_pairs={{0,16},{16,32},{32,48},{48,64},{64,80},{80,96},{96,112},{112,0},{1... | collective-permute-start | bytes 331784 | tf_op jit(solution)/shard_map/ppermute | solution.py:938
  52.3 7.5 %collective-permute-start.15 = (bf16[12,768]{1,0:T(8,128)(2,1)S(1)}, bf16[12,768]{1,0:T(8,128)(2,1)S(1)}, u32[]{:S(2)}, u32[]{:S(2)}) collective-permute-start(bf16[12,768]{1,0:T(8,128)(2,1)S(1)} %get-tuple-element.139), channel_id=1, source_target_pairs={{0,4},{1,5},{2,6},{3,7},{4,8},{5,9},{6,10},{7,11},{8,12},{9,13},{1... | collective-permute-start | bytes 55304 | tf_op jit(solution)/shard_map/ppermute | solution.py:992
  55.8 4.7 %collective-permute-start.16 = (bf16[12,768]{1,0:T(8,128)(2,1)S(1)}, bf16[12,768]{1,0:T(8,128)(2,1)S(1)}, u32[]{:S(2)}, u32[]{:S(2)}) collective-permute-start(bf16[12,768]{1,0:T(8,128)(2,1)S(1)} %get-tuple-element.140), channel_id=1, source_target_pairs={{0,12},{1,13},{2,14},{3,15},{4,0},{5,1},{6,2},{7,3},{8,4},{9,5},{1... | collective-permute-start | bytes 55304 | tf_op jit(solution)/shard_map/ppermute | solution.py:993
  60.5 6.0 %collective-permute-start.17 = (bf16[12,768]{1,0:T(8,128)(2,1)S(1)}, bf16[12,768]{1,0:T(8,128)(2,1)S(1)}, u32[]{:S(2)}, u32[]{:S(2)}) collective-permute-start(bf16[12,768]{1,0:T(8,128)(2,1)S(1)} %relay.1), channel_id=1, source_target_pairs={{0,4},{1,5},{2,6},{3,7},{4,8},{5,9},{6,10},{7,11},{8,12},{9,13},{1... | collective-permute-start | bytes 55304 | tf_op jit(solution)/shard_map/ppermute | solution.py:998
  66.6 3.9 %collective-permute-start.18 = (f32[6,768]{1,0:T(8,128)S(1)}, f32[6,768]{1,0:T(8,128)S(1)}, u32[]{:S(2)}, u32[]{:S(2)}) collective-permute-start(f32[6,768]{1,0:T(8,128)S(1)} %get-tuple-element.152), channel_id=1, source_target_pairs={{0,2},{1,3},{2,0},{3,1},{4,6},{5,7},{6,4},{7,5},{8,10},{9,11},{10,... | collective-permute-start | bytes 55304 | tf_op jit(solution)/shard_map/ppermute | solution.py:1003

commit v14 on v12

--- a/solution.py
+++ b/solution.py
@@ -928,9 +928,9 @@
 
     first, last = side_cols(cells)
     left, right = lon_halo(first, last)
-    conv = inner_conv(cells, kernel, (0,))
     grad, w_expand, w_reduce = after((grad, w_expand, w_reduce), first, last)
     rows = mask_rows(counts, grad)
+    conv = inner_conv(after(cells, rows), kernel, (0,))
     expand, reduce, expand_t, bias = arrange(w_expand[0], w_reduce[0], b_expand)
     left, right = after((left, right), rows, bias, conv)
     up, down = side_rows(cells, left, right)
@@ -956,13 +956,13 @@
     left, right = lon_halo(first, last)
     own, parts = after((own, (part_one, part_two, part_three)), first, last)
     own, *sent = split_four(own, parts)
-    parts = [lax.ppermute(sent[i], every_axis, plane_pairs(i + 1, False)) for i in (0, 2, 1)]
+    parts = [lax.ppermute(sent[i], every_axis, plane_pairs(i + 1, False)) for i in (1, 0, 2)]
     back = back_conv(after(conv_grad, sent), kernel, (0, 1))
     (conv_grad, left, right), parts = after(((conv_grad, left, right), parts), back)
     up, down = side_rows(conv_grad, left, right)
 
     own, *sent = split_ring(*after((own, parts), up, down))
-    parts = [lax.ppermute(sent[i], every_axis, ring_pairs(i + 1)) for i in (0, 2, 1)]
+    parts = [lax.ppermute(sent[i], every_axis, ring_pairs(i + 1)) for i in (1, 0, 2)]
     top, bottom = lat_halo(up, down)
     back += back_conv(after(conv_grad, sent, top, bottom), kernel, (2,))
 

time: 70.3 us -> 70 us (level)
    unnamed x24 -> x22, local copies, waits for them, and re-layouts: 2.33 us -> 2.15 us
where the time goes in v14:
time: 70 us; the launch traced here: 69.9 us
  Pallas kernels  31.6 us (45%)
  starting transfers between devices  28.4 us (41%)
  waiting for transfers between devices  6.78 us (10%)
  local copies, waits for them, and re-layouts  2.15 us (3%)
  between operations  0.9 us (1%)
    ppermute x3, starting transfers between devices, local(): lax.ppermute(sent[i], every_axis, ring_pairs(i + 1))  9.14 us
    pallas_call x2, Pallas kernels, inner_conv(): pl.pallas_call(functools.partial(inner_conv_body, parts), out_shape=(shap...  6.22 us
    ppermute x3, starting transfers between devices, local(): lax.ppermute(sent[i], every_axis, plane_pairs(i + 1, False))  5.45 us
    pallas_call x1, Pallas kernels, hidden_far(): pl.pallas_call(far_body, out_shape=(jax.ShapeDtypeStruct((half, 2 * chann...  4.68 us
    ppermute x2, starting transfers between devices, lon_halo(): right = lax.ppermute(first, 'lon', shifted('lon', -1))  4.11 us
    pallas_call x2, Pallas kernels, back_conv(): pl.pallas_call(functools.partial(back_conv_body, parts), out_shape=(shape...  4 us
    ppermute x2, starting transfers between devices, lat_halo(): bottom = lax.ppermute(up, 'lat', shifted('lat', -1))  3.79 us
    ppermute x1, starting transfers between devices, local(): part_two = lax.ppermute(two, every_axis, plane_pairs(2, True))  3.32 us
  transfers between devices with their start and end apart: 19, of which 6 were waited for; matrix products, arithmetic and copies ran while one was open for 0% of the time, Pallas kernels for 34%

profile of v14, /device:TPU:32, one launch (start us, length us, event | category | flops | bytes accessed | tf_op | source)
XLA Modules:
  0.0 69.9 jit_solution(17321529745574399398)
XLA Ops:
  0.6 1.4 %copy-done = f32[1,32,32,384]{3,2,1,0:T(8,128)S(1)} copy-done((f32[1,32,32,384]{3,2,1,0:T(8,128)S(1)}, f32[1,32,32,384]{3,2,1,0:T(8,128)}, u32[]{:S(2)}) %copy-start) | copy-done | bytes 1572888
  2.3 1.1 %collective-permute-start.1 = (bf16[3,32,384]{2,1,0:T(8,128)(2,1)S(1)}, bf16[3,32,384]{2,1,0:T(8,128)(2,1)S(1)}, u32[]{:S(2)}, u32[]{:S(2)}) collective-permute-start(bf16[3,32,384]{2,1,0:T(8,128)(2,1)S(1)} %get-tuple-element.79), channel_id=1, source_target_pairs={{0,15},{1,0},{2,1},{3,2},{4,3},{5,4},{6,5},{7,6},{8,7},{9,8},{10,9... | collective-permute-start | bytes 221192 | tf_op jit(solution)/shard_map/ppermute | solution.py:906
  3.5 1.0 %collective-permute-start = (bf16[3,32,384]{2,1,0:T(8,128)(2,1)S(1)}, bf16[3,32,384]{2,1,0:T(8,128)(2,1)S(1)}, u32[]{:S(2)}, u32[]{:S(2)}) collective-permute-start(bf16[3,32,384]{2,1,0:T(8,128)(2,1)S(1)} %get-tuple-element.80), channel_id=1, source_target_pairs={{0,1},{1,2},{2,3},{3,4},{4,5},{5,6},{6,7},{7,8},{8,9},{9,10},{10,1... | collective-permute-start | bytes 221192 | tf_op jit(solution)/shard_map/ppermute | solution.py:905
  4.5 0.7 mask_rows.1.refs_1_
  5.1 0.7 %copy-done.1 = f32[1,32,32,384]{3,2,1,0:T(8,128)S(1)} copy-done((f32[1,32,32,384]{3,2,1,0:T(8,128)S(1)}, f32[1,32,32,384]{3,2,1,0:T(8,128)}, u32[]{:S(2)}) %copy-start.1) | copy-done | bytes 1572888
  5.9 2.1 %inner_conv.2.conv0_ref = f32[1024,128]{1,0:T(8,128)S(1)} custom-call(f32[1024,384]{1,0:T(8,128)S(1)} %bitcast.11, f32[49,1,384]{2,1,0:T(1,128)S(1)} %bitcast.17), custom_call_target="tpu_custom_call" | custom-call | flops 2529999872 | bytes 1048576 | tf_op jit(solution)/shard_map/inner_conv/pallas_call | solution.py:87
  8.0 1.6 %arrange.1 = (bf16[1536,384]{1,0:T(8,128)(2,1)S(1)}, bf16[1536,384]{1,0:T(8,128)(2,1)S(1)}, bf16[384,1536]{1,0:T(8,128)(2,1)S(1)}, f32[1536,128]{1,0:T(8,128)S(1)}) custom-call(bf16[1536,384]{1,0:T(8,128)(2,1)S(1)} %bitcast.27, bf16[1536,384]{1,0:T(8,128)(2,1)S(1)} %bitcast.28, f32[1,1536]{1,0:T(1,128)S(1)} %copy-done.8), custom_call_target="tpu_custom_call" | custom-call | flops 1724999936 | bytes 1048576 | tf_op jit(solution)/shard_map/arrange/pallas_call | solution.py:406
  9.7 1.9 %collective-permute-start.3 = (bf16[3,48,384]{2,1,0:T(8,128)(2,1)S(1)}, bf16[3,48,384]{2,1,0:T(8,128)(2,1)S(1)}, u32[]{:S(2)}, u32[]{:S(2)}) collective-permute-start(bf16[3,48,384]{2,1,0:T(8,128)(2,1)S(1)} %get-tuple-element.89), channel_id=1, source_target_pairs={{0,112},{16,0},{32,16},{48,32},{64,48},{80,64},{96,80},{112,96},{1... | collective-permute-start | bytes 331784 | tf_op jit(solution)/shard_map/ppermute | solution.py:912
  11.6 4.1 %inner_conv.3 = (f32[1024,128]{1,0:T(8,128)S(1)}, f32[1024,128]{1,0:T(8,128)S(1)}) custom-call(f32[1024,384]{1,0:T(8,128)S(1)} %bitcast.13, f32[49,1,384]{2,1,0:T(1,128)S(1)} %bitcast.18), custom_call_target="tpu_custom_call" | custom-call | flops 5059999744 | bytes 1048576 | tf_op jit(solution)/shard_map/inner_conv/pallas_call | solution.py:87
  15.7 1.2 %collective-permute-done.2.top_ref = bf16[3,48,384]{2,1,0:T(8,128)(2,1)S(1)} collective-permute-done((bf16[3,48,384]{2,1,0:T(8,128)(2,1)S(1)}, bf16[3,48,384]{2,1,0:T(8,128)(2,1)S(1)}, u32[]{:S(2)}, u32[]{:S(2)}) %collective-permute-start.2) | collective-permute-done | bytes 110624 | tf_op jit(solution)/shard_map/ppermute | solution.py:911
  17.0 1.9 %normalise.1 = (f32[1024,384]{1,0:T(8,128)S(1)}, f32[1024,128]{1,0:T(8,128)S(1)}, bf16[1024,384]{1,0:T(8,128)(2,1)S(1)}) custom-call(f32[1024,128]{1,0:T(8,128)S(1)} %inner_conv.2.conv0_ref, f32[1024,128]{1,0:T(8,128)S(1)} %get-tuple-element.92.conv1_ref, f32[1024,128]{1,0:T(8,128)S(1)} %get-tuple-element.93.conv2_ref, f32[49,1,384]{2,1,0:T(1,128)S(1)} %bitcast.19, ...), custom_call_target="tpu_custom_call" | custom-call | flops 3220000000 | bytes 1048576 | tf_op jit(solution)/shard_map/normalise/pallas_call | solution.py:315
  18.9 4.7 %hidden_far.1 = (bf16[768,768]{1,0:T(8,128)(2,1)S(1)}, bf16[768,1024]{1,0:T(8,128)(2,1)S(1)}) custom-call(bf16[1024,384]{1,0:T(8,128)(2,1)S(1)} %get-tuple-element.94.refs_0_, bf16[1024,384]{1,0:T(8,128)(2,1)S(1)} %mask_rows.1.refs_1_, bf16[1536,384]{1,0:T(8,128)(2,1)S(1)} %get-tuple-element.95.refs_2_, bf16[1536,384]{1,0:T(8,128)(2,1)S(1)} %get-tuple-element.96.refs_3_, ...), custom_call_target="tpu_custom_call" | custom-call | flops 5750000128 | bytes 1048576 | tf_op jit(solution)/shard_map/hidden_far/pallas_call | solution.py:531
  23.9 2.5 %near_first.1 = (f32[384,768]{1,0:T(8,128)S(1)}, bf16[768,1024]{1,0:T(8,128)(2,1)S(1)}) custom-call(bf16[1024,384]{1,0:T(8,128)(2,1)S(1)} %get-tuple-element.94.refs_0_, bf16[1024,384]{1,0:T(8,128)(2,1)S(1)} %mask_rows.1.refs_1_, bf16[1536,384]{1,0:T(8,128)(2,1)S(1)} %get-tuple-element.95.refs_2_, bf16[1536,384]{1,0:T(8,128)(2,1)S(1)} %get-tuple-element.96.refs_3_, ...), custom_call_target="tpu_custom_call" | custom-call | flops 3449999872 | bytes 1048576 | tf_op jit(solution)/shard_map/near_first/pallas_call | solution.py:564
  26.9 3.3 %collective-permute-start.6 = (bf16[192,768]{1,0:T(8,128)(2,1)S(1)}, bf16[192,768]{1,0:T(8,128)(2,1)S(1)}, u32[]{:S(2)}, u32[]{:S(2)}) collective-permute-start(bf16[192,768]{1,0:T(8,128)(2,1)S(1)} %get-tuple-element.102), channel_id=1, source_target_pairs={{0,64},{1,65},{2,66},{3,67},{4,68},{5,69},{6,70},{7,71},{8,72},{9,... | collective-permute-start | bytes 884744 | tf_op jit(solution)/shard_map/ppermute | solution.py:949
  30.2 2.6 %near_last.1 = (f32[192,768]{1,0:T(8,128)S(1)}, bf16[192,768]{1,0:T(8,128)(2,1)S(1)}, bf16[768,1024]{1,0:T(8,128)(2,1)S(1)}) custom-call(bf16[1024,384]{1,0:T(8,128)(2,1)S(1)} %get-tuple-element.94.refs_0_, bf16[1024,384]{1,0:T(8,128)(2,1)S(1)} %mask_rows.1.refs_1_, ...), custom_call_target="tpu_custom_call", output_to_operand_aliasing={{2}: (6, {})} | custom-call | flops 3449999872 | bytes 1048576 | tf_op jit(solution)/shard_map/near_last/pallas_call | solution.py:625
  32.8 0.7 collective-permute-start.7
  33.5 1.3 %collective-permute-done.5.first_ref = bf16[192,768]{1,0:T(8,128)(2,1)S(1)} collective-permute-done((bf16[192,768]{1,0:T(8,128)(2,1)S(1)}, bf16[192,768]{1,0:T(8,128)(2,1)S(1)}, u32[]{:S(2)}, u32[]{:S(2)}) %collective-permute-start.5) | collective-permute-done | bytes 294944 | tf_op jit(solution)/shard_map/ppermute | solution.py:948
  34.8 2.1 %norm_back.1 = (f32[32,32,384]{2,1,0:T(8,128)S(1)}, bf16[3,32,384]{2,1,0:T(8,128)(2,1)S(1)}, bf16[3,32,384]{2,1,0:T(8,128)(2,1)S(1)}) custom-call(bf16[384,1536]{1,0:T(8,128)(2,1)S(1)} %get-tuple-element.83.turned_ref, bf16[768,1024]{1,0:T(8,128)(2,1)S(1)} %get-tuple-element.105.other_ref, bf16[768,1024]{1,0:T(8,128)(2,1)S(1)} %get-tuple-element.106.mine_ref, ...), custom_call_target="tpu_custom_call" | custom-call | flops 230000000 | bytes 1048576 | tf_op jit(solution)/shard_map/norm_back/pallas_call | solution.py:673
  37.0 3.0 %collective-permute-start.9 = (bf16[3,32,384]{2,1,0:T(8,128)(2,1)S(1)}, bf16[3,32,384]{2,1,0:T(8,128)(2,1)S(1)}, u32[]{:S(2)}, u32[]{:S(2)}) collective-permute-start(bf16[3,32,384]{2,1,0:T(8,128)(2,1)S(1)} %get-tuple-element.114), channel_id=1, source_target_pairs={{0,15},{1,0},{2,1},{3,2},{4,3},{5,4},{6,5},{7,6},{8,7},{9,8},{10,9... | collective-permute-start | bytes 221192 | tf_op jit(solution)/shard_map/ppermute | solution.py:906
  40.6 1.9 %collective-permute-start.11 = (bf16[48,768]{1,0:T(8,128)(2,1)S(1)}, bf16[48,768]{1,0:T(8,128)(2,1)S(1)}, u32[]{:S(2)}, u32[]{:S(2)}) collective-permute-start(bf16[48,768]{1,0:T(8,128)(2,1)S(1)} %get-tuple-element.120), channel_id=1, source_target_pairs={{0,1},{1,128},{2,3},{3,130},{4,5},{5,132},{6,7},{7,134},{8,9},{9,1... | collective-permute-start | bytes 221192 | tf_op jit(solution)/shard_map/ppermute | solution.py:959
  42.6 2.7 %collective-permute-start.10 = (bf16[48,768]{1,0:T(8,128)(2,1)S(1)}, bf16[48,768]{1,0:T(8,128)(2,1)S(1)}, u32[]{:S(2)}, u32[]{:S(2)}) collective-permute-start(bf16[48,768]{1,0:T(8,128)(2,1)S(1)} %get-tuple-element.121), channel_id=1, source_target_pairs={{0,128},{1,129},{2,130},{3,131},{4,132},{5,133},{6,134},{7,135},{8... | collective-permute-start | bytes 221192 | tf_op jit(solution)/shard_map/ppermute | solution.py:959
  45.3 0.8 %collective-permute-start.12 = (bf16[48,768]{1,0:T(8,128)(2,1)S(1)}, bf16[48,768]{1,0:T(8,128)(2,1)S(1)}, u32[]{:S(2)}, u32[]{:S(2)}) collective-permute-start(bf16[48,768]{1,0:T(8,128)(2,1)S(1)} %get-tuple-element.122), channel_id=1, source_target_pairs={{0,129},{1,0},{2,131},{3,2},{4,133},{5,4},{6,135},{7,6},{8,137},{9... | collective-permute-start | bytes 221192 | tf_op jit(solution)/shard_map/ppermute | solution.py:959
  46.1 2.7 %back_conv.2 = (f32[1024,128]{1,0:T(8,128)S(1)}, f32[1024,128]{1,0:T(8,128)S(1)}) custom-call(f32[1024,384]{1,0:T(8,128)S(1)} %bitcast.24, f32[49,1,384]{2,1,0:T(1,128)S(1)} %bitcast.20), custom_call_target="tpu_custom_call" | custom-call | flops 3449999872 | bytes 1048576 | tf_op jit(solution)/shard_map/back_conv/pallas_call | solution.py:137
  48.8 0.9 %collective-permute-done.12.third_ref = bf16[48,768]{1,0:T(8,128)(2,1)S(1)} collective-permute-done((bf16[48,768]{1,0:T(8,128)(2,1)S(1)}, bf16[48,768]{1,0:T(8,128)(2,1)S(1)}, u32[]{:S(2)}, u32[]{:S(2)}) %collective-permute-start.12) | collective-permute-done | bytes 73760 | tf_op jit(solution)/shard_map/ppermute | solution.py:959
  49.7 1.9 %collective-permute-start.14 = (bf16[3,48,384]{2,1,0:T(8,128)(2,1)S(1)}, bf16[3,48,384]{2,1,0:T(8,128)(2,1)S(1)}, u32[]{:S(2)}, u32[]{:S(2)}) collective-permute-start(bf16[3,48,384]{2,1,0:T(8,128)(2,1)S(1)} %get-tuple-element.133), channel_id=1, source_target_pairs={{0,112},{16,0},{32,16},{48,32},{64,48},{80,64},{96,80},{112,96},{1... | collective-permute-start | bytes 331784 | tf_op jit(solution)/shard_map/ppermute | solution.py:912
  51.7 4.4 %collective-permute-start.16 = (bf16[12,768]{1,0:T(8,128)(2,1)S(1)}, bf16[12,768]{1,0:T(8,128)(2,1)S(1)}, u32[]{:S(2)}, u32[]{:S(2)}) collective-permute-start(bf16[12,768]{1,0:T(8,128)(2,1)S(1)} %get-tuple-element.139), channel_id=1, source_target_pairs={{0,4},{1,5},{2,6},{3,7},{4,8},{5,9},{6,10},{7,11},{8,12},{9,13},{1... | collective-permute-start | bytes 55304 | tf_op jit(solution)/shard_map/ppermute | solution.py:965
  56.1 4.5 %collective-permute-start.15 = (bf16[12,768]{1,0:T(8,128)(2,1)S(1)}, bf16[12,768]{1,0:T(8,128)(2,1)S(1)}, u32[]{:S(2)}, u32[]{:S(2)}) collective-permute-start(bf16[12,768]{1,0:T(8,128)(2,1)S(1)} %get-tuple-element.140), channel_id=1, source_target_pairs={{0,8},{1,9},{2,10},{3,11},{4,12},{5,13},{6,14},{7,15},{8,0},{9,1},... | collective-permute-start | bytes 55304 | tf_op jit(solution)/shard_map/ppermute | solution.py:965
  60.9 1.3 %back_conv.3.conv2_ref = f32[1024,128]{1,0:T(8,128)S(1)} custom-call(f32[1024,384]{1,0:T(8,128)S(1)} %bitcast.26, f32[49,1,384]{2,1,0:T(1,128)S(1)} %bitcast.21), custom_call_target="tpu_custom_call" | custom-call | flops 1724999936 | bytes 1048576 | tf_op jit(solution)/shard_map/back_conv/pallas_call | solution.py:137
  62.2 2.1 %finish_inner.1 = (f32[1024,384]{1,0:T(8,128)}, f32[6,32,384]{2,1,0:T(8,128)S(1)}) custom-call(s32[4,4]{1,0:T(4,128)S(1)} %copy-done.4, f32[1024,128]{1,0:T(8,128)S(1)} %get-tuple-element.124.conv0_ref, f32[1024,128]{1,0:T(8,128)S(1)} %get-tuple-element.125.conv1_ref, f32[1024,128]{1,0:T(8,128)S(1)} %back_conv.3.conv2_ref, f32[49,1,384]{2,1,0:T(1,128)S(1)} %bitcast.22, ...), custom_call_target="tpu_custom_call" | custom-call | flops 2529999872 | bytes 1048576 | tf_op jit(solution)/shard_map/finish_inner/pallas_call | solution.py:707
  64.3 1.0 %collective-permute-done.17.refs_2_ = bf16[12,768]{1,0:T(8,128)(2,1)S(1)} collective-permute-done((bf16[12,768]{1,0:T(8,128)(2,1)S(1)}, bf16[12,768]{1,0:T(8,128)(2,1)S(1)}, u32[]{:S(2)}, u32[]{:S(2)}) %collective-permute-start.17) | collective-permute-done | bytes 18464 | tf_op jit(solution)/shard_map/ppermute | solution.py:965
  65.5 1.8 %finish_outer.1 = f32[1024,384]{1,0:T(8,128)} custom-call(s32[4,4]{1,0:T(4,128)S(1)} %copy-done.4, f32[1024,128]{1,0:T(8,128)S(1)} %get-tuple-element.124.conv0_ref, f32[1024,128]{1,0:T(8,128)S(1)} %get-tuple-element.125.conv1_ref, f32[1024,128]{1,0:T(8,128)S(1)} %back_conv.3.conv2_ref, f32[49,1,384]{2,1,0:T(1,128)S(1)} %bitcast.23, ...), custom_call_target="tpu_custom_call", output_to_operand_aliasing={{}: (9, {})} | custom-call | flops 1150000000 | bytes 1048576 | tf_op jit(solution)/shard_map/finish_outer/pallas_call | solution.py:744
  67.3 2.0 %collective-permute-done.18.arrived_ref = f32[6,768]{1,0:T(8,128)S(1)} collective-permute-done((f32[6,768]{1,0:T(8,128)S(1)}, f32[6,768]{1,0:T(8,128)S(1)}, u32[]{:S(2)}, u32[]{:S(2)}) %collective-permute-start.18) | collective-permute-done | bytes 18464 | tf_op jit(solution)/shard_map/ppermute | solution.py:972
  (49 shorter events, 3.0 us)
Async XLA Ops:
  0.6 1.4 %copy-start = (f32[1,32,32,384]{3,2,1,0:T(8,128)S(1)}, f32[1,32,32,384]{3,2,1,0:T(8,128)}, u32[]{:S(2)}) copy-start(f32[1,32,32,384]{3,2,1,0:T(8,128)} %param.10) | copy-start | bytes 4718596
  2.0 2.4 %copy-start.2 = (f32[1,32,32,384]{3,2,1,0:T(8,128)S(1)}, f32[1,32,32,384]{3,2,1,0:T(8,128)}, u32[]{:S(2)}) copy-start(f32[1,32,32,384]{3,2,1,0:T(8,128)} %param.11) | copy-start | bytes 4718596
  2.0 2.4 %copy-start.4 = (s32[4,4]{1,0:T(4,128)S(1)}, s32[4,4]{1,0:T(4,128)}, u32[]{:S(2)}) copy-start(s32[4,4]{1,0:T(4,128)} %counts_ref.5) | copy-start | bytes 196
  2.3 7.2 %collective-permute-start.1 = (bf16[3,32,384]{2,1,0:T(8,128)(2,1)S(1)}, bf16[3,32,384]{2,1,0:T(8,128)(2,1)S(1)}, u32[]{:S(2)}, u32[]{:S(2)}) collective-permute-start(bf16[3,32,384]{2,1,0:T(8,128)(2,1)S(1)} %get-tuple-element.79), channel_id=1, source_target_pairs={{0,15},{1,0},{2,1},{3,2},{4,3},{5,4},{6,5},{7,6},{8,7},{9,8},{10,9... | collective-permute-start | bytes 221192 | tf_op jit(solution)/shard_map/ppermute | solution.py:906
  3.5 6.1 %collective-permute-start = (bf16[3,32,384]{2,1,0:T(8,128)(2,1)S(1)}, bf16[3,32,384]{2,1,0:T(8,128)(2,1)S(1)}, u32[]{:S(2)}, u32[]{:S(2)}) collective-permute-start(bf16[3,32,384]{2,1,0:T(8,128)(2,1)S(1)} %get-tuple-element.80), channel_id=1, source_target_pairs={{0,1},{1,2},{2,3},{3,4},{4,5},{5,6},{6,7},{7,8},{8,9},{9,10},{10,1... | collective-permute-start | bytes 221192 | tf_op jit(solution)/shard_map/ppermute | solution.py:905
  4.5 1.4 %copy-start.1 = (f32[1,32,32,384]{3,2,1,0:T(8,128)S(1)}, f32[1,32,32,384]{3,2,1,0:T(8,128)}, u32[]{:S(2)}) copy-start(f32[1,32,32,384]{3,2,1,0:T(8,128)} %param.10) | copy-start | bytes 4718596
  4.5 1.4 %copy-start.3 = (f32[1,49,384]{2,0,1:T(1,128)S(1)}, f32[1,49,384]{2,0,1:T(1,128)}, u32[]{:S(2)}) copy-start(f32[1,49,384]{2,0,1:T(1,128)} %param.13) | copy-start | bytes 225796
  5.9 2.1 %copy-start.6 = (bf16[1,1536,384]{2,1,0:T(8,128)(2,1)S(1)}, bf16[1,1536,384]{2,1,0:T(8,128)(2,1)}, u32[]{:S(2)}) copy-start(bf16[1,1536,384]{2,1,0:T(8,128)(2,1)} %param.17) | copy-start | bytes 3538948
  5.9 2.1 %copy-start.7 = (bf16[1,1536,384]{2,1,0:T(8,128)(2,1)S(1)}, bf16[1,1536,384]{2,1,0:T(8,128)(2,1)}, u32[]{:S(2)}) copy-start(bf16[1,1536,384]{2,1,0:T(8,128)(2,1)} %param.19) | copy-start | bytes 3538948
  5.9 2.1 %copy-start.8 = (f32[1,1536]{1,0:T(1,128)S(1)}, f32[1,1536]{1,0:T(1,128)}, u32[]{:S(2)}) copy-start(f32[1,1536]{1,0:T(1,128)} %bias_ref.2) | copy-start | bytes 18436
  9.7 6.1 %collective-permute-start.3 = (bf16[3,48,384]{2,1,0:T(8,128)(2,1)S(1)}, bf16[3,48,384]{2,1,0:T(8,128)(2,1)S(1)}, u32[]{:S(2)}, u32[]{:S(2)}) collective-permute-start(bf16[3,48,384]{2,1,0:T(8,128)(2,1)S(1)} %get-tuple-element.89), channel_id=1, source_target_pairs={{0,112},{16,0},{32,16},{48,32},{64,48},{80,64},{96,80},{112,96},{1... | collective-permute-start | bytes 331784 | tf_op jit(solution)/shard_map/ppermute | solution.py:912
  11.6 5.4 %copy-start.5 = (f32[1,384]{1,0:T(1,128)S(1)}, f32[1,384]{1,0:T(1,128)}, u32[]{:S(2)}) copy-start(f32[1,384]{1,0:T(1,128)} %gain_ref.3) | copy-start | bytes 4612
  11.6 5.4 %copy-start.9 = (f32[1,384]{1,0:T(1,128)S(1)}, f32[1,384]{1,0:T(1,128)}, u32[]{:S(2)}) copy-start(f32[1,384]{1,0:T(1,128)} %bias_ref.3) | copy-start | bytes 4612
  11.6 5.4 %copy-start.10 = (f32[1,384]{1,0:T(1,128)S(1)}, f32[1,384]{1,0:T(1,128)}, u32[]{:S(2)}) copy-start(f32[1,384]{1,0:T(1,128)} %shift_ref.1) | copy-start | bytes 4612
  11.6 5.4 %collective-permute-start.2 = (bf16[3,48,384]{2,1,0:T(8,128)(2,1)S(1)}, bf16[3,48,384]{2,1,0:T(8,128)(2,1)S(1)}, u32[]{:S(2)}, u32[]{:S(2)}) collective-permute-start(bf16[3,48,384]{2,1,0:T(8,128)(2,1)S(1)} %get-tuple-element.90), channel_id=1, source_target_pairs={{0,16},{16,32},{32,48},{48,64},{64,80},{80,96},{96,112},{112,0},{1... | collective-permute-start | bytes 331784 | tf_op jit(solution)/shard_map/ppermute | solution.py:911
  23.6 3.1 %collective-permute-start.4 = (bf16[768,768]{1,0:T(8,128)(2,1)S(1)}, bf16[768,768]{1,0:T(8,128)(2,1)S(1)}, u32[]{:S(2)}, u32[]{:S(2)}) collective-permute-start(bf16[768,768]{1,0:T(8,128)(2,1)S(1)} %get-tuple-element.99), channel_id=1, source_target_pairs={{0,16},{16,0},{32,48},{48,32},{64,80},{80,64},{96,112},{112,96},{1... | collective-permute-start | bytes 3538952 | tf_op jit(solution)/shard_map/ppermute | solution.py:945
  26.8 8.0 %collective-permute-start.5 = (bf16[192,768]{1,0:T(8,128)(2,1)S(1)}, bf16[192,768]{1,0:T(8,128)(2,1)S(1)}, u32[]{:S(2)}, u32[]{:S(2)}) collective-permute-start(bf16[192,768]{1,0:T(8,128)(2,1)S(1)} %get-tuple-element.100), channel_id=1, source_target_pairs={{0,32},{1,33},{2,34},{3,35},{4,36},{5,37},{6,38},{7,39},{8,40},{9,... | collective-permute-start | bytes 884744 | tf_op jit(solution)/shard_map/ppermute | solution.py:948
  26.9 13.0 %collective-permute-start.6 = (bf16[192,768]{1,0:T(8,128)(2,1)S(1)}, bf16[192,768]{1,0:T(8,128)(2,1)S(1)}, u32[]{:S(2)}, u32[]{:S(2)}) collective-permute-start(bf16[192,768]{1,0:T(8,128)(2,1)S(1)} %get-tuple-element.102), channel_id=1, source_target_pairs={{0,64},{1,65},{2,66},{3,67},{4,68},{5,69},{6,70},{7,71},{8,72},{9,... | collective-permute-start | bytes 884744 | tf_op jit(solution)/shard_map/ppermute | solution.py:949
  32.8 7.6 %collective-permute-start.7 = (bf16[192,768]{1,0:T(8,128)(2,1)S(1)}, bf16[192,768]{1,0:T(8,128)(2,1)S(1)}, u32[]{:S(2)}, u32[]{:S(2)}) collective-permute-start(bf16[192,768]{1,0:T(8,128)(2,1)S(1)} %get-tuple-element.104), channel_id=1, source_target_pairs={{0,96},{1,97},{2,98},{3,99},{4,100},{5,101},{6,102},{7,103},{8,104... | collective-permute-start | bytes 884744 | tf_op jit(solution)/shard_map/ppermute | solution.py:951
  37.0 11.8 %collective-permute-start.9 = (bf16[3,32,384]{2,1,0:T(8,128)(2,1)S(1)}, bf16[3,32,384]{2,1,0:T(8,128)(2,1)S(1)}, u32[]{:S(2)}, u32[]{:S(2)}) collective-permute-start(bf16[3,32,384]{2,1,0:T(8,128)(2,1)S(1)} %get-tuple-element.114), channel_id=1, source_target_pairs={{0,15},{1,0},{2,1},{3,2},{4,3},{5,4},{6,5},{7,6},{8,7},{9,8},{10,9... | collective-permute-start | bytes 221192 | tf_op jit(solution)/shard_map/ppermute | solution.py:906
  40.0 9.7 %collective-permute-start.8 = (bf16[3,32,384]{2,1,0:T(8,128)(2,1)S(1)}, bf16[3,32,384]{2,1,0:T(8,128)(2,1)S(1)}, u32[]{:S(2)}, u32[]{:S(2)}) collective-permute-start(bf16[3,32,384]{2,1,0:T(8,128)(2,1)S(1)} %get-tuple-element.115), channel_id=1, source_target_pairs={{0,1},{1,2},{2,3},{3,4},{4,5},{5,6},{6,7},{7,8},{8,9},{9,10},{10,1... | collective-permute-start | bytes 221192 | tf_op jit(solution)/shard_map/ppermute | solution.py:905
  40.6 8.1 %collective-permute-start.11 = (bf16[48,768]{1,0:T(8,128)(2,1)S(1)}, bf16[48,768]{1,0:T(8,128)(2,1)S(1)}, u32[]{:S(2)}, u32[]{:S(2)}) collective-permute-start(bf16[48,768]{1,0:T(8,128)(2,1)S(1)} %get-tuple-element.120), channel_id=1, source_target_pairs={{0,1},{1,128},{2,3},{3,130},{4,5},{5,132},{6,7},{7,134},{8,9},{9,1... | collective-permute-start | bytes 221192 | tf_op jit(solution)/shard_map/ppermute | solution.py:959
  42.6 6.2 %collective-permute-start.10 = (bf16[48,768]{1,0:T(8,128)(2,1)S(1)}, bf16[48,768]{1,0:T(8,128)(2,1)S(1)}, u32[]{:S(2)}, u32[]{:S(2)}) collective-permute-start(bf16[48,768]{1,0:T(8,128)(2,1)S(1)} %get-tuple-element.121), channel_id=1, source_target_pairs={{0,128},{1,129},{2,130},{3,131},{4,132},{5,133},{6,134},{7,135},{8... | collective-permute-start | bytes 221192 | tf_op jit(solution)/shard_map/ppermute | solution.py:959
  45.3 4.4 %collective-permute-start.12 = (bf16[48,768]{1,0:T(8,128)(2,1)S(1)}, bf16[48,768]{1,0:T(8,128)(2,1)S(1)}, u32[]{:S(2)}, u32[]{:S(2)}) collective-permute-start(bf16[48,768]{1,0:T(8,128)(2,1)S(1)} %get-tuple-element.122), channel_id=1, source_target_pairs={{0,129},{1,0},{2,131},{3,2},{4,133},{5,4},{6,135},{7,6},{8,137},{9... | collective-permute-start | bytes 221192 | tf_op jit(solution)/shard_map/ppermute | solution.py:959
  49.7 11.1 %collective-permute-start.14 = (bf16[3,48,384]{2,1,0:T(8,128)(2,1)S(1)}, bf16[3,48,384]{2,1,0:T(8,128)(2,1)S(1)}, u32[]{:S(2)}, u32[]{:S(2)}) collective-permute-start(bf16[3,48,384]{2,1,0:T(8,128)(2,1)S(1)} %get-tuple-element.133), channel_id=1, source_target_pairs={{0,112},{16,0},{32,16},{48,32},{64,48},{80,64},{96,80},{112,96},{1... | collective-permute-start | bytes 331784 | tf_op jit(solution)/shard_map/ppermute | solution.py:912
  51.6 9.2 %collective-permute-start.13 = (bf16[3,48,384]{2,1,0:T(8,128)(2,1)S(1)}, bf16[3,48,384]{2,1,0:T(8,128)(2,1)S(1)}, u32[]{:S(2)}, u32[]{:S(2)}) collective-permute-start(bf16[3,48,384]{2,1,0:T(8,128)(2,1)S(1)} %get-tuple-element.134), channel_id=1, source_target_pairs={{0,16},{16,32},{32,48},{48,64},{64,80},{80,96},{96,112},{112,0},{1... | collective-permute-start | bytes 331784 | tf_op jit(solution)/shard_map/ppermute | solution.py:911
  51.7 12.6 %collective-permute-start.16 = (bf16[12,768]{1,0:T(8,128)(2,1)S(1)}, bf16[12,768]{1,0:T(8,128)(2,1)S(1)}, u32[]{:S(2)}, u32[]{:S(2)}) collective-permute-start(bf16[12,768]{1,0:T(8,128)(2,1)S(1)} %get-tuple-element.139), channel_id=1, source_target_pairs={{0,4},{1,5},{2,6},{3,7},{4,8},{5,9},{6,10},{7,11},{8,12},{9,13},{1... | collective-permute-start | bytes 55304 | tf_op jit(solution)/shard_map/ppermute | solution.py:965
  56.1 8.2 %collective-permute-start.15 = (bf16[12,768]{1,0:T(8,128)(2,1)S(1)}, bf16[12,768]{1,0:T(8,128)(2,1)S(1)}, u32[]{:S(2)}, u32[]{:S(2)}) collective-permute-start(bf16[12,768]{1,0:T(8,128)(2,1)S(1)} %get-tuple-element.140), channel_id=1, source_target_pairs={{0,8},{1,9},{2,10},{3,11},{4,12},{5,13},{6,14},{7,15},{8,0},{9,1},... | collective-permute-start | bytes 55304 | tf_op jit(solution)/shard_map/ppermute | solution.py:965
  60.6 4.7 %collective-permute-start.17 = (bf16[12,768]{1,0:T(8,128)(2,1)S(1)}, bf16[12,768]{1,0:T(8,128)(2,1)S(1)}, u32[]{:S(2)}, u32[]{:S(2)}) collective-permute-start(bf16[12,768]{1,0:T(8,128)(2,1)S(1)} %get-tuple-element.141), channel_id=1, source_target_pairs={{0,12},{1,13},{2,14},{3,15},{4,0},{5,1},{6,2},{7,3},{8,4},{9,5},{1... | collective-permute-start | bytes 55304 | tf_op jit(solution)/shard_map/ppermute | solution.py:965
  65.4 3.9 %collective-permute-start.18 = (f32[6,768]{1,0:T(8,128)S(1)}, f32[6,768]{1,0:T(8,128)S(1)}, u32[]{:S(2)}, u32[]{:S(2)}) collective-permute-start(f32[6,768]{1,0:T(8,128)S(1)} %get-tuple-element.150), channel_id=1, source_target_pairs={{0,2},{1,3},{2,0},{3,1},{4,6},{5,7},{6,4},{7,5},{8,10},{9,11},{10,... | collective-permute-start | bytes 55304 | tf_op jit(solution)/shard_map/ppermute | solution.py:972
